TPU v7x, 32 devices: a whole 2x2x4 slice. The times are simulated.
32 devices in a mesh: batch: 4 (over y, core), seq: 8 (over z, x).
Axes of the slice: x: 2, y: 2, z: 4, core: 2. Of those that a mesh axis runs over, the one named last changes fastest.
Arguments:
- block_input: bfloat16 [4, 2048, 2048], P('batch', 'seq'), may hold values from -6 to 6
- out_grad: bfloat16 [4, 2048, 2048], P('batch', 'seq'), may hold values from -10 to 10
- norm_gains: float32 [2, 2048], P(None, ('batch', 'seq')), may hold values from 0 to 6
- mixer_weight: float32 [2048, 7680], P(('batch', 'seq')), may hold values from -1 to 1
- gate_weight: float32 [2560, 320], P(('batch', 'seq')), may hold values from -0.25 to 0.25
- chan_params: float32 [8, 2560], P(None, ('batch', 'seq')), may hold values from -3 to 16
- mlp_weight: float32 [2048, 18432], P(('batch', 'seq')), may hold values from -1 to 1
- first_gains: float32 [2, 2048], P(None, ('batch', 'seq')), may hold values from -0.00061035156 to 0.00061035156
- first_mixer: float32 [2048, 7680], P(('batch', 'seq')), may hold values from -0.00021362305 to 0.00021362305
- first_gate: float32 [2560, 320], P(('batch', 'seq')), may hold values from -0.00021362305 to 0.00021362305
- first_chan: float32 [8, 2560], P(None, ('batch', 'seq')), may hold values from -0.00061035156 to 0.00061035156
- first_mlp: float32 [2048, 18432], P(('batch', 'seq')), may hold values from -0.00021362305 to 0.00021362305
- second_gains: float32 [2, 2048], P(None, ('batch', 'seq')), may hold values from 1.10454215e-11 to 1.6568132e-10
- second_mixer: float32 [2048, 7680], P(('batch', 'seq')), may hold values from 9.204517e-12 to 1.4727228e-10
- second_gate: float32 [2560, 320], P(('batch', 'seq')), may hold values from 9.204517e-12 to 1.4727228e-10
- second_chan: float32 [8, 2560], P(None, ('batch', 'seq')), may hold values from 8.284066e-11 to 1.3254505e-09
- second_mlp: float32 [2048, 18432], P(('batch', 'seq')), may hold values from 9.204517e-12 to 1.4727228e-10
Outputs:
- block_output: bfloat16 [4, 2048, 2048], P('batch', 'seq')
- input_grad: float32 [4, 2048, 2048], P('batch', 'seq')
- grad_norm: float32 [], replicated
- new_first_gains: float32 [2, 2048], P(None, ('batch', 'seq'))
- new_second_gains: float32 [2, 2048], P(None, ('batch', 'seq'))
- new_gains: float32 [2, 2048], P(None, ('batch', 'seq'))
- new_first_mixer: float32 [2048, 7680], P(('batch', 'seq'))
- new_second_mixer: float32 [2048, 7680], P(('batch', 'seq'))
- new_mixer: float32 [2048, 7680], P(('batch', 'seq'))
- new_first_gate: float32 [2560, 320], P(('batch', 'seq'))
- new_second_gate: float32 [2560, 320], P(('batch', 'seq'))
- new_gate: float32 [2560, 320], P(('batch', 'seq'))
- new_first_chan: float32 [8, 2560], P(None, ('batch', 'seq'))
- new_second_chan: float32 [8, 2560], P(None, ('batch', 'seq'))
- new_chan: float32 [8, 2560], P(None, ('batch', 'seq'))
- new_first_mlp: float32 [2048, 18432], P(('batch', 'seq'))
- new_second_mlp: float32 [2048, 18432], P(('batch', 'seq'))
- new_mlp: float32 [2048, 18432], P(('batch', 'seq'))
All inputs are finite; a program needn't handle non-finite values.
Results may differ from a plain program's by a relative error of at most 0.017.
Values may be sent and summed in bfloat16 or wider, within the bound.
A program may use at most 704 MiB of HBM per device.

v0:
```python
import jax
import jax.numpy as jnp
from jax import lax
from jax.sharding import PartitionSpec as P

STEP = 10


norm_eps = 1e-06
clip_limit = 1.0
beta_first = 0.9
beta_second = 0.999
adam_eps = 1e-08
rate_matrix = 0.05
rate_gains = 0.8
rate_channel = 2.0
decay_matrix = 0.1


def from_behind(block, axis, distance):
    devices = range(lax.axis_size(axis))
    route = [(i - distance, i) for i in devices if i - distance in devices]
    return lax.ppermute(block, axis, route)


def entering(x, axis, combine, identity, reverse):
    length, mine = (lax.axis_size(axis), lax.axis_index(axis))
    everything = jax.tree.map(lambda part: lax.all_gather(part, axis), x)
    start = jax.tree.map(
        lambda part, zero: jnp.broadcast_to(jnp.asarray(zero, part.dtype), part.shape), x, identity
    )

    def step(k, before):
        at = length - 1 - k if reverse else k
        reached = at > mine if reverse else at < mine
        new = combine(before, jax.tree.map(lambda part: part[at], everything))
        return jax.tree.map(lambda a, b: jnp.where(reached, a, b), new, before)

    return lax.fori_loop(0, length, step, start)


def link(earlier, later):
    return (earlier[0] * later[0], later[0] * earlier[1] + later[1])


def coefficients(conv_value, pre_recur, pre_input, lambda_row):
    recur_gate = jax.nn.sigmoid(pre_recur)
    input_gate = jax.nn.sigmoid(pre_input)
    log_decay = -8.0 * jax.nn.softplus(-lambda_row) * recur_gate
    decays = jnp.exp(log_decay)
    scale_in = jnp.sqrt(-jnp.expm1(2.0 * log_decay))
    return (decays, scale_in * input_gate * conv_value)


def gelu_product(gate_up):
    half_width = gate_up.shape[1] // 2
    return jax.nn.gelu(gate_up[:, :half_width]) * gate_up[:, half_width:]


def normalize(values, gain):
    inverse = lax.rsqrt(jnp.mean(values * values, axis=-1, keepdims=True) + norm_eps)
    scaled = values * inverse
    return (scaled, inverse, (scaled * gain).astype(jnp.bfloat16))


def normalize_back(grad_normed, scaled, inverse, gain):
    grad_scaled = grad_normed * gain
    gain_grad = jnp.sum(grad_normed * scaled, axis=0)
    inner = jnp.mean(grad_scaled * scaled, axis=-1, keepdims=True)
    return (inverse * (grad_scaled - scaled * inner), gain_grad)


def contract_last(left, right):
    return lax.dot_general(
        left, right, (((1,), (1,)), ((), ())), preferred_element_type=jnp.float32
    )


def contract_first(left, right):
    return lax.dot_general(
        left, right, (((0,), (0,)), ((), ())), preferred_element_type=jnp.float32
    )


def adam_step(weight, grad, first, second, factor, rate, decay_rate):
    clipped = grad * factor
    first_new = beta_first * first + (1.0 - beta_first) * clipped
    second_new = beta_second * second + (1.0 - beta_second) * clipped * clipped
    first_hat = first_new / (1.0 - beta_first**STEP)
    second_hat = second_new / (1.0 - beta_second**STEP)
    weight_new = weight - rate * (
        first_hat / (jnp.sqrt(second_hat) + adam_eps) + decay_rate * weight
    )
    return (first_new, second_new, weight_new)


def on_device(
    block_input,
    out_grad,
    norm_gains,
    mixer_weight,
    gate_weight,
    chan_params,
    mlp_weight,
    first_gains,
    first_mixer,
    first_gate,
    first_chan,
    first_mlp,
    second_gains,
    second_mixer,
    second_gate,
    second_chan,
    second_mlp,
):
    inputs = block_input[0].astype(jnp.float32)
    cotangent = out_grad[0].astype(jnp.float32)
    tokens = inputs.shape[0]
    lru_width = mixer_weight.shape[1] // 3
    hidden_width = mlp_weight.shape[1] // 3
    head_dim = gate_weight.shape[1] // 2
    head_count = lru_width // head_dim
    mixer_parts = (
        norm_gains.astype(jnp.bfloat16),
        mixer_weight.astype(jnp.bfloat16),
        gate_weight.astype(jnp.bfloat16),
        chan_params.astype(jnp.bfloat16),
    )
    gains_full, mixer_full, gate_full, chan_full = (
        lax.all_gather(mixer_parts[0], ("batch", "seq"), axis=1, tiled=True),
        lax.all_gather(mixer_parts[1], ("batch", "seq"), axis=0, tiled=True),
        lax.all_gather(mixer_parts[2], ("batch", "seq"), axis=0, tiled=True),
        lax.all_gather(mixer_parts[3], ("batch", "seq"), axis=1, tiled=True),
    )
    channel = chan_full.astype(jnp.float32)
    scaled_one, inverse_one, normed_one = normalize(inputs, gains_full[0].astype(jnp.float32))
    projected = jnp.dot(
        normed_one, mixer_full[:, : 2 * lru_width], preferred_element_type=jnp.float32
    )
    branch_gate = projected[:, :lru_width]
    branch_conv = projected[:, lru_width:].astype(jnp.bfloat16)
    previous = from_behind(branch_conv[tokens - 3 :], "seq", 1)
    extended = jnp.concatenate([previous, branch_conv], axis=0).astype(jnp.float32)
    conv_sum = channel[4]
    for tap_index in range(4):
        conv_sum = conv_sum + channel[tap_index] * extended[3 - tap_index : 3 - tap_index + tokens]
    conv_low = conv_sum.astype(jnp.bfloat16)
    conv_value = conv_low.astype(jnp.float32)
    gate_pre = jnp.einsum(
        "thi,hij->thj",
        conv_low.reshape(tokens, head_count, head_dim),
        gate_full.reshape(head_count, head_dim, 2 * head_dim),
        preferred_element_type=jnp.float32,
    )
    pre_recur = gate_pre[:, :, :head_dim].reshape(tokens, lru_width) + channel[5]
    pre_input = gate_pre[:, :, head_dim:].reshape(tokens, lru_width) + channel[6]
    (decays, drive_terms), coeff_back = jax.vjp(
        coefficients, conv_value, pre_recur, pre_input, channel[7]
    )
    prefix_decay, local_states = lax.associative_scan(link, (decays, drive_terms))
    identity_pair = (jnp.ones((lru_width,), jnp.float32), jnp.zeros((lru_width,), jnp.float32))
    carry_decay, carry_state = entering(
        (prefix_decay[-1], local_states[-1]), "seq", link, identity_pair, False
    )
    states = local_states + prefix_decay * carry_state
    gelu_gate, gelu_back = jax.vjp(jax.nn.gelu, branch_gate)
    mixed_low = (states * gelu_gate).astype(jnp.bfloat16)
    mixer_out = contract_last(mixed_low, mixer_full[:, 2 * lru_width :])
    residual = inputs + mixer_out
    scaled_two, inverse_two, normed_two = normalize(residual, gains_full[1].astype(jnp.float32))
    grad_out_low = cotangent.astype(jnp.bfloat16)
    mlp_full = lax.all_gather(mlp_weight.astype(jnp.bfloat16), ("batch", "seq"), axis=0, tiled=True)
    gate_up = jnp.dot(
        normed_two, mlp_full[:, : 2 * hidden_width], preferred_element_type=jnp.float32
    )
    hidden_value, hidden_back = jax.vjp(gelu_product, gate_up)
    hidden_low = hidden_value.astype(jnp.bfloat16)
    mlp_out = contract_last(hidden_low, mlp_full[:, 2 * hidden_width :])
    grad_hidden = jnp.dot(
        grad_out_low, mlp_full[:, 2 * hidden_width :], preferred_element_type=jnp.float32
    )
    (grad_gate_up,) = hidden_back(grad_hidden)
    grad_gu_low = grad_gate_up.astype(jnp.bfloat16)
    grad_normed_two = contract_last(grad_gu_low, mlp_full[:, : 2 * hidden_width])
    mlp_grad = lax.psum_scatter(
        jnp.concatenate(
            [contract_first(normed_two, grad_gu_low), contract_first(grad_out_low, hidden_low)],
            axis=1,
        ),
        ("batch", "seq"),
        scatter_dimension=0,
        tiled=True,
    )
    block_output = (residual + mlp_out).astype(jnp.bfloat16)
    grad_from_second, gain_two_grad = normalize_back(
        grad_normed_two, scaled_two, inverse_two, gains_full[1].astype(jnp.float32)
    )
    grad_residual = cotangent + grad_from_second
    grad_mixer_out = grad_residual.astype(jnp.bfloat16)
    grad_mixed = jnp.dot(
        grad_mixer_out, mixer_full[:, 2 * lru_width :], preferred_element_type=jnp.float32
    )
    out_proj_grad = contract_first(grad_mixer_out, mixed_low)
    grad_states = grad_mixed * gelu_gate
    (grad_branch_gate,) = gelu_back(grad_mixed * states)
    shifted_decay = jnp.concatenate([decays[1:], jnp.ones((1, lru_width), jnp.float32)], axis=0)
    suffix_decay, local_grads = lax.associative_scan(
        link, (shifted_decay, grad_states), reverse=True
    )
    carry_back, incoming = entering(
        (prefix_decay[-1], decays[0] * local_grads[0]), "seq", link, identity_pair, True
    )
    grad_total = local_grads + suffix_decay * incoming
    state_before = jnp.concatenate([carry_state[None, :], states[:-1]], axis=0)
    grad_conv_rec, grad_pre_recur, grad_pre_input, grad_lambda = coeff_back(
        (grad_total * state_before, grad_total)
    )
    grad_recur_low = grad_pre_recur.astype(jnp.bfloat16)
    grad_input_low = grad_pre_input.astype(jnp.bfloat16)
    grad_gates = jnp.concatenate(
        [
            grad_recur_low.reshape(tokens, head_count, head_dim),
            grad_input_low.reshape(tokens, head_count, head_dim),
        ],
        axis=2,
    )
    gate_term = jnp.einsum(
        "thi,thj->hij",
        conv_low.reshape(tokens, head_count, head_dim),
        grad_gates,
        preferred_element_type=jnp.float32,
    ).reshape(lru_width, 2 * head_dim)
    grad_conv_gate = jnp.einsum(
        "thj,hij->thi",
        grad_gates,
        gate_full.reshape(head_count, head_dim, 2 * head_dim),
        preferred_element_type=jnp.float32,
    ).reshape(tokens, lru_width)
    grad_conv_low = (grad_conv_gate + grad_conv_rec).astype(jnp.bfloat16)
    following = from_behind(grad_conv_low[:3], "seq", -1)
    grad_extended = jnp.concatenate([grad_conv_low, following], axis=0).astype(jnp.float32)
    grad_conv_value = grad_conv_low.astype(jnp.float32)
    tap_grads = [
        jnp.sum(grad_conv_value * extended[3 - tap_index : 3 - tap_index + tokens], axis=0)
        for tap_index in range(4)
    ]
    grad_branch_conv = channel[0] * grad_extended[0:tokens]
    for tap_index in range(1, 4):
        grad_branch_conv = (
            grad_branch_conv + channel[tap_index] * grad_extended[tap_index : tap_index + tokens]
        )
    chan_term = jnp.stack(
        tap_grads
        + [
            jnp.sum(grad_conv_value, axis=0),
            jnp.sum(grad_recur_low.astype(jnp.float32), axis=0),
            jnp.sum(grad_input_low.astype(jnp.float32), axis=0),
            grad_lambda,
        ]
    )
    grad_projected = jnp.concatenate(
        [grad_branch_gate.astype(jnp.bfloat16), grad_branch_conv.astype(jnp.bfloat16)], axis=1
    )
    mixer_term = jnp.concatenate(
        [contract_first(normed_one, grad_projected), out_proj_grad], axis=1
    )
    grad_normed_one = contract_last(grad_projected, mixer_full[:, : 2 * lru_width])
    grad_from_first, gain_one_grad = normalize_back(
        grad_normed_one, scaled_one, inverse_one, gains_full[0].astype(jnp.float32)
    )
    input_grad = grad_residual + grad_from_first
    gains_term = jnp.stack([gain_one_grad, gain_two_grad])
    gains_grad, mixer_grad, gate_grad, chan_grad = (
        lax.psum_scatter(gains_term, ("batch", "seq"), scatter_dimension=1, tiled=True),
        lax.psum_scatter(mixer_term, ("batch", "seq"), scatter_dimension=0, tiled=True),
        lax.psum_scatter(gate_term, ("batch", "seq"), scatter_dimension=0, tiled=True),
        lax.psum_scatter(chan_term, ("batch", "seq"), scatter_dimension=1, tiled=True),
    )
    local_squares = (
        jnp.sum(gains_grad * gains_grad)
        + jnp.sum(mixer_grad * mixer_grad)
        + jnp.sum(gate_grad * gate_grad)
        + jnp.sum(chan_grad * chan_grad)
        + jnp.sum(mlp_grad * mlp_grad)
    )
    total_squares = lax.psum(local_squares, ("batch", "seq"))
    grad_norm = jnp.sqrt(total_squares)
    factor = clip_limit / jnp.maximum(grad_norm, clip_limit)
    gains_up = adam_step(norm_gains, gains_grad, first_gains, second_gains, factor, rate_gains, 0.0)
    mixer_up = adam_step(
        mixer_weight, mixer_grad, first_mixer, second_mixer, factor, rate_matrix, decay_matrix
    )
    gate_up_new = adam_step(
        gate_weight, gate_grad, first_gate, second_gate, factor, rate_matrix, decay_matrix
    )
    chan_up = adam_step(chan_params, chan_grad, first_chan, second_chan, factor, rate_channel, 0.0)
    mlp_up = adam_step(
        mlp_weight, mlp_grad, first_mlp, second_mlp, factor, rate_matrix, decay_matrix
    )
    return (
        block_output[None],
        input_grad[None],
        grad_norm,
        gains_up[0],
        gains_up[1],
        gains_up[2],
        mixer_up[0],
        mixer_up[1],
        mixer_up[2],
        gate_up_new[0],
        gate_up_new[1],
        gate_up_new[2],
        chan_up[0],
        chan_up[1],
        chan_up[2],
        mlp_up[0],
        mlp_up[1],
        mlp_up[2],
    )


def solution(mesh):
    in_specs = (
        P("batch", "seq", None),
        P("batch", "seq", None),
        P(None, ("batch", "seq")),
        P(("batch", "seq"), None),
        P(("batch", "seq"), None),
        P(None, ("batch", "seq")),
        P(("batch", "seq"), None),
        P(None, ("batch", "seq")),
        P(("batch", "seq"), None),
        P(("batch", "seq"), None),
        P(None, ("batch", "seq")),
        P(("batch", "seq"), None),
        P(None, ("batch", "seq")),
        P(("batch", "seq"), None),
        P(("batch", "seq"), None),
        P(None, ("batch", "seq")),
        P(("batch", "seq"), None),
    )
    out_specs = (
        P("batch", "seq", None),
        P("batch", "seq", None),
        P(),
        P(None, ("batch", "seq")),
        P(None, ("batch", "seq")),
        P(None, ("batch", "seq")),
        P(("batch", "seq"), None),
        P(("batch", "seq"), None),
        P(("batch", "seq"), None),
        P(("batch", "seq"), None),
        P(("batch", "seq"), None),
        P(("batch", "seq"), None),
        P(None, ("batch", "seq")),
        P(None, ("batch", "seq")),
        P(None, ("batch", "seq")),
        P(("batch", "seq"), None),
        P(("batch", "seq"), None),
        P(("batch", "seq"), None),
    )
    return jax.shard_map(
        on_device, mesh=mesh, in_specs=in_specs, out_specs=out_specs, check_vma=False
    )
```

profile of v0, /device:TPU:0, one launch (start us, length us, event | category | flops | bytes accessed | tf_op | source)
XLA Modules:
  0.0 3323.8 jit_solution(8219152854268600894)
XLA Ops:
  14.8 70.5 %all-gather.1 = bf16[32,64,2]{1,2,0:T(2,128)(2,1)S(1)} all-gather(bf16[1,64,2]{1,2,0:T(2,128)(2,1)S(1)} %convert_bitcast_fusion.1), channel_id=1, replica_groups=mesh['batch'=4,'seq'=8] {'batch','seq'}, dimensions={0}, use_global_device_ids=true | all-gather | bytes 8448 | tf_op jit(solution)/shard_map/all_gather | solution.py:130
  85.4 65.5 %all-gather = bf16[32,80,8]{1,2,0:T(8,128)(2,1)S(1)} all-gather(bf16[1,80,8]{1,2,0:T(8,128)(2,1)S(1)} %convert_bitcast_fusion), channel_id=1, replica_groups=mesh['batch'=4,'seq'=8] {'batch','seq'}, dimensions={0}, use_global_device_ids=true | all-gather | bytes 42240 | tf_op jit(solution)/shard_map/all_gather | solution.py:133
  151.5 48.9 %all-gather.9.cloned.1.call-done = bf16[2048,7680]{1,0:T(8,128)(2,1)} async-done(((bf16[64,7680]{1,0:T(8,128)(2,1)}), bf16[2048,7680]{1,0:T(8,128)(2,1)}) %all-gather.9.cloned.1.call-update) | async-done | bytes 31457296 | tf_op jit(solution)/shard_map/all_gather | solution.py:131
  200.4 11.4 fusion.132
  223.3 35.0 %all-gather.11.cloned.1.call-done = bf16[2560,320]{1,0:T(8,128)(2,1)} async-done(((bf16[80,320]{1,0:T(8,128)(2,1)}), bf16[2560,320]{1,0:T(8,128)(2,1)}) %all-gather.11.cloned.1.call-update) | async-done | bytes 1638416 | tf_op jit(solution)/shard_map/all_gather | solution.py:132
  271.1 7.0 convert_multiply_fusion.5
  280.2 5.7 slice.678
  286.0 5.7 slice.624
  291.7 5.6 slice.623
  374.7 4.9 pad.217
  385.0 9.0 pad.235
  396.5 9.2 pad.219
  405.7 4.2 fusion.74
  411.1 9.4 pad.234
  421.4 31.1 all-gather.2
  455.0 9.1 pad.218
  465.0 38.9 %all-gather.3 = f32[8,1,2560]{2,1,0:T(1,128)S(1)} all-gather(f32[1,1,2560]{2,1,0:T(1,128)S(1)} %add_bitcast_fusion), channel_id=1, replica_groups=mesh['batch'=4,'seq'=8] {'seq'}, dimensions={0}, use_global_device_ids=true | all-gather | bytes 92160 | tf_op jit(solution)/shard_map/all_gather | solution.py:28
  505.4 10.7 slice.715
  516.1 10.7 slice.706
  526.9 10.7 slice.708
  537.6 7.2 multiply_convert_fusion.1
  544.8 6.2 multiply_reduce_fusion.4
  551.1 107.7 %all-gather.13.cloned.1.call-done = bf16[2048,18432]{1,0:T(8,128)(2,1)} async-done(((bf16[64,18432]{1,0:T(8,128)(2,1)}), bf16[2048,18432]{1,0:T(8,128)(2,1)}) %all-gather.13.cloned.1.call-update) | async-done | bytes 75497488 | tf_op jit(solution)/shard_map/all_gather | solution.py:172
  658.9 25.8 fusion.2
  684.7 22.7 fusion.60
  707.4 26.5 multiply_reduce_fusion.2
  736.9 8.7 fusion.38
  747.7 5.6 slice.767
  757.5 5.6 slice.709
  763.0 10.7 slice.710
  773.7 6.5 slice.712
  850.2 6.7 slice.768
  887.3 4.9 pad.266
  892.1 4.8 pad.267
  896.9 4.9 pad.251
  909.1 5.2 pad.252
  914.3 9.2 pad.253
  924.6 4.4 add.680
  929.0 8.7 fusion.81
  939.9 12.9 rev.8
  952.8 30.6 all-gather.4
  983.4 8.0 while.31
  991.4 4.4 pad.268
  995.8 9.2 pad.269
  1008.7 21.0 rev.9
  1029.7 8.4 multiply_reduce_fusion.1
  1038.1 5.8 convert_reduce_fusion.2
  1048.8 4.6 fusion.72
  1056.6 6.7 fusion.46
  1071.0 11.8 fusion.67
  1087.0 4.7 fusion.71
  1093.0 17.7 fusion.70
  1110.7 42.1 %pad_maximum_fusion.1 = f32[2048,7680]{1,0:T(8,128)} fusion(f32[2048,2560]{1,0:T(8,128)} %fusion.81, f32[2048,5120]{1,0:T(8,128)} %fusion.70), kind=kLoop, calls=%fused_computation.7 | loop fusion | flops 15728640 | bytes 125829120 | tf_op jit(solution)/shard_map/concatenate | solution.py:264
  1154.1 21.5 convolution_bitcast_fusion
  1175.6 37.5 %fusion.78 = f32[2048,12288]{1,0:T(8,128)} fusion(f32[256,6144]{1,0:T(8,128)} %get-tuple-element.350, f32[256,6144]{1,0:T(8,128)} %get-tuple-element.349, f32[256,2048]{1,0:T(8,128)S(1)} %copy-done.20, f32[2048]{0:T(1024)S(1)} %bitcast.106, f32[256]{0:T(256)S(1)} %copy-done.70), kind=kOutput, calls=%fused_computation.144 | convolution fusion | flops 12892766208 | bytes 115352576 | tf_op jit(solution)/shard_map/dot_general | solution.py:80
  1213.1 98.4 %pad_maximum_fusion = f32[2048,18432]{1,0:T(8,128)} fusion(f32[2048,6144]{1,0:T(8,128)} %convolution_bitcast_fusion, f32[2048,12288]{1,0:T(8,128)} %fusion.78), kind=kLoop, calls=%fused_computation.6 | loop fusion | flops 37748736 | bytes 301989888 | tf_op jit(solution)/shard_map/concatenate | solution.py:186
  1311.5 13.6 fusion.57
  1326.6 23.9 reduce-scatter.18.cloned.1.call-done
  1352.0 104.7 %reduce-scatter.12.cloned.1.call-done = f32[80,320]{1,0:T(8,128)} async-done(((f32[2560,320]{1,0:T(8,128)}), f32[80,320]{1,0:T(8,128)}) %reduce-scatter.12.cloned.1.call-update) | async-done | bytes 102416 | tf_op jit(solution)/shard_map/reduce_scatter | solution.py:276
  1458.2 518.0 %reduce-scatter.10.cloned.1.call-done = f32[64,7680]{1,0:T(8,128)} async-done(((f32[2048,7680]{1,0:T(8,128)}), f32[64,7680]{1,0:T(8,128)}) %reduce-scatter.10.cloned.1.call-update) | async-done | bytes 1966096 | tf_op jit(solution)/shard_map/reduce_scatter | solution.py:275
  1981.6 1265.8 %reduce-scatter.14.cloned.1.call-done = f32[64,18432]{1,0:T(8,128)} async-done(((f32[2048,18432]{1,0:T(8,128)}), f32[64,18432]{1,0:T(8,128)}) %reduce-scatter.14.cloned.1.call-update) | async-done | bytes 4718608 | tf_op jit(solution)/shard_map/reduce_scatter | solution.py:185
  3256.3 39.6 %psum.7 = f32[]{:T(128)} all-reduce(f32[]{:T(128)S(6)} %add.698), channel_id=1, replica_groups=mesh['batch'=4,'seq'=8] {'batch','seq'}, use_global_device_ids=true, to_apply=%region_28.29 | all-reduce | flops 1 | bytes 8 | tf_op jit(solution)/shard_map/psum | solution.py:286
  3298.7 7.5 multiply_subtract_fusion.1
  3307.6 8.0 multiply_subtract_fusion
  (595 shorter events, 298.6 us)
Async XLA Ops:
  7.2 193.2 %all-gather.9.cloned.1.call-start = ((), (), s32[]{:S(2)}) async-start(), calls=%async_computation.5 | async-start | bytes 32440320 | tf_op jit(solution)/shard_map/all_gather | solution.py:131
  9.9 248.5 %all-gather.11.cloned.1.call-start = ((), (), s32[]{:S(2)}) async-start(), calls=%async_computation.6 | async-start | bytes 2027520 | tf_op jit(solution)/shard_map/all_gather | solution.py:132
  10.6 74.8 %copy-start.109 = (f32[8,80]{1,0:T(8,128)S(1)}, f32[8,80]{1,0:T(8,128)}, u32[]{:S(2)}) copy-start(f32[8,80]{1,0:T(8,128)} %param.26) | copy-start | bytes 7684
  10.6 648.2 %all-gather.13.cloned.1.call-start = ((), (), s32[]{:S(2)}) async-start(), calls=%async_computation.7 | async-start | bytes 77856768 | tf_op jit(solution)/shard_map/all_gather | solution.py:172
  14.7 136.4 %copy-start.13 = (bf16[1,256,2048]{2,1,0:T(8,128)(2,1)S(1)}, bf16[1,256,2048]{2,1,0:T(8,128)(2,1)}, u32[]{:S(2)}) copy-start(bf16[1,256,2048]{2,1,0:T(8,128)(2,1)} %param.21) | copy-start | bytes 3145732
  14.7 1310.4 %reduce-scatter.16.cloned.1.call-start = ((), (), s32[]{:S(2)}) async-start(), calls=%async_computation.11 | async-start | bytes 1081344
  151.1 64.8 %copy-start.68 = (f32[2560,8]{0,1:T(8,128)}, f32[2560,8]{0,1:T(8,128)S(1)}, u32[]{:S(2)}) copy-start(f32[2560,8]{0,1:T(8,128)S(1)} %reshape.121) | copy-start | bytes 245764
  151.4 60.3 %copy-start.106 = (f32[256]{0:T(256)}, f32[256]{0:T(256)S(1)}, u32[]{:S(2)}) copy-start(f32[256]{0:T(256)S(1)} %add_rsqrt_fusion.1) | copy-start | bytes 3076
  151.4 60.3 %copy-start.80 = (f32[1,2048]{1,0:T(1,128)}, f32[1,2048]{1,0:T(1,128)S(1)}, u32[]{:S(2)}) copy-start(f32[1,2048]{1,0:T(1,128)S(1)} %get-tuple-element.431) | copy-start | bytes 24580
  151.5 582.4 %copy-start.48 = (f32[1,2048]{1,0:T(1,128)}, f32[1,2048]{1,0:T(1,128)S(1)}, u32[]{:S(2)}) copy-start(f32[1,2048]{1,0:T(1,128)S(1)} %get-tuple-element.430) | copy-start | bytes 24580
  213.3 4.8 collective-permute-start
  216.6 54.5 %copy-start.58 = (f32[2560]{0:T(1024)}, f32[2560]{0:T(1024)S(1)}, u32[]{:S(2)}) copy-start(f32[2560]{0:T(1024)S(1)} %get-tuple-element.293) | copy-start | bytes 30724
  216.6 54.5 %copy-start.60 = (f32[2560]{0:T(1024)}, f32[2560]{0:T(1024)S(1)}, u32[]{:S(2)}) copy-start(f32[2560]{0:T(1024)S(1)} %get-tuple-element.294) | copy-start | bytes 30724
  216.6 54.5 %copy-start.62 = (f32[2560]{0:T(1024)}, f32[2560]{0:T(1024)S(1)}, u32[]{:S(2)}) copy-start(f32[2560]{0:T(1024)S(1)} %get-tuple-element.295) | copy-start | bytes 30724
  216.6 54.5 %copy-start.64 = (f32[2560]{0:T(1024)}, f32[2560]{0:T(1024)S(1)}, u32[]{:S(2)}) copy-start(f32[2560]{0:T(1024)S(1)} %get-tuple-element.296) | copy-start | bytes 30724
  216.6 54.5 %copy-start.72 = (f32[2560]{0:T(1024)}, f32[2560]{0:T(1024)S(1)}, u32[]{:S(2)}) copy-start(f32[2560]{0:T(1024)S(1)} %get-tuple-element.291) | copy-start | bytes 30724
  216.6 54.5 %copy-start.74 = (f32[2560]{0:T(1024)}, f32[2560]{0:T(1024)S(1)}, u32[]{:S(2)}) copy-start(f32[2560]{0:T(1024)S(1)} %get-tuple-element.292) | copy-start | bytes 30724
  216.6 54.5 %copy-start.76 = (f32[2560]{0:T(1024)}, f32[2560]{0:T(1024)S(1)}, u32[]{:S(2)}) copy-start(f32[2560]{0:T(1024)S(1)} %get-tuple-element.400) | copy-start | bytes 30724
  216.6 54.5 %copy-start.78 = (f32[2560]{0:T(1024)}, f32[2560]{0:T(1024)S(1)}, u32[]{:S(2)}) copy-start(f32[2560]{0:T(1024)S(1)} %get-tuple-element.297) | copy-start | bytes 30724
  218.5 52.7 %copy-start = (f32[259,2560]{1,0:T(8,128)}, f32[259,2560]{1,0:T(8,128)S(1)}, u32[]{:S(2)}) copy-start(f32[259,2560]{1,0:T(8,128)S(1)} %maximum_convert_fusion) | copy-start | bytes 7956484
  411.1 41.4 %copy-start.103 = (f32[1,2560]{1,0:T(1,128)S(1)}, f32[1,2560]{1,0:T(1,128)}, u32[]{:S(2)}) copy-start(f32[1,2560]{1,0:T(1,128)} %slice.808) | copy-start | bytes 30724
  504.8 22.1 copy-start.67
  551.1 156.3 %copy-start.19 = (f32[256,2048]{1,0:T(8,128)}, f32[256,2048]{1,0:T(8,128)S(1)}, u32[]{:S(2)}) copy-start(f32[256,2048]{1,0:T(8,128)S(1)} %get-tuple-element.435) | copy-start | bytes 6291460
  551.1 182.7 %copy-start.69 = (f32[256]{0:T(256)}, f32[256]{0:T(256)S(1)}, u32[]{:S(2)}) copy-start(f32[256]{0:T(256)S(1)} %add_rsqrt_fusion) | copy-start | bytes 3076
  658.9 25.8 copy-start.35
  736.8 192.2 %copy-start.6 = (f32[256,2048]{1,0:T(8,128)}, f32[256,2048]{1,0:T(8,128)S(1)}, u32[]{:S(2)}) copy-start(f32[256,2048]{1,0:T(8,128)S(1)} %multiply_add_fusion.3) | copy-start | bytes 6291460
  810.7 39.5 %copy-start.32 = (f32[127,2560]{1,0:T(8,128)S(1)}, f32[127,2560]{1,0:T(8,128)}, u32[]{:S(2)}) copy-start(f32[127,2560]{1,0:T(8,128)} %slice.767) | copy-start | bytes 3901444
  843.7 18.2 copy-start.71
  939.9 43.4 %copy-start.66 = (f32[2560]{0:T(1024)S(1)}, f32[2560]{0:T(1024)}, u32[]{:S(2)}) copy-start(f32[2560]{0:T(1024)} %custom-call.1) | copy-start | bytes 30724
  1008.6 21.0 copy-start.1
  1008.6 21.0 copy-start.59
  1008.6 21.0 copy-start.61
  1008.6 21.0 copy-start.63
  1008.6 21.0 copy-start.65
  1008.6 21.0 copy-start.73
  1008.6 21.0 copy-start.75
  1008.6 21.0 copy-start.77
  1008.6 21.0 copy-start.79
  1008.6 21.0 copy-start.86
  1063.3 5.7 collective-permute-start.1
  1070.5 12.2 copy-start.28
  1071.0 13.2 copy-start.90
  1084.1 266.4 %reduce-scatter.18.cloned.1.call-start = ((), (), s32[]{:S(2)}) async-start(), calls=%async_computation.12 | async-start | bytes 1351680
  1086.9 369.8 %reduce-scatter.12.cloned.1.call-start = ((), (), s32[]{:S(2)}) async-start(), calls=%async_computation.9 | async-start | bytes 4055040 | tf_op jit(solution)/shard_map/reduce_scatter | solution.py:276
  1091.7 884.5 %reduce-scatter.10.cloned.1.call-start = ((), (), s32[]{:S(2)}) async-start(), calls=%async_computation.8 | async-start | bytes 64880640 | tf_op jit(solution)/shard_map/reduce_scatter | solution.py:275
  1152.9 2094.5 %reduce-scatter.14.cloned.1.call-start = ((), (), s32[]{:S(2)}) async-start(), calls=%async_computation.10 | async-start | bytes 155713536 | tf_op jit(solution)/shard_map/reduce_scatter | solution.py:185
  1154.1 21.5 copy-start.20
  1154.1 21.5 copy-start.49
  1154.1 21.5 copy-start.70
  1311.5 13.6 copy-start.118
  1978.8 1273.4 %copy-start.7 = (f32[256,2048]{1,0:T(8,128)S(1)}, f32[256,2048]{1,0:T(8,128)}, u32[]{:S(2)}) copy-start(f32[256,2048]{1,0:T(8,128)} %copy-done.6) | copy-start | bytes 6291460
  1978.8 1273.4 %copy-start.82 = (f32[1,2048]{1,0:T(1,128)S(1)}, f32[1,2048]{1,0:T(1,128)}, u32[]{:S(2)}) copy-start(f32[1,2048]{1,0:T(1,128)} %copy-done.80) | copy-start | bytes 24580
  1978.9 1273.4 %copy-start.108 = (f32[256]{0:T(256)S(1)}, f32[256]{0:T(256)}, u32[]{:S(2)}) copy-start(f32[256]{0:T(256)} %copy-done.106) | copy-start | bytes 3076
  3252.3 44.3 %copy-start.115 = (f32[2,64]{1,0:T(2,128)S(1)}, f32[2,64]{1,0:T(2,128)}, u32[]{:S(2)}) copy-start(f32[2,64]{1,0:T(2,128)} %param.23) | copy-start | bytes 1540
  3252.3 44.3 %copy-start.116 = (f32[2,64]{1,0:T(2,128)S(1)}, f32[2,64]{1,0:T(2,128)}, u32[]{:S(2)}) copy-start(f32[2,64]{1,0:T(2,128)} %param.33) | copy-start | bytes 1540
  3252.3 44.3 %copy-start.117 = (f32[2,64]{1,0:T(2,128)S(1)}, f32[2,64]{1,0:T(2,128)}, u32[]{:S(2)}) copy-start(f32[2,64]{1,0:T(2,128)} %param.28) | copy-start | bytes 1540
  3252.3 44.9 %copy-start.110 = (f32[8,80]{1,0:T(8,128)S(1)}, f32[8,80]{1,0:T(8,128)}, u32[]{:S(2)}) copy-start(f32[8,80]{1,0:T(8,128)} %param.26) | copy-start | bytes 7684
  3252.3 44.9 %copy-start.112 = (f32[8,80]{1,0:T(8,128)S(1)}, f32[8,80]{1,0:T(8,128)}, u32[]{:S(2)}) copy-start(f32[8,80]{1,0:T(8,128)} %param.36) | copy-start | bytes 7684
  3252.3 44.9 %copy-start.113 = (f32[8,80]{1,0:T(8,128)S(1)}, f32[8,80]{1,0:T(8,128)}, u32[]{:S(2)}) copy-start(f32[8,80]{1,0:T(8,128)} %param.31) | copy-start | bytes 7684
  3252.4 45.5 %copy-start.56 = (f32[80,320]{1,0:T(8,128)S(1)}, f32[80,320]{1,0:T(8,128)}, u32[]{:S(2)}) copy-start(f32[80,320]{1,0:T(8,128)} %param.25) | copy-start | bytes 307204
  3252.4 45.5 %copy-start.57 = (f32[80,320]{1,0:T(8,128)S(1)}, f32[80,320]{1,0:T(8,128)}, u32[]{:S(2)}) copy-start(f32[80,320]{1,0:T(8,128)} %reduce-scatter.12.cloned.1.call-done) | copy-start | bytes 307204
  3252.4 45.5 %copy-start.84 = (f32[80,320]{1,0:T(8,128)S(1)}, f32[80,320]{1,0:T(8,128)}, u32[]{:S(2)}) copy-start(f32[80,320]{1,0:T(8,128)} %param.35) | copy-start | bytes 307204
  3252.4 45.5 %copy-start.85 = (f32[80,320]{1,0:T(8,128)S(1)}, f32[80,320]{1,0:T(8,128)}, u32[]{:S(2)}) copy-start(f32[80,320]{1,0:T(8,128)} %param.30) | copy-start | bytes 307204
  3252.4 53.7 %slice-start = ((s8[4718592]{0:T(1024)(128)(4,1)}), s8[524288]{0:T(1024)(128)(4,1)S(1)}, s32[]{:S(2)}) async-start(s8[4718592]{0:T(1024)(128)(4,1)} %bitcast.84), calls=%async_computation.13 | async-start | bytes 1048576
  (69 other events, 260.1 us)
Sparse Core Ops, SparseCore 0:
  11.6 188.7 all-gather.8
  203.9 54.3 all-gather.10
  261.4 397.4 all-gather.12
  1084.3 132.1 reduce-scatter.15
  1218.6 131.9 reduce-scatter.17
  1356.4 100.2 reduce-scatter.11
  1463.1 513.0 reduce-scatter.9
  1983.8 1263.6 reduce-scatter.13
where the time goes:
time: 3340 us; the launch traced here: 3320 us
  waiting for transfers between devices  2110 us (63%)
  local copies, waits for them, and re-layouts  389 us (12%)
  other arithmetic  299 us (9%)
  blocking collectives  276 us (8%)
  matrix products  224 us (7%)
    reduce_scatter x1, waiting for transfers between devices, on_device(): lax.psum_scatter(jnp.concatenate([contract_first(normed_two, grad_gu_low)...  1270 us
    reduce_scatter x1, waiting for transfers between devices, on_device(): lax.psum_scatter(mixer_term, ('batch', 'seq'), scatter_dimension=0, tiled...  518 us
    slice x57, local copies, waits for them, and re-layouts, on_device(): lax.associative_scan(link, (shifted_decay, grad_states), reverse=True)  134 us
    all_gather x1, waiting for transfers between devices, on_device(): lax.all_gather(mlp_weight.astype(jnp.bfloat16), ('batch', 'seq'), axis=0,...  108 us
    reduce_scatter x1, waiting for transfers between devices, on_device(): lax.psum_scatter(gate_term, ('batch', 'seq'), scatter_dimension=0, tiled=...  105 us
    all_gather x3, blocking collectives, entering(): everything = jax.tree.map(lambda part: lax.all_gather(part, axis), x)  101 us
    concatenate x1, other arithmetic, on_device(): jnp.concatenate([contract_first(normed_two, grad_gu_low), contract_first(...  98.4 us
    dot_general x4, matrix products, contract_first(): lax.dot_general(left, right, (((0,), (0,)), ((), ())), preferred_element_...  85.4 us
  transfers between devices with their start and end apart: 10, of which 8 were waited for; matrix products, arithmetic and copies ran while one was open for 15% of the time, Pallas kernels for 0%

commit v1 on v0

v1 whole, which is shorter than its diff:
```python
import functools
import math

import jax
import jax.numpy as jnp
from jax import lax
from jax.experimental import pallas as pl
from jax.experimental.pallas import tpu as pltpu
from jax.sharding import PartitionSpec as P

STEP = 10
norm_eps = 1e-06
clip_limit = 1.0
beta_first = 0.9
beta_second = 0.999
adam_eps = 1e-08
rate_matrix = 0.05
rate_gains = 0.8
rate_channel = 2.0
decay_matrix = 0.1

MESH = pl.DeviceIdType.MESH
F32 = jnp.float32
BF16 = jnp.bfloat16
ANY = pl.BlockSpec(memory_space=pl.ANY)
VM = pl.BlockSpec(memory_space=pltpu.VMEM)
FLIPS = [(fy, fc, fx) for fy in (0, 1) for fc in (0, 1) for fx in (0, 1) if fy + fc + fx]
GELU_SCALE = math.sqrt(2.0 / math.pi)


def place():
    b = lax.axis_index("batch")
    s = lax.axis_index("seq")
    y, z = b // 2, s // 2
    return y, b - 2 * y, z, s - 2 * z


def device(y, c, z, x):
    return (y * 2 + c, z * 2 + x)


def rank(y, c, x):
    return (y * 2 + c) * 2 + x


def flip(v, f):
    return 1 - v if f else v


def greet(peers):
    barrier = pltpu.get_barrier_semaphore()
    for peer in peers:
        pl.semaphore_signal(barrier, inc=1, device_id=peer, device_id_type=MESH)
    pl.semaphore_wait(barrier, len(peers))


def remote(src, dst, send, recv, to):
    copy = pltpu.make_async_remote_copy(
        src_ref=src, dst_ref=dst, send_sem=send, recv_sem=recv, device_id=to, device_id_type=MESH
    )
    copy.start()
    return copy


def params(collective_id, vmem=None):
    return pltpu.CompilerParams(
        collective_id=collective_id, has_side_effects=True, vmem_limit_bytes=vmem
    )


DMA = pltpu.SemaphoreType.DMA


def gather_kernel(a, o, loc, ss, rs):
    y, c, z, x = place()
    to_x, to_y, to_c = device(y, c, z, 1 - x), device(1 - y, c, z, x), device(y, 1 - c, z, x)
    greet((to_x, to_y, to_c))
    me, bx, by, bd = rank(y, c, x), rank(y, c, 1 - x), rank(1 - y, c, x), rank(1 - y, c, 1 - x)
    half = a.shape[0] // 2
    lo, hi = pl.ds(0, half), pl.ds(half, half)
    done = []

    def send(src, dst, k, to):
        copy = remote(src, dst, ss.at[k], rs.at[k], to)
        done.append(copy)
        return copy

    s0 = send(a.at[lo], o.at[me, lo], 0, to_x)
    s1 = send(a.at[hi], o.at[me, hi], 1, to_y)
    s2 = send(a.at[hi], o.at[me, hi], 2, to_x)
    s3 = send(a.at[lo], o.at[me, lo], 3, to_y)
    s4 = send(a, o.at[me], 4, to_c)
    own = pltpu.make_async_copy(a, o.at[me], loc)
    own.start()

    def pass_on(block, part, k):
        return send(o.at[block, part], o.at[block, part], k, to_c)

    s0.wait_recv()
    s5 = send(o.at[bx, lo], o.at[bx, lo], 5, to_y)
    last = [s4, pass_on(bx, lo, 7)]
    s1.wait_recv()
    s6 = send(o.at[by, hi], o.at[by, hi], 6, to_x)
    last.append(pass_on(by, hi, 8))
    s2.wait_recv()
    last.append(pass_on(bx, hi, 9))
    s3.wait_recv()
    last.append(pass_on(by, lo, 10))
    s5.wait_recv()
    last.append(pass_on(bd, lo, 11))
    s6.wait_recv()
    last.append(pass_on(bd, hi, 12))
    for copy in last:
        copy.wait_recv()
    for copy in done:
        copy.wait_send()
    own.wait()


def plane_gather(a, collective_id):
    rows, width = a.shape
    out = pl.pallas_call(
        gather_kernel,
        out_shape=jax.ShapeDtypeStruct((8, rows, width), a.dtype),
        in_specs=[ANY],
        out_specs=ANY,
        scratch_shapes=[DMA, DMA((13,)), DMA((13,))],
        compiler_params=params(collective_id),
        cost_estimate=pl.CostEstimate(flops=0, bytes_accessed=120 * 2**20, transcendentals=0),
    )(a)
    return out.reshape(8 * rows, width)


def scatter_kernel(p, o, mine, sib, part, got, loc, ss, rs):
    y, c, z, x = place()
    to_x, to_y, to_c = device(y, c, z, 1 - x), device(1 - y, c, z, x), device(y, 1 - c, z, x)
    greet((to_x, to_y, to_c))
    half = o.shape[0] // 2
    step = 16
    cut = (pl.ds(0, half), pl.ds(half, half))
    where = ((1 - y, 1 - x), (1 - y, x), (y, 1 - x), (y, x))
    order = [(0, 0), (0, 1), (1, 0), (2, 1), (2, 0), (1, 1), (3, 0), (3, 1)]
    from_c, own, sends = {}, {}, []
    for n, (t, h) in enumerate(order):
        ty, tx = where[t]
        own[t, h] = pltpu.make_async_copy(
            p.at[rank(ty, c, tx), cut[h]], mine.at[t, h], loc.at[n]
        )
        own[t, h].start()
        from_c[t, h] = remote(
            p.at[rank(ty, 1 - c, tx), cut[h]], sib.at[t, h], ss.at[n], rs.at[n], to_c
        )
        sends.append(from_c[t, h])

    def add(dst, t, h, extra):
        own[t, h].wait()
        from_c[t, h].wait_recv()

        @pl.loop(0, half // step)
        def _(i):
            at = pl.ds(pl.multiple_of(i * step, step), step)
            total = mine[t, h, at].astype(F32) + sib[t, h, at].astype(F32)
            for ref in extra:
                total = total + ref[at].astype(F32)
            dst[at] = total.astype(dst.dtype)

    def send(k, slot, to):
        copy = remote(part.at[k], got.at[slot], ss.at[8 + k], rs.at[8 + slot], to)
        sends.append(copy)
        return copy

    def arrival(slot):
        return pltpu.make_async_remote_copy(
            src_ref=part.at[0], dst_ref=got.at[slot], send_sem=ss.at[8], recv_sem=rs.at[8 + slot],
            device_id=to_x, device_id_type=MESH,
        )

    add(part.at[0], 0, 0, ())
    send(0, 1, to_y)
    add(part.at[1], 0, 1, ())
    send(1, 3, to_x)
    add(part.at[2], 1, 0, ())
    send(2, 0, to_y)
    add(part.at[3], 2, 1, ())
    send(3, 2, to_x)
    arrival(1).wait_recv()
    add(part.at[4], 2, 0, (got.at[1],))
    send(4, 4, to_x)
    arrival(3).wait_recv()
    add(part.at[5], 1, 1, (got.at[3],))
    send(5, 5, to_y)
    arrival(0).wait_recv()
    arrival(4).wait_recv()
    add(o.at[cut[0]], 3, 0, (got.at[0], got.at[4]))
    arrival(2).wait_recv()
    arrival(5).wait_recv()
    add(o.at[cut[1]], 3, 1, (got.at[2], got.at[5]))
    for copy in sends:
        copy.wait_send()


def plane_scatter(p, collective_id):
    width = p.shape[1]
    rows = p.shape[0] // 8
    half = rows // 2
    return pl.pallas_call(
        scatter_kernel,
        out_shape=jax.ShapeDtypeStruct((rows, width), F32),
        in_specs=[ANY],
        out_specs=VM,
        scratch_shapes=[
            pltpu.VMEM((4, 2, half, width), BF16),
            pltpu.VMEM((4, 2, half, width), BF16),
            pltpu.VMEM((6, half, width), BF16),
            pltpu.VMEM((6, half, width), BF16),
            DMA((8,)),
            DMA((14,)),
            DMA((14,)),
        ],
        compiler_params=params(collective_id, 40 * 2**20),
        cost_estimate=pl.CostEstimate(flops=0, bytes_accessed=140 * 2**20, transcendentals=0),
    )(p.reshape(8, rows, width))


def exchange_steps(a, o, loc, ss, rs):
    y, c, z, x = place()
    me = rank(y, c, x)
    copies = []
    for n, (fy, fc, fx) in enumerate(FLIPS):
        ty, tc, tx = flip(y, fy), flip(c, fc), flip(x, fx)
        copies.append(
            remote(a.at[rank(ty, tc, tx)], o.at[me], ss.at[n], rs.at[n], device(ty, tc, z, tx))
        )
    own = pltpu.make_async_copy(a.at[me], o.at[me], loc)
    own.start()
    return copies, own


def plane_peers():
    y, c, z, x = place()
    return [device(flip(y, fy), flip(c, fc), z, flip(x, fx)) for fy, fc, fx in FLIPS]


def line_peers(length):
    y, c, z, x = place()
    return [device(y, c, lax.rem(z + k, length), x) for k in range(1, length)]


def exchange_kernel(a, o, loc, ss, rs):
    greet(plane_peers())
    copies, own = exchange_steps(a, o, loc, ss, rs)
    for copy in copies:
        copy.wait()
    own.wait()


def plane_exchange(a, collective_id):
    return pl.pallas_call(
        exchange_kernel,
        out_shape=jax.ShapeDtypeStruct(a.shape, a.dtype),
        in_specs=[ANY],
        out_specs=ANY,
        scratch_shapes=[DMA, DMA((7,)), DMA((7,))],
        compiler_params=params(collective_id),
        cost_estimate=pl.CostEstimate(flops=0, bytes_accessed=80 * 2**20, transcendentals=0),
    )(a)


def first_kernel(length, wm, gn, gp, wm_o, gn_o, gp_o, loc, ss, rs, line_s, line_r, gain_s, gain_r, move_s, move_r):
    y, c, z, x = place()
    s = 2 * z + x
    me = rank(y, c, x)
    line = line_peers(length)
    plane = plane_peers()
    to_z, to_x = lax.rem(s, length), s // length
    moves = jnp.where(jnp.logical_and(to_z == z, to_x == x), 0, 1)
    src = x * length + z
    from_z = src // 2
    from_x = src - 2 * from_z
    barrier = pltpu.get_barrier_semaphore()
    for peer in line + plane:
        pl.semaphore_signal(barrier, inc=1, device_id=peer, device_id_type=MESH)

    @pl.when(moves == 1)
    def _():
        pl.semaphore_signal(barrier, inc=1, device_id=device(y, c, to_z, to_x), device_id_type=MESH)
        pl.semaphore_signal(barrier, inc=1, device_id=device(y, c, from_z, from_x), device_id_type=MESH)

    pl.semaphore_wait(barrier, len(line) + len(plane) + 2 * moves)

    copies, own = exchange_steps(wm, wm_o, loc.at[0], ss, rs)
    gain_own = pltpu.make_async_copy(gn, gn_o.at[me, z], loc.at[1])
    gain_own.start()
    gains = [
        remote(gn, gn_o.at[me, z], line_s.at[0, k], line_r.at[0, k], line[k]) for k in range(length - 1)
    ]

    @pl.when(moves == 1)
    def _():
        copy = remote(gp, gp_o.at[to_z], move_s, move_r, device(y, c, to_z, to_x))
        copy.wait()

    @pl.when(moves == 0)
    def _():
        copy = pltpu.make_async_copy(gp, gp_o.at[z], loc.at[2])
        copy.start()
        copy.wait()

    gates = [
        remote(gp_o.at[z], gp_o.at[z], line_s.at[1, k], line_r.at[1, k], line[k])
        for k in range(length - 1)
    ]
    gain_own.wait()
    for copy in gains:
        copy.wait()
    spread = [
        remote(gn_o.at[me], gn_o.at[me], gain_s.at[n], gain_r.at[n], plane[n]) for n in range(7)
    ]
    for copy in spread + gates + copies:
        copy.wait()
    own.wait()


def first(wm, gn, gp, length, collective_id):
    return pl.pallas_call(
        functools.partial(first_kernel, length),
        out_shape=(
            jax.ShapeDtypeStruct(wm.shape, wm.dtype),
            jax.ShapeDtypeStruct((8, length) + gn.shape, gn.dtype),
            jax.ShapeDtypeStruct((length,) + gp.shape, gp.dtype),
        ),
        in_specs=[ANY] * 3,
        out_specs=(ANY,) * 3,
        scratch_shapes=[
            DMA((3,)), DMA((7,)), DMA((7,)), DMA((2, length)), DMA((2, length)),
            DMA((7,)), DMA((7,)), DMA, DMA,
        ],
        compiler_params=params(collective_id),
    )(wm, gn, gp)


def last_kernel(
    length, wm, gn, gp, sq, wm_o, gn_o, gp_o, sq_o,
    gn_in, gn_mid, gn_got, gn_fin, gp_got, gp_sum, gp_fin, sq_plane, sq_line, sq_mid,
    loc, ss, rs, gs, gr, ls, lr, move_s, move_r,
):
    y, c, z, x = place()
    s = 2 * z + x
    me = rank(y, c, x)
    line = line_peers(length)
    plane = plane_peers()
    owner = x * length + z
    to_z = owner // 2
    to_x = owner - 2 * to_z
    from_z, from_x = lax.rem(s, length), s // length
    moves = jnp.where(jnp.logical_and(to_z == z, to_x == x), 0, 1)
    barrier = pltpu.get_barrier_semaphore()
    for peer in line + plane:
        pl.semaphore_signal(barrier, inc=1, device_id=peer, device_id_type=MESH)

    @pl.when(moves == 1)
    def _():
        pl.semaphore_signal(barrier, inc=1, device_id=device(y, c, to_z, to_x), device_id_type=MESH)
        pl.semaphore_signal(barrier, inc=1, device_id=device(y, c, from_z, from_x), device_id_type=MESH)

    pl.semaphore_wait(barrier, len(line) + len(plane) + 2 * moves)

    gain = []
    for n, (fy, fc, fx) in enumerate(FLIPS):
        to = rank(flip(y, fy), flip(c, fc), flip(x, fx))
        gain.append(remote(gn.at[to], gn_in.at[n], gs.at[0, n], gr.at[0, n], plane[n]))
    gate = [
        remote(gp.at[k + 1], gp_got.at[k], ls.at[0, k], lr.at[0, k], line[k]) for k in range(length - 1)
    ]
    copies, own = exchange_steps(wm, wm_o, loc, ss, rs)
    for copy in gain:
        copy.wait()
    total = gn[me]
    for n in range(7):
        total = total + gn_in[n]
    gn_mid[...] = total
    gain_line = [
        remote(gn_mid.at[k + 1], gn_got.at[k], ls.at[1, k], lr.at[1, k], line[k])
        for k in range(length - 1)
    ]
    for copy in gate:
        copy.wait()
    total = gp[0]
    for k in range(length - 1):
        total = total + gp_got[k]
    gp_sum[...] = total

    @pl.when(moves == 1)
    def _():
        copy = remote(gp_sum, gp_fin, move_s, move_r, device(y, c, to_z, to_x))
        copy.wait()

    @pl.when(moves == 0)
    def _():
        gp_fin[...] = gp_sum[...]

    for copy in gain_line:
        copy.wait()
    total = gn_mid[0]
    for k in range(length - 1):
        total = total + gn_got[k]
    gn_o[...] = total
    gates = gp_fin[...]
    gp_o[...] = gates

    def tiles(v):
        v = v * v
        if v.shape[0] > 8:
            v = jnp.sum(v.reshape(v.shape[0] // 8, 8, v.shape[1]), axis=0)
        part = v[:, :128]
        for n in range(1, v.shape[1] // 128):
            part = part + v[:, n * 128 : (n + 1) * 128]
        return part

    sq_plane[me] = sq[...] + tiles(total) + tiles(gates)
    sums = [
        remote(sq_plane.at[me], sq_plane.at[me], gs.at[1, n], gr.at[1, n], plane[n]) for n in range(7)
    ]
    for copy in sums:
        copy.wait()
    total = sq_plane[0]
    for n in range(1, 8):
        total = total + sq_plane[n]
    sq_line[z] = total
    sums = [
        remote(sq_line.at[z], sq_line.at[z], ls.at[2, k], lr.at[2, k], line[k])
        for k in range(length - 1)
    ]
    for copy in sums:
        copy.wait()
    total = sq_line[0]
    for n in range(1, length):
        total = total + sq_line[n]
    sq_o[...] = total
    for copy in copies:
        copy.wait()
    own.wait()


def last(wm, gn, gp, sq, length, collective_id):
    small, rows = gn.shape[2:], gp.shape[1:]
    return pl.pallas_call(
        functools.partial(last_kernel, length),
        out_shape=(
            jax.ShapeDtypeStruct(wm.shape, wm.dtype),
            jax.ShapeDtypeStruct(small, F32),
            jax.ShapeDtypeStruct(rows, F32),
            jax.ShapeDtypeStruct((8, 128), F32),
        ),
        in_specs=[ANY, VM, VM, VM],
        out_specs=(ANY, VM, VM, VM),
        scratch_shapes=[
            pltpu.VMEM((7, length) + small, F32),
            pltpu.VMEM((length,) + small, F32),
            pltpu.VMEM((length,) + small, F32),
            pltpu.VMEM(small, F32),
            pltpu.VMEM((length,) + rows, F32),
            pltpu.VMEM(rows, F32),
            pltpu.VMEM(rows, F32),
            pltpu.VMEM((8, 8, 128), F32),
            pltpu.VMEM((length, 8, 128), F32),
            pltpu.VMEM((8, 128), F32),
            DMA, DMA((7,)), DMA((7,)), DMA((2, 7)), DMA((2, 7)),
            DMA((3, length)), DMA((3, length)), DMA, DMA,
        ],
        compiler_params=params(collective_id, 24 * 2**20),
    )(wm, gn, gp, sq)


def minus_expm1(v):
    series = 1.0 + v * (1.0 / 8.0)
    for n in (7.0, 6.0, 5.0, 4.0, 3.0, 2.0):
        series = 1.0 + series * v * (1.0 / n)
    return jnp.where(v > -0.5, -v * series, 1.0 - jnp.exp(v))


def gelu_parts(v):
    inner = jnp.tanh(GELU_SCALE * (v + 0.044715 * v * v * v))
    return 0.5 * v * (1.0 + inner), inner


def gelu_slope(v, inner):
    return 0.5 * (1.0 + inner) + 0.5 * v * (1.0 - inner * inner) * GELU_SCALE * (
        1.0 + 3.0 * 0.044715 * v * v
    )


CHUNK = 64


def forward_kernel(
    length, proj, gate, chan, mixed, decay_o, width_o, recur_o, enter_o, conv_o, xe, se, ends_o,
    pre, loc_h, ends, carry, hs, hr, es, er,
):
    y, c, z, x = place()
    line = line_peers(length)
    greet(line)
    seqs, span, rc = mixed.shape
    chunks = span // CHUNK

    @pl.loop(0, seqs * chunks)
    def _(i):
        b = i // chunks
        r = pl.multiple_of((i - b * chunks) * CHUNK, CHUNK)
        xe[b, pl.ds(r + 8, CHUNK)] = proj[b, pl.ds(r, CHUNK), rc:].astype(BF16).astype(F32)

    ahead = device(y, c, lax.rem(z + 1, length), x)
    halo = remote(xe.at[:, pl.ds(span, 8)], xe.at[:, pl.ds(0, 8)], hs, hr, ahead)
    halo.wait()

    @pl.when(z == 0)
    def _():
        xe[:, 0:8] = jnp.zeros((seqs, 8, rc), F32)

    @pl.loop(0, seqs * chunks)
    def _(i):
        b = i // chunks
        r = pl.multiple_of((i - b * chunks) * CHUNK, CHUNK)
        at = pl.ds(r, CHUNK)
        window = xe[b, pl.ds(r, CHUNK + 8)]
        total = chan[4:5] + chan[0:1] * window[8:]
        for k in (1, 2, 3):
            total = total + chan[k : k + 1] * pltpu.roll(window, k, 0)[8:]
        low = total.astype(BF16)
        conv_o[b, at] = low
        value = low.astype(F32)
        gates = jnp.dot(low, gate[...], preferred_element_type=F32)
        recur = jax.nn.sigmoid(gates[:, :rc] + chan[5:6])
        enter = jax.nn.sigmoid(gates[:, rc:] + chan[6:7])
        log_decay = -chan[7:8] * recur
        decay = jnp.exp(log_decay)
        width = jnp.sqrt(minus_expm1(2.0 * log_decay))
        recur_o[b, at] = recur
        enter_o[b, at] = enter
        decay_o[b, at] = decay
        width_o[b, at] = width
        loc_h[b, at] = width * enter * value

    row = lax.broadcasted_iota(jnp.int32, (8, rc), 0)

    def tile(i, held):
        at = pl.ds(pl.multiple_of(i * 8, 8), 8)
        new = []
        for b in range(seqs):
            a, h = decay_o[b, at], loc_h[b, at]
            for n in (1, 2, 4):
                keep = row >= n
                h = h + jnp.where(keep, a * pltpu.roll(h, n, 0), 0.0)
                a = jnp.where(keep, a * pltpu.roll(a, n, 0), a)
            h = h + a * held[b][1]
            a = a * held[b][0]
            loc_h[b, at] = h
            pre[b, at] = a
            new.append((a[7:8], h[7:8]))
        return tuple(new)

    one, zero = jnp.ones((1, rc), F32), jnp.zeros((1, rc), F32)
    final = lax.fori_loop(0, span // 8, tile, ((one, zero),) * seqs)
    for b in range(seqs):
        ends[z, 0, b] = jnp.broadcast_to(final[b][0], (8, rc))
        ends[z, 1, b] = jnp.broadcast_to(final[b][1], (8, rc))
        ends_o[b] = jnp.broadcast_to(final[b][0], (8, rc))
    moves = [remote(ends.at[z], ends.at[z], es.at[k], er.at[k], line[k]) for k in range(length - 1)]
    for copy in moves:
        copy.wait()
    carry[...] = jnp.zeros_like(carry)
    for k in range(length):
        carry[...] = jnp.where(k < z, ends[k, 0] * carry[...] + ends[k, 1], carry[...])

    for b in range(seqs):
        se[b, 0:8] = carry[b]

    @pl.loop(0, seqs * chunks)
    def _(i):
        b = i // chunks
        r = pl.multiple_of((i - b * chunks) * CHUNK, CHUNK)
        at = pl.ds(r, CHUNK)
        state = loc_h[b, at] + pre[b, at] * carry[b, 0:1]
        se[b, pl.ds(r + 8, CHUNK)] = state
        gelu, _ = gelu_parts(proj[b, at, :rc])
        mixed[b, at] = (state * gelu).astype(BF16)


def recur_forward(proj, gate, chan, length, collective_id):
    seqs, span, rc = proj.shape[0], proj.shape[1], proj.shape[2] // 2
    full = jax.ShapeDtypeStruct((seqs, span, rc), F32)
    longer = jax.ShapeDtypeStruct((seqs, span + 8, rc), F32)
    low = jax.ShapeDtypeStruct((seqs, span, rc), BF16)
    return pl.pallas_call(
        functools.partial(forward_kernel, length),
        out_shape=(
            low, full, full, full, full, low, longer, longer,
            jax.ShapeDtypeStruct((seqs, 8, rc), F32),
        ),
        in_specs=[VM] * 3,
        out_specs=(VM,) * 9,
        scratch_shapes=[
            pltpu.VMEM((seqs, span, rc), F32),
            pltpu.VMEM((seqs, span, rc), F32),
            pltpu.VMEM((length, 2, seqs, 8, rc), F32),
            pltpu.VMEM((seqs, 8, rc), F32),
            DMA, DMA, DMA((length,)), DMA((length,)),
        ],
        compiler_params=params(collective_id, 56 * 2**20),
        cost_estimate=pl.CostEstimate(
            flops=2 * seqs * span * rc * rc * 2, bytes_accessed=100 * 2**20, transcendentals=0
        ),
    )(proj, gate, chan)


def backward_kernel(
    length, dmix, gate, chan, decay, width, recur, enter, conv, xe, se, ends_f, proj,
    dproj, dgate, gchan, suffix, grad, de, ends, carry, hs, hr, es, er,
):
    y, c, z, x = place()
    line = line_peers(length)
    greet(line)
    seqs, span, rc = decay.shape
    chunks = span // CHUNK

    @pl.loop(0, seqs * chunks)
    def _(i):
        b = i // chunks
        r = pl.multiple_of((i - b * chunks) * CHUNK, CHUNK)
        at = pl.ds(r, CHUNK)
        branch = proj[b, at]
        gelu, inner = gelu_parts(branch)
        above = dmix[b, at]
        state = se[b, pl.ds(r + 8, CHUNK)]
        grad[b, at] = above * gelu
        dproj[b, at, :rc] = (above * state * gelu_slope(branch, inner)).astype(BF16)

    row = lax.broadcasted_iota(jnp.int32, (8, rc), 0)

    def tile(i, held):
        at = pl.ds(pl.multiple_of(span - 8 - i * 8, 8), 8)
        new = []
        for b in range(seqs):
            product, total, following = held[b]
            plain, h = decay[b, at], grad[b, at]
            a = jnp.where(row == 7, following, pltpu.roll(plain, 7, 0))
            for n in (1, 2, 4):
                keep = row < 8 - n
                h = h + jnp.where(keep, a * pltpu.roll(h, 8 - n, 0), 0.0)
                a = jnp.where(keep, a * pltpu.roll(a, 8 - n, 0), a)
            h = h + a * total
            a = a * product
            grad[b, at] = h
            suffix[b, at] = a
            new.append((a[0:1], h[0:1], plain[0:1]))
        return tuple(new)

    one, zero = jnp.ones((1, rc), F32), jnp.zeros((1, rc), F32)
    final = lax.fori_loop(0, span // 8, tile, ((one, zero, one),) * seqs)
    for b in range(seqs):
        ends[z, 0, b] = ends_f[b]
        ends[z, 1, b] = jnp.broadcast_to(final[b][1] * final[b][2], (8, rc))
    moves = [remote(ends.at[z], ends.at[z], es.at[k], er.at[k], line[k]) for k in range(length - 1)]
    for copy in moves:
        copy.wait()
    carry[...] = jnp.zeros_like(carry)
    for k in reversed(range(length)):
        carry[...] = jnp.where(k > z, ends[k, 0] * carry[...] + ends[k, 1], carry[...])

    gchan[...] = jnp.zeros_like(gchan)

    def fold(v):
        return jnp.sum(v.reshape(v.shape[0] // 8, 8, v.shape[1]), axis=0)

    @pl.loop(0, seqs * chunks)
    def _(i):
        b = i // chunks
        r = pl.multiple_of((i - b * chunks) * CHUNK, CHUNK)
        at = pl.ds(r, CHUNK)
        g = grad[b, at] + suffix[b, at] * carry[b, 0:1]
        a, w, ra, ri = decay[b, at], width[b, at], recur[b, at], enter[b, at]
        value = conv[b, at].astype(F32)
        before = pltpu.roll(se[b, pl.ds(r, CHUNK + 8)], 1, 0)[8:]
        dla = g * before * a - g * ri * value * (a * a) / w
        slope = dla * ra * (1.0 - ra)
        dpa = (-chan[7:8] * slope).astype(BF16)
        dpi = (g * w * value * ri * (1.0 - ri)).astype(BF16)
        dgate[b, at, :rc] = dpa
        dgate[b, at, rc:] = dpi
        gchan[5] += fold(dpa.astype(F32))
        gchan[6] += fold(dpi.astype(F32))
        gchan[7] += fold(dla * ra)
        back = lax.dot_general(
            dgate[b, at], gate[...], (((1,), (1,)), ((), ())), preferred_element_type=F32
        )
        dcv = (g * w * ri + back).astype(BF16).astype(F32)
        de[b, at] = dcv
        gchan[4] += fold(dcv)

    behind = device(y, c, lax.rem(z + length - 1, length), x)
    halo = remote(de.at[:, pl.ds(0, 8)], de.at[:, pl.ds(span, 8)], hs, hr, behind)
    halo.wait()

    @pl.when(z == length - 1)
    def _():
        de[:, span:] = jnp.zeros((seqs, 8, rc), F32)

    @pl.loop(0, seqs * chunks)
    def _(i):
        b = i // chunks
        r = pl.multiple_of((i - b * chunks) * CHUNK, CHUNK)
        at = pl.ds(r, CHUNK)
        window = de[b, pl.ds(r, CHUNK + 8)]
        inputs = xe[b, pl.ds(r, CHUNK + 8)]
        dcv = window[:CHUNK]
        total = chan[0:1] * dcv
        gchan[0] += fold(dcv * inputs[8:])
        for k in (1, 2, 3):
            total = total + chan[k : k + 1] * pltpu.roll(window, CHUNK + 8 - k, 0)[:CHUNK]
            gchan[k] += fold(dcv * pltpu.roll(inputs, k, 0)[8:])
        dproj[b, at, rc:] = total.astype(BF16)


def recur_backward(dmix, gate, chan, kept, proj, length, collective_id):
    decay, width, recur, enter, conv, xe, se, ends = kept
    seqs, span, rc = decay.shape
    wide = jax.ShapeDtypeStruct((seqs, span, 2 * rc), BF16)
    return pl.pallas_call(
        functools.partial(backward_kernel, length),
        grid=(1,),
        out_shape=(wide, wide, jax.ShapeDtypeStruct((8, 8, rc), F32)),
        in_specs=[VM] * 11 + [pl.BlockSpec((seqs, span, rc), lambda i: (0, 0, 0))],
        out_specs=(VM,) * 3,
        scratch_shapes=[
            pltpu.VMEM((seqs, span, rc), F32),
            pltpu.VMEM((seqs, span, rc), F32),
            pltpu.VMEM((seqs, span + 8, rc), F32),
            pltpu.VMEM((length, 2, seqs, 8, rc), F32),
            pltpu.VMEM((seqs, 8, rc), F32),
            DMA, DMA, DMA((length,)), DMA((length,)),
        ],
        compiler_params=params(collective_id, 60 * 2**20),
        cost_estimate=pl.CostEstimate(
            flops=2 * seqs * span * rc * rc * 2, bytes_accessed=120 * 2**20, transcendentals=0
        ),
    )(dmix, gate, chan, decay, width, recur, enter, conv, xe, se, ends, proj)


def routes(length, senders):
    pairs = [(z, z + 1) for z in range(length - 1) if z in senders]
    return [(2 * a + x, 2 * b + x) for a, b in pairs for x in range(2)]


def line_gather(block, length):
    up_routes = routes(length, range(length))
    down_routes = [(b, a) for a, b in up_routes]
    up = down = block
    ups, downs = [], []
    for _ in range(length - 1):
        up = lax.ppermute(up, "seq", up_routes)
        down = lax.ppermute(down, "seq", down_routes)
        ups.append(up)
        downs.append(down)
    z = lax.axis_index("seq") // 2
    blocks = [block]
    for k in range(1, length):
        blocks.append(jnp.where(z + k < length, downs[k - 1], ups[length - k - 1]))
    return blocks


def line_scatter(blocks, length):
    up = down = None
    for hop in range(1, length):
        up_routes = routes(length, range(hop))
        down_routes = [
            (2 * (length - 1 - a // 2) + a % 2, 2 * (length - 1 - b // 2) + b % 2) for a, b in up_routes
        ]
        up_block, down_block = blocks[length - hop], blocks[hop]
        if up is not None:
            up_block = (up_block.astype(F32) + up.astype(F32)).astype(BF16)
            down_block = (down_block.astype(F32) + down.astype(F32)).astype(BF16)
        up = lax.ppermute(up_block, "seq", up_routes)
        down = lax.ppermute(down_block, "seq", down_routes)
    return blocks[0].astype(F32) + up.astype(F32) + down.astype(F32)


def contract_last(left, right):
    return lax.dot_general(
        left, right, (((1,), (1,)), ((), ())), preferred_element_type=F32
    )


def contract_first(left, right):
    return lax.dot_general(
        left, right, (((0,), (0,)), ((), ())), preferred_element_type=F32
    )


def adam_step(weight, grad, first, second, factor, rate, decay_rate):
    clipped = grad * factor
    first_new = beta_first * first + (1.0 - beta_first) * clipped
    second_new = beta_second * second + (1.0 - beta_second) * clipped * clipped
    first_hat = first_new / (1.0 - beta_first**STEP)
    second_hat = second_new / (1.0 - beta_second**STEP)
    weight_new = weight - rate * (
        first_hat / (jnp.sqrt(second_hat) + adam_eps) + decay_rate * weight
    )
    return (first_new, second_new, weight_new)


def normalize(values, gain):
    inverse = lax.rsqrt(jnp.mean(values * values, axis=-1, keepdims=True) + norm_eps)
    scaled = values * inverse
    return (scaled, inverse, (scaled * gain).astype(BF16))


def normalize_back(grad_normed, scaled, inverse, gain):
    grad_scaled = grad_normed * gain
    gain_grad = jnp.sum(grad_normed * scaled, axis=0)
    inner = jnp.mean(grad_scaled * scaled, axis=-1, keepdims=True)
    return (inverse * (grad_scaled - scaled * inner), gain_grad)


def on_device(
    block_input,
    out_grad,
    norm_gains,
    mixer_weight,
    gate_weight,
    chan_params,
    mlp_weight,
    first_gains,
    first_mixer,
    first_gate,
    first_chan,
    first_mlp,
    second_gains,
    second_mixer,
    second_gate,
    second_chan,
    second_mlp,
):
    length = lax.axis_size("seq") // 2
    z = lax.axis_index("seq") // 2
    tokens, model = block_input.shape[1:]
    share = mixer_weight.shape[0]
    pair = 2 * share
    lru = mixer_weight.shape[1] // 3
    hidden = mlp_weight.shape[1] // 3
    r8, f8 = lru // 8, hidden // 8
    rc = -(-r8 // 128) * 128
    head = gate_weight.shape[1] // 2
    heads = r8 // head
    gate_rows = gate_weight.shape[0]
    gate_pad = -(-gate_rows // 16) * 16

    def turned(v):
        lead = v.shape[:-1]
        v = v.reshape(lead + (4, length, pair)).swapaxes(-2, -3)
        return jnp.roll(v, -z, axis=-3).reshape(lead + (model,))

    def turned_back(v):
        lead = v.shape[:-1]
        v = jnp.roll(v.reshape(lead + (length, 4, pair)), z, axis=-3)
        return v.swapaxes(-2, -3).reshape(lead + (model,))

    mixer_out = (
        mixer_weight.astype(BF16).reshape(share, 3, 8, r8).transpose(2, 0, 1, 3).reshape(8, share, 3 * r8)
    )
    mlp_out = (
        mlp_weight.astype(BF16).reshape(share, 3, 8, f8).transpose(2, 0, 1, 3).reshape(8, share, 3 * f8)
    )
    gains_out = jnp.pad(norm_gains, ((0, 6), (0, 128 - share)))
    gate_out = jnp.pad(
        jnp.concatenate([gate_weight, chan_params.T], axis=1).astype(BF16),
        ((0, gate_pad - gate_rows), (0, rc - 2 * head - 8)),
    )
    mixer_in, gains_in, gate_in = first(mixer_out, gains_out, gate_out, length, 1)
    gains = gains_in[:, :, :2, :share].astype(BF16).astype(F32)
    gains = gains.reshape(4, 2, length, 2, share).transpose(3, 0, 2, 1, 4).reshape(2, model)
    gains = turned(gains)
    gate_own = gate_in[:, :gate_rows].reshape(r8, rc)
    chan = gate_own[:, 2 * head : 2 * head + 8].astype(F32).T
    lam = chan[7]
    fill = jnp.concatenate([jnp.zeros((7, rc - r8), F32), jnp.ones((1, rc - r8), F32)])
    chan = jnp.concatenate([chan[:7], 8.0 * jax.nn.softplus(-lam)[None]])
    chan = jnp.concatenate([chan, fill], axis=1)
    gate = jnp.zeros((rc, 2, rc), BF16)
    for h in range(heads):
        at = slice(h * head, (h + 1) * head)
        block = gate_own[at, : 2 * head].reshape(head, 2, head)
        gate = gate.at[at, :, at].set(block)
    gate = gate.reshape(rc, 2 * rc)

    mixer_blocks = line_gather(mixer_in.reshape(8 * share, 3 * r8), length)
    inputs = turned(block_input[0].astype(F32))
    cotangent_low = turned(out_grad[0])
    cotangent = cotangent_low.astype(F32)
    scaled_one, inverse_one, normed_one = normalize(inputs, gains[0])
    normed_one = plane_gather(normed_one, 2)
    mlp_in = plane_exchange(mlp_out, 3)
    mlp_blocks = line_gather(mlp_in.reshape(8 * share, 3 * f8), length)
    grad_out = plane_gather(cotangent_low, 4)

    mixer_full = jnp.concatenate(mixer_blocks)
    parts = [jnp.pad(mixer_full[:, n * r8 : (n + 1) * r8], ((0, 0), (0, rc - r8))) for n in range(3)]
    mixer_first = jnp.concatenate(parts[:2], axis=1)
    mixer_last = parts[2]
    span = 2 * tokens
    projected = jnp.dot(normed_one, mixer_first, preferred_element_type=F32)
    projected = projected.reshape(4, span, 2 * rc)
    mixed, *kept = recur_forward(projected, gate, chan, length, 5)
    mixed = mixed.reshape(4 * span, rc)
    mixer_sum = plane_scatter(contract_last(mixed, mixer_last).astype(BF16), 6)
    residual = inputs + mixer_sum
    scaled_two, inverse_two, normed_two = normalize(residual, gains[1])
    normed_two = plane_gather(normed_two, 7)

    mlp_full = jnp.concatenate(mlp_blocks)
    mlp_gate, mlp_up, mlp_down = (mlp_full[:, n * f8 : (n + 1) * f8] for n in range(3))
    gg = jnp.dot(normed_two, mlp_gate, preferred_element_type=F32)
    uu = jnp.dot(normed_two, mlp_up, preferred_element_type=F32)
    dhid = jnp.dot(grad_out, mlp_down, preferred_element_type=F32)
    gelu, inner = gelu_parts(gg)
    hid = (gelu * uu).astype(BF16)
    dgg = (dhid * uu * gelu_slope(gg, inner)).astype(BF16)
    duu = (dhid * gelu).astype(BF16)
    dnormed_two = contract_last(dgg, mlp_gate) + contract_last(duu, mlp_up)
    dnormed_two = plane_scatter(dnormed_two.astype(BF16), 8)

    def line_sum(term):
        term = term.astype(BF16)
        rows = term.shape[0] // length
        return line_scatter([term[k * rows : (k + 1) * rows] for k in range(length)], length)

    down_grad = line_sum(contract_first(grad_out, hid))
    gate_grad = line_sum(contract_first(normed_two, dgg))
    up_grad = line_sum(contract_first(normed_two, duu))
    mlp_sum = plane_scatter(contract_last(hid, mlp_down).astype(BF16), 9)
    block_output = turned_back((residual + mlp_sum).astype(BF16))

    grad_from_second, gain_two_grad = normalize_back(dnormed_two, scaled_two, inverse_two, gains[1])
    grad_residual = cotangent + grad_from_second
    dmz = plane_gather(grad_residual.astype(BF16), 10)
    dmix = jnp.dot(dmz, mixer_last, preferred_element_type=F32).reshape(4, span, rc)
    out_grad_sum = line_sum(contract_first(dmz, mixed)[:, :r8])
    dproj, dgate, chan_grad = recur_backward(dmix, gate, chan, kept, projected, length, 11)
    dproj = dproj.reshape(4 * span, 2 * rc)
    dgate = dgate.reshape(4 * span, 2 * rc)
    dnormed_one = plane_scatter(contract_last(dproj, mixer_first).astype(BF16), 12)
    first_grad = contract_first(normed_one, dproj)
    proj_grad_sum = line_sum(
        jnp.concatenate([first_grad[:, :r8], first_grad[:, rc : rc + r8]], axis=1)
    )
    gate_full_grad = contract_first(kept[4].reshape(4 * span, rc), dgate)

    grad_from_first, gain_one_grad = normalize_back(dnormed_one, scaled_one, inverse_one, gains[0])
    input_grad = turned_back(grad_residual + grad_from_first)

    mlp_sums = [gate_grad, up_grad, down_grad]
    mixer_sums = [proj_grad_sum, out_grad_sum]
    squares = sum(jnp.sum(g * g) for g in mlp_sums + mixer_sums)
    mlp_back = jnp.stack([g.astype(BF16).reshape(8, share, f8) for g in mlp_sums], axis=2)
    mlp_back = plane_exchange(mlp_back.reshape(8, share, 3 * f8), 13)
    mixer_back = jnp.concatenate([g.astype(BF16).reshape(8, share, -1) for g in mixer_sums], axis=2)

    gains_back = jnp.stack([gain_one_grad, gain_two_grad])
    gains_back = gains_back.reshape(2, length, 8, share).transpose(2, 1, 0, 3)
    gains_back = jnp.pad(gains_back, ((0, 0), (0, 0), (0, 6), (0, 128 - share)))
    blocks = []
    for h in range(heads):
        at = slice(h * head, (h + 1) * head)
        blocks.append(
            jnp.concatenate([gate_full_grad[at, at], gate_full_grad[at, rc + h * head : rc + (h + 1) * head]], axis=1)
        )
    gate_grad_own = jnp.concatenate(blocks)
    chan_grad = jnp.sum(chan_grad, axis=1)[:, :r8]
    chan_grad = jnp.concatenate([chan_grad[:7], (8.0 * jax.nn.sigmoid(-lam) * chan_grad[7])[None]])
    gate_back = jnp.concatenate([gate_grad_own, chan_grad.T], axis=1).reshape(length, gate_rows, 2 * head + 8)
    gate_back = jnp.pad(
        gate_back, ((0, 0), (0, gate_pad - gate_rows), (0, rc - 2 * head - 8))
    )
    gate_back = jnp.roll(gate_back, -z, axis=0)
    squares_in = jnp.zeros((8, 128), F32).at[0, 0].set(squares)
    mixer_back, gains_sum, gate_sum, squares_sum = last(
        mixer_back, gains_back, gate_back, squares_in, length, 14
    )

    grad_norm = jnp.sqrt(jnp.sum(squares_sum))
    factor = clip_limit / jnp.maximum(grad_norm, clip_limit)
    mixer_grad = mixer_back.astype(F32).reshape(8, share, 3, r8).transpose(1, 2, 0, 3).reshape(share, 3 * lru)
    mlp_grad = mlp_back.astype(F32).reshape(8, share, 3, f8).transpose(1, 2, 0, 3).reshape(share, 3 * hidden)
    gains_up = adam_step(
        norm_gains, gains_sum[:2, :share], first_gains, second_gains, factor, rate_gains, 0.0
    )
    mixer_up = adam_step(
        mixer_weight, mixer_grad, first_mixer, second_mixer, factor, rate_matrix, decay_matrix
    )
    gate_up = adam_step(
        gate_weight, gate_sum[:gate_rows, : 2 * head], first_gate, second_gate, factor, rate_matrix, decay_matrix
    )
    chan_up = adam_step(
        chan_params, gate_sum[:gate_rows, 2 * head : 2 * head + 8].T, first_chan, second_chan, factor,
        rate_channel, 0.0,
    )
    mlp_up = adam_step(
        mlp_weight, mlp_grad, first_mlp, second_mlp, factor, rate_matrix, decay_matrix
    )
    return (
        block_output[None],
        input_grad[None],
        grad_norm,
        *gains_up,
        *mixer_up,
        *gate_up,
        *chan_up,
        *mlp_up,
    )


def solution(mesh):
    rows = P(("batch", "seq"), None)
    columns = P(None, ("batch", "seq"))
    data = P("batch", "seq", None)
    weights = (columns, rows, rows, columns, rows)
    in_specs = (data, data) + weights * 3
    triples = tuple(spec for spec in weights for _ in range(3))
    return jax.shard_map(
        on_device,
        mesh=mesh,
        in_specs=in_specs,
        out_specs=(data, data, P()) + triples,
        check_vma=False,
    )
```

time: 3340 us -> 1230 us (0.37)
  waiting for transfers between devices: 2110 us -> 129 us
  Pallas kernels: 0 us -> 554 us
  blocking collectives: 276 us -> 0 us
  local copies, waits for them, and re-layouts: 389 us -> 155 us
  other arithmetic: 299 us -> 121 us
  starting transfers between devices: 4.58 us -> 110 us
  matrix products: 224 us -> 141 us
    reduce_scatter x3 -> x0, waiting for transfers between devices: 1890 us -> none  [the longest x1 1270 us: on_device(): lax.psum_scatter(jnp.concatenate([contract_first(normed_two, grad_gu_low)...]
    pallas_call x0 -> x14, Pallas kernels: none -> 554 us  [the longest x4 161 us: plane_scatter(): pl.pallas_call(scatter_kernel, out_shape=jax.ShapeDtypeStruct((rows, widt...]
    all_gather x5 -> x0, blocking collectives: 237 us -> none  [the longest x3 101 us: entering(): everything = jax.tree.map(lambda part: lax.all_gather(part, axis), x)]
    all_gather x3 -> x0, waiting for transfers between devices: 192 us -> none  [the longest x1 108 us: on_device(): lax.all_gather(mlp_weight.astype(jnp.bfloat16), ('batch', 'seq'), axis=0,...]
    slice x114 -> x13, local copies, waits for them, and re-layouts: 204 us -> 12.4 us  [the longest x4 6.63 us: line_sum(): term[k * rows:(k + 1) * rows]]
    concatenate x28 -> x10, other arithmetic: 153 us -> 25.8 us  [the longest x1 18.5 us: on_device(): mlp_full = jnp.concatenate(mlp_blocks)]
    ppermute x2 -> x42, waiting for transfers between devices: 4.2 us -> 129 us  [the longest x15 77.5 us: line_scatter(): up = lax.ppermute(up_block, 'seq', up_routes)]
    ppermute x2 -> x42, starting transfers between devices: 4.04 us -> 110 us  [the longest x15 49.6 us: line_scatter(): up = lax.ppermute(up_block, 'seq', up_routes)]
  transfers between devices with their start and end apart: 10 -> 42, of which waited for: 8 -> 11; matrix products, arithmetic and copies ran while one was open for 15% -> 20% of each run, Pallas kernels for 0% -> 40%
where the time goes in v1:
time: 1230 us; the launch traced here: 1220 us
  Pallas kernels  554 us (45%)
  local copies, waits for them, and re-layouts  155 us (13%)
  matrix products  141 us (11%)
  waiting for transfers between devices  129 us (10%)
  other arithmetic  121 us (10%)
  starting transfers between devices  110 us (9%)
    pallas_call x4, Pallas kernels, plane_scatter(): pl.pallas_call(scatter_kernel, out_shape=jax.ShapeDtypeStruct((rows, widt...  161 us
    pallas_call x4, Pallas kernels, plane_gather(): pl.pallas_call(gather_kernel, out_shape=jax.ShapeDtypeStruct((8, rows, wi...  159 us
    ppermute x15, waiting for transfers between devices, line_scatter(): up = lax.ppermute(up_block, 'seq', up_routes)  77.5 us
    pallas_call x1, Pallas kernels, recur_forward(): pl.pallas_call(functools.partial(forward_kernel, length), out_shape=(low,...  61.7 us
    pallas_call x2, Pallas kernels, plane_exchange(): pl.pallas_call(exchange_kernel, out_shape=jax.ShapeDtypeStruct(a.shape, a...  58.7 us
    ppermute x15, starting transfers between devices, line_scatter(): up = lax.ppermute(up_block, 'seq', up_routes)  49.6 us
    pallas_call x1, Pallas kernels, recur_backward(): pl.pallas_call(functools.partial(backward_kernel, length), grid=(1,), out...  48 us
    dot_general x5, matrix products, contract_last(): lax.dot_general(left, right, (((1,), (1,)), ((), ())), preferred_element_...  47.3 us
  transfers between devices with their start and end apart: 42, of which 11 were waited for; matrix products, arithmetic and copies ran while one was open for 20% of the time, Pallas kernels for 40%

profile of v1, /device:TPU:0, one launch (start us, length us, event | category | flops | bytes accessed | tf_op | source)
XLA Modules:
  0.0 1217.1 jit_solution(7691462371703363017)
XLA Ops:
  9.3 21.2 %shard_map.304 = (bf16[8,64,960]{2,1,0:T(8,128)(2,1)}, f32[8,4,8,128]{3,2,1,0:T(8,128)}, bf16[4,80,384]{2,1,0:T(8,128)(2,1)}) custom-call(bf16[8,64,960]{2,1,0:T(8,128)(2,1)} %reshape.284.wm, f32[8,128]{1,0:T(8,128)} %pad.40.gn, bf16[80,384]{1,0:T(8,128)(2,1)} %fusion.57.gp), custom_call_target="tpu_custom_call" | custom-call | tf_op jit(solution)/shard_map/pallas_call | solution.py:325
  34.0 5.5 collective-permute-start.1
  43.8 4.6 reshape.295.a
  48.4 29.5 %shard_map.309 = bf16[8,64,2304]{2,1,0:T(8,128)(2,1)} custom-call(bf16[8,64,2304]{2,1,0:T(8,128)(2,1)} %reshape.295.a), custom_call_target="tpu_custom_call" | custom-call | bytes 83886080 | tf_op jit(solution)/shard_map/pallas_call | solution.py:258
  79.2 6.0 collective-permute-start.7
  101.2 5.5 collective-permute-start.2
  109.5 45.1 %collective-permute-done.4 = bf16[512,960]{0,1:T(8,128)(2,1)} collective-permute-done((bf16[512,960]{0,1:T(8,128)(2,1)}, bf16[512,960]{0,1:T(8,128)(2,1)}, u32[]{:S(2)}, u32[]{:S(2)}) %collective-permute-start.4) | collective-permute-done | bytes 983072 | tf_op jit(solution)/shard_map/ppermute | solution.py:761
  155.9 5.7 collective-permute-start.3
  163.7 39.0 %shard_map.305 = bf16[8,256,2048]{2,1,0:T(8,128)(2,1)} custom-call(bf16[256,2048]{1,0:T(8,128)(2,1)} %multiply_convert_fusion.3.a), custom_call_target="tpu_custom_call" | custom-call | bytes 125829120 | tf_op jit(solution)/shard_map/pallas_call | solution.py:122
  205.0 27.9 %scatter.11 = bf16[384,2,384]{2,1,0:T(2,128)(2,1)} dynamic-update-slice(bf16[384,2,384]{2,1,0:T(2,128)(2,1)} %scatter.10, bf16[160,2,160]{2,1,0:T(2,128)(2,1)S(1)} %reshape.289, s32[]{:T(128)} %constant.251.clone.1, s32[]{:T(128)} %constant.240.clone.1, s32[]{:T(128)} %constant.251.clone.1) | dynamic-update-slice | bytes 204804 | tf_op jit(solution)/shard_map/scatter | solution.py:892
  236.4 40.6 %shard_map.311 = bf16[8,256,2048]{2,1,0:T(8,128)(2,1)} custom-call(bf16[256,2048]{1,0:T(8,128)(2,1)} %reshape.299.a), custom_call_target="tpu_custom_call" | custom-call | bytes 125829120 | tf_op jit(solution)/shard_map/pallas_call | solution.py:122
  291.8 6.1 collective-permute-start.8
  311.9 8.5 fusion.10.proj
  320.4 61.7 %shard_map.306 = (bf16[4,512,384]{2,1,0:T(8,128)(2,1)}, f32[4,512,384]{2,1,0:T(8,128)}, f32[4,512,384]{2,1,0:T(8,128)}, f32[4,512,384]{2,1,0:T(8,128)}, f32[4,51...) custom-call(f32[4,512,768]{2,1,0:T(8,128)} %fusion.10.proj, ...), custom_call_target="tpu_custom_call" | custom-call | flops 1207959552 | bytes 104857600 | tf_op jit(solution)/shard_map/pallas_call | solution.py:594
  383.5 6.2 convolution_convert_fusion.2
  389.7 40.4 %shard_map.307 = f32[256,2048]{1,0:T(8,128)S(1)} custom-call(bf16[8,256,2048]{2,1,0:T(8,128)(2,1)S(1)} %bitcast.106), custom_call_target="tpu_custom_call" | custom-call | bytes 146800640 | tf_op jit(solution)/shard_map/pallas_call | solution.py:206
  430.5 5.1 collective-permute-start.9
  436.8 39.3 %shard_map.308 = bf16[8,256,2048]{2,1,0:T(8,128)(2,1)} custom-call(bf16[256,2048]{1,0:T(8,128)(2,1)} %multiply_convert_fusion.2.a), custom_call_target="tpu_custom_call" | custom-call | bytes 125829120 | tf_op jit(solution)/shard_map/pallas_call | solution.py:122
  480.1 6.1 collective-permute-done.9
  488.2 18.5 %pad_maximum_fusion = bf16[2048,2304]{1,0:T(8,128)(2,1)S(1)} fusion(bf16[512,2304]{1,0:T(8,128)(2,1)S(1)} %broadcast_select_fusion, bf16[512,2304]{1,0:T(8,128)(2,1)S(1)} %broadcast_select_fusion.1, bf16[512,2304]{1,0:T(8,128)(2,1)S(1)} %broadcast_select_fusion.2, bf16[512,2304]{1,0:T(8,128)(2,1)S(1)} %bitcast.114), kind=kLoop, calls=%fused_computation.3 | loop fusion | flops 37748736 | bytes 18874368 | tf_op jit(solution)/shard_map/concatenate | solution.py:919
  506.8 7.0 fusion.17
  513.9 8.7 fusion.12
  522.6 17.4 %fusion.6 = (bf16[2048,768]{1,0:T(8,128)(2,1)}, bf16[2048,768]{1,0:T(8,128)(2,1)}, bf16[2048,768]{1,0:T(8,128)(2,1)}) fusion(f32[2048,768]{1,0:T(8,128)} %fusion.12, f32[2048,768]{1,0:T(8,128)S(1)} %fusion.17, bf16[2048,2048]{1,0:T(8,128)(2,1)} %bitcast.127, bf16[2048,2304]{1,0:T(8,128)(2,1)S(1)} %pad_maximum_fusion), kind=kOutput, calls=%fused_computation.14 | convolution fusion | flops 6481772544 | bytes 33554432 | tf_op jit(solution)/shard_map/dot_general | solution.py:921
  540.0 11.5 convolution_convert_fusion.4
  551.6 9.6 fusion.15
  561.2 7.4 convolution_convert_fusion.3
  568.6 9.1 convolution_convert_fusion.1
  578.9 5.3 collective-permute-start.36
  585.8 8.9 convolution_convert_fusion.5
  594.7 11.5 add_convert_fusion
  606.2 39.4 %shard_map.312 = f32[256,2048]{1,0:T(8,128)S(1)} custom-call(bf16[8,256,2048]{2,1,0:T(8,128)(2,1)S(1)} %bitcast.105), custom_call_target="tpu_custom_call" | custom-call | bytes 146800640 | tf_op jit(solution)/shard_map/pallas_call | solution.py:206
  648.4 39.9 %shard_map.313 = bf16[8,256,2048]{2,1,0:T(8,128)(2,1)} custom-call(bf16[256,2048]{1,0:T(8,128)(2,1)} %fusion.72.a), custom_call_target="tpu_custom_call" | custom-call | bytes 125829120 | tf_op jit(solution)/shard_map/pallas_call | solution.py:122
  688.3 10.0 fusion.32.dmix
  698.3 48.0 %shard_map.314 = (bf16[4,512,768]{2,1,0:T(8,128)(2,1)}, bf16[4,512,768]{2,1,0:T(8,128)(2,1)}, f32[8,8,384]{2,1,0:T(8,128)}) custom-call(f32[4,512,384]{2,1,0:T(8,128)} %fusion.32.dmix, bf16[384,768]{1,0:T(8,128)(2,1)} %bitcast.142, f32[8,384]{1,0:T(8,128)} %pad_maximum_fusion.6.chan, f32[4,512,384]{2,1,0:T(8,128)} %get-tuple-element.79.decay, ...), custom_call_target="tpu_custom_call" | custom-call | flops 1207959552 | bytes 125829120 | tf_op jit(solution)/shard_map/pallas_call | solution.py:728
  746.3 11.0 convolution_convert_fusion
  757.3 9.3 convolution_convert_fusion.6
  771.3 3.5 convolution_convert_fusion.7
  788.8 40.7 %shard_map.315 = f32[256,2048]{1,0:T(8,128)S(1)} custom-call(bf16[8,256,2048]{2,1,0:T(8,128)(2,1)S(1)} %bitcast.104), custom_call_target="tpu_custom_call" | custom-call | bytes 146800640 | tf_op jit(solution)/shard_map/pallas_call | solution.py:206
  833.5 40.3 %shard_map.310 = f32[256,2048]{1,0:T(8,128)S(1)} custom-call(bf16[8,256,2048]{2,1,0:T(8,128)(2,1)S(1)} %bitcast.103), custom_call_target="tpu_custom_call" | custom-call | bytes 146800640 | tf_op jit(solution)/shard_map/pallas_call | solution.py:206
  917.3 8.5 collective-permute-done.30
  925.9 4.3 collective-permute-start.20
  934.8 7.8 collective-permute-done.24
  948.3 15.4 %collective-permute-done.20 = bf16[512,320]{0,1:T(8,128)(2,1)S(1)} collective-permute-done((bf16[512,320]{0,1:T(8,128)(2,1)S(1)}, bf16[512,320]{0,1:T(8,128)(2,1)S(1)}, u32[]{:S(2)}, u32[]{:S(2)}) %collective-permute-start.20) | collective-permute-done | bytes 327712 | tf_op jit(solution)/shard_map/ppermute | solution.py:782
  963.7 5.3 collective-permute-start.31
  974.0 6.5 collective-permute-done.37
  988.6 8.9 collective-permute-done.31
  997.5 4.4 collective-permute-start.38
  1005.0 9.3 collective-permute-done.25
  1014.3 4.4 collective-permute-start.32
  1023.7 7.4 collective-permute-done.38
  1031.1 4.4 collective-permute-start.26
  1040.3 7.6 collective-permute-done.32
  1047.9 5.2 collective-permute-start.14
  1058.9 5.9 collective-permute-done.26
  1067.1 6.3 pad_maximum_fusion.2
  1073.4 7.1 reshape.311.a
  1080.5 29.2 %shard_map.317 = bf16[8,64,2304]{2,1,0:T(8,128)(2,1)} custom-call(bf16[8,64,2304]{2,1,0:T(8,128)(2,1)} %reshape.311.a), custom_call_target="tpu_custom_call" | custom-call | bytes 83886080 | tf_op jit(solution)/shard_map/pallas_call | solution.py:258
  1118.6 44.6 %shard_map.316 = (bf16[8,64,960]{2,1,0:T(8,128)(2,1)S(1)}, f32[8,128]{1,0:T(8,128)S(1)}, f32[80,384]{1,0:T(8,128)S(1)}, f32[8,128]{1,0:T(8,128)S(1)}) custom-call(bf16[8,64,960]{2,1,0:T(8,128)(2,1)S(1)} %pad_maximum_fusion.3.wm, f32[8,4,8,128]{3,2,1,0:T(8,128)S(1)} %pad.45.gn, f32[4,80,384]{2,1,0:T(8,128)S(1)} %fusion.52.gp, f32[8,128]{1,0:T(8,128)S(1)} %scatter.14.sq), custom_call_target="tpu_custom_call" | custom-call | tf_op jit(solution)/shard_map/pallas_call | solution.py:447
  1164.5 4.3 convert_multiply_fusion
  1168.8 8.2 mul.529
  1176.9 5.5 copy.199
  1182.5 3.6 copy.207
  1198.4 13.1 %multiply_subtract_fusion = (f32[64,18432]{1,0:T(8,128)}, f32[64,18432]{1,0:T(8,128)}, f32[64,18432]{1,0:T(8,128)}) fusion(f32[64,18432]{1,0:T(8,128)} %param.33, f32[64,18432]{1,0:T(8,128)} %bitcast.108, f32[64,18432]{1,0:T(8,128)} %param.43, f32[64,18432]{1,0:T(8,128)} %param.38), kind=kLoop, calls=%fused_computation.21 | loop fusion | flops 17694720 | bytes 33030144 | tf_op jit(solution)/shard_map/sub | solution.py:805
  1211.6 3.6 multiply_subtract_fusion.1
  (350 shorter events, 217.5 us)
Async XLA Ops:
  32.7 67.1 %collective-permute-start = (bf16[512,960]{0,1:T(8,128)(2,1)}, bf16[512,960]{0,1:T(8,128)(2,1)}, u32[]{:S(2)}, u32[]{:S(2)}) collective-permute-start(bf16[512,960]{0,1:T(8,128)(2,1)} %copy.170), channel_id=1, source_target_pairs={{2,0},{3,1},{4,2},{5,3},{6,4},{7,5},{10,8},{11,9},{12,10},{13,11},... | collective-permute-start | bytes 2949128 | tf_op jit(solution)/shard_map/ppermute | solution.py:761
  34.0 67.2 %collective-permute-start.1 = (bf16[512,960]{0,1:T(8,128)(2,1)}, bf16[512,960]{0,1:T(8,128)(2,1)}, u32[]{:S(2)}, u32[]{:S(2)}) collective-permute-start(bf16[512,960]{0,1:T(8,128)(2,1)} %copy.170), channel_id=1, source_target_pairs={{0,2},{1,3},{2,4},{3,5},{4,6},{5,7},{8,10},{9,11},{10,12},{11,13},... | collective-permute-start | bytes 2949128 | tf_op jit(solution)/shard_map/ppermute | solution.py:760
  48.4 36.8 %copy-start.34 = (bf16[1,256,2048]{2,1,0:T(8,128)(2,1)S(1)}, bf16[1,256,2048]{2,1,0:T(8,128)(2,1)}, u32[]{:S(2)}) copy-start(bf16[1,256,2048]{2,1,0:T(8,128)(2,1)} %param.27) | copy-start | bytes 3145732
  77.9 212.6 %collective-permute-start.6 = (bf16[512,2304]{1,0:T(8,128)(2,1)}, bf16[512,2304]{1,0:T(8,128)(2,1)}, u32[]{:S(2)}, u32[]{:S(2)}) collective-permute-start(bf16[512,2304]{1,0:T(8,128)(2,1)} %bitcast.112), channel_id=1, source_target_pairs={{2,0},{3,1},{4,2},{5,3},{6,4},{7,5},{10,8},{11,9},{12,10},{13,11},... | collective-permute-start | bytes 7077896 | tf_op jit(solution)/shard_map/ppermute | solution.py:761
  79.2 212.6 %collective-permute-start.7 = (bf16[512,2304]{1,0:T(8,128)(2,1)}, bf16[512,2304]{1,0:T(8,128)(2,1)}, u32[]{:S(2)}, u32[]{:S(2)}) collective-permute-start(bf16[512,2304]{1,0:T(8,128)(2,1)} %bitcast.113), channel_id=1, source_target_pairs={{0,2},{1,3},{2,4},{3,5},{4,6},{5,7},{8,10},{9,11},{10,12},{11,13},... | collective-permute-start | bytes 7077896 | tf_op jit(solution)/shard_map/ppermute | solution.py:760
  95.0 335.1 %copy-start.2 = (f32[256,2048]{1,0:T(8,128)}, f32[256,2048]{1,0:T(8,128)S(1)}, u32[]{:S(2)}) copy-start(f32[256,2048]{1,0:T(8,128)S(1)} %reshape.282) | copy-start | bytes 6291460
  99.8 56.1 %copy-start.51 = (f32[8,80]{1,0:T(8,128)S(1)}, f32[8,80]{1,0:T(8,128)}, u32[]{:S(2)}) copy-start(f32[8,80]{1,0:T(8,128)} %param.42) | copy-start | bytes 7684
  99.8 179.4 %copy-start.46 = (f32[8,320]{1,0:T(8,128)}, f32[8,320]{1,0:T(8,128)S(1)}, u32[]{:S(2)}) copy-start(f32[8,320]{1,0:T(8,128)S(1)} %convert_bitcast_fusion) | copy-start | bytes 30724
  99.8 54.8 %collective-permute-start.4 = (bf16[512,960]{0,1:T(8,128)(2,1)}, bf16[512,960]{0,1:T(8,128)(2,1)}, u32[]{:S(2)}, u32[]{:S(2)}) collective-permute-start(bf16[512,960]{0,1:T(8,128)(2,1)} %collective-permute-done), channel_id=1, source_target_pairs={{2,0},{3,1},{4,2},{5,3},{6,4},{7,5},{10,8},{11,9},{12,10},{13,11},... | collective-permute-start | bytes 2949128 | tf_op jit(solution)/shard_map/ppermute | solution.py:761
  101.1 61.8 %copy-start.48 = (f32[256]{0:T(256)}, f32[256]{0:T(256)S(1)}, u32[]{:S(2)}) copy-start(f32[256]{0:T(256)S(1)} %add_rsqrt_fusion.1) | copy-start | bytes 3076
  101.2 54.8 %collective-permute-start.2 = (bf16[512,960]{0,1:T(8,128)(2,1)}, bf16[512,960]{0,1:T(8,128)(2,1)}, u32[]{:S(2)}, u32[]{:S(2)}) collective-permute-start(bf16[512,960]{0,1:T(8,128)(2,1)} %collective-permute-done.1), channel_id=1, source_target_pairs={{0,2},{1,3},{2,4},{3,5},{4,6},{5,7},{8,10},{9,11},{10,12},{11,13},... | collective-permute-start | bytes 2949128 | tf_op jit(solution)/shard_map/ppermute | solution.py:760
  108.3 54.6 %copy-start.47 = (f32[8,80]{1,0:T(8,128)S(1)}, f32[8,80]{1,0:T(8,128)}, u32[]{:S(2)}) copy-start(f32[8,80]{1,0:T(8,128)} %param.32) | copy-start | bytes 7684
  154.6 143.2 %collective-permute-start.5 = (bf16[512,960]{0,1:T(8,128)(2,1)}, bf16[512,960]{0,1:T(8,128)(2,1)}, u32[]{:S(2)}, u32[]{:S(2)}) collective-permute-start(bf16[512,960]{0,1:T(8,128)(2,1)} %collective-permute-done.4), channel_id=1, source_target_pairs={{2,0},{3,1},{4,2},{5,3},{6,4},{7,5},{10,8},{11,9},{12,10},{13,11},... | collective-permute-start | bytes 2949128 | tf_op jit(solution)/shard_map/ppermute | solution.py:761
  155.9 146.4 %collective-permute-start.3 = (bf16[512,960]{0,1:T(8,128)(2,1)}, bf16[512,960]{0,1:T(8,128)(2,1)}, u32[]{:S(2)}, u32[]{:S(2)}) collective-permute-start(bf16[512,960]{0,1:T(8,128)(2,1)} %collective-permute-done.2), channel_id=1, source_target_pairs={{0,2},{1,3},{2,4},{3,5},{4,6},{5,7},{8,10},{9,11},{10,12},{11,13},... | collective-permute-start | bytes 2949128 | tf_op jit(solution)/shard_map/ppermute | solution.py:760
  236.4 42.8 %copy-start.54 = (f32[8,64]{1,0:T(8,128)S(1)}, f32[8,64]{1,0:T(8,128)}, u32[]{:S(2)}) copy-start(f32[8,64]{1,0:T(8,128)} %constant.253.clone.1) | copy-start | bytes 6148
  290.5 91.7 %collective-permute-start.10 = (bf16[512,2304]{1,0:T(8,128)(2,1)}, bf16[512,2304]{1,0:T(8,128)(2,1)}, u32[]{:S(2)}, u32[]{:S(2)}) collective-permute-start(bf16[512,2304]{1,0:T(8,128)(2,1)} %collective-permute-done.6), channel_id=1, source_target_pairs={{2,0},{3,1},{4,2},{5,3},{6,4},{7,5},{10,8},{11,9},{12,10},{13,11},... | collective-permute-start | bytes 7077896 | tf_op jit(solution)/shard_map/ppermute | solution.py:761
  291.8 138.7 %collective-permute-start.8 = (bf16[512,2304]{1,0:T(8,128)(2,1)}, bf16[512,2304]{1,0:T(8,128)(2,1)}, u32[]{:S(2)}, u32[]{:S(2)}) collective-permute-start(bf16[512,2304]{1,0:T(8,128)(2,1)} %collective-permute-done.7), channel_id=1, source_target_pairs={{0,2},{1,3},{2,4},{3,5},{4,6},{5,7},{8,10},{9,11},{10,12},{11,13},... | collective-permute-start | bytes 7077896 | tf_op jit(solution)/shard_map/ppermute | solution.py:760
  308.7 74.8 %copy-start.33 = (bf16[2048,320]{1,0:T(8,128)(2,1)}, bf16[2048,320]{1,0:T(8,128)(2,1)S(1)}, u32[]{:S(2)}) copy-start(bf16[2048,320]{1,0:T(8,128)(2,1)S(1)} %get-tuple-element.218) | copy-start | bytes 3932164
  382.2 95.9 %collective-permute-start.11 = (bf16[512,2304]{1,0:T(8,128)(2,1)}, bf16[512,2304]{1,0:T(8,128)(2,1)}, u32[]{:S(2)}, u32[]{:S(2)}) collective-permute-start(bf16[512,2304]{1,0:T(8,128)(2,1)} %collective-permute-done.10), channel_id=1, source_target_pairs={{2,0},{3,1},{4,2},{5,3},{6,4},{7,5},{10,8},{11,9},{12,10},{13,11},... | collective-permute-start | bytes 7077896 | tf_op jit(solution)/shard_map/ppermute | solution.py:761
  430.5 55.7 %collective-permute-start.9 = (bf16[512,2304]{1,0:T(8,128)(2,1)}, bf16[512,2304]{1,0:T(8,128)(2,1)S(1)}, u32[]{:S(2)}, u32[]{:S(2)}) collective-permute-start(bf16[512,2304]{1,0:T(8,128)(2,1)} %collective-permute-done.8), channel_id=1, source_target_pairs={{0,2},{1,3},{2,4},{3,5},{4,6},{5,7},{8,10},{9,11},{10,12},{11,13},... | collective-permute-start | bytes 7077896 | tf_op jit(solution)/shard_map/ppermute | solution.py:760
  486.1 20.6 %slice-start.6 = ((s8[8388608]{0:T(1024)(128)(4,1)}), s8[4194304]{0:T(1024)(128)(4,1)S(1)}, s32[]{:S(2)}) async-start(s8[8388608]{0:T(1024)(128)(4,1)} %bitcast.129), calls=%async_computation.6 | async-start | bytes 8388608
  488.2 25.6 %slice-start.2 = ((s8[8388608]{0:T(1024)(128)(4,1)}), s8[4194304]{0:T(1024)(128)(4,1)S(1)}, s32[]{:S(2)}) async-start(s8[8388608]{0:T(1024)(128)(4,1)} %bitcast.121), calls=%async_computation.2 | async-start | bytes 8388608
  506.8 61.8 %copy-start.13 = (bf16[2048,2304]{1,0:T(8,128)(2,1)}, bf16[2048,2304]{1,0:T(8,128)(2,1)S(1)}, u32[]{:S(2)}) copy-start(bf16[2048,2304]{1,0:T(8,128)(2,1)S(1)} %pad_maximum_fusion) | copy-start | bytes 28311556
  540.0 21.1 %slice-start.4 = ((s8[8388608]{0:T(1024)(128)(4,1)}), s8[4194304]{0:T(1024)(128)(4,1)S(1)}, s32[]{:S(2)}) async-start(s8[8388608]{0:T(1024)(128)(4,1)} %bitcast.124), calls=%async_computation.4 | async-start | bytes 8388608
  561.2 24.6 %slice-start.8 = ((s8[8388608]{0:T(1024)(128)(4,1)}), s8[4194304]{0:T(1024)(128)(4,1)S(1)}, s32[]{:S(2)}) async-start(s8[8388608]{0:T(1024)(128)(4,1)} %bitcast.132), calls=%async_computation.8 | async-start | bytes 8388608
  578.9 332.1 %collective-permute-start.36 = (bf16[512,768]{1,0:T(8,128)(2,1)}, bf16[512,768]{1,0:T(8,128)(2,1)}, u32[]{:S(2)}, u32[]{:S(2)}) collective-permute-start(bf16[512,768]{1,0:T(8,128)(2,1)} %get-tuple-element.226), channel_id=1, source_target_pairs={{0,2},{1,3},{8,10},{9,11},{16,18},{17,19},{24,26},{25,27}} | collective-permute-start | bytes 2359304 | tf_op jit(solution)/shard_map/ppermute | solution.py:782
  584.2 328.9 %collective-permute-start.39 = (bf16[512,768]{1,0:T(8,128)(2,1)}, bf16[512,768]{1,0:T(8,128)(2,1)}, u32[]{:S(2)}, u32[]{:S(2)}) collective-permute-start(bf16[512,768]{1,0:T(8,128)(2,1)} %get-tuple-element.227), channel_id=1, source_target_pairs={{6,4},{7,5},{14,12},{15,13},{22,20},{23,21},{30,28},{31,29}} | collective-permute-start | bytes 2359304 | tf_op jit(solution)/shard_map/ppermute | solution.py:783
  606.2 39.4 %copy-start.6 = (f32[256,2048]{1,0:T(8,128)S(1)}, f32[256,2048]{1,0:T(8,128)}, u32[]{:S(2)}) copy-start(f32[256,2048]{1,0:T(8,128)} %copy-done.5) | copy-start | bytes 6291460
  698.3 48.0 %copy-start.31 = (bf16[2048,384]{1,0:T(8,128)(2,1)S(1)}, bf16[2048,384]{1,0:T(8,128)(2,1)}, u32[]{:S(2)}) copy-start(bf16[2048,384]{1,0:T(8,128)(2,1)} %copy-done.30) | copy-start | bytes 4718596
  746.3 24.9 %slice-start.10 = ((s8[8388608]{0:T(1024)(128)(4,1)}), s8[4194304]{0:T(1024)(128)(4,1)S(1)}, s32[]{:S(2)}) async-start(s8[8388608]{0:T(1024)(128)(4,1)} %bitcast.136), calls=%async_computation.10 | async-start | bytes 8388608
  768.8 140.9 %collective-permute-start.12 = (bf16[512,640]{0,1:T(8,128)(2,1)}, bf16[512,640]{0,1:T(8,128)(2,1)}, u32[]{:S(2)}, u32[]{:S(2)}) collective-permute-start(bf16[512,640]{0,1:T(8,128)(2,1)} %pad_maximum_fusion.4), channel_id=1, source_target_pairs={{0,2},{1,3},{8,10},{9,11},{16,18},{17,19},{24,26},{25,27}} | collective-permute-start | bytes 1966088 | tf_op jit(solution)/shard_map/ppermute | solution.py:782
  775.8 112.5 %collective-permute-start.18 = (bf16[512,320]{0,1:T(8,128)(2,1)}, bf16[512,320]{0,1:T(8,128)(2,1)}, u32[]{:S(2)}, u32[]{:S(2)}) collective-permute-start(bf16[512,320]{0,1:T(8,128)(2,1)} %get-tuple-element.250), channel_id=1, source_target_pairs={{0,2},{1,3},{8,10},{9,11},{16,18},{17,19},{24,26},{25,27}} | collective-permute-start | bytes 983048 | tf_op jit(solution)/shard_map/ppermute | solution.py:782
  777.8 110.5 %collective-permute-start.21 = (bf16[512,320]{0,1:T(8,128)(2,1)}, bf16[512,320]{0,1:T(8,128)(2,1)}, u32[]{:S(2)}, u32[]{:S(2)}) collective-permute-start(bf16[512,320]{0,1:T(8,128)(2,1)} %get-tuple-element.251), channel_id=1, source_target_pairs={{6,4},{7,5},{14,12},{15,13},{22,20},{23,21},{30,28},{31,29}} | collective-permute-start | bytes 983048 | tf_op jit(solution)/shard_map/ppermute | solution.py:783
  788.8 40.7 %copy-start.3 = (f32[256,2048]{1,0:T(8,128)S(1)}, f32[256,2048]{1,0:T(8,128)}, u32[]{:S(2)}) copy-start(f32[256,2048]{1,0:T(8,128)} %copy-done.2) | copy-start | bytes 6291460
  788.8 40.8 %copy-start.42 = (f32[1,4,4,128]{3,2,1,0:T(4,128)S(1)}, f32[1,4,4,128]{3,2,1,0:T(4,128)}, u32[]{:S(2)}) copy-start(f32[1,4,4,128]{3,2,1,0:T(4,128)} %copy-done.41) | copy-start | bytes 24580
  788.8 40.8 %copy-start.49 = (f32[256]{0:T(256)S(1)}, f32[256]{0:T(256)}, u32[]{:S(2)}) copy-start(f32[256]{0:T(256)} %copy-done.48) | copy-start | bytes 3076
  833.5 40.4 %copy-start.4 = (f32[256,2048]{1,0:T(8,128)S(1)}, f32[256,2048]{1,0:T(8,128)}, u32[]{:S(2)}) copy-start(f32[256,2048]{1,0:T(8,128)} %copy-done.2) | copy-start | bytes 6291460
  833.5 40.4 %copy-start.7 = (f32[256,2048]{1,0:T(8,128)S(1)}, f32[256,2048]{1,0:T(8,128)}, u32[]{:S(2)}) copy-start(f32[256,2048]{1,0:T(8,128)} %copy-done.5) | copy-start | bytes 6291460
  833.5 40.4 %copy-start.11 = (bf16[256,2048]{1,0:T(8,128)(2,1)S(1)}, bf16[256,2048]{1,0:T(8,128)(2,1)}, u32[]{:S(2)}) copy-start(bf16[256,2048]{1,0:T(8,128)(2,1)} %reshape.299.a) | copy-start | bytes 3145732
  890.5 14.1 %collective-permute-start.19 = (bf16[512,320]{0,1:T(8,128)(2,1)}, bf16[512,320]{0,1:T(8,128)(2,1)}, u32[]{:S(2)}, u32[]{:S(2)}) collective-permute-start(bf16[512,320]{0,1:T(8,128)(2,1)} %get-tuple-element.248), channel_id=1, source_target_pairs={{0,2},{1,3},{2,4},{3,5},{8,10},{9,11},{10,12},{11,13},{16,18},{17,... | collective-permute-start | bytes 983048 | tf_op jit(solution)/shard_map/ppermute | solution.py:782
  892.5 15.1 %collective-permute-start.22 = (bf16[512,320]{0,1:T(8,128)(2,1)}, bf16[512,320]{0,1:T(8,128)(2,1)}, u32[]{:S(2)}, u32[]{:S(2)}) collective-permute-start(bf16[512,320]{0,1:T(8,128)(2,1)} %get-tuple-element.249), channel_id=1, source_target_pairs={{6,4},{7,5},{4,2},{5,3},{14,12},{15,13},{12,10},{13,11},{22,20},{2... | collective-permute-start | bytes 983048 | tf_op jit(solution)/shard_map/ppermute | solution.py:783
  904.7 21.2 %collective-permute-start.30 = (bf16[512,768]{1,0:T(8,128)(2,1)}, bf16[512,768]{1,0:T(8,128)(2,1)S(1)}, u32[]{:S(2)}, u32[]{:S(2)}) collective-permute-start(bf16[512,768]{1,0:T(8,128)(2,1)} %get-tuple-element.232), channel_id=1, source_target_pairs={{0,2},{1,3},{8,10},{9,11},{16,18},{17,19},{24,26},{25,27}} | collective-permute-start | bytes 2359304 | tf_op jit(solution)/shard_map/ppermute | solution.py:782
  907.7 22.5 %collective-permute-start.33 = (bf16[512,768]{1,0:T(8,128)(2,1)}, bf16[512,768]{1,0:T(8,128)(2,1)S(1)}, u32[]{:S(2)}, u32[]{:S(2)}) collective-permute-start(bf16[512,768]{1,0:T(8,128)(2,1)} %get-tuple-element.233), channel_id=1, source_target_pairs={{6,4},{7,5},{14,12},{15,13},{22,20},{23,21},{30,28},{31,29}} | collective-permute-start | bytes 2359304 | tf_op jit(solution)/shard_map/ppermute | solution.py:783
  909.7 32.9 %collective-permute-start.24 = (bf16[512,768]{1,0:T(8,128)(2,1)S(1)}, bf16[512,768]{1,0:T(8,128)(2,1)S(1)}, u32[]{:S(2)}, u32[]{:S(2)}) collective-permute-start(bf16[512,768]{1,0:T(8,128)(2,1)S(1)} %get-tuple-element.238), channel_id=1, source_target_pairs={{0,2},{1,3},{8,10},{9,11},{16,18},{17,19},{24,26},{25,27}} | collective-permute-start | bytes 2359304 | tf_op jit(solution)/shard_map/ppermute | solution.py:782
  911.1 32.8 %collective-permute-start.27 = (bf16[512,768]{1,0:T(8,128)(2,1)S(1)}, bf16[512,768]{1,0:T(8,128)(2,1)S(1)}, u32[]{:S(2)}, u32[]{:S(2)}) collective-permute-start(bf16[512,768]{1,0:T(8,128)(2,1)S(1)} %get-tuple-element.239), channel_id=1, source_target_pairs={{6,4},{7,5},{14,12},{15,13},{22,20},{23,21},{30,28},{31,29}} | collective-permute-start | bytes 2359304 | tf_op jit(solution)/shard_map/ppermute | solution.py:783
  913.1 55.8 %collective-permute-start.13 = (bf16[512,640]{0,1:T(8,128)(2,1)S(1)}, bf16[512,640]{0,1:T(8,128)(2,1)S(1)}, u32[]{:S(2)}, u32[]{:S(2)}) collective-permute-start(bf16[512,640]{0,1:T(8,128)(2,1)S(1)} %fusion.36), channel_id=1, source_target_pairs={{0,2},{1,3},{2,4},{3,5},{8,10},{9,11},{10,12},{11,13},{16,18},{17,... | collective-permute-start | bytes 1966088 | tf_op jit(solution)/shard_map/ppermute | solution.py:782
  925.9 37.8 %collective-permute-start.20 = (bf16[512,320]{0,1:T(8,128)(2,1)S(1)}, bf16[512,320]{0,1:T(8,128)(2,1)S(1)}, u32[]{:S(2)}, u32[]{:S(2)}) collective-permute-start(bf16[512,320]{0,1:T(8,128)(2,1)S(1)} %get-tuple-element.246), channel_id=1, source_target_pairs={{0,2},{1,3},{2,4},{3,5},{4,6},{5,7},{8,10},{9,11},{10,12},{11,13},... | collective-permute-start | bytes 983048 | tf_op jit(solution)/shard_map/ppermute | solution.py:782
  930.2 50.4 %collective-permute-start.37 = (bf16[512,768]{1,0:T(8,128)(2,1)S(1)}, bf16[512,768]{1,0:T(8,128)(2,1)S(1)}, u32[]{:S(2)}, u32[]{:S(2)}) collective-permute-start(bf16[512,768]{1,0:T(8,128)(2,1)S(1)} %get-tuple-element.224), channel_id=1, source_target_pairs={{0,2},{1,3},{2,4},{3,5},{8,10},{9,11},{10,12},{11,13},{16,18},{17,... | collective-permute-start | bytes 2359304 | tf_op jit(solution)/shard_map/ppermute | solution.py:782
  942.6 29.2 %collective-permute-start.23 = (bf16[512,320]{0,1:T(8,128)(2,1)S(1)}, bf16[512,320]{0,1:T(8,128)(2,1)S(1)}, u32[]{:S(2)}, u32[]{:S(2)}) collective-permute-start(bf16[512,320]{0,1:T(8,128)(2,1)S(1)} %get-tuple-element.247), channel_id=1, source_target_pairs={{6,4},{7,5},{4,2},{5,3},{2,0},{3,1},{14,12},{15,13},{12,10},{13,11... | collective-permute-start | bytes 983048 | tf_op jit(solution)/shard_map/ppermute | solution.py:783
  943.9 41.5 %collective-permute-start.40 = (bf16[512,768]{1,0:T(8,128)(2,1)}, bf16[512,768]{1,0:T(8,128)(2,1)}, u32[]{:S(2)}, u32[]{:S(2)}) collective-permute-start(bf16[512,768]{1,0:T(8,128)(2,1)} %get-tuple-element.225), channel_id=1, source_target_pairs={{6,4},{7,5},{4,2},{5,3},{14,12},{15,13},{12,10},{13,11},{22,20},{2... | collective-permute-start | bytes 2359304 | tf_op jit(solution)/shard_map/ppermute | solution.py:783
  963.7 33.8 %collective-permute-start.31 = (bf16[512,768]{1,0:T(8,128)(2,1)}, bf16[512,768]{1,0:T(8,128)(2,1)}, u32[]{:S(2)}, u32[]{:S(2)}) collective-permute-start(bf16[512,768]{1,0:T(8,128)(2,1)} %get-tuple-element.230), channel_id=1, source_target_pairs={{0,2},{1,3},{2,4},{3,5},{8,10},{9,11},{10,12},{11,13},{16,18},{17,... | collective-permute-start | bytes 2359304 | tf_op jit(solution)/shard_map/ppermute | solution.py:782
  968.9 33.0 %collective-permute-start.34 = (bf16[512,768]{1,0:T(8,128)(2,1)}, bf16[512,768]{1,0:T(8,128)(2,1)}, u32[]{:S(2)}, u32[]{:S(2)}) collective-permute-start(bf16[512,768]{1,0:T(8,128)(2,1)} %get-tuple-element.231), channel_id=1, source_target_pairs={{6,4},{7,5},{4,2},{5,3},{14,12},{15,13},{12,10},{13,11},{22,20},{2... | collective-permute-start | bytes 2359304 | tf_op jit(solution)/shard_map/ppermute | solution.py:783
  971.8 42.5 %collective-permute-start.25 = (bf16[512,768]{1,0:T(8,128)(2,1)}, bf16[512,768]{1,0:T(8,128)(2,1)}, u32[]{:S(2)}, u32[]{:S(2)}) collective-permute-start(bf16[512,768]{1,0:T(8,128)(2,1)} %get-tuple-element.236), channel_id=1, source_target_pairs={{0,2},{1,3},{2,4},{3,5},{8,10},{9,11},{10,12},{11,13},{16,18},{17,... | collective-permute-start | bytes 2359304 | tf_op jit(solution)/shard_map/ppermute | solution.py:782
  980.5 38.2 %collective-permute-start.15 = (bf16[512,640]{0,1:T(8,128)(2,1)}, bf16[512,640]{0,1:T(8,128)(2,1)}, u32[]{:S(2)}, u32[]{:S(2)}) collective-permute-start(bf16[512,640]{0,1:T(8,128)(2,1)} %get-tuple-element.204), channel_id=1, source_target_pairs={{6,4},{7,5},{14,12},{15,13},{22,20},{23,21},{30,28},{31,29}} | collective-permute-start | bytes 1966088 | tf_op jit(solution)/shard_map/ppermute | solution.py:783
  985.4 36.0 %collective-permute-start.28 = (bf16[512,768]{1,0:T(8,128)(2,1)}, bf16[512,768]{1,0:T(8,128)(2,1)S(1)}, u32[]{:S(2)}, u32[]{:S(2)}) collective-permute-start(bf16[512,768]{1,0:T(8,128)(2,1)} %get-tuple-element.237), channel_id=1, source_target_pairs={{6,4},{7,5},{4,2},{5,3},{14,12},{15,13},{12,10},{13,11},{22,20},{2... | collective-permute-start | bytes 2359304 | tf_op jit(solution)/shard_map/ppermute | solution.py:783
  997.5 33.6 %collective-permute-start.38 = (bf16[512,768]{1,0:T(8,128)(2,1)S(1)}, bf16[512,768]{1,0:T(8,128)(2,1)S(1)}, u32[]{:S(2)}, u32[]{:S(2)}) collective-permute-start(bf16[512,768]{1,0:T(8,128)(2,1)S(1)} %get-tuple-element.222), channel_id=1, source_target_pairs={{0,2},{1,3},{2,4},{3,5},{4,6},{5,7},{8,10},{9,11},{10,12},{11,13},... | collective-permute-start | bytes 2359304 | tf_op jit(solution)/shard_map/ppermute | solution.py:782
  1001.9 33.6 %collective-permute-start.41 = (bf16[512,768]{1,0:T(8,128)(2,1)S(1)}, bf16[512,768]{1,0:T(8,128)(2,1)S(1)}, u32[]{:S(2)}, u32[]{:S(2)}) collective-permute-start(bf16[512,768]{1,0:T(8,128)(2,1)S(1)} %get-tuple-element.223), channel_id=1, source_target_pairs={{6,4},{7,5},{4,2},{5,3},{2,0},{3,1},{14,12},{15,13},{12,10},{13,11... | collective-permute-start | bytes 2359304 | tf_op jit(solution)/shard_map/ppermute | solution.py:783
  1014.3 33.6 %collective-permute-start.32 = (bf16[512,768]{1,0:T(8,128)(2,1)S(1)}, bf16[512,768]{1,0:T(8,128)(2,1)S(1)}, u32[]{:S(2)}, u32[]{:S(2)}) collective-permute-start(bf16[512,768]{1,0:T(8,128)(2,1)S(1)} %get-tuple-element.228), channel_id=1, source_target_pairs={{0,2},{1,3},{2,4},{3,5},{4,6},{5,7},{8,10},{9,11},{10,12},{11,13},... | collective-permute-start | bytes 2359304 | tf_op jit(solution)/shard_map/ppermute | solution.py:782
  1018.8 34.4 %collective-permute-start.35 = (bf16[512,768]{1,0:T(8,128)(2,1)S(1)}, bf16[512,768]{1,0:T(8,128)(2,1)S(1)}, u32[]{:S(2)}, u32[]{:S(2)}) collective-permute-start(bf16[512,768]{1,0:T(8,128)(2,1)S(1)} %get-tuple-element.229), channel_id=1, source_target_pairs={{6,4},{7,5},{4,2},{5,3},{2,0},{3,1},{14,12},{15,13},{12,10},{13,11... | collective-permute-start | bytes 2359304 | tf_op jit(solution)/shard_map/ppermute | solution.py:783
  1021.4 34.1 %collective-permute-start.16 = (bf16[512,640]{0,1:T(8,128)(2,1)S(1)}, bf16[512,640]{0,1:T(8,128)(2,1)S(1)}, u32[]{:S(2)}, u32[]{:S(2)}) collective-permute-start(bf16[512,640]{0,1:T(8,128)(2,1)S(1)} %fusion.37), channel_id=1, source_target_pairs={{6,4},{7,5},{4,2},{5,3},{14,12},{15,13},{12,10},{13,11},{22,20},{2... | collective-permute-start | bytes 1966088 | tf_op jit(solution)/shard_map/ppermute | solution.py:783
  1031.1 33.7 %collective-permute-start.26 = (bf16[512,768]{1,0:T(8,128)(2,1)S(1)}, bf16[512,768]{1,0:T(8,128)(2,1)S(1)}, u32[]{:S(2)}, u32[]{:S(2)}) collective-permute-start(bf16[512,768]{1,0:T(8,128)(2,1)S(1)} %get-tuple-element.234), channel_id=1, source_target_pairs={{0,2},{1,3},{2,4},{3,5},{4,6},{5,7},{8,10},{9,11},{10,12},{11,13},... | collective-permute-start | bytes 2359304 | tf_op jit(solution)/shard_map/ppermute | solution.py:782
  1035.5 29.3 %collective-permute-start.29 = (bf16[512,768]{1,0:T(8,128)(2,1)S(1)}, bf16[512,768]{1,0:T(8,128)(2,1)S(1)}, u32[]{:S(2)}, u32[]{:S(2)}) collective-permute-start(bf16[512,768]{1,0:T(8,128)(2,1)S(1)} %get-tuple-element.235), channel_id=1, source_target_pairs={{6,4},{7,5},{4,2},{5,3},{2,0},{3,1},{14,12},{15,13},{12,10},{13,11... | collective-permute-start | bytes 2359304 | tf_op jit(solution)/shard_map/ppermute | solution.py:783
  1047.9 63.7 %collective-permute-start.14 = (bf16[512,640]{0,1:T(8,128)(2,1)}, bf16[512,640]{0,1:T(8,128)(2,1)}, u32[]{:S(2)}, u32[]{:S(2)}) collective-permute-start(bf16[512,640]{0,1:T(8,128)(2,1)} %get-tuple-element.203), channel_id=1, source_target_pairs={{0,2},{1,3},{2,4},{3,5},{4,6},{5,7},{8,10},{9,11},{10,12},{11,13},... | collective-permute-start | bytes 1966088 | tf_op jit(solution)/shard_map/ppermute | solution.py:782
  1057.6 54.0 %collective-permute-start.17 = (bf16[512,640]{0,1:T(8,128)(2,1)}, bf16[512,640]{0,1:T(8,128)(2,1)}, u32[]{:S(2)}, u32[]{:S(2)}) collective-permute-start(bf16[512,640]{0,1:T(8,128)(2,1)} %add_convert_fusion.8), channel_id=1, source_target_pairs={{6,4},{7,5},{4,2},{5,3},{2,0},{3,1},{14,12},{15,13},{12,10},{13,11... | collective-permute-start | bytes 1966088 | tf_op jit(solution)/shard_map/ppermute | solution.py:783
  (53 other events, 349.0 us)

commit v2 on v1

--- a/solution.py
+++ b/solution.py
@@ -71,70 +71,193 @@
 DMA = pltpu.SemaphoreType.DMA
 
 
-def gather_kernel(a, o, loc, ss, rs):
+def gather_peers():
     y, c, z, x = place()
-    to_x, to_y, to_c = device(y, c, z, 1 - x), device(1 - y, c, z, x), device(y, 1 - c, z, x)
-    greet((to_x, to_y, to_c))
-    me, bx, by, bd = rank(y, c, x), rank(y, c, 1 - x), rank(1 - y, c, x), rank(1 - y, c, 1 - x)
-    half = a.shape[0] // 2
-    lo, hi = pl.ds(0, half), pl.ds(half, half)
-    done = []
-
-    def send(src, dst, k, to):
-        copy = remote(src, dst, ss.at[k], rs.at[k], to)
-        done.append(copy)
+    return [device(y, c, z, 1 - x), device(1 - y, c, z, x), device(y, 1 - c, z, x)]
+
+
+class Gather:
+    def __init__(self, a, o, loc, ss, rs):
+        y, c, z, x = place()
+        self.to_x, self.to_y, self.to_c = gather_peers()
+        self.me, self.bx = rank(y, c, x), rank(y, c, 1 - x)
+        self.by, self.bd = rank(1 - y, c, x), rank(1 - y, c, 1 - x)
+        half = a.shape[0] // 2
+        self.lo, self.hi = pl.ds(0, half), pl.ds(half, half)
+        self.a, self.o, self.loc, self.ss, self.rs = a, o, loc, ss, rs
+        self.done = []
+
+    def send(self, src, dst, k, to):
+        copy = remote(src, dst, self.ss.at[k], self.rs.at[k], to)
+        self.done.append(copy)
         return copy
 
-    s0 = send(a.at[lo], o.at[me, lo], 0, to_x)
-    s1 = send(a.at[hi], o.at[me, hi], 1, to_y)
-    s2 = send(a.at[hi], o.at[me, hi], 2, to_x)
-    s3 = send(a.at[lo], o.at[me, lo], 3, to_y)
-    s4 = send(a, o.at[me], 4, to_c)
-    own = pltpu.make_async_copy(a, o.at[me], loc)
-    own.start()
-
-    def pass_on(block, part, k):
-        return send(o.at[block, part], o.at[block, part], k, to_c)
-
-    s0.wait_recv()
-    s5 = send(o.at[bx, lo], o.at[bx, lo], 5, to_y)
-    last = [s4, pass_on(bx, lo, 7)]
-    s1.wait_recv()
-    s6 = send(o.at[by, hi], o.at[by, hi], 6, to_x)
-    last.append(pass_on(by, hi, 8))
-    s2.wait_recv()
-    last.append(pass_on(bx, hi, 9))
-    s3.wait_recv()
-    last.append(pass_on(by, lo, 10))
-    s5.wait_recv()
-    last.append(pass_on(bd, lo, 11))
-    s6.wait_recv()
-    last.append(pass_on(bd, hi, 12))
-    for copy in last:
-        copy.wait_recv()
-    for copy in done:
-        copy.wait_send()
-    own.wait()
-
-
-def plane_gather(a, collective_id):
+    def relay(self, block, part, k, to):
+        return self.send(self.o.at[block, part], self.o.at[block, part], k, to)
+
+    def begin(self):
+        a, o, me, lo, hi = self.a, self.o, self.me, self.lo, self.hi
+        self.s0 = self.send(a.at[lo], o.at[me, lo], 0, self.to_x)
+        self.s1 = self.send(a.at[hi], o.at[me, hi], 1, self.to_y)
+        self.s2 = self.send(a.at[hi], o.at[me, hi], 2, self.to_x)
+        self.s3 = self.send(a.at[lo], o.at[me, lo], 3, self.to_y)
+        self.s4 = self.send(a, o.at[me], 4, self.to_c)
+        self.own = pltpu.make_async_copy(a, o.at[me], self.loc)
+        self.own.start()
+
+    def middle(self):
+        self.s0.wait_recv()
+        self.s5 = self.relay(self.bx, self.lo, 5, self.to_y)
+        self.last = [self.s4, self.relay(self.bx, self.lo, 7, self.to_c)]
+        self.s1.wait_recv()
+        self.s6 = self.relay(self.by, self.hi, 6, self.to_x)
+        self.last.append(self.relay(self.by, self.hi, 8, self.to_c))
+
+    def end(self):
+        self.s2.wait_recv()
+        self.last.append(self.relay(self.bx, self.hi, 9, self.to_c))
+        self.s3.wait_recv()
+        self.last.append(self.relay(self.by, self.lo, 10, self.to_c))
+        self.s5.wait_recv()
+        self.last.append(self.relay(self.bd, self.lo, 11, self.to_c))
+        self.s6.wait_recv()
+        self.last.append(self.relay(self.bd, self.hi, 12, self.to_c))
+        for copy in self.last:
+            copy.wait_recv()
+        for copy in self.done:
+            copy.wait_send()
+        self.own.wait()
+
+
+class Hop:
+    def __init__(self, kind, hop, length, refs, ss, rs):
+        y, c, z, x = place()
+        self.kind, self.hop, self.length, self.z = kind, hop, length, z
+        self.up = device(y, c, lax.rem(z + 1, length), x)
+        self.down = device(y, c, lax.rem(z + length - 1, length), x)
+        self.ss, self.rs = ss, rs
+        if kind == "gather":
+            self.line = LineGather(refs[0], length, ss, rs)
+            return
+        n = len(refs) // (3 if hop == 1 else 4)
+        if hop == 1:
+            up, down = [r.at[length - 1] for r in refs[:n]], [r.at[1] for r in refs[:n]]
+        else:
+            up, down = refs[:n], refs[n : 2 * n]
+        self.pairs = tuple(zip(up, refs[-2 * n : -n])), tuple(zip(down, refs[-n:]))
+
+    def peers(self):
+        return [self.up, self.down]
+
+    def when(self, up, down, act):
+        for way, condition in enumerate((up, down)):
+
+            @pl.when(condition)
+            def _():
+                for n, (src, dst) in enumerate(self.pairs[way]):
+                    act(
+                        pltpu.make_async_remote_copy(
+                            src, dst, self.ss.at[way, n], self.rs.at[way, n],
+                            device_id=(self.up, self.down)[way], device_id_type=MESH,
+                        )
+                    )
+
+    def sending(self):
+        return self.z <= self.hop - 1, self.z >= self.length - self.hop
+
+    def start(self):
+        if self.kind == "gather":
+            self.line.start(self.hop)
+        else:
+            self.when(*self.sending(), lambda copy: copy.start())
+
+    def finish(self):
+        if self.kind == "gather":
+            self.line.arrive(self.hop)
+            self.line.sends(self.hop, lambda copy: copy.wait_send())
+            return
+        z, last = self.z, self.length - 1
+        self.when(
+            jnp.logical_and(z >= 1, z <= self.hop),
+            jnp.logical_and(z <= last - 1, z >= last - self.hop),
+            lambda copy: copy.wait_recv(),
+        )
+        self.when(*self.sending(), lambda copy: copy.wait_send())
+
+
+def hop_results(carried):
+    kind, hop, operands = carried
+    shapes = [v.shape[1:] if kind == "scatter" and hop == 1 else v.shape for v in operands]
+    shapes = [jax.ShapeDtypeStruct(shape, v.dtype) for shape, v in zip(shapes, operands)]
+    return shapes * 2 if kind == "scatter" and hop == 1 else shapes
+
+
+def call_carrying(body, operands, in_specs, out_shapes, out_specs, scratch, carried, length, **kwargs):
+    if carried is None:
+        results = pl.pallas_call(
+            functools.partial(body, None), out_shape=tuple(out_shapes), in_specs=list(in_specs),
+            out_specs=tuple(out_specs), scratch_shapes=list(scratch), **kwargs,
+        )(*operands)
+        return results, ()
+    kind, hop, extra = carried
+    more = hop_results(carried)
+    ins, outs = len(operands), len(out_shapes)
+
+    def kernel(*refs):
+        hop_in, rest = refs[ins : ins + len(extra)], refs[ins + len(extra) :]
+        hop_out, (ss, rs) = rest[outs : outs + len(more)], rest[-2:]
+        used = hop_out if kind == "gather" else tuple(hop_in) + tuple(hop_out)
+        body(
+            Hop(kind, hop, length, used, ss, rs), *refs[:ins], *rest[:outs], *rest[outs + len(more) : -2]
+        )
+
+    results = pl.pallas_call(
+        kernel,
+        out_shape=tuple(out_shapes) + tuple(more),
+        in_specs=list(in_specs) + [ANY] * len(extra),
+        out_specs=tuple(out_specs) + (ANY,) * len(more),
+        scratch_shapes=list(scratch) + [DMA((2, length)), DMA((2, length))],
+        input_output_aliases={ins: outs} if kind == "gather" else {},
+        **kwargs,
+    )(*operands, *extra)
+    return results[:outs], results[outs:]
+
+
+def gather_kernel(hop, a, o, loc, ss, rs):
+    greet(gather_peers() + (hop.peers() if hop else []))
+    steps = Gather(a, o, loc, ss, rs)
+    steps.begin()
+    if hop:
+        hop.start()
+    steps.middle()
+    steps.end()
+    if hop:
+        hop.finish()
+
+
+def plane_gather(a, collective_id, carried=None, length=0):
     rows, width = a.shape
-    out = pl.pallas_call(
-        gather_kernel,
-        out_shape=jax.ShapeDtypeStruct((8, rows, width), a.dtype),
-        in_specs=[ANY],
-        out_specs=ANY,
-        scratch_shapes=[DMA, DMA((13,)), DMA((13,))],
+    (out,), more = call_carrying(
+        gather_kernel, [a], [ANY], [jax.ShapeDtypeStruct((8, rows, width), a.dtype)], [ANY],
+        [DMA, DMA((13,)), DMA((13,))], carried, length,
         compiler_params=params(collective_id),
         cost_estimate=pl.CostEstimate(flops=0, bytes_accessed=120 * 2**20, transcendentals=0),
-    )(a)
-    return out.reshape(8 * rows, width)
-
-
-def scatter_kernel(p, o, mine, sib, part, got, loc, ss, rs):
+    )
+    return out.reshape(8 * rows, width), more
+
+
+def scatter_kernel(hop, p, o, mine, sib, part, got, loc, ss, rs):
+    greet(gather_peers() + (hop.peers() if hop else []))
+    if hop:
+        hop.start()
+    scatter_steps(p, o, mine, sib, part, got, loc, ss, rs)
+    if hop:
+        hop.finish()
+
+
+def scatter_steps(p, o, mine, sib, part, got, loc, ss, rs, mark=lambda: None):
     y, c, z, x = place()
-    to_x, to_y, to_c = device(y, c, z, 1 - x), device(1 - y, c, z, x), device(y, 1 - c, z, x)
-    greet((to_x, to_y, to_c))
+    to_x, to_y, to_c = gather_peers()
     half = o.shape[0] // 2
     step = 16
     cut = (pl.ds(0, half), pl.ds(half, half))
@@ -189,6 +312,7 @@
     arrival(3).wait_recv()
     add(part.at[5], 1, 1, (got.at[3],))
     send(5, 5, to_y)
+    mark()
     arrival(0).wait_recv()
     arrival(4).wait_recv()
     add(o.at[cut[0]], 3, 0, (got.at[0], got.at[4]))
@@ -199,27 +323,29 @@
         copy.wait_send()
 
 
-def plane_scatter(p, collective_id):
+def scatter_scratch(half, width):
+    return [
+        pltpu.VMEM((4, 2, half, width), BF16),
+        pltpu.VMEM((4, 2, half, width), BF16),
+        pltpu.VMEM((6, half, width), BF16),
+        pltpu.VMEM((6, half, width), BF16),
+        DMA((8,)),
+        DMA((14,)),
+        DMA((14,)),
+    ]
+
+
+def plane_scatter(p, collective_id, carried=None, length=0):
     width = p.shape[1]
     rows = p.shape[0] // 8
-    half = rows // 2
-    return pl.pallas_call(
-        scatter_kernel,
-        out_shape=jax.ShapeDtypeStruct((rows, width), F32),
-        in_specs=[ANY],
-        out_specs=VM,
-        scratch_shapes=[
-            pltpu.VMEM((4, 2, half, width), BF16),
-            pltpu.VMEM((4, 2, half, width), BF16),
-            pltpu.VMEM((6, half, width), BF16),
-            pltpu.VMEM((6, half, width), BF16),
-            DMA((8,)),
-            DMA((14,)),
-            DMA((14,)),
-        ],
+    (out,), more = call_carrying(
+        scatter_kernel, [p.reshape(8, rows, width)], [ANY],
+        [jax.ShapeDtypeStruct((rows, width), F32)], [VM],
+        scatter_scratch(rows // 2, width), carried, length,
         compiler_params=params(collective_id, 40 * 2**20),
         cost_estimate=pl.CostEstimate(flops=0, bytes_accessed=140 * 2**20, transcendentals=0),
-    )(p.reshape(8, rows, width))
+    )
+    return out, more
 
 
 def exchange_steps(a, o, loc, ss, rs):
@@ -246,30 +372,194 @@
     return [device(y, c, lax.rem(z + k, length), x) for k in range(1, length)]
 
 
-def exchange_kernel(a, o, loc, ss, rs):
-    greet(plane_peers())
-    copies, own = exchange_steps(a, o, loc, ss, rs)
+class LineGather:
+    def __init__(self, buf, length, ss, rs):
+        y, c, z, x = place()
+        self.z, self.length, self.buf, self.ss, self.rs = z, length, buf, ss, rs
+        self.up = device(y, c, lax.rem(z + 1, length), x)
+        self.down = device(y, c, lax.rem(z + length - 1, length), x)
+
+    def copy(self, hop, upward):
+        length, buf = self.length, self.buf
+        src, dst = ((length - hop + 1) % length, length - hop) if upward else (hop - 1, hop)
+        way = 0 if upward else 1
+        return pltpu.make_async_remote_copy(
+            src_ref=buf.at[src], dst_ref=buf.at[dst], send_sem=self.ss.at[way, hop - 1],
+            recv_sem=self.rs.at[way, hop - 1], device_id=self.up if upward else self.down,
+            device_id_type=MESH,
+        )
+
+    def sends(self, hop, act):
+        z, length = self.z, self.length
+
+        @pl.when(jnp.logical_and(z + 1 < length, z >= hop - 1))
+        def _():
+            act(self.copy(hop, True))
+
+        @pl.when(jnp.logical_and(z >= 1, z + hop - 1 < length))
+        def _():
+            act(self.copy(hop, False))
+
+    def start(self, hop):
+        self.sends(hop, lambda copy: copy.start())
+
+    def arrive(self, hop):
+        z, length = self.z, self.length
+
+        @pl.when(z >= hop)
+        def _():
+            self.copy(hop, True).wait_recv()
+
+        @pl.when(z + hop < length)
+        def _():
+            self.copy(hop, False).wait_recv()
+
+    def finish(self):
+        for hop in range(1, self.length):
+            self.sends(hop, lambda copy: copy.wait_send())
+
+
+class LineScatter:
+    def __init__(self, g, total, up_mine, down_mine, up_got, down_got, loc, ss, rs):
+        y, c, z, x = place()
+        self.length = length = g.shape[0]
+        self.g, self.total = g, total
+        self.mine, self.got = (up_mine, down_mine), (up_got, down_got)
+        self.loc, self.ss, self.rs = loc, ss, rs
+        self.to = (device(y, c, lax.rem(z + 1, length), x), device(y, c, lax.rem(z + length - 1, length), x))
+        self.far = (z, length - 1 - z)
+
+    def load(self, way, hop):
+        k = self.length - hop if way == 0 else hop
+        return pltpu.make_async_copy(self.g.at[k], self.mine[way].at[hop - 1], self.loc.at[way, hop - 1])
+
+    def load_own(self):
+        return pltpu.make_async_copy(self.g.at[0], self.total, self.loc.at[0, self.length - 1])
+
+    def copy(self, way, hop):
+        return pltpu.make_async_remote_copy(
+            src_ref=self.mine[way].at[hop - 1], dst_ref=self.got[way].at[hop - 1],
+            send_sem=self.ss.at[way, hop - 1], recv_sem=self.rs.at[way, hop - 1],
+            device_id=self.to[way], device_id_type=MESH,
+        )
+
+    def begin(self):
+        for hop in range(1, self.length):
+            for way in (0, 1):
+                self.load(way, hop).start()
+        self.load_own().start()
+
+    def add(self, dst, src):
+        @pl.loop(0, dst.shape[0] // 16)
+        def _(i):
+            at = pl.ds(pl.multiple_of(i * 16, 16), 16)
+            dst[at] = (dst[at].astype(F32) + src[at].astype(F32)).astype(dst.dtype)
+
+    def start(self, hop):
+        for way in (0, 1):
+            far = self.far[way]
+            self.load(way, hop).wait()
+            if hop > 1:
+
+                @pl.when(jnp.logical_and(far >= 1, far <= hop - 1))
+                def _():
+                    self.copy(way, hop - 1).wait_recv()
+                    self.add(self.mine[way].at[hop - 1], self.got[way].at[hop - 2])
+
+            @pl.when(far <= hop - 1)
+            def _():
+                self.copy(way, hop).start()
+
+    def end(self, result):
+        last = self.length - 1
+        self.load_own().wait()
+        for way in (0, 1):
+
+            @pl.when(self.far[way] >= 1)
+            def _():
+                self.copy(way, last).wait_recv()
+
+        def each(act):
+            @pl.loop(0, result.shape[0] // 16)
+            def _(i):
+                act(pl.ds(pl.multiple_of(i * 16, 16), 16))
+
+        def own(at):
+            result[at] = self.total[at].astype(F32)
+
+        each(own)
+        for way in (0, 1):
+
+            @pl.when(self.far[way] >= 1)
+            def _():
+                def more(at):
+                    result[at] += self.got[way][last - 1, at].astype(F32)
+
+                each(more)
+
+        for hop in range(1, self.length):
+            for way in (0, 1):
+
+                @pl.when(self.far[way] <= hop - 1)
+                def _():
+                    self.copy(way, hop).wait_send()
+
+
+def closing_kernel(p, e, g, o, e_o, g_o, *scratch):
+    scatter_refs, exchange_refs, line_refs = scratch[:7], scratch[7:10], scratch[10:]
+    length = g.shape[0]
+    greet(plane_peers() + line_peers(length))
+    line = LineScatter(g, *line_refs)
+    line.begin()
+    line.start(1)
+    hops = list(range(2, length))
+
+    def mark():
+        if hops:
+            line.start(hops.pop(0))
+
+    scatter_steps(p, o, *scatter_refs, mark=mark)
+    copies, own = exchange_steps(e, e_o, *exchange_refs)
+    while hops:
+        mark()
+    line.end(g_o)
     for copy in copies:
         copy.wait()
     own.wait()
 
 
-def plane_exchange(a, collective_id):
+def closing(p, e, g, collective_id):
+    rows, width = p.shape[0] // 8, p.shape[1]
+    length = g.shape[0]
+    hops = (length - 1,) + g.shape[1:]
     return pl.pallas_call(
-        exchange_kernel,
-        out_shape=jax.ShapeDtypeStruct(a.shape, a.dtype),
-        in_specs=[ANY],
-        out_specs=ANY,
-        scratch_shapes=[DMA, DMA((7,)), DMA((7,))],
-        compiler_params=params(collective_id),
-        cost_estimate=pl.CostEstimate(flops=0, bytes_accessed=80 * 2**20, transcendentals=0),
-    )(a)
-
-
-def first_kernel(length, wm, gn, gp, wm_o, gn_o, gp_o, loc, ss, rs, line_s, line_r, gain_s, gain_r, move_s, move_r):
+        closing_kernel,
+        out_shape=(
+            jax.ShapeDtypeStruct((rows, width), F32),
+            jax.ShapeDtypeStruct(e.shape, e.dtype),
+            jax.ShapeDtypeStruct(g.shape[1:], F32),
+        ),
+        in_specs=[ANY] * 3,
+        out_specs=(VM, ANY, VM),
+        scratch_shapes=scatter_scratch(rows // 2, width)
+        + [DMA, DMA((7,)), DMA((7,)), pltpu.VMEM(g.shape[1:], BF16)]
+        + [pltpu.VMEM(hops, BF16)] * 4
+        + [DMA((2, length))] * 3,
+        compiler_params=params(collective_id, 56 * 2**20),
+        cost_estimate=pl.CostEstimate(flops=0, bytes_accessed=250 * 2**20, transcendentals=0),
+    )(p.reshape(8, rows, width), e, g)
+
+
+def first_kernel(
+    length, inputs, mixer_w, mlp_w, gn, gp, normed_o, wm_o, wf_o, gains_o, gp_o,
+    normed, gn_all, wm, wf, loc, ms, mr, fs, fr, line_s, line_r, gain_s, gain_r, move_s, move_r,
+    gather_s, gather_r, hop_s, hop_r,
+):
     y, c, z, x = place()
     s = 2 * z + x
     me = rank(y, c, x)
+    rows, width = inputs.shape
+    pair = width // (4 * length)
     line = line_peers(length)
     plane = plane_peers()
     to_z, to_x = lax.rem(s, length), s // length
@@ -288,12 +578,24 @@
 
     pl.semaphore_wait(barrier, len(line) + len(plane) + 2 * moves)
 
-    copies, own = exchange_steps(wm, wm_o, loc.at[0], ss, rs)
-    gain_own = pltpu.make_async_copy(gn, gn_o.at[me, z], loc.at[1])
-    gain_own.start()
+    gn_all[me, z] = gn[...]
     gains = [
-        remote(gn, gn_o.at[me, z], line_s.at[0, k], line_r.at[0, k], line[k]) for k in range(length - 1)
+        remote(gn, gn_all.at[me, z], line_s.at[0, k], line_r.at[0, k], line[k]) for k in range(length - 1)
     ]
+    for pack, source in ((wm, mixer_w), (wf, mlp_w)):
+        part = pack.shape[2] // 3
+        for t in range(8):
+            for j in range(3):
+                start = (j * 8 + t) * part
+                pack[t, :, j * part : (j + 1) * part] = source[:, start : start + part].astype(BF16)
+        if pack is wm:
+            for copy in gains:
+                copy.wait()
+            spread = [
+                remote(gn_all.at[me], gn_all.at[me], gain_s.at[n], gain_r.at[n], plane[n])
+                for n in range(7)
+            ]
+            mixer, mixer_own = exchange_steps(wm, wm_o.at[0], loc.at[0], ms, mr)
 
     @pl.when(moves == 1)
     def _():
@@ -310,33 +612,71 @@
         remote(gp_o.at[z], gp_o.at[z], line_s.at[1, k], line_r.at[1, k], line[k])
         for k in range(length - 1)
     ]
-    gain_own.wait()
-    for copy in gains:
+    for copy in spread:
         copy.wait()
-    spread = [
-        remote(gn_o.at[me], gn_o.at[me], gain_s.at[n], gain_r.at[n], plane[n]) for n in range(7)
-    ]
-    for copy in spread + gates + copies:
+    for k in range(length):
+        other = lax.rem(z + k, length)
+        for b in range(4):
+            at = slice((4 * k + b) * pair, (4 * k + b + 1) * pair)
+            gains_o[:, at] = (gn_all[2 * b, other] + gn_all[2 * b + 1, other])[:, :pair]
+
+    @pl.loop(0, rows // 16)
+    def _(i):
+        at = pl.ds(pl.multiple_of(i * 16, 16), 16)
+        v = inputs[at].astype(F32)
+        inverse = lax.rsqrt(jnp.sum(v * v, axis=-1, keepdims=True) * (1.0 / width) + norm_eps)
+        normed[at] = (v * inverse * gains_o[0:1]).astype(BF16)
+
+    gather = Gather(normed, normed_o, loc.at[1], gather_s, gather_r)
+    gather.begin()
+    for copy in mixer:
         copy.wait()
-    own.wait()
-
-
-def first(wm, gn, gp, length, collective_id):
+    mixer_own.wait()
+    hops = LineGather(wm_o, length, hop_s, hop_r)
+    hops.start(1)
+    feed, feed_own = exchange_steps(wf, wf_o.at[0], loc.at[3], fs, fr)
+    gather.middle()
+    hops.arrive(1)
+    if length > 2:
+        hops.start(2)
+    gather.end()
+    for hop in range(2, length):
+        hops.arrive(hop)
+        if hop + 1 < length:
+            hops.start(hop + 1)
+    for copy in feed + gates:
+        copy.wait()
+    feed_own.wait()
+    hops.finish()
+
+
+def first(inputs, mixer, mlp, gn, gp, length, collective_id):
+    rows, width = inputs.shape
+    share = mixer.shape[0]
+    wm, wf = (8, share, mixer.shape[1] // 8), (8, share, mlp.shape[1] // 8)
     return pl.pallas_call(
         functools.partial(first_kernel, length),
         out_shape=(
-            jax.ShapeDtypeStruct(wm.shape, wm.dtype),
-            jax.ShapeDtypeStruct((8, length) + gn.shape, gn.dtype),
+            jax.ShapeDtypeStruct((8, rows, width), BF16),
+            jax.ShapeDtypeStruct((length,) + wm, BF16),
+            jax.ShapeDtypeStruct((length,) + wf, BF16),
+            jax.ShapeDtypeStruct((8, width), F32),
             jax.ShapeDtypeStruct((length,) + gp.shape, gp.dtype),
         ),
-        in_specs=[ANY] * 3,
-        out_specs=(ANY,) * 3,
+        in_specs=[VM, VM, VM, VM, ANY],
+        out_specs=(ANY, ANY, ANY, VM, ANY),
         scratch_shapes=[
-            DMA((3,)), DMA((7,)), DMA((7,)), DMA((2, length)), DMA((2, length)),
-            DMA((7,)), DMA((7,)), DMA, DMA,
+            pltpu.VMEM((rows, width), BF16),
+            pltpu.VMEM((8, length, 8, 128), F32),
+            pltpu.VMEM(wm, BF16),
+            pltpu.VMEM(wf, BF16),
+            DMA((4,)), DMA((7,)), DMA((7,)), DMA((7,)), DMA((7,)),
+            DMA((2, length)), DMA((2, length)), DMA((7,)), DMA((7,)), DMA, DMA,
+            DMA((13,)), DMA((13,)), DMA((2, length)), DMA((2, length)),
         ],
-        compiler_params=params(collective_id),
-    )(wm, gn, gp)
+        compiler_params=params(collective_id, 40 * 2**20),
+        cost_estimate=pl.CostEstimate(flops=0, bytes_accessed=300 * 2**20, transcendentals=0),
+    )(inputs, mixer, mlp, gn, gp)
 
 
 def last_kernel(
@@ -494,14 +834,23 @@
 
 
 def forward_kernel(
-    length, proj, gate, chan, mixed, decay_o, width_o, recur_o, enter_o, conv_o, xe, se, ends_o,
-    pre, loc_h, ends, carry, hs, hr, es, er,
+    hop, length, proj, gate, chan, above, mixed, decay_o, width_o, recur_o, enter_o, conv_o, xe, se, ends_o, above_o,
+    pre, loc_h, ends, carry, hs, hr, es, er, gather_l, gather_s, gather_r,
 ):
     y, c, z, x = place()
     line = line_peers(length)
-    greet(line)
+    greet(line + gather_peers())
     seqs, span, rc = mixed.shape
     chunks = span // CHUNK
+    gather = Gather(above, above_o, gather_l, gather_s, gather_r)
+    ahead = device(y, c, lax.rem(z + 1, length), x)
+    for b in range(seqs):
+        xe[b, span : span + 8] = proj[b, span - 8 : span, rc:].astype(BF16).astype(F32)
+    halo = remote(xe.at[:, pl.ds(span, 8)], xe.at[:, pl.ds(0, 8)], hs, hr, ahead)
+    halo.wait_send()
+    gather.begin()
+    if hop:
+        hop.start()
 
     @pl.loop(0, seqs * chunks)
     def _(i):
@@ -509,9 +858,7 @@
         r = pl.multiple_of((i - b * chunks) * CHUNK, CHUNK)
         xe[b, pl.ds(r + 8, CHUNK)] = proj[b, pl.ds(r, CHUNK), rc:].astype(BF16).astype(F32)
 
-    ahead = device(y, c, lax.rem(z + 1, length), x)
-    halo = remote(xe.at[:, pl.ds(span, 8)], xe.at[:, pl.ds(0, 8)], hs, hr, ahead)
-    halo.wait()
+    halo.wait_recv()
 
     @pl.when(z == 0)
     def _():
@@ -541,6 +888,7 @@
         width_o[b, at] = width
         loc_h[b, at] = width * enter * value
 
+    gather.middle()
     row = lax.broadcasted_iota(jnp.int32, (8, rc), 0)
 
     def tile(i, held):
@@ -585,32 +933,41 @@
         gelu, _ = gelu_parts(proj[b, at, :rc])
         mixed[b, at] = (state * gelu).astype(BF16)
 
-
-def recur_forward(proj, gate, chan, length, collective_id):
+    gather.end()
+    if hop:
+        hop.finish()
+
+
+def recur_forward(proj, gate, chan, above, length, collective_id, carried):
     seqs, span, rc = proj.shape[0], proj.shape[1], proj.shape[2] // 2
     full = jax.ShapeDtypeStruct((seqs, span, rc), F32)
     longer = jax.ShapeDtypeStruct((seqs, span + 8, rc), F32)
     low = jax.ShapeDtypeStruct((seqs, span, rc), BF16)
-    return pl.pallas_call(
-        functools.partial(forward_kernel, length),
-        out_shape=(
+    return call_carrying(
+        lambda hop, *refs: forward_kernel(hop, length, *refs),
+        [proj, gate, chan, above],
+        [VM, VM, VM, ANY],
+        (
             low, full, full, full, full, low, longer, longer,
             jax.ShapeDtypeStruct((seqs, 8, rc), F32),
+            jax.ShapeDtypeStruct((8,) + above.shape, above.dtype),
         ),
-        in_specs=[VM] * 3,
-        out_specs=(VM,) * 9,
-        scratch_shapes=[
+        (VM,) * 9 + (ANY,),
+        [
             pltpu.VMEM((seqs, span, rc), F32),
             pltpu.VMEM((seqs, span, rc), F32),
             pltpu.VMEM((length, 2, seqs, 8, rc), F32),
             pltpu.VMEM((seqs, 8, rc), F32),
             DMA, DMA, DMA((length,)), DMA((length,)),
+            DMA, DMA((13,)), DMA((13,)),
         ],
+        carried,
+        length,
         compiler_params=params(collective_id, 56 * 2**20),
         cost_estimate=pl.CostEstimate(
             flops=2 * seqs * span * rc * rc * 2, bytes_accessed=100 * 2**20, transcendentals=0
         ),
-    )(proj, gate, chan)
+    )
 
 
 def backward_kernel(
@@ -806,6 +1163,35 @@
         first_hat / (jnp.sqrt(second_hat) + adam_eps) + decay_rate * weight
     )
     return (first_new, second_new, weight_new)
+
+
+def adam_kernel(rate, decay_rate, factor, w, g, m, v, m_o, v_o, w_o):
+    first_new, second_new, weight_new = adam_step(
+        w[...], g[0].astype(F32), m[...], v[...], factor[0:1, 0:1], rate, decay_rate
+    )
+    m_o[...] = first_new
+    v_o[...] = second_new
+    w_o[...] = weight_new
+
+
+def adam_blocks(weight, grad, first, second, factor, rate, decay_rate):
+    rows, part = grad.shape[1], grad.shape[2] // 3
+    block = pl.BlockSpec((rows, part), lambda t, j: (0, j * 8 + t))
+    shape = jax.ShapeDtypeStruct(weight.shape, F32)
+    return pl.pallas_call(
+        functools.partial(adam_kernel, rate, decay_rate),
+        grid=(8, 3),
+        out_shape=(shape,) * 3,
+        in_specs=[
+            pl.BlockSpec((8, 128), lambda t, j: (0, 0)),
+            block,
+            pl.BlockSpec((1, rows, part), lambda t, j: (t, 0, j)),
+            block,
+            block,
+        ],
+        out_specs=(block,) * 3,
+        cost_estimate=pl.CostEstimate(flops=0, bytes_accessed=7 * 4 * weight.size, transcendentals=0),
+    )(jnp.full((8, 128), factor), weight, grad, first, second)
 
 
 def normalize(values, gain):
@@ -864,59 +1250,71 @@
         v = jnp.roll(v.reshape(lead + (length, 4, pair)), z, axis=-3)
         return v.swapaxes(-2, -3).reshape(lead + (model,))
 
-    mixer_out = (
-        mixer_weight.astype(BF16).reshape(share, 3, 8, r8).transpose(2, 0, 1, 3).reshape(8, share, 3 * r8)
-    )
-    mlp_out = (
-        mlp_weight.astype(BF16).reshape(share, 3, 8, f8).transpose(2, 0, 1, 3).reshape(8, share, 3 * f8)
-    )
-    gains_out = jnp.pad(norm_gains, ((0, 6), (0, 128 - share)))
+    x = lax.axis_index("seq") - 2 * z
+    low_gains = norm_gains.astype(BF16).astype(F32)
+    gains_out = jnp.where(
+        x == 0,
+        jnp.pad(low_gains, ((0, 6), (0, 128 - share))),
+        jnp.pad(low_gains, ((0, 6), (share, 128 - 2 * share))),
+    )
     gate_out = jnp.pad(
         jnp.concatenate([gate_weight, chan_params.T], axis=1).astype(BF16),
         ((0, gate_pad - gate_rows), (0, rc - 2 * head - 8)),
     )
-    mixer_in, gains_in, gate_in = first(mixer_out, gains_out, gate_out, length, 1)
-    gains = gains_in[:, :, :2, :share].astype(BF16).astype(F32)
-    gains = gains.reshape(4, 2, length, 2, share).transpose(3, 0, 2, 1, 4).reshape(2, model)
-    gains = turned(gains)
+    inputs_low = turned(block_input[0])
+    normed_one, mixer_in, mlp_full, gains, gate_in = first(
+        inputs_low, mixer_weight, mlp_weight, gains_out, gate_out, length, 1
+    )
+    normed_one = normed_one.reshape(8 * tokens, model)
+    inputs = inputs_low.astype(F32)
+    inverse_one = lax.rsqrt(jnp.mean(inputs * inputs, axis=-1, keepdims=True) + norm_eps)
+    scaled_one = inputs * inverse_one
     gate_own = gate_in[:, :gate_rows].reshape(r8, rc)
     chan = gate_own[:, 2 * head : 2 * head + 8].astype(F32).T
     lam = chan[7]
     fill = jnp.concatenate([jnp.zeros((7, rc - r8), F32), jnp.ones((1, rc - r8), F32)])
     chan = jnp.concatenate([chan[:7], 8.0 * jax.nn.softplus(-lam)[None]])
     chan = jnp.concatenate([chan, fill], axis=1)
-    gate = jnp.zeros((rc, 2, rc), BF16)
+    gate = []
     for h in range(heads):
-        at = slice(h * head, (h + 1) * head)
-        block = gate_own[at, : 2 * head].reshape(head, 2, head)
-        gate = gate.at[at, :, at].set(block)
-    gate = gate.reshape(rc, 2 * rc)
-
-    mixer_blocks = line_gather(mixer_in.reshape(8 * share, 3 * r8), length)
-    inputs = turned(block_input[0].astype(F32))
+        block = gate_own[h * head : (h + 1) * head, : 2 * head]
+        at = ((0, 0), (h * head, rc - (h + 1) * head))
+        gate.append(
+            jnp.concatenate([jnp.pad(block[:, :head], at), jnp.pad(block[:, head:], at)], axis=1)
+        )
+    gate = jnp.pad(jnp.concatenate(gate), ((0, rc - r8), (0, 0)))
+
     cotangent_low = turned(out_grad[0])
     cotangent = cotangent_low.astype(F32)
-    scaled_one, inverse_one, normed_one = normalize(inputs, gains[0])
-    normed_one = plane_gather(normed_one, 2)
-    mlp_in = plane_exchange(mlp_out, 3)
-    mlp_blocks = line_gather(mlp_in.reshape(8 * share, 3 * f8), length)
-    grad_out = plane_gather(cotangent_low, 4)
-
-    mixer_full = jnp.concatenate(mixer_blocks)
+    carried = length == 4
+    if not carried:
+        mlp_full = jnp.concatenate(line_gather(mlp_full[0].reshape(8 * share, 3 * f8), length))
+
+    def carry_gather(hop):
+        return ("gather", hop, (mlp_full,)) if carried else None
+
+    mixer_full = mixer_in.reshape(model, 3 * r8)
     parts = [jnp.pad(mixer_full[:, n * r8 : (n + 1) * r8], ((0, 0), (0, rc - r8))) for n in range(3)]
     mixer_first = jnp.concatenate(parts[:2], axis=1)
     mixer_last = parts[2]
     span = 2 * tokens
     projected = jnp.dot(normed_one, mixer_first, preferred_element_type=F32)
     projected = projected.reshape(4, span, 2 * rc)
-    mixed, *kept = recur_forward(projected, gate, chan, length, 5)
+    (mixed, *kept, grad_out), more = recur_forward(
+        projected, gate, chan, cotangent_low, length, 5, carry_gather(1)
+    )
+    (mlp_full,) = more or (mlp_full,)
+    grad_out = grad_out.reshape(8 * tokens, model)
     mixed = mixed.reshape(4 * span, rc)
-    mixer_sum = plane_scatter(contract_last(mixed, mixer_last).astype(BF16), 6)
+    mixer_sum, more = plane_scatter(
+        contract_last(mixed, mixer_last).astype(BF16), 6, carry_gather(2), length
+    )
+    (mlp_full,) = more or (mlp_full,)
     residual = inputs + mixer_sum
     scaled_two, inverse_two, normed_two = normalize(residual, gains[1])
-    normed_two = plane_gather(normed_two, 7)
-
-    mlp_full = jnp.concatenate(mlp_blocks)
+    normed_two, more = plane_gather(normed_two, 7, carry_gather(3), length)
+    (mlp_full,) = more or (mlp_full,)
+    mlp_full = mlp_full.reshape(model, 3 * f8)
     mlp_gate, mlp_up, mlp_down = (mlp_full[:, n * f8 : (n + 1) * f8] for n in range(3))
     gg = jnp.dot(normed_two, mlp_gate, preferred_element_type=F32)
     uu = jnp.dot(normed_two, mlp_up, preferred_element_type=F32)
@@ -926,43 +1324,72 @@
     dgg = (dhid * uu * gelu_slope(gg, inner)).astype(BF16)
     duu = (dhid * gelu).astype(BF16)
     dnormed_two = contract_last(dgg, mlp_gate) + contract_last(duu, mlp_up)
-    dnormed_two = plane_scatter(dnormed_two.astype(BF16), 8)
-
-    def line_sum(term):
-        term = term.astype(BF16)
-        rows = term.shape[0] // length
-        return line_scatter([term[k * rows : (k + 1) * rows] for k in range(length)], length)
-
-    down_grad = line_sum(contract_first(grad_out, hid))
-    gate_grad = line_sum(contract_first(normed_two, dgg))
-    up_grad = line_sum(contract_first(normed_two, duu))
-    mlp_sum = plane_scatter(contract_last(hid, mlp_down).astype(BF16), 9)
-    block_output = turned_back((residual + mlp_sum).astype(BF16))
-
+
+    def terms(v):
+        return v.astype(BF16).reshape(length, 8 * share, f8)
+
+    mlp_terms = [
+        terms(contract_first(normed_two, dgg)),
+        terms(contract_first(normed_two, duu)),
+        terms(contract_first(grad_out, hid)),
+    ]
+
+    def carry_scatter(hop, got):
+        if not carried:
+            return None
+        if hop == 1:
+            return ("scatter", 1, mlp_terms)
+        return ("scatter", hop, add_got(got, length - hop, hop))
+
+    def add_got(got, up, down):
+        sums = []
+        for n, term in enumerate(mlp_terms):
+            below = jnp.where(z >= 1, got[n].astype(F32), 0.0)
+            sums.append((term[up].astype(F32) + below).astype(BF16))
+        for n, term in enumerate(mlp_terms):
+            above = jnp.where(z <= length - 2, got[3 + n].astype(F32), 0.0)
+            sums.append((term[down].astype(F32) + above).astype(BF16))
+        return sums
+
+    dnormed_two, got = plane_scatter(dnormed_two.astype(BF16), 8, carry_scatter(1, None), length)
     grad_from_second, gain_two_grad = normalize_back(dnormed_two, scaled_two, inverse_two, gains[1])
     grad_residual = cotangent + grad_from_second
-    dmz = plane_gather(grad_residual.astype(BF16), 10)
+    dmz, got = plane_gather(grad_residual.astype(BF16), 10, carry_scatter(2, got), length)
+    mlp_sum, got = plane_scatter(
+        contract_last(hid, mlp_down).astype(BF16), 9, carry_scatter(3, got), length
+    )
+    block_output = turned_back((residual + mlp_sum).astype(BF16))
+    if carried:
+        mlp_sums = [
+            mlp_terms[n][0].astype(F32)
+            + jnp.where(z >= 1, got[n].astype(F32), 0.0)
+            + jnp.where(z <= length - 2, got[3 + n].astype(F32), 0.0)
+            for n in range(3)
+        ]
+    else:
+        mlp_sums = [line_scatter([term[k] for k in range(length)], length) for term in mlp_terms]
+    mlp_back = jnp.concatenate([g.astype(BF16).reshape(8, share, f8) for g in mlp_sums], axis=2)
+
     dmix = jnp.dot(dmz, mixer_last, preferred_element_type=F32).reshape(4, span, rc)
-    out_grad_sum = line_sum(contract_first(dmz, mixed)[:, :r8])
     dproj, dgate, chan_grad = recur_backward(dmix, gate, chan, kept, projected, length, 11)
     dproj = dproj.reshape(4 * span, 2 * rc)
     dgate = dgate.reshape(4 * span, 2 * rc)
-    dnormed_one = plane_scatter(contract_last(dproj, mixer_first).astype(BF16), 12)
-    first_grad = contract_first(normed_one, dproj)
-    proj_grad_sum = line_sum(
-        jnp.concatenate([first_grad[:, :r8], first_grad[:, rc : rc + r8]], axis=1)
+    proj_grad = contract_first(normed_one, dproj)
+    last_grad = contract_first(dmz, mixed)
+    mixer_terms = jnp.concatenate(
+        [proj_grad[:, :r8], proj_grad[:, rc : rc + r8], last_grad[:, :r8]], axis=1
+    )
+    mixer_terms = mixer_terms.astype(BF16).reshape(length, 8 * share, 3 * r8)
+    dnormed_one, mlp_back, mixer_sums = closing(
+        contract_last(dproj, mixer_first).astype(BF16), mlp_back, mixer_terms, 12
     )
     gate_full_grad = contract_first(kept[4].reshape(4 * span, rc), dgate)
 
     grad_from_first, gain_one_grad = normalize_back(dnormed_one, scaled_one, inverse_one, gains[0])
     input_grad = turned_back(grad_residual + grad_from_first)
 
-    mlp_sums = [gate_grad, up_grad, down_grad]
-    mixer_sums = [proj_grad_sum, out_grad_sum]
-    squares = sum(jnp.sum(g * g) for g in mlp_sums + mixer_sums)
-    mlp_back = jnp.stack([g.astype(BF16).reshape(8, share, f8) for g in mlp_sums], axis=2)
-    mlp_back = plane_exchange(mlp_back.reshape(8, share, 3 * f8), 13)
-    mixer_back = jnp.concatenate([g.astype(BF16).reshape(8, share, -1) for g in mixer_sums], axis=2)
+    squares = sum(jnp.sum(g * g) for g in mlp_sums + [mixer_sums])
+    mixer_back = mixer_sums.astype(BF16).reshape(8, share, 3 * r8)
 
     gains_back = jnp.stack([gain_one_grad, gain_two_grad])
     gains_back = gains_back.reshape(2, length, 8, share).transpose(2, 1, 0, 3)
@@ -989,7 +1416,6 @@
     grad_norm = jnp.sqrt(jnp.sum(squares_sum))
     factor = clip_limit / jnp.maximum(grad_norm, clip_limit)
     mixer_grad = mixer_back.astype(F32).reshape(8, share, 3, r8).transpose(1, 2, 0, 3).reshape(share, 3 * lru)
-    mlp_grad = mlp_back.astype(F32).reshape(8, share, 3, f8).transpose(1, 2, 0, 3).reshape(share, 3 * hidden)
     gains_up = adam_step(
         norm_gains, gains_sum[:2, :share], first_gains, second_gains, factor, rate_gains, 0.0
     )
@@ -1003,8 +1429,8 @@
         chan_params, gate_sum[:gate_rows, 2 * head : 2 * head + 8].T, first_chan, second_chan, factor,
         rate_channel, 0.0,
     )
-    mlp_up = adam_step(
-        mlp_weight, mlp_grad, first_mlp, second_mlp, factor, rate_matrix, decay_matrix
+    mlp_up = adam_blocks(
+        mlp_weight, mlp_back, first_mlp, second_mlp, factor, rate_matrix, decay_matrix
     )
     return (
         block_output[None],

time: 1230 us -> 940 us (0.76)
  waiting for transfers between devices: 129 us -> 0 us
  starting transfers between devices: 110 us -> 0 us
  local copies, waits for them, and re-layouts: 155 us -> 67.8 us
  Pallas kernels: 554 us -> 634 us
  other arithmetic: 121 us -> 65.1 us
  matrix products: 141 us -> 156 us
    ppermute x42 -> x0, waiting for transfers between devices: 129 us -> none  [the longest x15 77.5 us: line_scatter(): up = lax.ppermute(up_block, 'seq', up_routes)]
    ppermute x42 -> x0, starting transfers between devices: 110 us -> none  [the longest x15 49.6 us: line_scatter(): up = lax.ppermute(up_block, 'seq', up_routes)]
    pallas_call x1, Pallas kernels: 21.2 us -> 110 us  [first(): pl.pallas_call(functools.partial(first_kernel, length), out_shape=(jax.Sh...]
    scatter x2 -> x0, local copies, waits for them, and re-layouts: 29.1 us -> none  [on_device(): gate = gate.at[at, :, at].set(block)]
    convert_element_type x18 -> x7, other arithmetic: 33.3 us -> 12.2 us  [the longest x5 10.6 us: add_got(): sums.append((term[down].astype(F32) + above).astype(BF16))]
    reshape x8 -> x0, local copies, waits for them, and re-layouts: 18.9 us -> none  [the longest x1 7.08 us: on_device(): mlp_back = plane_exchange(mlp_back.reshape(8, share, 3 * f8), 13)]
    pallas_call x1, Pallas kernels: 44.6 us -> 26.6 us  [last(): pl.pallas_call(functools.partial(last_kernel, length), out_shape=(jax.Sha...]
    concatenate x4 -> x3, other arithmetic: 21.6 us -> 6.96 us  [the longest x1 5.26 us: on_device(): jnp.concatenate([proj_grad[:, :r8], proj_grad[:, rc:rc + r8], last_grad[:...]
  transfers between devices with their start and end apart: 42 -> 0, of which waited for: 11 -> 0; matrix products, arithmetic and copies ran while one was open for 20% -> 0% of each run, Pallas kernels for 40% -> 0%
where the time goes in v2:
time: 940 us; the launch traced here: 930 us
  Pallas kernels  634 us (67%)
  matrix products  156 us (17%)
  local copies, waits for them, and re-layouts  67.8 us (7%)
  other arithmetic  65.1 us (7%)
    pallas_call x6, Pallas kernels, call_carrying(): pl.pallas_call(kernel, out_shape=tuple(out_shapes) + tuple(more), in_spec...  349 us
    pallas_call x1, Pallas kernels, first(): pl.pallas_call(functools.partial(first_kernel, length), out_shape=(jax.Sh...  110 us
    pallas_call x1, Pallas kernels, closing(): pl.pallas_call(closing_kernel, out_shape=(jax.ShapeDtypeStruct((rows, wid...  80.3 us
    dot_general x5, matrix products, contract_last(): lax.dot_general(left, right, (((1,), (1,)), ((), ())), preferred_element_...  51.9 us
    dot_general x6, matrix products, contract_first(): lax.dot_general(left, right, (((0,), (0,)), ((), ())), preferred_element_...  49.7 us
    pallas_call x1, Pallas kernels, recur_backward(): pl.pallas_call(functools.partial(backward_kernel, length), grid=(1,), out...  45.6 us
    pallas_call x1, Pallas kernels, last(): pl.pallas_call(functools.partial(last_kernel, length), out_shape=(jax.Sha...  26.6 us
    unnamed x143, local copies, waits for them, and re-layouts  23.2 us

profile of v2, /device:TPU:0, one launch (start us, length us, event | category | flops | bytes accessed | tf_op | source)
XLA Modules:
  0.0 929.7 jit_solution(15240668188804906964)
XLA Ops:
  0.7 1.8 reshape_squeeze.6
  3.1 3.3 multiply_reduce_fusion.2
  6.4 1.8 reshape.218.inputs
  9.3 2.3 copy-done.2
  11.6 110.4 %shard_map.304 = (bf16[8,256,2048]{2,1,0:T(8,128)(2,1)}, bf16[4,8,64,960]{3,2,1,0:T(8,128)(2,1)S(1)}, bf16[4,8,64,2304]{3,2,1,0:T(8,128)(2,1)}, f32[8,2048]{1,0:T(8,128)S(1)}, bf16[4,80,384]{2,1,0:T(8,128)(2,1)S(1)}) custom-call(bf16[256,2048]{1,0:T(8,128)(2,1)S(1)} %reshape.218.inputs, f32[64,7680]{1,0:T(8,128)S(1)} %copy-done.7, ...), custom_call_target="tpu_custom_call" | custom-call | bytes 314572800 | tf_op jit(solution)/shard_map/pallas_call | solution.py:657
  122.0 2.0 copy-done.8
  126.1 4.2 fusion.90
  130.3 2.1 slice_select_fusion
  132.5 8.5 fusion.9.refs_0_.proj
  141.0 1.8 reshape_squeeze.7
  144.6 1.6 reshape.221.refs_3_
  146.2 80.3 %shard_map.305 = (bf16[4,512,384]{2,1,0:T(8,128)(2,1)}, f32[4,512,384]{2,1,0:T(8,128)}, f32[4,512,384]{2,1,0:T(8,128)}, f32[4,512,384]{2,1,0:T(8,128)}, f32[4,51...) custom-call(f32[4,512,768]{2,1,0:T(8,128)} %fusion.9.refs_0_.proj, ...), custom_call_target="tpu_custom_call", output_to_operand_aliasing={{10}: (4, {})} | custom-call | flops 1207959552 | bytes 104857600 | tf_op jit(solution)/shard_map/pallas_call | solution.py:214
  226.6 6.2 convolution_convert_fusion.2
  232.8 54.8 %shard_map.306 = (f32[256,2048]{1,0:T(8,128)S(1)}, bf16[4,8,64,2304]{3,2,1,0:T(8,128)(2,1)}) custom-call(bf16[8,256,2048]{2,1,0:T(8,128)(2,1)S(1)} %bitcast.90, bf16[4,8,64,2304]{3,2,1,0:T(8,128)(2,1)} %get-tuple-element.90.refs_1_), custom_call_target="tpu_custom_call", output_to_operand_aliasing={{1}: (1, {})} | custom-call | bytes 146800640 | tf_op jit(solution)/shard_map/pallas_call | solution.py:214
  289.9 53.8 %shard_map.307 = (bf16[8,256,2048]{2,1,0:T(8,128)(2,1)}, bf16[4,8,64,2304]{3,2,1,0:T(8,128)(2,1)}) custom-call(bf16[256,2048]{1,0:T(8,128)(2,1)} %multiply_convert_fusion.2.refs_0_, bf16[4,8,64,2304]{3,2,1,0:T(8,128)(2,1)} %get-tuple-element.93.refs_1_), custom_call_target="tpu_custom_call", output_to_operand_aliasing={{1}: (1, {})} | custom-call | bytes 125829120 | tf_op jit(solution)/shard_map/pallas_call | solution.py:214
  343.8 10.2 %fusion.15 = f32[2048,768]{1,0:T(8,128)S(1)} fusion(bf16[2048,2048]{1,0:T(8,128)(2,1)} %bitcast.131, bf16[2048,2304]{1,0:T(8,128)(2,1)} %bitcast.96), kind=kOutput, calls=%fused_computation.33 | convolution fusion | flops 6442450944 | bytes 17825792 | tf_op jit(solution)/shard_map/dot_general | solution.py:1320
  354.0 8.5 fusion.19
  362.5 17.6 %multiply_convert_fusion = (bf16[2048,768]{1,0:T(8,128)(2,1)}, bf16[2048,768]{1,0:T(8,128)(2,1)}, bf16[2048,768]{1,0:T(8,128)(2,1)}) fusion(f32[2048,768]{1,0:T(8,128)} %fusion.19, f32[2048,768]{1,0:T(8,128)S(1)} %fusion.15, bf16[2048,2048]{1,0:T(8,128)(2,1)} %bitcast.129, bf16[2048,2304]{1,0:T(8,128)(2,1)S(1)} %bitcast.101), kind=kOutput, calls=%fused_computation.14 | convolution fusion | flops 6481772544 | bytes 33554432 | tf_op jit(solution)/shard_map/dot_general | solution.py:1321
  380.1 11.5 %convolution_convert_fusion.4 = bf16[2048,768]{1,0:T(8,128)(2,1)} fusion(bf16[2048,2048]{1,0:T(8,128)(2,1)} %bitcast.130, bf16[2048,768]{1,0:T(8,128)(2,1)} %get-tuple-element.233), kind=kOutput, calls=%fused_computation.22 | convolution fusion | flops 6444023808 | bytes 14680064 | tf_op jit(solution)/shard_map/dot_general | solution.py:1151
  391.7 9.4 %convolution_convert_fusion.5 = bf16[2048,768]{1,0:T(8,128)(2,1)S(1)} fusion(bf16[2048,2048]{1,0:T(8,128)(2,1)} %bitcast.132, bf16[2048,768]{1,0:T(8,128)(2,1)S(1)} %copy-done.65), kind=kOutput, calls=%fused_computation.23 | convolution fusion | flops 6444023808 | bytes 14680064 | tf_op jit(solution)/shard_map/dot_general | solution.py:1151
  401.1 7.5 convolution_convert_fusion.6
  408.6 12.6 %fusion.17 = f32[2048,2048]{1,0:T(8,128)} fusion(bf16[2048,768]{1,0:T(8,128)(2,1)S(1)} %copy-done.64, bf16[2048,2304]{1,0:T(8,128)(2,1)} %bitcast.97), kind=kOutput, calls=%fused_computation.35 | convolution fusion | flops 6442450944 | bytes 23068672 | tf_op jit(solution)/shard_map/dot_general | solution.py:1145
  421.2 13.4 %add_convert_fusion = bf16[2048,2048]{1,0:T(8,128)(2,1)} fusion(f32[2048,2048]{1,0:T(8,128)} %fusion.17, bf16[2048,768]{1,0:T(8,128)(2,1)S(1)} %copy-done.65, bf16[2048,2304]{1,0:T(8,128)(2,1)} %bitcast.98), kind=kOutput, calls=%fused_computation | convolution fusion | flops 6450839552 | bytes 31457280 | tf_op jit(solution)/shard_map/dot_general | solution.py:1145
  434.6 52.0 %shard_map.308 = (f32[256,2048]{1,0:T(8,128)S(1)}, bf16[512,768]{1,0:T(8,128)(2,1)S(1)}, bf16[512,768]{1,0:T(8,128)(2,1)S(1)}, bf16[512,768]{1,0:T(8,128)(2,1)S(...) custom-call(bf16[8,256,2048]{2,1,0:T(8,128)(2,1)} %bitcast.106, ...), custom_call_target="tpu_custom_call" | custom-call | bytes 146800640 | tf_op jit(solution)/shard_map/pallas_call | solution.py:214
  491.1 3.3 fusion.37
  494.5 3.8 fusion.33
  499.6 1.6 fusion.83.refs_0_
  501.2 52.2 %shard_map.309 = (bf16[8,256,2048]{2,1,0:T(8,128)(2,1)}, bf16[512,768]{1,0:T(8,128)(2,1)}, bf16[512,768]{1,0:T(8,128)(2,1)}, bf16[512,768]{1,0:T(8,128)(2,1)}, b...) custom-call(bf16[256,2048]{1,0:T(8,128)(2,1)} %fusion.83.refs_0_, ...), custom_call_target="tpu_custom_call" | custom-call | bytes 125829120 | tf_op jit(solution)/shard_map/pallas_call | solution.py:214
  553.4 2.5 add_convert_fusion.2
  560.9 10.7 %convolution_convert_fusion.1 = bf16[2048,2048]{1,0:T(8,128)(2,1)} fusion(bf16[2048,768]{1,0:T(8,128)(2,1)S(1)} %copy-done.66, bf16[2048,2304]{1,0:T(8,128)(2,1)} %bitcast.99), kind=kOutput, calls=%fused_computation.4 | convolution fusion | flops 6446645248 | bytes 14680064 | tf_op jit(solution)/shard_map/dot_general | solution.py:1145
  571.6 56.1 %shard_map.310 = (f32[256,2048]{1,0:T(8,128)S(1)}, bf16[512,768]{1,0:T(8,128)(2,1)S(1)}, bf16[512,768]{1,0:T(8,128)(2,1)S(1)}, bf16[512,768]{1,0:T(8,128)(2,1)S(...) custom-call(bf16[8,256,2048]{2,1,0:T(8,128)(2,1)} %bitcast.105, ...), custom_call_target="tpu_custom_call" | custom-call | bytes 146800640 | tf_op jit(solution)/shard_map/pallas_call | solution.py:214
  627.8 2.3 multiply_reduce_fusion.7
  630.1 2.0 multiply_reduce_fusion.6
  633.4 3.4 multiply_reduce_fusion.5
  637.4 7.3 fusion.95
  644.9 1.6 copy.116
  646.4 10.0 %fusion.38.dmix = f32[4,512,384]{2,1,0:T(8,128)} fusion(bf16[4,512,2048]{2,1,0:T(8,128)(2,1)} %bitcast.128, bf16[2048,320]{1,0:T(8,128)(2,1)} %get-tuple-element.240), kind=kOutput, calls=%fused_computation.84 | convolution fusion | flops 3221225472 | bytes 12845056 | tf_op jit(solution)/shard_map/dot_general | solution.py:1373
  656.4 45.6 %shard_map.311 = (bf16[4,512,768]{2,1,0:T(8,128)(2,1)}, bf16[4,512,768]{2,1,0:T(8,128)(2,1)}, f32[8,8,384]{2,1,0:T(8,128)}) custom-call(f32[4,512,384]{2,1,0:T(8,128)} %fusion.38.dmix, bf16[384,768]{1,0:T(8,128)(2,1)} %pad.63.refs_1_.gate, f32[8,384]{1,0:T(8,128)} %pad_maximum_fusion.3.refs_2_.chan, f32[4,512,384]{2,1,0:T(8,128)} %get-tuple-element.112.decay, ...), custom_call_target="tpu_custom_call" | custom-call | flops 1207959552 | bytes 125829120 | tf_op jit(solution)/shard_map/pallas_call | solution.py:1085
  702.0 10.2 %convolution_convert_fusion.3 = bf16[2048,768]{0,1:T(8,128)(2,1)S(1)} fusion(bf16[2048,2048]{1,0:T(8,128)(2,1)} %bitcast.125, bf16[2048,768]{1,0:T(8,128)(2,1)} %bitcast.137), kind=kOutput, calls=%fused_computation.21 | convolution fusion | flops 6444023808 | bytes 14680064 | tf_op jit(solution)/shard_map/dot_general | solution.py:1151
  713.4 2.5 copy.114
  716.0 1.5 copy.115
  717.5 5.3 pad_maximum_fusion.g
  722.8 1.6 pad_maximum_fusion.1.e
  725.5 9.0 convolution_convert_fusion
  734.5 80.3 %shard_map.312 = (f32[256,2048]{1,0:T(8,128)}, bf16[8,64,2304]{2,1,0:T(8,128)(2,1)}, f32[512,960]{1,0:T(8,128)}) custom-call(bf16[8,256,2048]{2,1,0:T(8,128)(2,1)} %bitcast.104, bf16[8,64,2304]{2,1,0:T(8,128)(2,1)} %pad_maximum_fusion.1.e, bf16[4,512,960]{2,1,0:T(8,128)(2,1)} %pad_maximum_fusion.g), custom_call_target="tpu_custom_call" | custom-call | bytes 262144000 | tf_op jit(solution)/shard_map/pallas_call | solution.py:535
  814.8 4.4 multiply_reduce_fusion
  819.9 3.8 convolution_bitcast_fusion
  826.3 1.5 pad_maximum_fusion.2
  832.0 26.6 %shard_map.313 = (bf16[8,64,960]{2,1,0:T(8,128)(2,1)S(1)}, f32[8,128]{1,0:T(8,128)S(1)}, f32[80,384]{1,0:T(8,128)S(1)}, f32[8,128]{1,0:T(8,128)S(1)}) custom-call(bf16[8,64,960]{2,1,0:T(8,128)(2,1)S(1)} %bitcast.93, f32[8,4,8,128]{3,2,1,0:T(8,128)S(1)} %pad.65.gn, f32[4,80,384]{2,1,0:T(8,128)S(1)} %copy-done.12, f32[8,128]{1,0:T(8,128)S(1)} %scatter.4.sq), custom_call_target="tpu_custom_call" | custom-call | tf_op jit(solution)/shard_map/pallas_call | solution.py:787
  861.5 21.9 %shard_map.314 = (f32[64,18432]{1,0:T(8,128)}, f32[64,18432]{1,0:T(8,128)}, f32[64,18432]{1,0:T(8,128)}) custom-call(f32[8,128]{1,0:T(8,128)} %broadcast_in_dim.32.factor, f32[64,18432]{1,0:T(8,128)} %w.1, bf16[8,64,2304]{2,1,0:T(8,128)(2,1)} %get-tuple-element.135.g, f32[64,18432]{1,0:T(8,128)} %m.1, f32[64,18432]{1,0:T(8,128)} %v.1), custom_call_target="tpu_custom_call" | custom-call | bytes 33030144 | tf_op jit(solution)/shard_map/pallas_call | solution.py:1181
  885.0 1.5 multiply_subtract_fusion.2
  886.6 1.4 copy.128
  888.0 1.4 copy.129
  889.5 1.4 copy.130
  890.9 1.7 multiply_subtract_fusion.1
  892.6 2.8 convert_multiply_fusion.1
  895.5 4.5 mul.429
  900.0 4.7 copy.122
  904.7 2.8 mul.431
  907.6 7.0 multiply_subtract_fusion
  915.2 3.0 fusion.27
  918.1 2.7 reshape.240
  922.2 1.8 broadcast_in_dim_reshape.7
  926.6 1.6 broadcast_in_dim_reshape.6
  (194 shorter events, 36.0 us)
Async XLA Ops:
  3.0 5.2 copy-start.53
  3.0 5.3 copy-start.49
  3.1 6.1 copy-start.44
  3.1 6.2 copy-start.7
  8.2 279.4 %copy-start = (bf16[256,2048]{1,0:T(8,128)(2,1)}, bf16[256,2048]{1,0:T(8,128)(2,1)S(1)}, u32[]{:S(2)}) copy-start(bf16[256,2048]{1,0:T(8,128)(2,1)S(1)} %reshape.218.inputs) | copy-start | bytes 3145732
  9.3 2.3 copy-start.2
  11.6 112.6 %copy-start.57 = (f32[8,64]{1,0:T(8,128)S(1)}, f32[8,64]{1,0:T(8,128)}, u32[]{:S(2)}) copy-start(f32[8,64]{1,0:T(8,128)} %constant.163.clone.1) | copy-start | bytes 6148
  122.0 2.0 copy-start.8
  126.1 4.2 copy-start.60
  126.1 6.4 copy-start.61
  130.3 10.7 %copy-start.35 = (bf16[2048,320]{1,0:T(8,128)(2,1)}, bf16[2048,320]{1,0:T(8,128)(2,1)S(1)}, u32[]{:S(2)}) copy-start(bf16[2048,320]{1,0:T(8,128)(2,1)S(1)} %get-tuple-element.241) | copy-start | bytes 3932164
  132.4 8.5 copy-start.37
  146.2 80.4 %copy-start.39 = (bf16[2048,320]{1,0:T(8,128)(2,1)S(1)}, bf16[2048,320]{1,0:T(8,128)(2,1)}, u32[]{:S(2)}) copy-start(bf16[2048,320]{1,0:T(8,128)(2,1)} %get-tuple-element.240) | copy-start | bytes 3932164
  288.0 55.8 %copy-start.24 = (f32[256,2048]{1,0:T(8,128)}, f32[256,2048]{1,0:T(8,128)S(1)}, u32[]{:S(2)}) copy-start(f32[256,2048]{1,0:T(8,128)S(1)} %get-tuple-element.230) | copy-start | bytes 6291460
  343.8 10.2 %copy-start.23 = (bf16[4,8,64,2304]{3,2,1,0:T(8,128)(2,1)S(1)}, bf16[4,8,64,2304]{3,2,1,0:T(8,128)(2,1)}, u32[]{:S(2)}) copy-start(bf16[4,8,64,2304]{3,2,1,0:T(8,128)(2,1)} %get-tuple-element.95) | copy-start | bytes 28311556
  343.8 10.2 %copy-start.62 = (bf16[8,256,2048]{2,1,0:T(8,128)(2,1)S(1)}, bf16[8,256,2048]{2,1,0:T(8,128)(2,1)}, u32[]{:S(2)}) copy-start(bf16[8,256,2048]{2,1,0:T(8,128)(2,1)} %get-tuple-element.94) | copy-start | bytes 25165828
  380.1 11.5 %copy-start.65 = (bf16[2048,768]{1,0:T(8,128)(2,1)S(1)}, bf16[2048,768]{1,0:T(8,128)(2,1)}, u32[]{:S(2)}) copy-start(bf16[2048,768]{1,0:T(8,128)(2,1)} %get-tuple-element.231) | copy-start | bytes 9437188
  380.1 21.0 %slice-start = ((s8[8388608]{0:T(1024)(128)(4,1)}), s8[4194304]{0:T(1024)(128)(4,1)S(1)}, s32[]{:S(2)}) async-start(s8[8388608]{0:T(1024)(128)(4,1)} %bitcast.134), calls=%async_computation | async-start | bytes 8388608
  391.7 9.5 %slice-start.1 = ((s8[8388608]{0:T(1024)(128)(4,1)}), s8[4194304]{0:T(1024)(128)(4,1)S(1)}, s32[]{:S(2)}) async-start(s8[8388608]{0:T(1024)(128)(4,1)} %bitcast.134), calls=%async_computation.1 | async-start | bytes 8388608
  391.7 9.5 %copy-start.64 = (bf16[2048,768]{1,0:T(8,128)(2,1)S(1)}, bf16[2048,768]{1,0:T(8,128)(2,1)}, u32[]{:S(2)}) copy-start(bf16[2048,768]{1,0:T(8,128)(2,1)} %get-tuple-element.232) | copy-start | bytes 9437188
  401.1 33.5 %copy-start.3 = (bf16[2048,768]{1,0:T(8,128)(2,1)}, bf16[2048,768]{1,0:T(8,128)(2,1)S(1)}, u32[]{:S(2)}) copy-start(bf16[2048,768]{1,0:T(8,128)(2,1)S(1)} %convolution_convert_fusion.5) | copy-start | bytes 9437188
  408.6 26.0 %copy-start.5 = (bf16[2048,768]{1,0:T(8,128)(2,1)}, bf16[2048,768]{1,0:T(8,128)(2,1)S(1)}, u32[]{:S(2)}) copy-start(bf16[2048,768]{1,0:T(8,128)(2,1)S(1)} %convolution_convert_fusion.6) | copy-start | bytes 9437188
  488.4 0.9 copy-start.18
  490.2 0.9 copy-start.22
  491.1 3.4 copy-start.15
  491.1 3.4 copy-start.17
  491.1 3.4 copy-start.19
  494.5 3.9 copy-start.25
  498.3 1.2 copy-start.27
  553.4 2.8 copy-start.4
  553.4 3.0 copy-start.42
  553.4 3.2 copy-start.43
  556.7 1.9 copy-start.6
  556.7 2.1 copy-start.40
  556.7 2.3 copy-start.41
  559.0 1.9 copy-start.66
  627.7 4.3 copy-start.10
  627.7 4.3 copy-start.20
  717.5 5.3 copy-start.32
  717.5 5.3 copy-start.33
  717.5 5.3 copy-start.34
  717.5 6.9 copy-start.63
  722.8 2.1 copy-start.36
  722.8 2.7 copy-start.38
  819.9 4.7 copy-start.46
  824.7 4.1 copy-start.1
  824.7 4.1 copy-start.47
  826.3 2.4 copy-start.29
  829.7 1.2 copy-start.9
  830.9 1.0 copy-start.12
  858.5 1.0 copy-start.13
  861.4 22.0 %copy-start.51 = (f32[8,80]{1,0:T(8,128)S(1)}, f32[8,80]{1,0:T(8,128)}, u32[]{:S(2)}) copy-start(f32[8,80]{1,0:T(8,128)} %get-tuple-element.270) | copy-start | bytes 7684
  861.5 22.1 %copy-start.55 = (f32[8,80]{1,0:T(8,128)S(1)}, f32[8,80]{1,0:T(8,128)}, u32[]{:S(2)}) copy-start(f32[8,80]{1,0:T(8,128)} %param.31) | copy-start | bytes 7684
  861.5 22.2 %copy-start.56 = (f32[8,80]{1,0:T(8,128)S(1)}, f32[8,80]{1,0:T(8,128)}, u32[]{:S(2)}) copy-start(f32[8,80]{1,0:T(8,128)} %param.36) | copy-start | bytes 7684
  861.5 22.9 %copy-start.50 = (f32[8,80]{1,0:T(8,128)S(1)}, f32[8,80]{1,0:T(8,128)}, u32[]{:S(2)}) copy-start(f32[8,80]{1,0:T(8,128)} %param.26) | copy-start | bytes 7684
  861.5 29.4 %copy-start.45 = (f32[80,320]{1,0:T(8,128)S(1)}, f32[80,320]{1,0:T(8,128)}, u32[]{:S(2)}) copy-start(f32[80,320]{1,0:T(8,128)} %param.25) | copy-start | bytes 307204
  907.5 7.0 copy-start.54
  907.5 7.0 copy-start.58
  907.5 7.0 copy-start.59
  907.5 7.6 copy-start.11
  907.5 7.6 copy-start.26
  907.5 7.6 copy-start.28
  907.5 7.6 copy-start.30
  922.2 1.9 copy-start.31
  (5 other events, 4.2 us)

commit v3 on v2

v3 whole, which is shorter than its diff:
```python
import functools
import math

import jax
import jax.numpy as jnp
from jax import lax
from jax.experimental import pallas as pl
from jax.experimental.pallas import tpu as pltpu
from jax.sharding import PartitionSpec as P

STEP = 10
norm_eps = 1e-06
clip_limit = 1.0
beta_first = 0.9
beta_second = 0.999
adam_eps = 1e-08
rate_matrix = 0.05
rate_gains = 0.8
rate_channel = 2.0
decay_matrix = 0.1

MESH = pl.DeviceIdType.MESH
F32 = jnp.float32
BF16 = jnp.bfloat16
ANY = pl.BlockSpec(memory_space=pl.ANY)
VM = pl.BlockSpec(memory_space=pltpu.VMEM)
FLIPS = [(fy, fc, fx) for fy in (0, 1) for fc in (0, 1) for fx in (0, 1) if fy + fc + fx]
GELU_SCALE = math.sqrt(2.0 / math.pi)


def place():
    b = lax.axis_index("batch")
    s = lax.axis_index("seq")
    y, z = b // 2, s // 2
    return y, b - 2 * y, z, s - 2 * z


def device(y, c, z, x):
    return (y * 2 + c, z * 2 + x)


def rank(y, c, x):
    return (y * 2 + c) * 2 + x


def flip(v, f):
    return 1 - v if f else v


def greet(peers):
    barrier = pltpu.get_barrier_semaphore()
    for peer in peers:
        pl.semaphore_signal(barrier, inc=1, device_id=peer, device_id_type=MESH)
    pl.semaphore_wait(barrier, len(peers))


def remote(src, dst, send, recv, to):
    copy = pltpu.make_async_remote_copy(
        src_ref=src, dst_ref=dst, send_sem=send, recv_sem=recv, device_id=to, device_id_type=MESH
    )
    copy.start()
    return copy


def params(collective_id, vmem=None):
    return pltpu.CompilerParams(
        collective_id=collective_id, has_side_effects=True, vmem_limit_bytes=vmem
    )


DMA = pltpu.SemaphoreType.DMA


def gather_peers():
    y, c, z, x = place()
    return [device(y, c, z, 1 - x), device(1 - y, c, z, x), device(y, 1 - c, z, x)]


class Gather:
    def __init__(self, a, o, loc, ss, rs):
        y, c, z, x = place()
        self.to_x, self.to_y, self.to_c = gather_peers()
        self.me, self.bx = rank(y, c, x), rank(y, c, 1 - x)
        self.by, self.bd = rank(1 - y, c, x), rank(1 - y, c, 1 - x)
        half = a.shape[0] // 2
        self.lo, self.hi = pl.ds(0, half), pl.ds(half, half)
        self.a, self.o, self.loc, self.ss, self.rs = a, o, loc, ss, rs
        self.done = []

    def send(self, src, dst, k, to):
        copy = remote(src, dst, self.ss.at[k], self.rs.at[k], to)
        self.done.append(copy)
        return copy

    def relay(self, block, part, k, to):
        return self.send(self.o.at[block, part], self.o.at[block, part], k, to)

    def begin(self):
        a, o, me, lo, hi = self.a, self.o, self.me, self.lo, self.hi
        self.s0 = self.send(a.at[lo], o.at[me, lo], 0, self.to_x)
        self.s1 = self.send(a.at[hi], o.at[me, hi], 1, self.to_y)
        self.s2 = self.send(a.at[hi], o.at[me, hi], 2, self.to_x)
        self.s3 = self.send(a.at[lo], o.at[me, lo], 3, self.to_y)
        self.s4 = self.send(a, o.at[me], 4, self.to_c)
        self.own = pltpu.make_async_copy(a, o.at[me], self.loc)
        self.own.start()

    def middle(self):
        self.s0.wait_recv()
        self.s5 = self.relay(self.bx, self.lo, 5, self.to_y)
        self.last = [self.s4, self.relay(self.bx, self.lo, 7, self.to_c)]
        self.s1.wait_recv()
        self.s6 = self.relay(self.by, self.hi, 6, self.to_x)
        self.last.append(self.relay(self.by, self.hi, 8, self.to_c))

    def end(self, mark=lambda: None):
        self.s2.wait_recv()
        self.last.append(self.relay(self.bx, self.hi, 9, self.to_c))
        self.s3.wait_recv()
        self.last.append(self.relay(self.by, self.lo, 10, self.to_c))
        mark()
        self.s5.wait_recv()
        self.last.append(self.relay(self.bd, self.lo, 11, self.to_c))
        self.s6.wait_recv()
        self.last.append(self.relay(self.bd, self.hi, 12, self.to_c))
        for copy in self.last:
            copy.wait_recv()
        for copy in self.done:
            copy.wait_send()
        self.own.wait()


def scatter_steps(p, o, mine, sib, part, got, loc, ss, rs, mark=lambda name: None):
    y, c, z, x = place()
    to_x, to_y, to_c = gather_peers()
    half = o.shape[0] // 2
    step = 16
    cut = (pl.ds(0, half), pl.ds(half, half))
    where = ((1 - y, 1 - x), (1 - y, x), (y, 1 - x), (y, x))
    order = [(0, 0), (0, 1), (1, 0), (2, 1), (2, 0), (1, 1), (3, 0), (3, 1)]
    from_c, own, sends = {}, {}, []
    for n, (t, h) in enumerate(order):
        ty, tx = where[t]
        own[t, h] = pltpu.make_async_copy(
            p.at[rank(ty, c, tx), cut[h]], mine.at[t, h], loc.at[n]
        )
        own[t, h].start()
        from_c[t, h] = remote(
            p.at[rank(ty, 1 - c, tx), cut[h]], sib.at[t, h], ss.at[n], rs.at[n], to_c
        )
        sends.append(from_c[t, h])

    def add(dst, t, h, extra):
        own[t, h].wait()
        from_c[t, h].wait_recv()

        @pl.loop(0, half // step)
        def _(i):
            at = pl.ds(pl.multiple_of(i * step, step), step)
            total = mine[t, h, at].astype(F32) + sib[t, h, at].astype(F32)
            for ref in extra:
                total = total + ref[at].astype(F32)
            dst[at] = total.astype(dst.dtype)

    def send(k, slot, to):
        copy = remote(part.at[k], got.at[slot], ss.at[8 + k], rs.at[8 + slot], to)
        sends.append(copy)
        return copy

    def arrival(slot):
        return pltpu.make_async_remote_copy(
            src_ref=part.at[0], dst_ref=got.at[slot], send_sem=ss.at[8], recv_sem=rs.at[8 + slot],
            device_id=to_x, device_id_type=MESH,
        )

    add(part.at[0], 0, 0, ())
    send(0, 1, to_y)
    add(part.at[1], 0, 1, ())
    send(1, 3, to_x)
    add(part.at[2], 1, 0, ())
    send(2, 0, to_y)
    add(part.at[3], 2, 1, ())
    send(3, 2, to_x)
    arrival(1).wait_recv()
    add(part.at[4], 2, 0, (got.at[1],))
    send(4, 4, to_x)
    mark("early")
    arrival(3).wait_recv()
    add(part.at[5], 1, 1, (got.at[3],))
    send(5, 5, to_y)
    mark("late")
    arrival(0).wait_recv()
    arrival(4).wait_recv()
    add(o.at[cut[0]], 3, 0, (got.at[0], got.at[4]))
    arrival(2).wait_recv()
    arrival(5).wait_recv()
    add(o.at[cut[1]], 3, 1, (got.at[2], got.at[5]))
    for copy in sends:
        copy.wait_send()


def scatter_scratch(half, width):
    return [
        pltpu.VMEM((4, 2, half, width), BF16),
        pltpu.VMEM((4, 2, half, width), BF16),
        pltpu.VMEM((6, half, width), BF16),
        pltpu.VMEM((6, half, width), BF16),
        DMA((8,)),
        DMA((14,)),
        DMA((14,)),
    ]


def exchange_steps(a, o, loc, ss, rs, columns=None):
    y, c, z, x = place()
    me = rank(y, c, x)
    dst = o.at[me] if columns is None else o.at[me, :, columns]
    copies = []
    for n, (fy, fc, fx) in enumerate(FLIPS):
        ty, tc, tx = flip(y, fy), flip(c, fc), flip(x, fx)
        copies.append(remote(a.at[rank(ty, tc, tx)], dst, ss.at[n], rs.at[n], device(ty, tc, z, tx)))
    own = pltpu.make_async_copy(a.at[me], dst, loc)
    own.start()
    return copies, own


def plane_peers():
    y, c, z, x = place()
    return [device(flip(y, fy), flip(c, fc), z, flip(x, fx)) for fy, fc, fx in FLIPS]


def line_peers(length):
    y, c, z, x = place()
    return [device(y, c, lax.rem(z + k, length), x) for k in range(1, length)]


class LineGather:
    def __init__(self, buf, length, ss, rs):
        y, c, z, x = place()
        self.z, self.length, self.buf, self.ss, self.rs = z, length, buf, ss, rs
        self.up = device(y, c, lax.rem(z + 1, length), x)
        self.down = device(y, c, lax.rem(z + length - 1, length), x)

    def copy(self, hop, upward):
        length, buf = self.length, self.buf
        src, dst = ((length - hop + 1) % length, length - hop) if upward else (hop - 1, hop)
        way = 0 if upward else 1
        return pltpu.make_async_remote_copy(
            src_ref=buf.at[src], dst_ref=buf.at[dst], send_sem=self.ss.at[way, hop - 1],
            recv_sem=self.rs.at[way, hop - 1], device_id=self.up if upward else self.down,
            device_id_type=MESH,
        )

    def sends(self, hop, act):
        z, length = self.z, self.length

        @pl.when(jnp.logical_and(z + 1 < length, z >= hop - 1))
        def _():
            act(self.copy(hop, True))

        @pl.when(jnp.logical_and(z >= 1, z + hop - 1 < length))
        def _():
            act(self.copy(hop, False))

    def start(self, hop):
        self.sends(hop, lambda copy: copy.start())

    def arrive(self, hop):
        z, length = self.z, self.length

        @pl.when(z >= hop)
        def _():
            self.copy(hop, True).wait_recv()

        @pl.when(z + hop < length)
        def _():
            self.copy(hop, False).wait_recv()

    def finish(self):
        for hop in range(1, self.length):
            self.sends(hop, lambda copy: copy.wait_send())


class LineScatter:
    def __init__(self, sources, length, total, up_mine, down_mine, up_got, down_got, loc, ss, rs):
        y, c, z, x = place()
        self.sources, self.length, self.total = sources, length, total
        self.mine, self.got = (up_mine, down_mine), (up_got, down_got)
        self.loc, self.ss, self.rs = loc, ss, rs
        self.to = (device(y, c, lax.rem(z + 1, length), x), device(y, c, lax.rem(z + length - 1, length), x))
        self.far = (z, length - 1 - z)

    def loads(self, way, hop):
        k = 0 if hop == 0 else self.length - hop if way == 0 else hop
        copies, at = [], 0
        for n, (ref, first, columns) in enumerate(self.sources):
            dst = self.mine[way].at[hop - 1] if hop else self.total
            copies.append(
                pltpu.make_async_copy(
                    ref.at[k, :, pl.ds(first, columns)], dst.at[:, pl.ds(at, columns)],
                    self.loc.at[way, hop, n],
                )
            )
            at += columns
        return copies

    def copy(self, way, hop):
        return pltpu.make_async_remote_copy(
            src_ref=self.mine[way].at[hop - 1], dst_ref=self.got[way].at[hop - 1],
            send_sem=self.ss.at[way, hop - 1], recv_sem=self.rs.at[way, hop - 1],
            device_id=self.to[way], device_id_type=MESH,
        )

    def begin(self):
        for hop in range(1, self.length):
            for way in (0, 1):
                for copy in self.loads(way, hop):
                    copy.start()
        for copy in self.loads(0, 0):
            copy.start()
        self.next = 1
        self.start()

    def start(self):
        hop = self.next
        if hop >= self.length:
            return
        self.next += 1
        for way in (0, 1):
            far = self.far[way]
            for copy in self.loads(way, hop):
                copy.wait()
            if hop > 1:

                @pl.when(jnp.logical_and(far >= 1, far <= hop - 1))
                def _():
                    self.copy(way, hop - 1).wait_recv()
                    dst, src = self.mine[way].at[hop - 1], self.got[way].at[hop - 2]

                    @pl.loop(0, dst.shape[0] // 16)
                    def _(i):
                        at = pl.ds(pl.multiple_of(i * 16, 16), 16)
                        dst[at] = (dst[at].astype(F32) + src[at].astype(F32)).astype(dst.dtype)

            @pl.when(far <= hop - 1)
            def _():
                self.copy(way, hop).start()

    def end(self, result, squares):
        while self.next < self.length:
            self.start()
        last = self.length - 1
        for copy in self.loads(0, 0):
            copy.wait()
        squares[...] = jnp.zeros_like(squares)

        def finish(ways):
            for way in ways:
                self.copy(way, last).wait_recv()

            @pl.loop(0, result.shape[0] // 16)
            def _(i):
                at = pl.ds(pl.multiple_of(i * 16, 16), 16)
                total = self.total[at].astype(F32)
                for way in ways:
                    total = total + self.got[way][last - 1, at].astype(F32)
                result[at] = total.astype(result.dtype)
                squares[...] += tile_of_squares(total)

        above, below = self.far[0] >= 1, self.far[1] >= 1
        pl.when(jnp.logical_and(above, below))(lambda: finish((0, 1)))
        pl.when(jnp.logical_not(above))(lambda: finish((1,)))
        pl.when(jnp.logical_not(below))(lambda: finish((0,)))
        for hop in range(1, self.length):
            for way in (0, 1):

                @pl.when(self.far[way] <= hop - 1)
                def _():
                    self.copy(way, hop).wait_send()


def fold(v):
    return jnp.sum(v.reshape(v.shape[0] // 8, 8, v.shape[1]), axis=0)


def tile_of_squares(v):
    v = fold(v * v)
    part = v[:, :128]
    for n in range(1, v.shape[1] // 128):
        part = part + v[:, n * 128 : (n + 1) * 128]
    if v.shape[1] % 128:
        rest = v[:, v.shape[1] // 128 * 128 :]
        part = part + jnp.concatenate([rest, jnp.zeros((8, 128 - rest.shape[1]), F32)], axis=1)
    return part


def line_scratch(length, rows, columns, sources):
    slots = pltpu.VMEM((length - 1, rows, columns), BF16)
    return [pltpu.VMEM((rows, columns), BF16)] + [slots] * 4 + [
        DMA((2, length, sources)), DMA((2, length)), DMA((2, length))
    ]


LINE_REFS = 8
SCATTER_REFS = 7
TILE = jax.ShapeDtypeStruct((8, 128), F32)


def line_neighbours(length):
    y, c, z, x = place()
    return [device(y, c, lax.rem(z + 1, length), x), device(y, c, lax.rem(z + length - 1, length), x)]


def rows_loop(rows, body):
    @pl.loop(0, rows // 16)
    def _(i):
        body(pl.ds(pl.multiple_of(i * 16, 16), 16))


def turned_tiles(length, pair):
    _, _, z, _ = place()
    for k in range(length):
        for b in range(4):
            yield k * 4 + b, pl.multiple_of((b * length + lax.rem(z + k, length)) * pair, pair)


def load_turned(ref, at, length, pair):
    if pair % 128:
        return ref[at]
    return jnp.concatenate([ref[at, pl.ds(src, pair)] for _, src in turned_tiles(length, pair)], axis=1)


def store_turned(ref, at, value, length, pair):
    if pair % 128:
        ref[at] = value
        return
    for n, dst in turned_tiles(length, pair):
        ref[at, pl.ds(dst, pair)] = value[:, n * pair : (n + 1) * pair]


def inverse_rms(v):
    return lax.rsqrt(jnp.sum(v * v, axis=-1, keepdims=True) * (1.0 / v.shape[-1]) + norm_eps)


def norm_rows_back(v, gain, grad):
    inverse = inverse_rms(v)
    scaled = v * inverse
    moved = grad * gain
    inner = jnp.sum(moved * scaled, axis=-1, keepdims=True) * (1.0 / v.shape[-1])
    return inverse * (moved - scaled * inner), fold(grad * scaled)


def middle_kernel(length, p, inputs, gains, w_in, residual, normed_o, w, *scratch):
    scatter_refs, (low, loc, gs, gr, hs, hr) = scratch[:SCATTER_REFS], scratch[SCATTER_REFS:]
    greet(gather_peers() + line_neighbours(length))
    hops = LineGather(w, length, hs, hr)
    hops.start(1)
    started = [1]

    def advance(name=None):
        if name != "early" and started[0] < length - 1:
            hops.arrive(started[0])
            started[0] += 1
            hops.start(started[0])

    scatter_steps(p, residual, *scatter_refs)

    def body(at):
        v = inputs[at].astype(F32) + residual[at]
        residual[at] = v
        low[at] = (v * inverse_rms(v) * gains[1:2]).astype(BF16)

    rows_loop(low.shape[0], body)
    gather = Gather(low, normed_o, loc, gs, gr)
    gather.begin()
    advance()
    gather.middle()
    gather.end(advance)
    while started[0] < length - 1:
        advance()
    hops.arrive(length - 1)
    hops.finish()


def middle(p, inputs, gains, w, length, collective_id):
    rows, width = inputs.shape
    return pl.pallas_call(
        functools.partial(middle_kernel, length),
        out_shape=(
            jax.ShapeDtypeStruct((rows, width), F32),
            jax.ShapeDtypeStruct((8, rows, width), BF16),
            jax.ShapeDtypeStruct(w.shape, w.dtype),
        ),
        in_specs=[ANY, VM, VM, ANY],
        out_specs=(VM, ANY, ANY),
        scratch_shapes=scatter_scratch(rows // 2, width)
        + [pltpu.VMEM((rows, width), BF16), DMA, DMA((13,)), DMA((13,)), DMA((2, length)), DMA((2, length))],
        input_output_aliases={3: 2},
        compiler_params=params(collective_id, 40 * 2**20),
        cost_estimate=pl.CostEstimate(flops=0, bytes_accessed=300 * 2**20, transcendentals=0),
    )(p.reshape(8, rows, width), inputs, gains, w)


def turn_kernel(length, cuts, p, residual, above, gains, *refs):
    terms, refs = refs[: len(cuts)], refs[len(cuts) :]
    back, gain, low_o, sums, squares, *scratch = refs
    scatter_refs, (total, low, loc, gs, gr), line_refs = (
        scratch[:SCATTER_REFS], scratch[SCATTER_REFS : SCATTER_REFS + 5], scratch[SCATTER_REFS + 5 :]
    )
    greet(gather_peers() + line_neighbours(length))
    line = LineScatter([(ref, *cut) for ref, cut in zip(terms, cuts)], length, *line_refs)
    line.begin()
    scatter_steps(p, total, *scatter_refs, mark=lambda name: line.start() if name == "late" else None)
    gain[...] = jnp.zeros_like(gain)

    def body(at):
        grad, gain_part = norm_rows_back(residual[at], gains[1:2], total[at])
        grad = above[at].astype(F32) + grad
        back[at] = grad
        low[at] = grad.astype(BF16)
        gain[...] += gain_part

    rows_loop(low.shape[0], body)
    gather = Gather(low, low_o, loc, gs, gr)
    gather.begin()
    gather.middle()
    line.start()
    gather.end()
    line.end(sums, squares)


def turn(p, residual, above, gains, terms, cuts, length, collective_id):
    rows, width = residual.shape
    line_rows, columns = terms[0].shape[1], sum(cut[1] for cut in cuts)
    return pl.pallas_call(
        functools.partial(turn_kernel, length, cuts),
        out_shape=(
            jax.ShapeDtypeStruct((rows, width), F32),
            jax.ShapeDtypeStruct((8, width), F32),
            jax.ShapeDtypeStruct((8, rows, width), BF16),
            jax.ShapeDtypeStruct((line_rows, columns), BF16),
            TILE,
        ),
        in_specs=[ANY, VM, VM, VM] + [ANY] * len(terms),
        out_specs=(VM, VM, ANY, VM, VM),
        scratch_shapes=scatter_scratch(rows // 2, width)
        + [pltpu.VMEM((rows, width), F32), pltpu.VMEM((rows, width), BF16), DMA, DMA((13,)), DMA((13,))]
        + line_scratch(length, line_rows, columns, len(cuts)),
        compiler_params=params(collective_id, 56 * 2**20),
        cost_estimate=pl.CostEstimate(flops=0, bytes_accessed=300 * 2**20, transcendentals=0),
    )(p.reshape(8, rows, width), residual, above, gains, *terms)


def output_kernel(length, cuts, p, residual, *refs):
    terms, refs = refs[: len(cuts)], refs[len(cuts) :]
    out, sums, squares, *scratch = refs
    scatter_refs, total, line_refs = (
        scratch[:SCATTER_REFS], scratch[SCATTER_REFS], scratch[SCATTER_REFS + 1 :]
    )
    greet(gather_peers() + line_neighbours(length))
    line = LineScatter([(ref, *cut) for ref, cut in zip(terms, cuts)], length, *line_refs)
    line.begin()
    scatter_steps(p, total, *scatter_refs, mark=lambda name: line.start())
    pair = out.shape[1] // (4 * length)

    def body(at):
        store_turned(out, at, (residual[at] + total[at]).astype(BF16), length, pair)

    rows_loop(out.shape[0], body)
    line.end(sums, squares)


def output(p, residual, terms, cuts, length, collective_id):
    rows, width = residual.shape
    line_rows, columns = terms[0].shape[1], sum(cut[1] for cut in cuts)
    return pl.pallas_call(
        functools.partial(output_kernel, length, cuts),
        out_shape=(
            jax.ShapeDtypeStruct((rows, width), BF16),
            jax.ShapeDtypeStruct((line_rows, columns), BF16),
            TILE,
        ),
        in_specs=[ANY, VM] + [ANY] * len(terms),
        out_specs=(VM, VM, VM),
        scratch_shapes=scatter_scratch(rows // 2, width)
        + [pltpu.VMEM((rows, width), F32)]
        + line_scratch(length, line_rows, columns, len(cuts)),
        compiler_params=params(collective_id, 48 * 2**20),
        cost_estimate=pl.CostEstimate(flops=0, bytes_accessed=150 * 2**20, transcendentals=0),
    )(p.reshape(8, rows, width), residual, *terms)


def closing_kernel(length, parts, p, g, *refs):
    blocks, refs = refs[:parts], refs[parts:]
    o, e_o, sums, squares, *scratch = refs
    scatter_refs, (loc, es, er), line_refs = (
        scratch[:SCATTER_REFS], scratch[SCATTER_REFS : SCATTER_REFS + 3], scratch[SCATTER_REFS + 3 :]
    )
    greet(plane_peers() + line_neighbours(length))
    line = LineScatter([(g, 0, g.shape[2])], length, *line_refs)
    line.begin()
    scatter_steps(p, o, *scatter_refs, mark=lambda name: line.start() if name == "late" else None)
    moves, at = [], 0
    for n, block in enumerate(blocks):
        columns = block.shape[2]
        moves.append(
            exchange_steps(block, e_o, loc.at[n], es.at[n], er.at[n], pl.ds(at, columns))
        )
        at += columns
    line.end(sums, squares)
    for copies, own in moves:
        for copy in copies:
            copy.wait()
        own.wait()


def closing(p, blocks, g, length, collective_id):
    rows, width = p.shape[0] // 8, p.shape[1]
    share = blocks[0].shape[0] // 8
    blocks = [block.reshape(8, share, block.shape[1]) for block in blocks]
    columns = sum(block.shape[2] for block in blocks)
    parts = len(blocks)
    return pl.pallas_call(
        functools.partial(closing_kernel, length, parts),
        out_shape=(
            jax.ShapeDtypeStruct((rows, width), F32),
            jax.ShapeDtypeStruct((8, share, columns), BF16),
            jax.ShapeDtypeStruct(g.shape[1:], BF16),
            TILE,
        ),
        in_specs=[ANY] * (2 + parts),
        out_specs=(VM, ANY, VM, VM),
        scratch_shapes=scatter_scratch(rows // 2, width)
        + [DMA((parts,)), DMA((parts, 7)), DMA((parts, 7))]
        + line_scratch(length, g.shape[1], g.shape[2], 1),
        compiler_params=params(collective_id, 56 * 2**20),
        cost_estimate=pl.CostEstimate(flops=0, bytes_accessed=250 * 2**20, transcendentals=0),
    )(p.reshape(8, rows, width), g, *blocks)


def first_kernel(
    length, inputs, above, mixer_w, mlp_w, gn, gp,
    normed_o, wm_o, wf_o, wd_o, gains_o, gp_o, inputs_o, above_o,
    normed, gn_all, wm, wf, wd, loc, ms, mr, fs, fr, line_s, line_r, gain_s, gain_r, move_s, move_r,
    gather_s, gather_r, hop_s, hop_r,
):
    y, c, z, x = place()
    s = 2 * z + x
    me = rank(y, c, x)
    rows, width = inputs.shape
    pair = width // (4 * length)
    line = line_peers(length)
    plane = plane_peers()
    to_z, to_x = lax.rem(s, length), s // length
    moves = jnp.where(jnp.logical_and(to_z == z, to_x == x), 0, 1)
    src = x * length + z
    from_z = src // 2
    from_x = src - 2 * from_z
    barrier = pltpu.get_barrier_semaphore()
    for peer in line + plane:
        pl.semaphore_signal(barrier, inc=1, device_id=peer, device_id_type=MESH)

    @pl.when(moves == 1)
    def _():
        pl.semaphore_signal(barrier, inc=1, device_id=device(y, c, to_z, to_x), device_id_type=MESH)
        pl.semaphore_signal(barrier, inc=1, device_id=device(y, c, from_z, from_x), device_id_type=MESH)

    pl.semaphore_wait(barrier, len(line) + len(plane) + 2 * moves)

    gn_all[me, z] = gn[...]
    gains = [
        remote(gn, gn_all.at[me, z], line_s.at[0, k], line_r.at[0, k], line[k]) for k in range(length - 1)
    ]
    for pack, source, js in ((wm, mixer_w, (0, 1, 2)), (wf, mlp_w, (0, 1)), (wd, mlp_w, (2,))):
        part = pack.shape[2] // len(js)
        for t in range(8):
            for n, j in enumerate(js):
                start = (j * 8 + t) * part
                pack[t, :, n * part : (n + 1) * part] = source[:, start : start + part].astype(BF16)
        if pack is wm:
            for copy in gains:
                copy.wait()
            spread = [
                remote(gn_all.at[me], gn_all.at[me], gain_s.at[n], gain_r.at[n], plane[n])
                for n in range(7)
            ]
            mixer, mixer_own = exchange_steps(wm, wm_o.at[0], loc.at[0], ms, mr)

    @pl.when(moves == 1)
    def _():
        copy = remote(gp, gp_o.at[to_z], move_s, move_r, device(y, c, to_z, to_x))
        copy.wait()

    @pl.when(moves == 0)
    def _():
        copy = pltpu.make_async_copy(gp, gp_o.at[z], loc.at[2])
        copy.start()
        copy.wait()

    gates = [
        remote(gp_o.at[z], gp_o.at[z], line_s.at[1, k], line_r.at[1, k], line[k])
        for k in range(length - 1)
    ]
    for copy in spread:
        copy.wait()
    for k in range(length):
        other = lax.rem(z + k, length)
        for b in range(4):
            at = slice((4 * k + b) * pair, (4 * k + b + 1) * pair)
            tile = (gn_all[2 * b, other] + gn_all[2 * b + 1, other])[:, :pair]
            gains_o[:, at] = tile.astype(BF16).astype(F32)

    def body(at):
        v = load_turned(inputs, at, length, pair)
        inputs_o[at] = v
        v = v.astype(F32)
        normed[at] = (v * inverse_rms(v) * gains_o[0:1]).astype(BF16)

    rows_loop(rows, body)

    gather = Gather(normed, normed_o, loc.at[1], gather_s, gather_r)
    gather.begin()
    for copy in mixer:
        copy.wait()
    mixer_own.wait()
    hops = LineGather(wm_o, length, hop_s, hop_r)
    hops.start(1)
    down, down_own = exchange_steps(wd, wd_o.at[0], loc.at[4], fs.at[1], fr.at[1])
    feed, feed_own = exchange_steps(wf, wf_o.at[0], loc.at[3], fs.at[0], fr.at[0])
    gather.middle()

    def turn_rows(at):
        above_o[at] = load_turned(above, at, length, pair)

    rows_loop(rows, turn_rows)
    hops.arrive(1)
    if length > 2:
        hops.start(2)
    gather.end()
    for hop in range(2, length):
        hops.arrive(hop)
        if hop + 1 < length:
            hops.start(hop + 1)
    for copy in down + feed + gates:
        copy.wait()
    down_own.wait()
    feed_own.wait()
    hops.finish()


def first(inputs, above, mixer, mlp, gn, gp, length, collective_id):
    rows, width = inputs.shape
    share = mixer.shape[0]
    wm, wf, wd = ((8, share, n) for n in (mixer.shape[1] // 8, mlp.shape[1] // 12, mlp.shape[1] // 24))
    low = jax.ShapeDtypeStruct((rows, width), BF16)
    return pl.pallas_call(
        functools.partial(first_kernel, length),
        out_shape=(
            jax.ShapeDtypeStruct((8, rows, width), BF16),
            jax.ShapeDtypeStruct((length,) + wm, BF16),
            jax.ShapeDtypeStruct((length,) + wf, BF16),
            jax.ShapeDtypeStruct((length,) + wd, BF16),
            jax.ShapeDtypeStruct((8, width), F32),
            jax.ShapeDtypeStruct((length,) + gp.shape, gp.dtype),
            low,
            low,
        ),
        in_specs=[VM] * 5 + [ANY],
        out_specs=(ANY, ANY, ANY, ANY, VM, ANY, VM, VM),
        scratch_shapes=[
            pltpu.VMEM((rows, width), BF16),
            pltpu.VMEM((8, length, 8, 128), F32),
            pltpu.VMEM(wm, BF16),
            pltpu.VMEM(wf, BF16),
            pltpu.VMEM(wd, BF16),
            DMA((5,)), DMA((7,)), DMA((7,)), DMA((2, 7)), DMA((2, 7)),
            DMA((2, length)), DMA((2, length)), DMA((7,)), DMA((7,)), DMA, DMA,
            DMA((13,)), DMA((13,)), DMA((2, length)), DMA((2, length)),
        ],
        compiler_params=params(collective_id, 40 * 2**20),
        cost_estimate=pl.CostEstimate(flops=0, bytes_accessed=300 * 2**20, transcendentals=0),
    )(inputs, above, mixer, mlp, gn, gp)


def last_kernel(
    length, share, heads_columns, wm, total, inputs, back, gains, gain_two, gp, sq,
    gw, gm, gv, pw, pm, pv,
    wm_o, grad_o, gm_o, gv_o, gw_o, pm_o, pv_o, pw_o, norm_o, factor_o,
    gain, row_sums, gn, gn_in, gn_mid, gn_got, gp_got, gp_sum, gp_fin, sq_plane, sq_line,
    loc, ss, rs, gs, gr, ls, lr, move_s, move_r,
):
    y, c, z, x = place()
    s = 2 * z + x
    me = rank(y, c, x)
    line = line_peers(length)
    plane = plane_peers()
    owner = x * length + z
    to_z = owner // 2
    to_x = owner - 2 * to_z
    from_z, from_x = lax.rem(s, length), s // length
    moves = jnp.where(jnp.logical_and(to_z == z, to_x == x), 0, 1)
    barrier = pltpu.get_barrier_semaphore()
    for peer in line + plane:
        pl.semaphore_signal(barrier, inc=1, device_id=peer, device_id_type=MESH)

    @pl.when(moves == 1)
    def _():
        pl.semaphore_signal(barrier, inc=1, device_id=device(y, c, to_z, to_x), device_id_type=MESH)
        pl.semaphore_signal(barrier, inc=1, device_id=device(y, c, from_z, from_x), device_id_type=MESH)

    pl.semaphore_wait(barrier, len(line) + len(plane) + 2 * moves)

    gate = [
        remote(gp.at[k + 1], gp_got.at[k], ls.at[0, k], lr.at[0, k], line[k]) for k in range(length - 1)
    ]
    rows, width = inputs.shape
    pair = width // (4 * length)
    gain[...] = jnp.zeros_like(gain)

    def body(at):
        grad, gain_part = norm_rows_back(inputs[at].astype(F32), gains[0:1], total[at])
        store_turned(grad_o, at, back[at] + grad, length, pair)
        gain[...] += gain_part

    rows_loop(rows, body)
    row = lax.broadcasted_iota(jnp.int32, (8, width), 0)
    ones = jnp.sum(gain[...], axis=0, keepdims=True)
    twos = jnp.sum(gain_two[...], axis=0, keepdims=True)
    row_sums[...] = jnp.where(row == 0, ones, jnp.where(row == 1, twos, 0.0))
    if pair < 128:
        gn[...] = jnp.zeros_like(gn)
    for k in range(length):
        for b in range(4):
            gn[b, k, :, :pair] = row_sums[:, (4 * k + b) * pair : (4 * k + b + 1) * pair]
    sends = []
    for n, (fy, fc, fx) in enumerate(FLIPS):
        to = flip(y, fy) * 2 + flip(c, fc)
        sends.append(remote(gn.at[to], gn_in.at[n], gs.at[0, n], gr.at[0, n], plane[n]))
    copies, own = exchange_steps(wm, wm_o, loc, ss, rs)
    for copy in gate:
        copy.wait()
    sums = gp[0]
    for k in range(length - 1):
        sums = sums + gp_got[k]
    gp_sum[...] = sums
    for copy in sends:
        copy.wait()
    sums = gn[2 * y + c]
    for n in range(7):
        sums = sums + gn_in[n]
    gn_mid[...] = sums
    sends = [
        remote(gn_mid.at[k + 1], gn_got.at[k], ls.at[1, k], lr.at[1, k], line[k])
        for k in range(length - 1)
    ]

    @pl.when(moves == 1)
    def _():
        copy = remote(gp_sum, gp_fin, move_s, move_r, device(y, c, to_z, to_x))
        copy.wait()

    @pl.when(moves == 0)
    def _():
        gp_fin[...] = gp_sum[...]

    for copy in sends:
        copy.wait()
    sums = gn_mid[0]
    for k in range(length - 1):
        sums = sums + gn_got[k]
    lane = lax.broadcasted_iota(jnp.int32, (8, 128), 1)
    mine = jnp.logical_and(lane >= x * share, lane < (x + 1) * share)
    gain_sum = jnp.where(mine, sums, 0.0)
    gate_sum = gp_fin[...]
    sq_plane[me] = sq[...] + gain_sum * gain_sum + tile_of_squares(gate_sum)
    sends = [
        remote(sq_plane.at[me], sq_plane.at[me], gs.at[1, n], gr.at[1, n], plane[n]) for n in range(7)
    ]
    for copy in sends:
        copy.wait()
    sums = sq_plane[0]
    for n in range(1, 8):
        sums = sums + sq_plane[n]
    sq_line[z] = sums
    sends = [
        remote(sq_line.at[z], sq_line.at[z], ls.at[2, k], lr.at[2, k], line[k])
        for k in range(length - 1)
    ]
    for copy in sends:
        copy.wait()
    sums = sq_line[0]
    for n in range(1, length):
        sums = sums + sq_line[n]
    sums = jnp.sum(jnp.sum(sums, axis=0, keepdims=True), axis=1, keepdims=True)
    norm = jnp.broadcast_to(jnp.sqrt(sums), (8, 128))
    factor = clip_limit / jnp.maximum(norm, clip_limit)
    norm_o[...] = norm
    factor_o[...] = factor
    gm_o[...], gv_o[...], gw_o[...] = adam_step(
        gw[...], gain_sum, gm[...], gv[...], factor, rate_gains, 0.0
    )
    column = lax.broadcasted_iota(jnp.int32, gate_sum.shape, 1)
    matrix = column < heads_columns
    pm_o[...], pv_o[...], pw_o[...] = adam_step(
        pw[...], gate_sum, pm[...], pv[...], factor[0:1, 0:1],
        jnp.where(matrix, rate_matrix, rate_channel), jnp.where(matrix, decay_matrix, 0.0),
    )
    for copy in copies:
        copy.wait()
    own.wait()


def last(wm, total, inputs, back, gains, gain_two, gp, sq, gain_state, gate_state, share, columns, length, collective_id):
    rows, width = inputs.shape
    tile, pack = TILE, jax.ShapeDtypeStruct(gp.shape[1:], F32)
    return pl.pallas_call(
        functools.partial(last_kernel, length, share, columns),
        out_shape=(
            jax.ShapeDtypeStruct(wm.shape, wm.dtype),
            jax.ShapeDtypeStruct((rows, width), F32),
            tile, tile, tile, pack, pack, pack, tile, tile,
        ),
        in_specs=[ANY] + [VM] * 13,
        out_specs=(ANY,) + (VM,) * 9,
        scratch_shapes=[
            pltpu.VMEM((8, width), F32),
            pltpu.VMEM((8, width), F32),
            pltpu.VMEM((4, length, 8, 128), F32),
            pltpu.VMEM((7, length, 8, 128), F32),
            pltpu.VMEM((length, 8, 128), F32),
            pltpu.VMEM((length, 8, 128), F32),
            pltpu.VMEM(gp.shape, F32),
            pltpu.VMEM(gp.shape[1:], F32),
            pltpu.VMEM(gp.shape[1:], F32),
            pltpu.VMEM((8, 8, 128), F32),
            pltpu.VMEM((length, 8, 128), F32),
            DMA, DMA((7,)), DMA((7,)), DMA((2, 7)), DMA((2, 7)),
            DMA((3, length)), DMA((3, length)), DMA, DMA,
        ],
        compiler_params=params(collective_id, 32 * 2**20),
    )(wm, total, inputs, back, gains, gain_two, gp, sq, *gain_state, *gate_state)


def minus_expm1(v):
    series = 1.0 + v * (1.0 / 8.0)
    for n in (7.0, 6.0, 5.0, 4.0, 3.0, 2.0):
        series = 1.0 + series * v * (1.0 / n)
    return jnp.where(v > -0.5, -v * series, 1.0 - jnp.exp(v))


def gelu_parts(v):
    inner = jnp.tanh(GELU_SCALE * (v + 0.044715 * v * v * v))
    return 0.5 * v * (1.0 + inner), inner


def gelu_slope(v, inner):
    return 0.5 * (1.0 + inner) + 0.5 * v * (1.0 - inner * inner) * GELU_SCALE * (
        1.0 + 3.0 * 0.044715 * v * v
    )


CHUNK = 64


def forward_kernel(
    length, proj, gate, chan, above, w_in, mixed, decay_o, width_o, recur_o, enter_o, conv_o, xe, se, ends_o, above_o, w,
    pre, loc_h, ends, carry, hs, hr, es, er, gather_l, gather_s, gather_r, hop_s, hop_r,
):
    y, c, z, x = place()
    line = line_peers(length)
    greet(line + gather_peers())
    seqs, span, rc = mixed.shape
    chunks = span // CHUNK
    gather = Gather(above, above_o, gather_l, gather_s, gather_r)
    ahead = device(y, c, lax.rem(z + 1, length), x)
    for b in range(seqs):
        xe[b, span : span + 8] = proj[b, span - 8 : span, rc:].astype(BF16).astype(F32)
    halo = remote(xe.at[:, pl.ds(span, 8)], xe.at[:, pl.ds(0, 8)], hs, hr, ahead)
    halo.wait_send()
    hops = LineGather(w, length, hop_s, hop_r)
    hops.start(1)
    gather.begin()

    @pl.loop(0, seqs * chunks)
    def _(i):
        b = i // chunks
        r = pl.multiple_of((i - b * chunks) * CHUNK, CHUNK)
        xe[b, pl.ds(r + 8, CHUNK)] = proj[b, pl.ds(r, CHUNK), rc:].astype(BF16).astype(F32)

    halo.wait_recv()

    @pl.when(z == 0)
    def _():
        xe[:, 0:8] = jnp.zeros((seqs, 8, rc), F32)

    def coefficients(i):
        b = i // chunks
        r = pl.multiple_of((i - b * chunks) * CHUNK, CHUNK)
        at = pl.ds(r, CHUNK)
        window = xe[b, pl.ds(r, CHUNK + 8)]
        total = chan[4:5] + chan[0:1] * window[8:]
        for k in (1, 2, 3):
            total = total + chan[k : k + 1] * pltpu.roll(window, k, 0)[8:]
        low = total.astype(BF16)
        conv_o[b, at] = low
        value = low.astype(F32)
        gates = jnp.dot(low, gate[...], preferred_element_type=F32)
        recur = jax.nn.sigmoid(gates[:, :rc] + chan[5:6])
        enter = jax.nn.sigmoid(gates[:, rc:] + chan[6:7])
        log_decay = -chan[7:8] * recur
        decay = jnp.exp(log_decay)
        width = jnp.sqrt(minus_expm1(2.0 * log_decay))
        recur_o[b, at] = recur
        enter_o[b, at] = enter
        decay_o[b, at] = decay
        width_o[b, at] = width
        loc_h[b, at] = width * enter * value

    half = seqs * chunks // 2
    pl.loop(0, half)(coefficients)
    gather.middle()
    hops.arrive(1)
    if length > 2:
        hops.start(2)
    pl.loop(half, seqs * chunks)(coefficients)
    row = lax.broadcasted_iota(jnp.int32, (8, rc), 0)

    def tile(i, held):
        at = pl.ds(pl.multiple_of(i * 8, 8), 8)
        new = []
        for b in range(seqs):
            a, h = decay_o[b, at], loc_h[b, at]
            for n in (1, 2, 4):
                keep = row >= n
                h = h + jnp.where(keep, a * pltpu.roll(h, n, 0), 0.0)
                a = jnp.where(keep, a * pltpu.roll(a, n, 0), a)
            h = h + a * held[b][1]
            a = a * held[b][0]
            loc_h[b, at] = h
            pre[b, at] = a
            new.append((a[7:8], h[7:8]))
        return tuple(new)

    one, zero = jnp.ones((1, rc), F32), jnp.zeros((1, rc), F32)
    final = lax.fori_loop(0, span // 8, tile, ((one, zero),) * seqs)
    for b in range(seqs):
        ends[z, 0, b] = jnp.broadcast_to(final[b][0], (8, rc))
        ends[z, 1, b] = jnp.broadcast_to(final[b][1], (8, rc))
        ends_o[b] = jnp.broadcast_to(final[b][0], (8, rc))
    moves = [remote(ends.at[z], ends.at[z], es.at[k], er.at[k], line[k]) for k in range(length - 1)]
    for copy in moves:
        copy.wait()
    if length > 3:
        hops.arrive(2)
        hops.start(3)
    carry[...] = jnp.zeros_like(carry)
    for k in range(length):
        carry[...] = jnp.where(k < z, ends[k, 0] * carry[...] + ends[k, 1], carry[...])

    for b in range(seqs):
        se[b, 0:8] = carry[b]

    @pl.loop(0, seqs * chunks)
    def _(i):
        b = i // chunks
        r = pl.multiple_of((i - b * chunks) * CHUNK, CHUNK)
        at = pl.ds(r, CHUNK)
        state = loc_h[b, at] + pre[b, at] * carry[b, 0:1]
        se[b, pl.ds(r + 8, CHUNK)] = state
        gelu, _ = gelu_parts(proj[b, at, :rc])
        mixed[b, at] = (state * gelu).astype(BF16)

    gather.end()
    for hop in range(min(3, length - 1), length):
        hops.arrive(hop)
        if hop + 1 < length:
            hops.start(hop + 1)
    hops.finish()


def recur_forward(proj, gate, chan, above, w, length, collective_id):
    seqs, span, rc = proj.shape[0], proj.shape[1], proj.shape[2] // 2
    full = jax.ShapeDtypeStruct((seqs, span, rc), F32)
    longer = jax.ShapeDtypeStruct((seqs, span + 8, rc), F32)
    low = jax.ShapeDtypeStruct((seqs, span, rc), BF16)
    return pl.pallas_call(
        functools.partial(forward_kernel, length),
        out_shape=(
            low, full, full, full, full, low, longer, longer,
            jax.ShapeDtypeStruct((seqs, 8, rc), F32),
            jax.ShapeDtypeStruct((8,) + above.shape, above.dtype),
            jax.ShapeDtypeStruct(w.shape, w.dtype),
        ),
        in_specs=[VM, VM, VM, ANY, ANY],
        out_specs=(VM,) * 9 + (ANY, ANY),
        scratch_shapes=[
            pltpu.VMEM((seqs, span, rc), F32),
            pltpu.VMEM((seqs, span, rc), F32),
            pltpu.VMEM((length, 2, seqs, 8, rc), F32),
            pltpu.VMEM((seqs, 8, rc), F32),
            DMA, DMA, DMA((length,)), DMA((length,)),
            DMA, DMA((13,)), DMA((13,)), DMA((2, length)), DMA((2, length)),
        ],
        input_output_aliases={4: 10},
        compiler_params=params(collective_id, 56 * 2**20),
        cost_estimate=pl.CostEstimate(
            flops=2 * seqs * span * rc * rc * 2, bytes_accessed=100 * 2**20, transcendentals=0
        ),
    )(proj, gate, chan, above, w)


def backward_kernel(
    length, cuts, dmix, gate, chan, decay, width, recur, enter, conv, xe, se, ends_f, proj, *refs
):
    terms, refs = refs[: len(cuts)], refs[len(cuts) :]
    dproj, dgate, gchan, sums, squares, suffix, grad, de, ends, carry, hs, hr, es, er, *line_refs = refs
    y, c, z, x = place()
    line = line_peers(length)
    greet(line)
    scatter = LineScatter([(ref, *cut) for ref, cut in zip(terms, cuts)], length, *line_refs)
    scatter.begin()
    seqs, span, rc = decay.shape
    chunks = span // CHUNK

    @pl.loop(0, seqs * chunks)
    def _(i):
        b = i // chunks
        r = pl.multiple_of((i - b * chunks) * CHUNK, CHUNK)
        at = pl.ds(r, CHUNK)
        branch = proj[b, at]
        gelu, inner = gelu_parts(branch)
        above = dmix[b, at]
        state = se[b, pl.ds(r + 8, CHUNK)]
        grad[b, at] = above * gelu
        dproj[b, at, :rc] = (above * state * gelu_slope(branch, inner)).astype(BF16)

    row = lax.broadcasted_iota(jnp.int32, (8, rc), 0)

    def tile(i, held):
        at = pl.ds(pl.multiple_of(span - 8 - i * 8, 8), 8)
        new = []
        for b in range(seqs):
            product, total, following = held[b]
            plain, h = decay[b, at], grad[b, at]
            a = jnp.where(row == 7, following, pltpu.roll(plain, 7, 0))
            for n in (1, 2, 4):
                keep = row < 8 - n
                h = h + jnp.where(keep, a * pltpu.roll(h, 8 - n, 0), 0.0)
                a = jnp.where(keep, a * pltpu.roll(a, 8 - n, 0), a)
            h = h + a * total
            a = a * product
            grad[b, at] = h
            suffix[b, at] = a
            new.append((a[0:1], h[0:1], plain[0:1]))
        return tuple(new)

    one, zero = jnp.ones((1, rc), F32), jnp.zeros((1, rc), F32)
    final = lax.fori_loop(0, span // 8, tile, ((one, zero, one),) * seqs)
    for b in range(seqs):
        ends[z, 0, b] = ends_f[b]
        ends[z, 1, b] = jnp.broadcast_to(final[b][1] * final[b][2], (8, rc))
    moves = [remote(ends.at[z], ends.at[z], es.at[k], er.at[k], line[k]) for k in range(length - 1)]
    for copy in moves:
        copy.wait()
    scatter.start()
    carry[...] = jnp.zeros_like(carry)
    for k in reversed(range(length)):
        carry[...] = jnp.where(k > z, ends[k, 0] * carry[...] + ends[k, 1], carry[...])

    gchan[...] = jnp.zeros_like(gchan)

    @pl.loop(0, seqs * chunks)
    def _(i):
        b = i // chunks
        r = pl.multiple_of((i - b * chunks) * CHUNK, CHUNK)
        at = pl.ds(r, CHUNK)
        g = grad[b, at] + suffix[b, at] * carry[b, 0:1]
        a, w, ra, ri = decay[b, at], width[b, at], recur[b, at], enter[b, at]
        value = conv[b, at].astype(F32)
        before = pltpu.roll(se[b, pl.ds(r, CHUNK + 8)], 1, 0)[8:]
        dla = g * before * a - g * ri * value * (a * a) / w
        slope = dla * ra * (1.0 - ra)
        dpa = (-chan[7:8] * slope).astype(BF16)
        dpi = (g * w * value * ri * (1.0 - ri)).astype(BF16)
        dgate[b, at, :rc] = dpa
        dgate[b, at, rc:] = dpi
        gchan[5] += fold(dpa.astype(F32))
        gchan[6] += fold(dpi.astype(F32))
        gchan[7] += fold(dla * ra)
        back = lax.dot_general(
            dgate[b, at], gate[...], (((1,), (1,)), ((), ())), preferred_element_type=F32
        )
        dcv = (g * w * ri + back).astype(BF16).astype(F32)
        de[b, at] = dcv
        gchan[4] += fold(dcv)

    behind = device(y, c, lax.rem(z + length - 1, length), x)
    halo = remote(de.at[:, pl.ds(0, 8)], de.at[:, pl.ds(span, 8)], hs, hr, behind)
    halo.wait()
    scatter.start()

    @pl.when(z == length - 1)
    def _():
        de[:, span:] = jnp.zeros((seqs, 8, rc), F32)

    @pl.loop(0, seqs * chunks)
    def _(i):
        b = i // chunks
        r = pl.multiple_of((i - b * chunks) * CHUNK, CHUNK)
        at = pl.ds(r, CHUNK)
        window = de[b, pl.ds(r, CHUNK + 8)]
        inputs = xe[b, pl.ds(r, CHUNK + 8)]
        dcv = window[:CHUNK]
        total = chan[0:1] * dcv
        gchan[0] += fold(dcv * inputs[8:])
        for k in (1, 2, 3):
            total = total + chan[k : k + 1] * pltpu.roll(window, CHUNK + 8 - k, 0)[:CHUNK]
            gchan[k] += fold(dcv * pltpu.roll(inputs, k, 0)[8:])
        dproj[b, at, rc:] = total.astype(BF16)

    scatter.end(sums, squares)


def recur_backward(dmix, gate, chan, kept, proj, terms, cuts, length, collective_id):
    decay, width, recur, enter, conv, xe, se, ends = kept
    seqs, span, rc = decay.shape
    wide = jax.ShapeDtypeStruct((seqs, span, 2 * rc), BF16)
    line_rows, columns = terms[0].shape[1], sum(cut[1] for cut in cuts)
    return pl.pallas_call(
        functools.partial(backward_kernel, length, cuts),
        grid=(1,),
        out_shape=(
            wide, wide, jax.ShapeDtypeStruct((8, 8, rc), F32),
            jax.ShapeDtypeStruct((line_rows, columns), BF16), TILE,
        ),
        in_specs=[VM] * 11 + [pl.BlockSpec((seqs, span, rc), lambda i: (0, 0, 0))] + [ANY] * len(terms),
        out_specs=(VM,) * 5,
        scratch_shapes=[
            pltpu.VMEM((seqs, span, rc), F32),
            pltpu.VMEM((seqs, span, rc), F32),
            pltpu.VMEM((seqs, span + 8, rc), F32),
            pltpu.VMEM((length, 2, seqs, 8, rc), F32),
            pltpu.VMEM((seqs, 8, rc), F32),
            DMA, DMA, DMA((length,)), DMA((length,)),
        ]
        + line_scratch(length, line_rows, columns, len(cuts)),
        compiler_params=params(collective_id, 62 * 2**20),
        cost_estimate=pl.CostEstimate(
            flops=2 * seqs * span * rc * rc * 2, bytes_accessed=120 * 2**20, transcendentals=0
        ),
    )(dmix, gate, chan, decay, width, recur, enter, conv, xe, se, ends, proj, *terms)


def contract_last(left, right):
    return lax.dot_general(
        left, right, (((1,), (1,)), ((), ())), preferred_element_type=F32
    )


def contract_first(left, right):
    return lax.dot_general(
        left, right, (((0,), (0,)), ((), ())), preferred_element_type=F32
    )


def adam_step(weight, grad, first, second, factor, rate, decay_rate):
    clipped = grad * factor
    first_new = beta_first * first + (1.0 - beta_first) * clipped
    second_new = beta_second * second + (1.0 - beta_second) * clipped * clipped
    first_hat = first_new / (1.0 - beta_first**STEP)
    second_hat = second_new / (1.0 - beta_second**STEP)
    weight_new = weight - rate * (
        first_hat / (jnp.sqrt(second_hat) + adam_eps) + decay_rate * weight
    )
    return (first_new, second_new, weight_new)


def adam_kernel(rate, decay_rate, factor, w, g, m, v, m_o, v_o, w_o):
    first_new, second_new, weight_new = adam_step(
        w[...], g[0].astype(F32), m[...], v[...], factor[0:1, 0:1], rate, decay_rate
    )
    m_o[...] = first_new
    v_o[...] = second_new
    w_o[...] = weight_new


def adam_blocks(weight, grad, first, second, factor, rate, decay_rate):
    rows, part = grad.shape[1], grad.shape[2] // 3
    block = pl.BlockSpec((rows, part), lambda t, j: (0, j * 8 + t))
    shape = jax.ShapeDtypeStruct(weight.shape, F32)
    return pl.pallas_call(
        functools.partial(adam_kernel, rate, decay_rate),
        grid=(8, 3),
        out_shape=(shape,) * 3,
        in_specs=[
            pl.BlockSpec((8, 128), lambda t, j: (0, 0)),
            block,
            pl.BlockSpec((1, rows, part), lambda t, j: (t, 0, j)),
            block,
            block,
        ],
        out_specs=(block,) * 3,
        cost_estimate=pl.CostEstimate(flops=0, bytes_accessed=7 * 4 * weight.size, transcendentals=0),
    )(factor, weight, grad, first, second)


def adam_pairs_kernel(rate, decay_rate, factor, w, g, m, v, m_o, v_o, w_o):
    part = g.shape[2] // 3
    for j in range(3):

        @pl.when(pl.program_id(1) == j)
        def _():
            at = slice(j * part, (j + 1) * part)
            grad = jnp.concatenate([g[0, :, at].astype(F32), g[1, :, at].astype(F32)], axis=1)
            first_new, second_new, weight_new = adam_step(
                w[...], grad, m[...], v[...], factor[0:1, 0:1], rate, decay_rate
            )
            m_o[...] = first_new
            v_o[...] = second_new
            w_o[...] = weight_new


def adam_pairs(weight, grad, first, second, factor, rate, decay_rate):
    rows, part = grad.shape[1], grad.shape[2] // 3
    block = pl.BlockSpec((rows, 2 * part), lambda t, j: (0, j * 4 + t))
    shape = jax.ShapeDtypeStruct(weight.shape, F32)
    return pl.pallas_call(
        functools.partial(adam_pairs_kernel, rate, decay_rate),
        grid=(4, 3),
        out_shape=(shape,) * 3,
        in_specs=[
            pl.BlockSpec((8, 128), lambda t, j: (0, 0)),
            block,
            pl.BlockSpec((2, rows, 3 * part), lambda t, j: (t, 0, 0)),
            block,
            block,
        ],
        out_specs=(block,) * 3,
        cost_estimate=pl.CostEstimate(flops=0, bytes_accessed=7 * 4 * weight.size, transcendentals=0),
    )(factor, weight, grad, first, second)


def on_device(
    block_input,
    out_grad,
    norm_gains,
    mixer_weight,
    gate_weight,
    chan_params,
    mlp_weight,
    first_gains,
    first_mixer,
    first_gate,
    first_chan,
    first_mlp,
    second_gains,
    second_mixer,
    second_gate,
    second_chan,
    second_mlp,
):
    length = lax.axis_size("seq") // 2
    z = lax.axis_index("seq") // 2
    tokens, model = block_input.shape[1:]
    share = mixer_weight.shape[0]
    pair = 2 * share
    lru = mixer_weight.shape[1] // 3
    hidden = mlp_weight.shape[1] // 3
    r8, f8 = lru // 8, hidden // 8
    rc = -(-r8 // 128) * 128
    head = gate_weight.shape[1] // 2
    heads = r8 // head
    gate_rows = gate_weight.shape[0]
    gate_pad = -(-gate_rows // 16) * 16

    x = lax.axis_index("seq") - 2 * z
    batch = lax.axis_index("batch")
    plain = pair % 128 == 0

    def turned(v):
        if plain:
            return v
        v = v.reshape(v.shape[0], 4, length, pair).swapaxes(1, 2)
        return jnp.roll(v, -z, axis=1).reshape(v.shape[0], model)

    def turned_back(v):
        if plain:
            return v
        v = jnp.roll(v.reshape(v.shape[0], length, 4, pair), z, axis=1)
        return v.swapaxes(1, 2).reshape(v.shape[0], model)

    def gain_tile(v):
        return jnp.where(
            x == 0,
            jnp.pad(v, ((0, 6), (0, 128 - share))),
            jnp.pad(v, ((0, 6), (share, 128 - 2 * share))),
        )

    def gain_rows(v):
        return jnp.where(x == 0, v[:2, :share], v[:2, share : 2 * share])

    def gate_pack(rows, channels):
        pack = jnp.concatenate([rows, channels.T], axis=1)
        return jnp.pad(pack, ((0, gate_pad - gate_rows), (0, rc - 2 * head - 8)))

    gain_state = [gain_tile(v) for v in (norm_gains, first_gains, second_gains)]
    gate_state = [
        gate_pack(*pair_of)
        for pair_of in ((gate_weight, chan_params), (first_gate, first_chan), (second_gate, second_chan))
    ]
    normed_one, mixer_full, mlp_gu, mlp_down, gains, gate_in, inputs, above = first(
        turned(block_input[0]),
        turned(out_grad[0]),
        mixer_weight,
        mlp_weight,
        gain_state[0],
        gate_state[0].astype(BF16),
        length,
        1,
    )
    normed_one = normed_one.reshape(8 * tokens, model)
    gate_own = gate_in[:, :gate_rows].reshape(r8, rc)
    chan = gate_own[:, 2 * head : 2 * head + 8].astype(F32).T
    lam = chan[7]
    fill = jnp.concatenate([jnp.zeros((7, rc - r8), F32), jnp.ones((1, rc - r8), F32)])
    chan = jnp.concatenate([chan[:7], 8.0 * jax.nn.softplus(-lam)[None]])
    chan = jnp.concatenate([chan, fill], axis=1)
    gate = []
    for h in range(heads):
        block = gate_own[h * head : (h + 1) * head, : 2 * head]
        at = ((0, 0), (h * head, rc - (h + 1) * head))
        gate.append(
            jnp.concatenate([jnp.pad(block[:, :head], at), jnp.pad(block[:, head:], at)], axis=1)
        )
    gate = jnp.pad(jnp.concatenate(gate), ((0, rc - r8), (0, 0)))

    mixer_full = mixer_full.reshape(model, 3 * r8)
    parts = [jnp.pad(mixer_full[:, n * r8 : (n + 1) * r8], ((0, 0), (0, rc - r8))) for n in range(3)]
    mixer_first = jnp.concatenate(parts[:2], axis=1)
    mixer_last = parts[2]
    span = 2 * tokens
    projected = jnp.dot(normed_one, mixer_first, preferred_element_type=F32)
    projected = projected.reshape(4, span, 2 * rc)
    mixed, *kept, grad_out, mlp_down = recur_forward(projected, gate, chan, above, mlp_down, length, 2)
    grad_out = grad_out.reshape(8 * tokens, model)
    mixed = mixed.reshape(4 * span, rc)
    residual, normed_two, mlp_gu = middle(
        contract_last(mixed, mixer_last).astype(BF16), inputs, gains, mlp_gu, length, 3
    )
    normed_two = normed_two.reshape(8 * tokens, model)
    mlp_gu = mlp_gu.reshape(model, 2 * f8)
    mlp_gate, mlp_up = mlp_gu[:, :f8], mlp_gu[:, f8:]
    mlp_down = mlp_down.reshape(model, f8)
    gg = jnp.dot(normed_two, mlp_gate, preferred_element_type=F32)
    uu = jnp.dot(normed_two, mlp_up, preferred_element_type=F32)
    dhid = jnp.dot(grad_out, mlp_down, preferred_element_type=F32)
    gelu, inner = gelu_parts(gg)
    hid = (gelu * uu).astype(BF16)
    dgg = (dhid * uu * gelu_slope(gg, inner)).astype(BF16)
    duu = (dhid * gelu).astype(BF16)
    dnormed_two = contract_last(dgg, mlp_gate) + contract_last(duu, mlp_up)

    def terms(v):
        return v.astype(BF16).reshape(length, 8 * share, f8)

    gate_terms = terms(contract_first(normed_two, dgg))
    up_terms = terms(contract_first(normed_two, duu))
    down_terms = terms(contract_first(grad_out, hid))
    up_cut = f8 // 256 * 128
    down_cut = f8 // 384 * 128

    grad_residual, gain_two, dmz, sums_one, squares_one = turn(
        dnormed_two.astype(BF16), residual, above, gains,
        (gate_terms, up_terms), ((0, f8), (0, up_cut)), length, 4,
    )
    dmz = dmz.reshape(8 * tokens, model)
    block_output, sums_two, squares_two = output(
        contract_last(hid, mlp_down).astype(BF16), residual,
        (up_terms, down_terms), ((up_cut, f8 - up_cut), (0, down_cut)), length, 5,
    )
    dmix = jnp.dot(dmz, mixer_last, preferred_element_type=F32).reshape(4, span, rc)
    dproj, dgate, chan_grad, sums_three, squares_three = recur_backward(
        dmix, gate, chan, kept, projected, (down_terms,), ((down_cut, f8 - down_cut),), length, 6
    )
    dproj = dproj.reshape(4 * span, 2 * rc)
    dgate = dgate.reshape(4 * span, 2 * rc)
    proj_grad = contract_first(normed_one, dproj)
    last_grad = contract_first(dmz, mixed)
    mixer_terms = jnp.concatenate(
        [proj_grad[:, :r8], proj_grad[:, rc : rc + r8], last_grad[:, :r8]], axis=1
    )
    mixer_terms = mixer_terms.astype(BF16).reshape(length, 8 * share, 3 * r8)
    dnormed_one, mlp_back, mixer_sums, squares_four = closing(
        contract_last(dproj, mixer_first).astype(BF16), (sums_one, sums_two, sums_three), mixer_terms,
        length, 7,
    )

    gate_full_grad = contract_first(kept[4].reshape(4 * span, rc), dgate)
    blocks = []
    for h in range(heads):
        at = slice(h * head, (h + 1) * head)
        blocks.append(
            jnp.concatenate([gate_full_grad[at, at], gate_full_grad[at, rc + h * head : rc + (h + 1) * head]], axis=1)
        )
    gate_grad_own = jnp.concatenate(blocks)
    chan_grad = jnp.sum(chan_grad, axis=1)[:, :r8]
    chan_grad = jnp.concatenate([chan_grad[:7], (8.0 * jax.nn.sigmoid(-lam) * chan_grad[7])[None]])
    gate_back = jnp.concatenate([gate_grad_own, chan_grad.T], axis=1).reshape(length, gate_rows, 2 * head + 8)
    gate_back = jnp.pad(
        gate_back, ((0, 0), (0, gate_pad - gate_rows), (0, rc - 2 * head - 8))
    )
    gate_back = jnp.roll(gate_back, -z, axis=0)
    mixer_back, input_grad, *small, norm, factor = last(
        mixer_sums.reshape(8, share, 3 * r8), dnormed_one, inputs, grad_residual, gains, gain_two,
        gate_back, squares_one + squares_two + squares_three + squares_four, gain_state, gate_state,
        share, 2 * head, length, 8,
    )
    gains_up = [gain_rows(v) for v in small[:3]]
    gate_up = [v[:gate_rows, : 2 * head] for v in small[3:]]
    chan_up = [v[:gate_rows, 2 * head : 2 * head + 8].T for v in small[3:]]
    mixer_up = adam_pairs(
        mixer_weight, mixer_back, first_mixer, second_mixer, factor, rate_matrix, decay_matrix
    )
    mlp_up = adam_blocks(
        mlp_weight, mlp_back, first_mlp, second_mlp, factor, rate_matrix, decay_matrix
    )
    return (
        turned_back(block_output)[None],
        turned_back(input_grad)[None],
        norm[0, 0],
        *gains_up,
        *mixer_up,
        *gate_up,
        *chan_up,
        *mlp_up,
    )


def solution(mesh):
    rows = P(("batch", "seq"), None)
    columns = P(None, ("batch", "seq"))
    data = P("batch", "seq", None)
    weights = (columns, rows, rows, columns, rows)
    in_specs = (data, data) + weights * 3
    triples = tuple(spec for spec in weights for _ in range(3))
    return jax.shard_map(
        on_device,
        mesh=mesh,
        in_specs=in_specs,
        out_specs=(data, data, P()) + triples,
        check_vma=False,
    )
```

time: 940 us -> 863 us (0.918)
  other arithmetic: 65.1 us -> 14.7 us
  local copies, waits for them, and re-layouts: 67.8 us -> 36.1 us
    reduce_sum x9 -> x0, other arithmetic: 17.7 us -> none  [the longest x4 12.1 us: on_device(): squares = sum((jnp.sum(g * g) for g in mlp_sums + [mixer_sums]))]
    mul x6 -> x0, local copies, waits for them, and re-layouts: 12.9 us -> none  [the longest x3 12 us: adam_step(): clipped = grad * factor]
    convert_element_type x8 -> x1, other arithmetic: 13.4 us -> 0.98 us  [on_device(): gate_state[0].astype(BF16)]
    sub x4 -> x0, other arithmetic: 10.8 us -> none  [adam_step(): weight - rate * (first_hat / (jnp.sqrt(second_hat) + adam_eps) + decay_ra...]
    pallas_call x9 -> x8, Pallas kernels: 502 us -> 508 us  [the longest x1 112 us: middle(): pl.pallas_call(functools.partial(middle_kernel, length), out_shape=(jax.S...]
    unnamed x143 -> x100, local copies, waits for them, and re-layouts: 23.2 us -> 24.1 us
where the time goes in v3:
time: 863 us; the launch traced here: 856 us
  Pallas kernels  643 us (75%)
  matrix products  162 us (19%)
  local copies, waits for them, and re-layouts  36.1 us (4%)
  other arithmetic  14.7 us (2%)
    pallas_call x1, Pallas kernels, first(): pl.pallas_call(functools.partial(first_kernel, length), out_shape=(jax.Sh...  113 us
    pallas_call x1, Pallas kernels, middle(): pl.pallas_call(functools.partial(middle_kernel, length), out_shape=(jax.S...  112 us
    pallas_call x1, Pallas kernels, turn(): pl.pallas_call(functools.partial(turn_kernel, length, cuts), out_shape=(j...  92.5 us
    pallas_call x1, Pallas kernels, closing(): pl.pallas_call(functools.partial(closing_kernel, length, parts), out_shap...  77.5 us
    pallas_call x1, Pallas kernels, recur_forward(): pl.pallas_call(functools.partial(forward_kernel, length), out_shape=(low,...  75.7 us
    pallas_call x1, Pallas kernels, recur_backward(): pl.pallas_call(functools.partial(backward_kernel, length, cuts), grid=(1,...  58.8 us
    pallas_call x1, Pallas kernels, output(): pl.pallas_call(functools.partial(output_kernel, length, cuts), out_shape=...  52.7 us
    dot_general x5, matrix products, contract_last(): lax.dot_general(left, right, (((1,), (1,)), ((), ())), preferred_element_...  50.1 us

profile of v3, /device:TPU:0, one launch (start us, length us, event | category | flops | bytes accessed | tf_op | source)
XLA Modules:
  0.0 856.3 jit_solution(12814584673942334903)
XLA Ops:
  0.7 0.8 pad_select_fusion.2.gn.gw
  1.5 0.8 pad_select_fusion
  2.4 0.8 copy.51
  3.1 0.8 copy.58
  3.9 0.8 copy.59
  4.7 1.0 fusion.49
  5.7 1.1 select_maximum_fusion
  6.7 1.5 copy-done.1
  8.3 1.2 copy-done.11
  9.5 1.2 copy-done.12
  10.7 113.1 %shard_map.304 = (bf16[8,256,2048]{2,1,0:T(8,128)(2,1)}, bf16[4,8,64,960]{3,2,1,0:T(8,128)(2,1)S(1)}, bf16[4,8,64,1536]{3,2,1,0:T(8,128)(2,1)}, bf16[4,8,64,768]...) custom-call(bf16[256,2048]{1,0:T(8,128)(2,1)S(1)} %bitcast.93, ...), custom_call_target="tpu_custom_call" | custom-call | bytes 314572800 | tf_op jit(solution)/shard_map/pallas_call | solution.py:756
  123.8 2.0 copy-done.2
  125.8 1.0 copy-done.4
  126.8 1.6 copy-done.7
  128.7 0.7 pad_maximum_fusion.2.chan
  129.6 0.9 pad.71.gate
  130.4 1.6 slice_select_fusion
  132.0 0.9 fusion.50
  133.2 0.9 copy-done.27
  134.1 10.8 %fusion.9.proj = f32[4,512,768]{2,1,0:T(8,128)} fusion(bf16[4,512,2048]{2,1,0:T(8,128)(2,1)} %bitcast.123, bf16[2048,320]{1,0:T(8,128)(2,1)S(1)} %get-tuple-element.170, bf16[2048,384]{1,0:T(8,128)(2,1)S(1)} %slice_select_fusion), kind=kOutput, calls=%fused_computation.24 | convolution fusion | flops 6451888128 | bytes 17563648 | tf_op jit(solution)/shard_map/dot_general | solution.py:1442
  144.9 75.7 %shard_map.305 = (bf16[4,512,384]{2,1,0:T(8,128)(2,1)}, f32[4,512,384]{2,1,0:T(8,128)}, f32[4,512,384]{2,1,0:T(8,128)}, f32[4,512,384]{2,1,0:T(8,128)}, f32[4,51...) custom-call(f32[4,512,768]{2,1,0:T(8,128)} %fusion.9.proj, ...), custom_call_target="tpu_custom_call", output_to_operand_aliasing={{10}: (4, {})} | custom-call | flops 1207959552 | bytes 104857600 | tf_op jit(solution)/shard_map/pallas_call | solution.py:1086
  220.6 11.9 %fusion.54 = f32[2048,768]{1,0:T(8,128)} fusion(bf16[2048,2048]{1,0:T(8,128)(2,1)} %bitcast.125, bf16[2048,768]{1,0:T(8,128)(2,1)} %bitcast.90), kind=kOutput, calls=%fused_computation.96 | convolution fusion | flops 6442450944 | bytes 17825792 | tf_op jit(solution)/shard_map/dot_general | solution.py:1456
  232.4 6.8 convolution_convert_fusion.2
  239.3 111.9 %shard_map.306 = (f32[256,2048]{1,0:T(8,128)S(1)}, bf16[8,256,2048]{2,1,0:T(8,128)(2,1)}, bf16[4,8,64,1536]{3,2,1,0:T(8,128)(2,1)S(1)}) custom-call(bf16[8,256,2048]{2,1,0:T(8,128)(2,1)} %bitcast.110, bf16[256,2048]{1,0:T(8,128)(2,1)S(1)} %get-tuple-element.79.inputs, f32[8,2048]{1,0:T(8,128)S(1)} %get-tuple-element.80.gains, ...), custom_call_target="tpu_custom_call", output_to_operand_aliasing={{2}: (3, {})} | custom-call | bytes 314572800 | tf_op jit(solution)/shard_map/pallas_call | solution.py:487
  351.2 11.4 %fusion.12 = f32[2048,768]{1,0:T(8,128)} fusion(bf16[2048,2048]{1,0:T(8,128)(2,1)} %bitcast.129, bf16[2048,1536]{1,0:T(8,128)(2,1)S(1)} %bitcast.84), kind=kOutput, calls=%fused_computation.27 | convolution fusion | flops 6442450944 | bytes 17825792 | tf_op jit(solution)/shard_map/dot_general | solution.py:1455
  362.7 17.4 %fusion.6 = (bf16[2048,768]{1,0:T(8,128)(2,1)S(1)}, bf16[2048,768]{1,0:T(8,128)(2,1)S(1)}, bf16[2048,768]{1,0:T(8,128)(2,1)}) fusion(f32[2048,768]{1,0:T(8,128)} %fusion.54, f32[2048,768]{1,0:T(8,128)} %fusion.12, bf16[2048,2048]{1,0:T(8,128)(2,1)} %bitcast.130, bf16[2048,1536]{1,0:T(8,128)(2,1)S(1)} %bitcast.85), kind=kOutput, calls=%fused_computation.12 | convolution fusion | flops 6481772544 | bytes 33554432 | tf_op jit(solution)/shard_map/dot_general | solution.py:1454
  380.1 12.5 %convolution_convert_fusion.5 = bf16[2048,768]{1,0:T(8,128)(2,1)} fusion(bf16[2048,2048]{1,0:T(8,128)(2,1)} %bitcast.126, bf16[2048,768]{1,0:T(8,128)(2,1)} %get-tuple-element.168), kind=kOutput, calls=%fused_computation.21 | convolution fusion | flops 6444023808 | bytes 14680064 | tf_op jit(solution)/shard_map/dot_general | solution.py:1261
  392.6 8.5 convolution_convert_fusion.4
  401.1 8.7 %convolution_convert_fusion.6 = bf16[2048,768]{1,0:T(8,128)(2,1)} fusion(bf16[2048,2048]{1,0:T(8,128)(2,1)S(1)} %bitcast.132, bf16[2048,768]{1,0:T(8,128)(2,1)S(1)} %get-tuple-element.167), kind=kOutput, calls=%fused_computation.22 | convolution fusion | flops 6444023808 | bytes 14680064 | tf_op jit(solution)/shard_map/dot_general | solution.py:1261
  409.8 11.0 %convolution_convert_fusion.1 = bf16[2048,2048]{1,0:T(8,128)(2,1)} fusion(bf16[2048,768]{1,0:T(8,128)(2,1)} %get-tuple-element.168, bf16[2048,768]{1,0:T(8,128)(2,1)S(1)} %bitcast.91), kind=kOutput, calls=%fused_computation.4 | convolution fusion | flops 6446645248 | bytes 14680064 | tf_op jit(solution)/shard_map/dot_general | solution.py:1255
  420.8 52.7 %shard_map.307 = (bf16[256,2048]{1,0:T(8,128)(2,1)S(1)}, bf16[512,640]{1,0:T(8,128)(2,1)S(1)}, f32[8,128]{1,0:T(8,128)S(1)}) custom-call(bf16[8,256,2048]{2,1,0:T(8,128)(2,1)} %bitcast.109, f32[256,2048]{1,0:T(8,128)S(1)} %get-tuple-element.85.residual, bf16[4,512,768]{2,1,0:T(8,128)(2,1)} %bitcast.105, bf16[4,512,768]{2,1,0:T(8,128)(2,1)} %bitcast.103), custom_call_target="tpu_custom_call" | custom-call | bytes 157286400 | tf_op jit(solution)/shard_map/pallas_call | solution.py:576
  473.5 1.0 copy-done.13
  474.5 0.9 copy-done.17
  475.4 9.8 %fusion.14 = f32[2048,2048]{1,0:T(8,128)} fusion(bf16[2048,768]{1,0:T(8,128)(2,1)S(1)} %get-tuple-element.166, bf16[2048,1536]{1,0:T(8,128)(2,1)S(1)} %bitcast.86), kind=kOutput, calls=%fused_computation.29 | convolution fusion | flops 6442450944 | bytes 23068672 | tf_op jit(solution)/shard_map/dot_general | solution.py:1255
  485.2 13.3 %add_convert_fusion = bf16[2048,2048]{1,0:T(8,128)(2,1)} fusion(f32[2048,2048]{1,0:T(8,128)} %fusion.14, bf16[2048,768]{1,0:T(8,128)(2,1)} %copy-done.41, bf16[2048,1536]{1,0:T(8,128)(2,1)S(1)} %bitcast.87), kind=kOutput, calls=%fused_computation | convolution fusion | flops 6450839552 | bytes 31457280 | tf_op jit(solution)/shard_map/dot_general | solution.py:1255
  498.5 92.5 %shard_map.308 = (f32[256,2048]{1,0:T(8,128)}, f32[8,2048]{1,0:T(8,128)}, bf16[8,256,2048]{2,1,0:T(8,128)(2,1)}, bf16[512,1152]{1,0:T(8,128)(2,1)}, f32[8,128]{1,0:T(8,128)}) custom-call(bf16[8,256,2048]{2,1,0:T(8,128)(2,1)} %bitcast.108, f32[256,2048]{1,0:T(8,128)} %copy-done, bf16[256,2048]{1,0:T(8,128)(2,1)} %copy-done.4, f32[8,2048]{1,0:T(8,128)} %copy-done.18, ...), custom_call_target="tpu_custom_call" | custom-call | bytes 314572800 | tf_op jit(solution)/shard_map/pallas_call | solution.py:535
  591.0 6.9 fusion.55
  598.0 2.0 copy.55
  600.0 10.0 %fusion.18.dmix = f32[4,512,384]{2,1,0:T(8,128)} fusion(bf16[4,512,2048]{2,1,0:T(8,128)(2,1)} %bitcast.128, bf16[2048,320]{1,0:T(8,128)(2,1)} %copy-done.29), kind=kOutput, calls=%fused_computation.35 | convolution fusion | flops 3221225472 | bytes 12845056 | tf_op jit(solution)/shard_map/dot_general | solution.py:1481
  610.0 58.8 %shard_map.309 = (bf16[4,512,768]{2,1,0:T(8,128)(2,1)}, bf16[4,512,768]{2,1,0:T(8,128)(2,1)}, f32[8,8,384]{2,1,0:T(8,128)}, bf16[512,512]{1,0:T(8,128)(2,1)}, f32[8,128]{1,0:T(8,128)}) custom-call(f32[4,512,384]{2,1,0:T(8,128)} %fusion.18.dmix, bf16[384,768]{1,0:T(8,128)(2,1)} %pad.71.gate, f32[8,384]{1,0:T(8,128)} %pad_maximum_fusion.2.chan, ...), custom_call_target="tpu_custom_call" | custom-call | flops 1207959552 | bytes 125829120 | tf_op jit(solution)/shard_map/pallas_call | solution.py:1229
  668.8 3.9 convolution_bitcast_fusion
  672.9 9.5 %convolution_convert_fusion.3 = bf16[2048,768]{0,1:T(8,128)(2,1)S(1)} fusion(bf16[2048,2048]{1,0:T(8,128)(2,1)} %bitcast.124, bf16[2048,768]{1,0:T(8,128)(2,1)S(1)} %bitcast.133), kind=kOutput, calls=%fused_computation.19 | convolution fusion | flops 6444023808 | bytes 14680064 | tf_op jit(solution)/shard_map/dot_general | solution.py:1261
  682.4 1.7 fusion.51
  684.1 0.7 slice_multiply_fusion
  685.4 2.6 copy.53
  688.0 2.5 copy.54
  690.6 5.0 pad_maximum_fusion.g
  695.5 9.1 %convolution_convert_fusion = bf16[2048,2048]{1,0:T(8,128)(2,1)} fusion(bf16[2048,768]{1,0:T(8,128)(2,1)S(1)} %bitcast.134, bf16[2048,320]{1,0:T(8,128)(2,1)S(1)} %copy-done.28, bf16[2048,384]{1,0:T(8,128)(2,1)S(1)} %copy-done.26), kind=kOutput, calls=%fused_computation.3 | convolution fusion | flops 6456082432 | bytes 14417920 | tf_op jit(solution)/shard_map/dot_general | solution.py:1255
  704.7 77.5 %shard_map.310 = (f32[256,2048]{1,0:T(8,128)}, bf16[8,64,2304]{2,1,0:T(8,128)(2,1)}, bf16[512,960]{1,0:T(8,128)(2,1)}, f32[8,128]{1,0:T(8,128)}) custom-call(bf16[8,256,2048]{2,1,0:T(8,128)(2,1)} %bitcast.107, bf16[4,512,960]{2,1,0:T(8,128)(2,1)} %pad_maximum_fusion.g, bf16[8,64,1152]{2,1,0:T(8,128)(2,1)} %bitcast.116, bf16[8,64,640]{2,1,0:T(8,128)(2,1)} %bitcast.99, ...), custom_call_target="tpu_custom_call" | custom-call | bytes 262144000 | tf_op jit(solution)/shard_map/pallas_call | solution.py:623
  782.2 0.7 add_add_fusion.sq
  782.9 1.6 copy-done.10
  784.5 1.2 copy-done.16
  785.7 28.2 %shard_map.311 = (bf16[8,64,960]{2,1,0:T(8,128)(2,1)S(1)}, f32[256,2048]{1,0:T(8,128)S(1)}, f32[8,128]{1,0:T(8,128)S(1)}, f32[8,128]{1,0:T(8,128)S(1)}, f32[8,12...) custom-call(bf16[8,64,960]{2,1,0:T(8,128)(2,1)S(1)} %bitcast.96, ...), custom_call_target="tpu_custom_call" | custom-call | tf_op jit(solution)/shard_map/pallas_call | solution.py:916
  813.9 1.0 copy-done.15
  817.4 0.7 copy.60
  818.1 0.7 copy.61
  818.9 0.7 copy.62
  819.5 10.4 %shard_map.312 = (f32[64,7680]{1,0:T(8,128)}, f32[64,7680]{1,0:T(8,128)}, f32[64,7680]{1,0:T(8,128)}) custom-call(f32[8,128]{1,0:T(8,128)} %copy-done.23, f32[64,7680]{1,0:T(8,128)} %w.2, bf16[8,64,960]{2,1,0:T(8,128)(2,1)} %copy-done.15, f32[64,7680]{1,0:T(8,128)} %m.2, f32[64,7680]{1,0:T(8,128)} %v.2), custom_call_target="tpu_custom_call" | custom-call | bytes 13762560 | tf_op jit(solution)/shard_map/pallas_call | solution.py:1327
  829.9 22.0 %shard_map.313 = (f32[64,18432]{1,0:T(8,128)}, f32[64,18432]{1,0:T(8,128)}, f32[64,18432]{1,0:T(8,128)}) custom-call(f32[8,128]{1,0:T(8,128)} %copy-done.23, f32[64,18432]{1,0:T(8,128)} %w.3, bf16[8,64,2304]{2,1,0:T(8,128)(2,1)} %get-tuple-element.124.g, f32[64,18432]{1,0:T(8,128)} %m.3, f32[64,18432]{1,0:T(8,128)} %v.3), custom_call_target="tpu_custom_call" | custom-call | bytes 33030144 | tf_op jit(solution)/shard_map/pallas_call | solution.py:1291
  851.9 1.0 copy.72
  852.8 1.3 copy.73
  854.2 0.6 copy.74
  854.8 0.6 copy.75
  855.5 0.6 copy.76
  (98 shorter events, 4.2 us)
Async XLA Ops:
  1.5 122.3 %copy-start.21 = (f32[8,128]{1,0:T(8,128)}, f32[8,128]{1,0:T(8,128)S(1)}, u32[]{:S(2)}) copy-start(f32[8,128]{1,0:T(8,128)S(1)} %pad_select_fusion.2.gn.gw) | copy-start | bytes 12292
  6.7 1.5 copy-start.1
  8.3 1.2 copy-start.11
  9.5 1.2 copy-start.12
  10.7 117.9 %copy-start.34 = (f32[8,64]{1,0:T(8,128)S(1)}, f32[8,64]{1,0:T(8,128)}, u32[]{:S(2)}) copy-start(f32[8,64]{1,0:T(8,128)} %constant.57.clone.1) | copy-start | bytes 6148
  10.7 119.7 %copy-start.35 = (pred[384]{0:T(512)(128)(4,1)S(1)}, pred[384]{0:T(512)(128)(4,1)}, u32[]{:S(2)}) copy-start(pred[384]{0:T(512)(128)(4,1)} %constant.54.clone.1) | copy-start | bytes 1156
  123.8 2.0 copy-start.2
  125.8 1.0 copy-start.4
  126.8 1.6 copy-start.7
  128.4 110.8 %copy-start.5 = (bf16[256,2048]{1,0:T(8,128)(2,1)}, bf16[256,2048]{1,0:T(8,128)(2,1)S(1)}, u32[]{:S(2)}) copy-start(bf16[256,2048]{1,0:T(8,128)(2,1)S(1)} %get-tuple-element.79.inputs) | copy-start | bytes 3145732
  128.4 110.8 %copy-start.18 = (f32[8,2048]{1,0:T(8,128)}, f32[8,2048]{1,0:T(8,128)S(1)}, u32[]{:S(2)}) copy-start(f32[8,2048]{1,0:T(8,128)S(1)} %get-tuple-element.80.gains) | copy-start | bytes 196612
  128.6 3.4 copy-start.3
  128.6 4.3 copy-start.31
  132.0 1.1 copy-start.25
  132.9 1.1 copy-start.27
  133.0 99.5 %copy-start.29 = (bf16[2048,320]{1,0:T(8,128)(2,1)}, bf16[2048,320]{1,0:T(8,128)(2,1)S(1)}, u32[]{:S(2)}) copy-start(bf16[2048,320]{1,0:T(8,128)(2,1)S(1)} %get-tuple-element.169) | copy-start | bytes 3932164
  144.9 94.4 %slice-start = ((s8[6291456]{0:T(1024)(128)(4,1)}), s8[2097152]{0:T(1024)(128)(4,1)S(1)}, s32[]{:S(2)}) async-start(s8[6291456]{0:T(1024)(128)(4,1)} %bitcast.82), calls=%async_computation | async-start | bytes 4194304
  220.5 11.9 %copy-start.39 = (bf16[4,512,384]{2,1,0:T(8,128)(2,1)S(1)}, bf16[4,512,384]{2,1,0:T(8,128)(2,1)}, u32[]{:S(2)}) copy-start(bf16[4,512,384]{2,1,0:T(8,128)(2,1)} %get-tuple-element.78) | copy-start | bytes 4718596
  220.5 18.7 %slice-start.1 = ((s8[6291456]{0:T(1024)(128)(4,1)}), s8[4194304]{0:T(1024)(128)(4,1)S(1)}, s32[]{:S(2)}) async-start(s8[6291456]{0:T(1024)(128)(4,1)} %bitcast.82), calls=%async_computation.1 | async-start | bytes 8388608
  351.2 69.5 %copy-start = (f32[256,2048]{1,0:T(8,128)}, f32[256,2048]{1,0:T(8,128)S(1)}, u32[]{:S(2)}) copy-start(f32[256,2048]{1,0:T(8,128)S(1)} %get-tuple-element.85.residual) | copy-start | bytes 6291460
  380.1 21.0 %copy-start.41 = (bf16[2048,768]{1,0:T(8,128)(2,1)}, bf16[2048,768]{1,0:T(8,128)(2,1)S(1)}, u32[]{:S(2)}) copy-start(bf16[2048,768]{1,0:T(8,128)(2,1)S(1)} %get-tuple-element.167) | copy-start | bytes 9437188
  380.1 12.5 %copy-start.36 = (bf16[8,256,2048]{2,1,0:T(8,128)(2,1)S(1)}, bf16[8,256,2048]{2,1,0:T(8,128)(2,1)}, u32[]{:S(2)}) copy-start(bf16[8,256,2048]{2,1,0:T(8,128)(2,1)} %get-tuple-element.82) | copy-start | bytes 25165828
  401.1 8.7 %copy-start.8 = (bf16[4,8,64,768]{3,2,1,0:T(8,128)(2,1)S(1)}, bf16[4,8,64,768]{3,2,1,0:T(8,128)(2,1)}, u32[]{:S(2)}) copy-start(bf16[4,8,64,768]{3,2,1,0:T(8,128)(2,1)} %get-tuple-element.84) | copy-start | bytes 9437188
  473.5 1.0 copy-start.13
  474.5 0.9 copy-start.17
  498.5 92.5 %copy-start.40 = (bf16[4,512,384]{2,1,0:T(8,128)(2,1)S(1)}, bf16[4,512,384]{2,1,0:T(8,128)(2,1)}, u32[]{:S(2)}) copy-start(bf16[4,512,384]{2,1,0:T(8,128)(2,1)} %get-tuple-element.78) | copy-start | bytes 4718596
  668.8 4.1 copy-start.37
  682.4 1.7 copy-start.30
  685.3 5.3 copy-start.24
  690.5 5.0 copy-start.26
  690.5 5.0 copy-start.28
  690.6 5.0 copy-start.38
  704.6 77.5 %copy-start.32 = (f32[8,128]{1,0:T(8,128)S(1)}, f32[8,128]{1,0:T(8,128)}, u32[]{:S(2)}) copy-start(f32[8,128]{1,0:T(8,128)} %get-tuple-element.107) | copy-start | bytes 12292
  704.6 77.5 %copy-start.33 = (f32[8,128]{1,0:T(8,128)S(1)}, f32[8,128]{1,0:T(8,128)}, u32[]{:S(2)}) copy-start(f32[8,128]{1,0:T(8,128)} %get-tuple-element.109) | copy-start | bytes 12292
  704.7 78.2 %copy-start.6 = (bf16[256,2048]{1,0:T(8,128)(2,1)S(1)}, bf16[256,2048]{1,0:T(8,128)(2,1)}, u32[]{:S(2)}) copy-start(bf16[256,2048]{1,0:T(8,128)(2,1)} %copy-done.5) | copy-start | bytes 3145732
  704.7 78.2 %copy-start.9 = (f32[256,2048]{1,0:T(8,128)S(1)}, f32[256,2048]{1,0:T(8,128)}, u32[]{:S(2)}) copy-start(f32[256,2048]{1,0:T(8,128)} %get-tuple-element.103.back) | copy-start | bytes 6291460
  704.7 78.2 %copy-start.19 = (f32[8,2048]{1,0:T(8,128)S(1)}, f32[8,2048]{1,0:T(8,128)}, u32[]{:S(2)}) copy-start(f32[8,2048]{1,0:T(8,128)} %copy-done.18) | copy-start | bytes 196612
  704.7 78.2 %copy-start.20 = (f32[8,2048]{1,0:T(8,128)S(1)}, f32[8,2048]{1,0:T(8,128)}, u32[]{:S(2)}) copy-start(f32[8,2048]{1,0:T(8,128)} %get-tuple-element.104.gain_two) | copy-start | bytes 196612
  704.7 78.2 %copy-start.22 = (f32[8,128]{1,0:T(8,128)S(1)}, f32[8,128]{1,0:T(8,128)}, u32[]{:S(2)}) copy-start(f32[8,128]{1,0:T(8,128)} %copy-done.21) | copy-start | bytes 12292
  782.9 1.6 copy-start.10
  784.5 1.2 copy-start.16
  813.9 1.0 copy-start.15
  814.9 4.6 copy-start.23
  829.9 22.0 %copy-start.14 = (bf16[256,2048]{1,0:T(8,128)(2,1)S(1)}, bf16[256,2048]{1,0:T(8,128)(2,1)}, u32[]{:S(2)}) copy-start(bf16[256,2048]{1,0:T(8,128)(2,1)} %copy-done.13) | copy-start | bytes 3145732

commit v4 on v3

--- a/solution.py
+++ b/solution.py
@@ -85,7 +85,7 @@
         half = a.shape[0] // 2
         self.lo, self.hi = pl.ds(0, half), pl.ds(half, half)
         self.a, self.o, self.loc, self.ss, self.rs = a, o, loc, ss, rs
-        self.done = []
+        self.done, self.last = [], []
 
     def send(self, src, dst, k, to):
         copy = remote(src, dst, self.ss.at[k], self.rs.at[k], to)
@@ -95,25 +95,33 @@
     def relay(self, block, part, k, to):
         return self.send(self.o.at[block, part], self.o.at[block, part], k, to)
 
+    def begin_half(self, half):
+        a, o, me = self.a, self.o, self.me
+        part = (self.lo, self.hi)[half]
+        if half == 0:
+            self.s0 = self.send(a.at[part], o.at[me, part], 0, self.to_x)
+            self.s3 = self.send(a.at[part], o.at[me, part], 3, self.to_y)
+        else:
+            self.s1 = self.send(a.at[part], o.at[me, part], 1, self.to_y)
+            self.s2 = self.send(a.at[part], o.at[me, part], 2, self.to_x)
+        self.last.append(self.send(a.at[part], o.at[me, part], (4, 13)[half], self.to_c))
+        if half == 1:
+            self.own = pltpu.make_async_copy(a, o.at[me], self.loc)
+            self.own.start()
+
     def begin(self):
-        a, o, me, lo, hi = self.a, self.o, self.me, self.lo, self.hi
-        self.s0 = self.send(a.at[lo], o.at[me, lo], 0, self.to_x)
-        self.s1 = self.send(a.at[hi], o.at[me, hi], 1, self.to_y)
-        self.s2 = self.send(a.at[hi], o.at[me, hi], 2, self.to_x)
-        self.s3 = self.send(a.at[lo], o.at[me, lo], 3, self.to_y)
-        self.s4 = self.send(a, o.at[me], 4, self.to_c)
-        self.own = pltpu.make_async_copy(a, o.at[me], self.loc)
-        self.own.start()
+        self.begin_half(0)
+        self.begin_half(1)
 
     def middle(self):
         self.s0.wait_recv()
         self.s5 = self.relay(self.bx, self.lo, 5, self.to_y)
-        self.last = [self.s4, self.relay(self.bx, self.lo, 7, self.to_c)]
+        self.last.append(self.relay(self.bx, self.lo, 7, self.to_c))
         self.s1.wait_recv()
         self.s6 = self.relay(self.by, self.hi, 6, self.to_x)
         self.last.append(self.relay(self.by, self.hi, 8, self.to_c))
 
-    def end(self, mark=lambda: None):
+    def relays(self, mark=lambda: None):
         self.s2.wait_recv()
         self.last.append(self.relay(self.bx, self.hi, 9, self.to_c))
         self.s3.wait_recv()
@@ -123,14 +131,20 @@
         self.last.append(self.relay(self.bd, self.lo, 11, self.to_c))
         self.s6.wait_recv()
         self.last.append(self.relay(self.bd, self.hi, 12, self.to_c))
+
+    def finish(self):
         for copy in self.last:
             copy.wait_recv()
         for copy in self.done:
             copy.wait_send()
         self.own.wait()
 
-
-def scatter_steps(p, o, mine, sib, part, got, loc, ss, rs, mark=lambda name: None):
+    def end(self, mark=lambda: None):
+        self.relays(mark)
+        self.finish()
+
+
+def scatter_steps(p, o, mine, sib, part, got, loc, ss, rs):
     y, c, z, x = place()
     to_x, to_y, to_c = gather_peers()
     half = o.shape[0] // 2
@@ -149,6 +163,7 @@
             p.at[rank(ty, 1 - c, tx), cut[h]], sib.at[t, h], ss.at[n], rs.at[n], to_c
         )
         sends.append(from_c[t, h])
+    yield "begun"
 
     def add(dst, t, h, extra):
         own[t, h].wait()
@@ -181,20 +196,23 @@
     send(2, 0, to_y)
     add(part.at[3], 2, 1, ())
     send(3, 2, to_x)
+    yield "sent"
     arrival(1).wait_recv()
     add(part.at[4], 2, 0, (got.at[1],))
     send(4, 4, to_x)
-    mark("early")
+    yield "early"
     arrival(3).wait_recv()
     add(part.at[5], 1, 1, (got.at[3],))
     send(5, 5, to_y)
-    mark("late")
+    yield "late"
     arrival(0).wait_recv()
     arrival(4).wait_recv()
     add(o.at[cut[0]], 3, 0, (got.at[0], got.at[4]))
+    yield "low half"
     arrival(2).wait_recv()
     arrival(5).wait_recv()
     add(o.at[cut[1]], 3, 1, (got.at[2], got.at[5]))
+    yield "high half"
     for copy in sends:
         copy.wait_send()
 
@@ -289,12 +307,13 @@
         self.loc, self.ss, self.rs = loc, ss, rs
         self.to = (device(y, c, lax.rem(z + 1, length), x), device(y, c, lax.rem(z + length - 1, length), x))
         self.far = (z, length - 1 - z)
+        self.next = 1
 
     def loads(self, way, hop):
         k = 0 if hop == 0 else self.length - hop if way == 0 else hop
         copies, at = [], 0
         for n, (ref, first, columns) in enumerate(self.sources):
-            dst = self.mine[way].at[hop - 1] if hop else self.total
+            dst = self.term(way, hop) if hop else self.total
             copies.append(
                 pltpu.make_async_copy(
                     ref.at[k, :, pl.ds(first, columns)], dst.at[:, pl.ds(at, columns)],
@@ -304,22 +323,21 @@
             at += columns
         return copies
 
+    def term(self, way, hop):
+        return self.mine[way].at[hop - 1]
+
     def copy(self, way, hop):
         return pltpu.make_async_remote_copy(
-            src_ref=self.mine[way].at[hop - 1], dst_ref=self.got[way].at[hop - 1],
+            src_ref=self.term(way, hop), dst_ref=self.got[way].at[hop - 1],
             send_sem=self.ss.at[way, hop - 1], recv_sem=self.rs.at[way, hop - 1],
             device_id=self.to[way], device_id_type=MESH,
         )
 
-    def begin(self):
-        for hop in range(1, self.length):
-            for way in (0, 1):
+    def load(self, hops):
+        for hop in hops:
+            for way in (0, 1) if hop else (0,):
                 for copy in self.loads(way, hop):
                     copy.start()
-        for copy in self.loads(0, 0):
-            copy.start()
-        self.next = 1
-        self.start()
 
     def start(self):
         hop = self.next
@@ -335,37 +353,35 @@
                 @pl.when(jnp.logical_and(far >= 1, far <= hop - 1))
                 def _():
                     self.copy(way, hop - 1).wait_recv()
-                    dst, src = self.mine[way].at[hop - 1], self.got[way].at[hop - 2]
-
-                    @pl.loop(0, dst.shape[0] // 16)
-                    def _(i):
-                        at = pl.ds(pl.multiple_of(i * 16, 16), 16)
-                        dst[at] = (dst[at].astype(F32) + src[at].astype(F32)).astype(dst.dtype)
+                    dst, src = self.term(way, hop), self.got[way].at[hop - 2]
+
+                    def add(at):
+                        dst[at] = dst[at] + src[at]
+
+                    rows_loop(dst.shape[0], add, unroll=4)
 
             @pl.when(far <= hop - 1)
             def _():
                 self.copy(way, hop).start()
 
-    def end(self, result, squares):
-        while self.next < self.length:
-            self.start()
+    def end(self, result, first_column, squares):
         last = self.length - 1
         for copy in self.loads(0, 0):
             copy.wait()
-        squares[...] = jnp.zeros_like(squares)
+        columns = pl.ds(first_column, self.total.shape[1])
 
         def finish(ways):
             for way in ways:
                 self.copy(way, last).wait_recv()
 
-            @pl.loop(0, result.shape[0] // 16)
-            def _(i):
-                at = pl.ds(pl.multiple_of(i * 16, 16), 16)
+            def add(at):
                 total = self.total[at].astype(F32)
                 for way in ways:
                     total = total + self.got[way][last - 1, at].astype(F32)
-                result[at] = total.astype(result.dtype)
+                result[at, columns] = total.astype(result.dtype)
                 squares[...] += tile_of_squares(total)
+
+            rows_loop(result.shape[0], add)
 
         above, below = self.far[0] >= 1, self.far[1] >= 1
         pl.when(jnp.logical_and(above, below))(lambda: finish((0, 1)))
@@ -377,6 +393,72 @@
                 @pl.when(self.far[way] <= hop - 1)
                 def _():
                     self.copy(way, hop).wait_send()
+
+
+class HeldLine(LineScatter):
+    def __init__(self, g, up_got, down_got, ss, rs):
+        y, c, z, x = place()
+        self.length = length = g.shape[0]
+        self.sources, self.g, self.total = (), g, g.at[0]
+        self.got, self.ss, self.rs = (up_got, down_got), ss, rs
+        self.to = line_neighbours(length)
+        self.far = (z, length - 1 - z)
+        self.next = 1
+
+    def term(self, way, hop):
+        return self.g.at[self.length - hop if way == 0 else hop]
+
+
+def chains_of(cuts):
+    whole = sum(cut[2] for cut in cuts)
+    left = -(-whole // 256) * 128
+    lists = [], []
+    for which, first_column, columns in cuts:
+        taken = min(columns, left)
+        if taken:
+            lists[0].append((which, first_column, taken))
+        if columns > taken:
+            lists[1].append((which, first_column + taken, columns - taken))
+        left -= taken
+    return lists
+
+
+class Lines:
+    def __init__(self, terms, cuts, length, refs):
+        self.chains, self.length = [], length
+        for n, cut in enumerate(chains_of(cuts)):
+            sources = [(terms[which], first_column, columns) for which, first_column, columns in cut]
+            self.chains.append(
+                LineScatter(sources, length, *refs[n * LINE_REFS : (n + 1) * LINE_REFS])
+            )
+        self.queue = [chain for _ in range(1, length) for chain in self.chains]
+
+    def begin(self):
+        for chain in self.chains:
+            chain.load((1,))
+        self.start()
+        self.start()
+        for chain in self.chains:
+            chain.load((*range(2, self.length), 0))
+
+    def start(self):
+        if self.queue:
+            self.queue.pop(0).start()
+
+    def end(self, result, squares):
+        while self.queue:
+            self.start()
+        squares[...] = jnp.zeros_like(squares)
+        at = 0
+        for chain in self.chains:
+            chain.end(result, at, squares)
+            at += chain.total.shape[1]
+
+
+def lines_scratch(length, rows, cuts):
+    return sum(
+        (line_scratch(length, rows, sum(cut[2] for cut in chain), len(chain)) for chain in chains_of(cuts)), []
+    )
 
 
 def fold(v):
@@ -411,8 +493,8 @@
     return [device(y, c, lax.rem(z + 1, length), x), device(y, c, lax.rem(z + length - 1, length), x)]
 
 
-def rows_loop(rows, body):
-    @pl.loop(0, rows // 16)
+def rows_loop(rows, body, start=0, unroll=2):
+    @pl.loop(start // 16, (start + rows) // 16, unroll=unroll)
     def _(i):
         body(pl.ds(pl.multiple_of(i * 16, 16), 16))
 
@@ -457,23 +539,27 @@
     hops.start(1)
     started = [1]
 
-    def advance(name=None):
-        if name != "early" and started[0] < length - 1:
+    def advance():
+        if started[0] < length - 1:
             hops.arrive(started[0])
             started[0] += 1
             hops.start(started[0])
-
-    scatter_steps(p, residual, *scatter_refs)
 
     def body(at):
         v = inputs[at].astype(F32) + residual[at]
         residual[at] = v
         low[at] = (v * inverse_rms(v) * gains[1:2]).astype(BF16)
 
-    rows_loop(low.shape[0], body)
+    half = low.shape[0] // 2
     gather = Gather(low, normed_o, loc, gs, gr)
-    gather.begin()
-    advance()
+    for name in scatter_steps(p, residual, *scatter_refs):
+        if name == "low half":
+            rows_loop(half, body)
+            gather.begin_half(0)
+        if name == "high half":
+            rows_loop(half, body, half)
+            gather.begin_half(1)
+            advance()
     gather.middle()
     gather.end(advance)
     while started[0] < length - 1:
@@ -494,7 +580,7 @@
         in_specs=[ANY, VM, VM, ANY],
         out_specs=(VM, ANY, ANY),
         scratch_shapes=scatter_scratch(rows // 2, width)
-        + [pltpu.VMEM((rows, width), BF16), DMA, DMA((13,)), DMA((13,)), DMA((2, length)), DMA((2, length))],
+        + [pltpu.VMEM((rows, width), BF16), DMA, DMA((14,)), DMA((14,)), DMA((2, length)), DMA((2, length))],
         input_output_aliases={3: 2},
         compiler_params=params(collective_id, 40 * 2**20),
         cost_estimate=pl.CostEstimate(flops=0, bytes_accessed=300 * 2**20, transcendentals=0),
@@ -502,15 +588,15 @@
 
 
 def turn_kernel(length, cuts, p, residual, above, gains, *refs):
-    terms, refs = refs[: len(cuts)], refs[len(cuts) :]
+    parts = 1 + max(cut[0] for cut in cuts)
+    terms, refs = refs[:parts], refs[parts:]
     back, gain, low_o, sums, squares, *scratch = refs
     scatter_refs, (total, low, loc, gs, gr), line_refs = (
         scratch[:SCATTER_REFS], scratch[SCATTER_REFS : SCATTER_REFS + 5], scratch[SCATTER_REFS + 5 :]
     )
     greet(gather_peers() + line_neighbours(length))
-    line = LineScatter([(ref, *cut) for ref, cut in zip(terms, cuts)], length, *line_refs)
+    line = Lines(terms, cuts, length, line_refs)
     line.begin()
-    scatter_steps(p, total, *scatter_refs, mark=lambda name: line.start() if name == "late" else None)
     gain[...] = jnp.zeros_like(gain)
 
     def body(at):
@@ -520,9 +606,18 @@
         low[at] = grad.astype(BF16)
         gain[...] += gain_part
 
-    rows_loop(low.shape[0], body)
+    half = low.shape[0] // 2
     gather = Gather(low, low_o, loc, gs, gr)
-    gather.begin()
+    for name in scatter_steps(p, total, *scatter_refs):
+        if name in ("early", "late"):
+            line.start()
+        if name == "low half":
+            rows_loop(half, body)
+            gather.begin_half(0)
+        if name == "high half":
+            rows_loop(half, body, half)
+            gather.begin_half(1)
+            line.start()
     gather.middle()
     line.start()
     gather.end()
@@ -531,7 +626,7 @@
 
 def turn(p, residual, above, gains, terms, cuts, length, collective_id):
     rows, width = residual.shape
-    line_rows, columns = terms[0].shape[1], sum(cut[1] for cut in cuts)
+    line_rows, columns = terms[0].shape[1], sum(cut[2] for cut in cuts)
     return pl.pallas_call(
         functools.partial(turn_kernel, length, cuts),
         out_shape=(
@@ -544,104 +639,167 @@
         in_specs=[ANY, VM, VM, VM] + [ANY] * len(terms),
         out_specs=(VM, VM, ANY, VM, VM),
         scratch_shapes=scatter_scratch(rows // 2, width)
-        + [pltpu.VMEM((rows, width), F32), pltpu.VMEM((rows, width), BF16), DMA, DMA((13,)), DMA((13,))]
-        + line_scratch(length, line_rows, columns, len(cuts)),
+        + [pltpu.VMEM((rows, width), F32), pltpu.VMEM((rows, width), BF16), DMA, DMA((14,)), DMA((14,))]
+        + lines_scratch(length, line_rows, cuts),
         compiler_params=params(collective_id, 56 * 2**20),
         cost_estimate=pl.CostEstimate(flops=0, bytes_accessed=300 * 2**20, transcendentals=0),
     )(p.reshape(8, rows, width), residual, above, gains, *terms)
 
 
-def output_kernel(length, cuts, p, residual, *refs):
-    terms, refs = refs[: len(cuts)], refs[len(cuts) :]
-    out, sums, squares, *scratch = refs
-    scatter_refs, total, line_refs = (
-        scratch[:SCATTER_REFS], scratch[SCATTER_REFS], scratch[SCATTER_REFS + 1 :]
-    )
-    greet(gather_peers() + line_neighbours(length))
-    line = LineScatter([(ref, *cut) for ref, cut in zip(terms, cuts)], length, *line_refs)
-    line.begin()
-    scatter_steps(p, total, *scatter_refs, mark=lambda name: line.start())
+def closing_kernel(
+    length, cut, part, x_in, dmz_in, dproj, mixed, first_w, q, residual, terms, block,
+    o, out, e_o, sums, squares,
+    x_part, dmz_part, g, back, total, up_got, down_got, ls, lr, load_s, free, loc, es, er, *scratch,
+):
+    scatter_refs, line_refs = scratch[:SCATTER_REFS], scratch[SCATTER_REFS:]
+    greet(plane_peers() + line_neighbours(length))
+    model, rc = first_w.shape[0], mixed.shape[1]
+    tokens = dproj.shape[0]
+    columns = x_part.shape[2]
+    steps = model // columns
+    rows = tokens // steps
+    line_rows = g.shape[1]
+
+    def loads(i, slot):
+        at = pl.ds(pl.multiple_of(i * columns, columns), columns)
+        return (
+            pltpu.make_async_copy(x_in.at[:, at], x_part.at[slot], load_s.at[0, slot]),
+            pltpu.make_async_copy(dmz_in.at[:, at], dmz_part.at[slot], load_s.at[1, slot]),
+        )
+
+    group = steps // 4
+    order = (3, 1, 2, 0)
+
+    def fetch(i, slot):
+        for copy in loads(i, slot):
+            copy.start()
+
+    fetch(order[0] * group, 0)
+    rest = LineScatter([(terms, *cut)], length, *line_refs)
+    rest.load((1,))
+    rest.start()
+    rest.load((*range(2, length), 0))
+    line = HeldLine(g, up_got, down_got, ls, lr)
+    output = scatter_steps(q, total, *scatter_refs)
+    next(output)
+    copies, own = exchange_steps(block, e_o, loc, es, er)
+
+    def compute(n):
+        @pl.loop(0, group)
+        def _(j):
+            count = n * group + j
+            slot = count - count // 2 * 2
+            i = order[n] * group + j
+
+            @pl.when(j + 1 < group)
+            def _():
+                fetch(i + 1, 1 - slot)
+
+            if n < 3:
+
+                @pl.when(j + 1 == group)
+                def _():
+                    fetch(order[n + 1] * group, 1 - slot)
+
+            for copy in loads(i, slot):
+                copy.wait()
+            front = contract_first(x_part[slot], dproj[...])
+            tail = contract_first(dmz_part[slot], mixed[...])
+            k = i * columns // line_rows
+            at = pl.ds(pl.multiple_of(i * columns - k * line_rows, columns), columns)
+            g[k, at] = jnp.concatenate(
+                [front[:, :part], front[:, rc : rc + part], tail[:, :part]], axis=1
+            ).astype(BF16)
+            block_of = i * rows // 256
+            at = pl.ds(pl.multiple_of(i * rows - block_of * 256, rows), rows)
+            mine = dproj[pl.ds(pl.multiple_of(i * rows, rows), rows)]
+            for first_column in range(0, model, 512):
+                cols = slice(first_column, first_column + 512)
+                back[block_of, at, cols] = contract_last(mine, first_w[cols]).astype(BF16)
+
+    compute(0)
+    next(output)
+    compute(1)
+    if length == 4:
+        line.start()
+    next(output)
+    rest.start()
+    compute(2)
+    next(output)
+    compute(3)
+    if length != 4:
+        line.start()
+    while rest.next < length:
+        rest.start()
+    for _ in output:
+        pass
+    for peer in gather_peers():
+        pl.semaphore_signal(free, inc=1, device_id=peer, device_id_type=MESH)
+    line.start()
+    pl.semaphore_wait(free, 3)
+    incoming = scatter_steps(back, o, *scatter_refs)
+    next(incoming)
     pair = out.shape[1] // (4 * length)
 
     def body(at):
         store_turned(out, at, (residual[at] + total[at]).astype(BF16), length, pair)
 
     rows_loop(out.shape[0], body)
-    line.end(sums, squares)
-
-
-def output(p, residual, terms, cuts, length, collective_id):
+    squares[...] = jnp.zeros_like(squares)
+    rest.end(sums, 0, squares)
+    for name in incoming:
+        if name == "early" and line.next < length:
+            line.start()
+    while line.next < length:
+        line.start()
+    line.end(sums, cut[1], squares)
+    for copy in copies:
+        copy.wait()
+    own.wait()
+
+
+def closing(x, dmz, dproj, mixed, first_w, q, residual, terms, cut, block, part, length, collective_id):
     rows, width = residual.shape
-    line_rows, columns = terms[0].shape[1], sum(cut[1] for cut in cuts)
+    tokens, model = x.shape
+    share = block.shape[0] // 8
+    block = block.reshape(8, share, block.shape[1])
+    line_rows = terms.shape[1]
+    columns = min(256, line_rows)
+    held = pltpu.VMEM((length - 1, line_rows, 3 * part), BF16)
     return pl.pallas_call(
-        functools.partial(output_kernel, length, cuts),
+        functools.partial(closing_kernel, length, cut, part),
         out_shape=(
+            jax.ShapeDtypeStruct((rows, width), F32),
             jax.ShapeDtypeStruct((rows, width), BF16),
-            jax.ShapeDtypeStruct((line_rows, columns), BF16),
+            jax.ShapeDtypeStruct(block.shape, BF16),
+            jax.ShapeDtypeStruct((line_rows, cut[1] + 3 * part), BF16),
             TILE,
         ),
-        in_specs=[ANY, VM] + [ANY] * len(terms),
-        out_specs=(VM, VM, VM),
-        scratch_shapes=scatter_scratch(rows // 2, width)
-        + [pltpu.VMEM((rows, width), F32)]
-        + line_scratch(length, line_rows, columns, len(cuts)),
-        compiler_params=params(collective_id, 48 * 2**20),
-        cost_estimate=pl.CostEstimate(flops=0, bytes_accessed=150 * 2**20, transcendentals=0),
-    )(p.reshape(8, rows, width), residual, *terms)
-
-
-def closing_kernel(length, parts, p, g, *refs):
-    blocks, refs = refs[:parts], refs[parts:]
-    o, e_o, sums, squares, *scratch = refs
-    scatter_refs, (loc, es, er), line_refs = (
-        scratch[:SCATTER_REFS], scratch[SCATTER_REFS : SCATTER_REFS + 3], scratch[SCATTER_REFS + 3 :]
-    )
-    greet(plane_peers() + line_neighbours(length))
-    line = LineScatter([(g, 0, g.shape[2])], length, *line_refs)
-    line.begin()
-    scatter_steps(p, o, *scatter_refs, mark=lambda name: line.start() if name == "late" else None)
-    moves, at = [], 0
-    for n, block in enumerate(blocks):
-        columns = block.shape[2]
-        moves.append(
-            exchange_steps(block, e_o, loc.at[n], es.at[n], er.at[n], pl.ds(at, columns))
-        )
-        at += columns
-    line.end(sums, squares)
-    for copies, own in moves:
-        for copy in copies:
-            copy.wait()
-        own.wait()
-
-
-def closing(p, blocks, g, length, collective_id):
-    rows, width = p.shape[0] // 8, p.shape[1]
-    share = blocks[0].shape[0] // 8
-    blocks = [block.reshape(8, share, block.shape[1]) for block in blocks]
-    columns = sum(block.shape[2] for block in blocks)
-    parts = len(blocks)
-    return pl.pallas_call(
-        functools.partial(closing_kernel, length, parts),
-        out_shape=(
-            jax.ShapeDtypeStruct((rows, width), F32),
-            jax.ShapeDtypeStruct((8, share, columns), BF16),
-            jax.ShapeDtypeStruct(g.shape[1:], BF16),
-            TILE,
+        in_specs=[ANY, ANY, VM, VM, VM, ANY, VM, ANY, ANY],
+        out_specs=(VM, VM, ANY, VM, VM),
+        scratch_shapes=[
+            pltpu.VMEM((2, tokens, columns), BF16),
+            pltpu.VMEM((2, tokens, columns), BF16),
+            pltpu.VMEM((length, line_rows, 3 * part), BF16),
+            pltpu.VMEM((8, rows, width), BF16),
+            pltpu.VMEM((rows, width), F32),
+            held, held,
+            DMA((2, length)), DMA((2, length)), DMA((2, 2)), pltpu.SemaphoreType.REGULAR,
+            DMA, DMA((7,)), DMA((7,)),
+        ]
+        + scatter_scratch(rows // 2, width)
+        + line_scratch(length, line_rows, cut[1], 1),
+        compiler_params=params(collective_id, 63 * 2**20),
+        cost_estimate=pl.CostEstimate(
+            flops=10 * tokens * model * dproj.shape[1] // 2, bytes_accessed=350 * 2**20, transcendentals=0
         ),
-        in_specs=[ANY] * (2 + parts),
-        out_specs=(VM, ANY, VM, VM),
-        scratch_shapes=scatter_scratch(rows // 2, width)
-        + [DMA((parts,)), DMA((parts, 7)), DMA((parts, 7))]
-        + line_scratch(length, g.shape[1], g.shape[2], 1),
-        compiler_params=params(collective_id, 56 * 2**20),
-        cost_estimate=pl.CostEstimate(flops=0, bytes_accessed=250 * 2**20, transcendentals=0),
-    )(p.reshape(8, rows, width), g, *blocks)
+    )(x, dmz, dproj, mixed, first_w, q.reshape(8, rows, width), residual, terms, block)
 
 
 def first_kernel(
-    length, inputs, above, mixer_w, mlp_w, gn, gp,
+    length, inputs, above, mixer_w, mlp_w, gains_w, gate_w, chan_w,
     normed_o, wm_o, wf_o, wd_o, gains_o, gp_o, inputs_o, above_o,
-    normed, gn_all, wm, wf, wd, loc, ms, mr, fs, fr, line_s, line_r, gain_s, gain_r, move_s, move_r,
+    gn, gp, normed, gn_all, wm, wf, wd, loc, ms, mr, fs, fr, line_s, line_r, gain_s, gain_r, move_s, move_r,
     gather_s, gather_r, hop_s, hop_r,
 ):
     y, c, z, x = place()
@@ -667,40 +825,60 @@
 
     pl.semaphore_wait(barrier, len(line) + len(plane) + 2 * moves)
 
+    share = gains_w.shape[1]
+    gn[...] = jnp.zeros_like(gn)
+    for n in (0, 1):
+
+        @pl.when(x == n)
+        def _():
+            gn[:2, n * share : (n + 1) * share] = gains_w[...]
+
+    gp[...] = jnp.zeros_like(gp)
+    channels = contract_first(chan_w[...].astype(BF16), unit(8))
+    gp[: gate_w.shape[0]] = jnp.concatenate(
+        [
+            gate_w[...],
+            channels,
+            jnp.zeros((gate_w.shape[0], gp.shape[1] - gate_w.shape[1] - 8), F32),
+        ],
+        axis=1,
+    ).astype(BF16)
     gn_all[me, z] = gn[...]
     gains = [
         remote(gn, gn_all.at[me, z], line_s.at[0, k], line_r.at[0, k], line[k]) for k in range(length - 1)
     ]
-    for pack, source, js in ((wm, mixer_w, (0, 1, 2)), (wf, mlp_w, (0, 1)), (wd, mlp_w, (2,))):
+    gate_move = pltpu.make_async_remote_copy(
+        src_ref=gp, dst_ref=gp_o.at[to_z], send_sem=move_s, recv_sem=move_r,
+        device_id=device(y, c, to_z, to_x), device_id_type=MESH,
+    )
+    gate_stay = pltpu.make_async_copy(gp, gp_o.at[z], loc.at[2])
+    pl.when(moves == 1)(lambda: gate_move.start())
+    pl.when(moves == 0)(lambda: gate_stay.start())
+
+    def fill(pack, source, js):
         part = pack.shape[2] // len(js)
         for t in range(8):
             for n, j in enumerate(js):
                 start = (j * 8 + t) * part
                 pack[t, :, n * part : (n + 1) * part] = source[:, start : start + part].astype(BF16)
-        if pack is wm:
-            for copy in gains:
-                copy.wait()
-            spread = [
-                remote(gn_all.at[me], gn_all.at[me], gain_s.at[n], gain_r.at[n], plane[n])
-                for n in range(7)
-            ]
-            mixer, mixer_own = exchange_steps(wm, wm_o.at[0], loc.at[0], ms, mr)
-
-    @pl.when(moves == 1)
-    def _():
-        copy = remote(gp, gp_o.at[to_z], move_s, move_r, device(y, c, to_z, to_x))
+
+    fill(wm, mixer_w, (0, 1, 2))
+    mixer, mixer_own = exchange_steps(wm, wm_o.at[0], loc.at[0], ms, mr)
+    for copy in gains:
         copy.wait()
-
-    @pl.when(moves == 0)
-    def _():
-        copy = pltpu.make_async_copy(gp, gp_o.at[z], loc.at[2])
-        copy.start()
-        copy.wait()
-
+    spread = [
+        remote(gn_all.at[me], gn_all.at[me], gain_s.at[n], gain_r.at[n], plane[n]) for n in range(7)
+    ]
+    pl.when(moves == 1)(lambda: gate_move.wait())
+    pl.when(moves == 0)(lambda: gate_stay.wait())
     gates = [
         remote(gp_o.at[z], gp_o.at[z], line_s.at[1, k], line_r.at[1, k], line[k])
         for k in range(length - 1)
     ]
+    fill(wd, mlp_w, (2,))
+    down, down_own = exchange_steps(wd, wd_o.at[0], loc.at[4], fs.at[1], fr.at[1])
+    fill(wf, mlp_w, (0, 1))
+    feed, feed_own = exchange_steps(wf, wf_o.at[0], loc.at[3], fs.at[0], fr.at[0])
     for copy in spread:
         copy.wait()
     for k in range(length):
@@ -709,38 +887,38 @@
             at = slice((4 * k + b) * pair, (4 * k + b + 1) * pair)
             tile = (gn_all[2 * b, other] + gn_all[2 * b + 1, other])[:, :pair]
             gains_o[:, at] = tile.astype(BF16).astype(F32)
+    for copy in mixer:
+        copy.wait()
+    mixer_own.wait()
+    hops = LineGather(wm_o, length, hop_s, hop_r)
+    hops.start(1)
 
     def body(at):
         v = load_turned(inputs, at, length, pair)
         inputs_o[at] = v
         v = v.astype(F32)
         normed[at] = (v * inverse_rms(v) * gains_o[0:1]).astype(BF16)
-
-    rows_loop(rows, body)
-
+        above_o[at] = load_turned(above, at, length, pair)
+
+    half = rows // 2
     gather = Gather(normed, normed_o, loc.at[1], gather_s, gather_r)
-    gather.begin()
-    for copy in mixer:
-        copy.wait()
-    mixer_own.wait()
-    hops = LineGather(wm_o, length, hop_s, hop_r)
-    hops.start(1)
-    down, down_own = exchange_steps(wd, wd_o.at[0], loc.at[4], fs.at[1], fr.at[1])
-    feed, feed_own = exchange_steps(wf, wf_o.at[0], loc.at[3], fs.at[0], fr.at[0])
-    gather.middle()
-
-    def turn_rows(at):
-        above_o[at] = load_turned(above, at, length, pair)
-
-    rows_loop(rows, turn_rows)
+    rows_loop(half, body)
+    gather.begin_half(0)
+    rows_loop(half, body, half)
+    gather.begin_half(1)
     hops.arrive(1)
     if length > 2:
         hops.start(2)
-    gather.end()
-    for hop in range(2, length):
+    gather.middle()
+    if length > 3:
+        hops.arrive(2)
+        hops.start(3)
+    gather.relays()
+    for hop in range(min(3, length - 1), length):
         hops.arrive(hop)
         if hop + 1 < length:
             hops.start(hop + 1)
+    gather.finish()
     for copy in down + feed + gates:
         copy.wait()
     down_own.wait()
@@ -748,8 +926,15 @@
     hops.finish()
 
 
-def first(inputs, above, mixer, mlp, gn, gp, length, collective_id):
+def unit(n):
+    return (
+        lax.broadcasted_iota(jnp.int32, (n, n), 0) == lax.broadcasted_iota(jnp.int32, (n, n), 1)
+    ).astype(BF16)
+
+
+def first(inputs, above, mixer, mlp, gains, gate, chan, rc, length, collective_id):
     rows, width = inputs.shape
+    pack = (-(-gate.shape[0] // 16) * 16, rc)
     share = mixer.shape[0]
     wm, wf, wd = ((8, share, n) for n in (mixer.shape[1] // 8, mlp.shape[1] // 12, mlp.shape[1] // 24))
     low = jax.ShapeDtypeStruct((rows, width), BF16)
@@ -761,13 +946,15 @@
             jax.ShapeDtypeStruct((length,) + wf, BF16),
             jax.ShapeDtypeStruct((length,) + wd, BF16),
             jax.ShapeDtypeStruct((8, width), F32),
-            jax.ShapeDtypeStruct((length,) + gp.shape, gp.dtype),
+            jax.ShapeDtypeStruct((length,) + pack, BF16),
             low,
             low,
         ),
-        in_specs=[VM] * 5 + [ANY],
+        in_specs=[VM] * 7,
         out_specs=(ANY, ANY, ANY, ANY, VM, ANY, VM, VM),
         scratch_shapes=[
+            pltpu.VMEM((8, 128), F32),
+            pltpu.VMEM(pack, BF16),
             pltpu.VMEM((rows, width), BF16),
             pltpu.VMEM((8, length, 8, 128), F32),
             pltpu.VMEM(wm, BF16),
@@ -775,17 +962,18 @@
             pltpu.VMEM(wd, BF16),
             DMA((5,)), DMA((7,)), DMA((7,)), DMA((2, 7)), DMA((2, 7)),
             DMA((2, length)), DMA((2, length)), DMA((7,)), DMA((7,)), DMA, DMA,
-            DMA((13,)), DMA((13,)), DMA((2, length)), DMA((2, length)),
+            DMA((14,)), DMA((14,)), DMA((2, length)), DMA((2, length)),
         ],
         compiler_params=params(collective_id, 40 * 2**20),
         cost_estimate=pl.CostEstimate(flops=0, bytes_accessed=300 * 2**20, transcendentals=0),
-    )(inputs, above, mixer, mlp, gn, gp)
+    )(inputs, above, mixer, mlp, gains, gate, chan)
 
 
 def last_kernel(
-    length, share, heads_columns, wm, total, inputs, back, gains, gain_two, gp, sq,
-    gw, gm, gv, pw, pm, pv,
-    wm_o, grad_o, gm_o, gv_o, gw_o, pm_o, pv_o, pw_o, norm_o, factor_o,
+    length, wm, total, inputs, back, gains, gain_two, gp, sq,
+    gains_w, gains_m, gains_v, gate_w, gate_m, gate_v, chan_w, chan_m, chan_v,
+    wm_o, grad_o, gains_mo, gains_vo, gains_wo, gate_mo, gate_vo, gate_wo, chan_mo, chan_vo, chan_wo,
+    norm_o, factor_o,
     gain, row_sums, gn, gn_in, gn_mid, gn_got, gp_got, gp_sum, gp_fin, sq_plane, sq_line,
     loc, ss, rs, gs, gr, ls, lr, move_s, move_r,
 ):
@@ -868,6 +1056,7 @@
     sums = gn_mid[0]
     for k in range(length - 1):
         sums = sums + gn_got[k]
+    share = gains_w.shape[1]
     lane = lax.broadcasted_iota(jnp.int32, (8, 128), 1)
     mine = jnp.logical_and(lane >= x * share, lane < (x + 1) * share)
     gain_sum = jnp.where(mine, sums, 0.0)
@@ -896,32 +1085,39 @@
     factor = clip_limit / jnp.maximum(norm, clip_limit)
     norm_o[...] = norm
     factor_o[...] = factor
-    gm_o[...], gv_o[...], gw_o[...] = adam_step(
-        gw[...], gain_sum, gm[...], gv[...], factor, rate_gains, 0.0
-    )
-    column = lax.broadcasted_iota(jnp.int32, gate_sum.shape, 1)
-    matrix = column < heads_columns
-    pm_o[...], pv_o[...], pw_o[...] = adam_step(
-        pw[...], gate_sum, pm[...], pv[...], factor[0:1, 0:1],
-        jnp.where(matrix, rate_matrix, rate_channel), jnp.where(matrix, decay_matrix, 0.0),
+    gain_own = jnp.where(x == 0, gain_sum[:2, :share], gain_sum[:2, share : 2 * share])
+    one = factor[0:1, 0:1]
+    gains_mo[...], gains_vo[...], gains_wo[...] = adam_step(
+        gains_w[...], gain_own, gains_m[...], gains_v[...], one, rate_gains, 0.0
+    )
+    gate_rows, columns = gate_w.shape
+    gate_mo[...], gate_vo[...], gate_wo[...] = adam_step(
+        gate_w[...], gate_sum[:gate_rows, :columns], gate_m[...], gate_v[...], one, rate_matrix, decay_matrix
+    )
+    channels = lax.dot_general(
+        unit(8).astype(F32), gate_sum[:gate_rows, columns : columns + 8], (((1,), (1,)), ((), ())),
+        precision=lax.Precision.HIGHEST, preferred_element_type=F32,
+    )
+    chan_mo[...], chan_vo[...], chan_wo[...] = adam_step(
+        chan_w[...], channels, chan_m[...], chan_v[...], one, rate_channel, 0.0
     )
     for copy in copies:
         copy.wait()
     own.wait()
 
 
-def last(wm, total, inputs, back, gains, gain_two, gp, sq, gain_state, gate_state, share, columns, length, collective_id):
+def last(wm, total, inputs, back, gains, gain_two, gp, sq, small, length, collective_id):
     rows, width = inputs.shape
-    tile, pack = TILE, jax.ShapeDtypeStruct(gp.shape[1:], F32)
+    states = [jax.ShapeDtypeStruct(v.shape, F32) for v in small]
     return pl.pallas_call(
-        functools.partial(last_kernel, length, share, columns),
+        functools.partial(last_kernel, length),
         out_shape=(
             jax.ShapeDtypeStruct(wm.shape, wm.dtype),
             jax.ShapeDtypeStruct((rows, width), F32),
-            tile, tile, tile, pack, pack, pack, tile, tile,
+            *states, TILE, TILE,
         ),
-        in_specs=[ANY] + [VM] * 13,
-        out_specs=(ANY,) + (VM,) * 9,
+        in_specs=[ANY] + [VM] * 16,
+        out_specs=(ANY,) + (VM,) * 12,
         scratch_shapes=[
             pltpu.VMEM((8, width), F32),
             pltpu.VMEM((8, width), F32),
@@ -938,7 +1134,7 @@
             DMA((3, length)), DMA((3, length)), DMA, DMA,
         ],
         compiler_params=params(collective_id, 32 * 2**20),
-    )(wm, total, inputs, back, gains, gain_two, gp, sq, *gain_state, *gate_state)
+    )(wm, total, inputs, back, gains, gain_two, gp, sq, *small)
 
 
 def minus_expm1(v):
@@ -965,7 +1161,15 @@
 def forward_kernel(
     length, proj, gate, chan, above, w_in, mixed, decay_o, width_o, recur_o, enter_o, conv_o, xe, se, ends_o, above_o, w,
     pre, loc_h, ends, carry, hs, hr, es, er, gather_l, gather_s, gather_r, hop_s, hop_r,
+    keep_s, *kept,
 ):
+    keeps = [
+        pltpu.make_async_copy(src, dst, keep_s.at[n])
+        for n, (src, dst) in enumerate(
+            zip(kept, (decay_o, width_o, recur_o, enter_o, conv_o, xe, se))
+        )
+    ]
+    decay_o, width_o, recur_o, enter_o, conv_o, xe, se = kept
     y, c, z, x = place()
     line = line_peers(length)
     greet(line + gather_peers())
@@ -1018,11 +1222,12 @@
 
     half = seqs * chunks // 2
     pl.loop(0, half)(coefficients)
-    gather.middle()
     hops.arrive(1)
     if length > 2:
         hops.start(2)
     pl.loop(half, seqs * chunks)(coefficients)
+    for copy in keeps[:-1]:
+        copy.start()
     row = lax.broadcasted_iota(jnp.int32, (8, rc), 0)
 
     def tile(i, held):
@@ -1053,6 +1258,7 @@
     if length > 3:
         hops.arrive(2)
         hops.start(3)
+    gather.middle()
     carry[...] = jnp.zeros_like(carry)
     for k in range(length):
         carry[...] = jnp.where(k < z, ends[k, 0] * carry[...] + ends[k, 1], carry[...])
@@ -1070,12 +1276,15 @@
         gelu, _ = gelu_parts(proj[b, at, :rc])
         mixed[b, at] = (state * gelu).astype(BF16)
 
+    keeps[-1].start()
     gather.end()
     for hop in range(min(3, length - 1), length):
         hops.arrive(hop)
         if hop + 1 < length:
             hops.start(hop + 1)
     hops.finish()
+    for copy in keeps:
+        copy.wait()
 
 
 def recur_forward(proj, gate, chan, above, w, length, collective_id):
@@ -1092,14 +1301,16 @@
             jax.ShapeDtypeStruct(w.shape, w.dtype),
         ),
         in_specs=[VM, VM, VM, ANY, ANY],
-        out_specs=(VM,) * 9 + (ANY, ANY),
+        out_specs=(VM,) + (ANY,) * 7 + (VM, ANY, ANY),
         scratch_shapes=[
             pltpu.VMEM((seqs, span, rc), F32),
             pltpu.VMEM((seqs, span, rc), F32),
             pltpu.VMEM((length, 2, seqs, 8, rc), F32),
             pltpu.VMEM((seqs, 8, rc), F32),
             DMA, DMA, DMA((length,)), DMA((length,)),
-            DMA, DMA((13,)), DMA((13,)), DMA((2, length)), DMA((2, length)),
+            DMA, DMA((14,)), DMA((14,)), DMA((2, length)), DMA((2, length)),
+            DMA((7,)),
+            *[pltpu.VMEM(v.shape, v.dtype) for v in (full, full, full, full, low, longer, longer)],
         ],
         input_output_aliases={4: 10},
         compiler_params=params(collective_id, 56 * 2**20),
@@ -1110,17 +1321,32 @@
 
 
 def backward_kernel(
-    length, cuts, dmix, gate, chan, decay, width, recur, enter, conv, xe, se, ends_f, proj, *refs
+    length, cuts, dmix, gate, chan, decay, width, recur, enter, conv, xe, se, ends_f, proj, block, *refs
 ):
-    terms, refs = refs[: len(cuts)], refs[len(cuts) :]
-    dproj, dgate, gchan, sums, squares, suffix, grad, de, ends, carry, hs, hr, es, er, *line_refs = refs
+    parts = 1 + max(cut[0] for cut in cuts)
+    terms, refs = refs[:parts], refs[parts:]
+    dproj, dgate, gchan, sums, squares, block_o, *refs = refs
+    suffix, grad, de, ends, carry, hs, hr, es, er, keep_s, move_l, move_s, move_r, *refs = refs
+    kept, line_refs = refs[:8], refs[8:]
+    loads = [
+        pltpu.make_async_copy(src, dst, keep_s.at[n])
+        for n, (src, dst) in enumerate(
+            zip((dmix, proj.at[:, :, pl.ds(0, decay.shape[2])], se, decay, width, recur, enter, conv, xe), (de.at[:, pl.ds(0, decay.shape[1])], *kept))
+        )
+    ]
+    proj, se, decay, width, recur, enter, conv, xe = kept
     y, c, z, x = place()
     line = line_peers(length)
-    greet(line)
-    scatter = LineScatter([(ref, *cut) for ref, cut in zip(terms, cuts)], length, *line_refs)
+    greet(line + plane_peers())
+    scatter = Lines(terms, cuts, length, line_refs)
     scatter.begin()
+    for copy in loads:
+        copy.start()
+    moves, own = exchange_steps(block, block_o, move_l, move_s, move_r)
     seqs, span, rc = decay.shape
     chunks = span // CHUNK
+    for copy in loads[:3]:
+        copy.wait()
 
     @pl.loop(0, seqs * chunks)
     def _(i):
@@ -1129,11 +1355,12 @@
         at = pl.ds(r, CHUNK)
         branch = proj[b, at]
         gelu, inner = gelu_parts(branch)
-        above = dmix[b, at]
+        above = de[b, at]
         state = se[b, pl.ds(r + 8, CHUNK)]
         grad[b, at] = above * gelu
         dproj[b, at, :rc] = (above * state * gelu_slope(branch, inner)).astype(BF16)
 
+    loads[3].wait()
     row = lax.broadcasted_iota(jnp.int32, (8, rc), 0)
 
     def tile(i, held):
@@ -1159,10 +1386,13 @@
     for b in range(seqs):
         ends[z, 0, b] = ends_f[b]
         ends[z, 1, b] = jnp.broadcast_to(final[b][1] * final[b][2], (8, rc))
-    moves = [remote(ends.at[z], ends.at[z], es.at[k], er.at[k], line[k]) for k in range(length - 1)]
-    for copy in moves:
+    tails = [remote(ends.at[z], ends.at[z], es.at[k], er.at[k], line[k]) for k in range(length - 1)]
+    for copy in tails:
         copy.wait()
     scatter.start()
+    scatter.start()
+    for copy in loads[4:]:
+        copy.wait()
     carry[...] = jnp.zeros_like(carry)
     for k in reversed(range(length)):
         carry[...] = jnp.where(k > z, ends[k, 0] * carry[...] + ends[k, 1], carry[...])
@@ -1198,6 +1428,7 @@
     halo = remote(de.at[:, pl.ds(0, 8)], de.at[:, pl.ds(span, 8)], hs, hr, behind)
     halo.wait()
     scatter.start()
+    scatter.start()
 
     @pl.when(z == length - 1)
     def _():
@@ -1219,22 +1450,25 @@
         dproj[b, at, rc:] = total.astype(BF16)
 
     scatter.end(sums, squares)
-
-
-def recur_backward(dmix, gate, chan, kept, proj, terms, cuts, length, collective_id):
+    for copy in moves:
+        copy.wait()
+    own.wait()
+
+
+def recur_backward(dmix, gate, chan, kept, proj, block, terms, cuts, length, collective_id):
     decay, width, recur, enter, conv, xe, se, ends = kept
     seqs, span, rc = decay.shape
     wide = jax.ShapeDtypeStruct((seqs, span, 2 * rc), BF16)
-    line_rows, columns = terms[0].shape[1], sum(cut[1] for cut in cuts)
+    line_rows, columns = terms[0].shape[1], sum(cut[2] for cut in cuts)
     return pl.pallas_call(
         functools.partial(backward_kernel, length, cuts),
-        grid=(1,),
         out_shape=(
             wide, wide, jax.ShapeDtypeStruct((8, 8, rc), F32),
             jax.ShapeDtypeStruct((line_rows, columns), BF16), TILE,
+            jax.ShapeDtypeStruct(block.shape, BF16),
         ),
-        in_specs=[VM] * 11 + [pl.BlockSpec((seqs, span, rc), lambda i: (0, 0, 0))] + [ANY] * len(terms),
-        out_specs=(VM,) * 5,
+        in_specs=[ANY, VM, VM] + [ANY] * 7 + [VM] + [ANY] * (2 + len(terms)),
+        out_specs=(VM,) * 5 + (ANY,),
         scratch_shapes=[
             pltpu.VMEM((seqs, span, rc), F32),
             pltpu.VMEM((seqs, span, rc), F32),
@@ -1242,13 +1476,21 @@
             pltpu.VMEM((length, 2, seqs, 8, rc), F32),
             pltpu.VMEM((seqs, 8, rc), F32),
             DMA, DMA, DMA((length,)), DMA((length,)),
+            DMA((9,)), DMA, DMA((7,)), DMA((7,)),
+            *[
+                pltpu.VMEM(shape, dtype)
+                for shape, dtype in (
+                    (decay.shape, F32), (se.shape, F32), (decay.shape, F32), (decay.shape, F32),
+                    (decay.shape, F32), (decay.shape, F32), (decay.shape, BF16), (xe.shape, F32),
+                )
+            ],
         ]
-        + line_scratch(length, line_rows, columns, len(cuts)),
+        + lines_scratch(length, line_rows, cuts),
         compiler_params=params(collective_id, 62 * 2**20),
         cost_estimate=pl.CostEstimate(
             flops=2 * seqs * span * rc * rc * 2, bytes_accessed=120 * 2**20, transcendentals=0
         ),
-    )(dmix, gate, chan, decay, width, recur, enter, conv, xe, se, ends, proj, *terms)
+    )(dmix, gate, chan, decay, width, recur, enter, conv, xe, se, ends, proj, block, *terms)
 
 
 def contract_last(left, right):
@@ -1261,6 +1503,72 @@
     return lax.dot_general(
         left, right, (((0,), (0,)), ((), ())), preferred_element_type=F32
     )
+
+
+def resident(shape):
+    return pl.BlockSpec(shape, lambda i: (0, 0), pipeline_mode=pl.Buffered(1))
+
+
+def feed_kernel(cut, x, above, gate_up, down, hid, dgate, dup, out, back):
+    f = hid.shape[1]
+    for first_column in range(0, f, cut):
+        at = slice(first_column, first_column + cut)
+        gg = jnp.dot(x[...], gate_up[:, at], preferred_element_type=F32)
+        uu = jnp.dot(x[...], gate_up[:, f + first_column : f + first_column + cut], preferred_element_type=F32)
+        dhid = jnp.dot(above[...], down[:, at], preferred_element_type=F32)
+        gelu, inner = gelu_parts(gg)
+        hid[:, at] = (gelu * uu).astype(BF16)
+        dgate[:, at] = (dhid * uu * gelu_slope(gg, inner)).astype(BF16)
+        dup[:, at] = (dhid * gelu).astype(BF16)
+    for first_column in range(0, x.shape[1], 512):
+        at = slice(first_column, first_column + 512)
+        out[:, at] = contract_last(hid[...], down[at]).astype(BF16)
+        both = contract_last(dgate[...], gate_up[at, :f]) + contract_last(dup[...], gate_up[at, f:])
+        back[:, at] = both.astype(BF16)
+
+
+def feed_forward_back(x, above, gate_up, down):
+    tokens, model = x.shape
+    f = down.shape[1]
+    rows = 256
+
+    def block(width):
+        return pl.BlockSpec((rows, width), lambda i: (i, 0))
+
+    return pl.pallas_call(
+        functools.partial(feed_kernel, 256),
+        grid=(tokens // rows,),
+        out_shape=tuple(jax.ShapeDtypeStruct((tokens, n), BF16) for n in (f, f, f, model, model)),
+        in_specs=[block(model), block(model), resident(gate_up.shape), resident(down.shape)],
+        out_specs=tuple(block(n) for n in (f, f, f, model, model)),
+        compiler_params=pltpu.CompilerParams(vmem_limit_bytes=48 * 2**20),
+        cost_estimate=pl.CostEstimate(
+            flops=12 * tokens * model * f, bytes_accessed=40 * 2**20, transcendentals=0
+        ),
+    )(x, above, gate_up, down)
+
+
+def feed_grads_kernel(x, above, hid, dgate, dup, gate_o, up_o, down_o):
+    gate_o[...] = contract_first(x[...], dgate[...]).astype(BF16)
+    up_o[...] = contract_first(x[...], dup[...]).astype(BF16)
+    down_o[...] = contract_first(above[...], hid[...]).astype(BF16)
+
+
+def feed_grads(x, above, hid, dgate, dup):
+    tokens, model = x.shape
+    f = hid.shape[1]
+    columns = pl.BlockSpec((tokens, 256), lambda i: (0, i))
+    return pl.pallas_call(
+        feed_grads_kernel,
+        grid=(model // 256,),
+        out_shape=(jax.ShapeDtypeStruct((model, f), BF16),) * 3,
+        in_specs=[columns, columns] + [resident(hid.shape)] * 3,
+        out_specs=(pl.BlockSpec((256, f), lambda i: (i, 0)),) * 3,
+        compiler_params=pltpu.CompilerParams(vmem_limit_bytes=48 * 2**20),
+        cost_estimate=pl.CostEstimate(
+            flops=6 * tokens * model * f, bytes_accessed=40 * 2**20, transcendentals=0
+        ),
+    )(x, above, hid, dgate, dup)
 
 
 def adam_step(weight, grad, first, second, factor, rate, decay_rate):
@@ -1275,69 +1583,38 @@
     return (first_new, second_new, weight_new)
 
 
-def adam_kernel(rate, decay_rate, factor, w, g, m, v, m_o, v_o, w_o):
+def adam_kernel(rate, decay_rate, sources, factor, w, m, v, *refs):
+    grads, (m_o, v_o, w_o) = refs[: len(sources)], refs[len(sources) :]
+    parts = []
+    for ref, pieces in zip(grads, sources):
+        for first, columns, at, stride in pieces:
+            for t in range(8):
+                parts.append((at + t * stride, ref[t, :, first : first + columns].astype(F32)))
+    parts.sort(key=lambda part: part[0])
+    grad = jnp.concatenate([part for _, part in parts], axis=1)
     first_new, second_new, weight_new = adam_step(
-        w[...], g[0].astype(F32), m[...], v[...], factor[0:1, 0:1], rate, decay_rate
+        w[...], grad, m[...], v[...], factor[0:1, 0:1], rate, decay_rate
     )
     m_o[...] = first_new
     v_o[...] = second_new
     w_o[...] = weight_new
 
 
-def adam_blocks(weight, grad, first, second, factor, rate, decay_rate):
-    rows, part = grad.shape[1], grad.shape[2] // 3
-    block = pl.BlockSpec((rows, part), lambda t, j: (0, j * 8 + t))
+def adam_rows(weight, grads, sources, first, second, factor, rate, decay_rate):
+    rows, width = weight.shape
+    step = min(rows, 16)
+    block = pl.BlockSpec((step, width), lambda i: (i, 0))
     shape = jax.ShapeDtypeStruct(weight.shape, F32)
     return pl.pallas_call(
-        functools.partial(adam_kernel, rate, decay_rate),
-        grid=(8, 3),
+        functools.partial(adam_kernel, rate, decay_rate, sources),
+        grid=(rows // step,),
         out_shape=(shape,) * 3,
-        in_specs=[
-            pl.BlockSpec((8, 128), lambda t, j: (0, 0)),
-            block,
-            pl.BlockSpec((1, rows, part), lambda t, j: (t, 0, j)),
-            block,
-            block,
-        ],
+        in_specs=[pl.BlockSpec((8, 128), lambda i: (0, 0)), block, block, block]
+        + [pl.BlockSpec((8, step, g.shape[2]), lambda i: (0, i, 0)) for g in grads],
         out_specs=(block,) * 3,
+        compiler_params=pltpu.CompilerParams(vmem_limit_bytes=48 * 2**20),
         cost_estimate=pl.CostEstimate(flops=0, bytes_accessed=7 * 4 * weight.size, transcendentals=0),
-    )(factor, weight, grad, first, second)
-
-
-def adam_pairs_kernel(rate, decay_rate, factor, w, g, m, v, m_o, v_o, w_o):
-    part = g.shape[2] // 3
-    for j in range(3):
-
-        @pl.when(pl.program_id(1) == j)
-        def _():
-            at = slice(j * part, (j + 1) * part)
-            grad = jnp.concatenate([g[0, :, at].astype(F32), g[1, :, at].astype(F32)], axis=1)
-            first_new, second_new, weight_new = adam_step(
-                w[...], grad, m[...], v[...], factor[0:1, 0:1], rate, decay_rate
-            )
-            m_o[...] = first_new
-            v_o[...] = second_new
-            w_o[...] = weight_new
-
-
-def adam_pairs(weight, grad, first, second, factor, rate, decay_rate):
-    rows, part = grad.shape[1], grad.shape[2] // 3
-    block = pl.BlockSpec((rows, 2 * part), lambda t, j: (0, j * 4 + t))
-    shape = jax.ShapeDtypeStruct(weight.shape, F32)
-    return pl.pallas_call(
-        functools.partial(adam_pairs_kernel, rate, decay_rate),
-        grid=(4, 3),
-        out_shape=(shape,) * 3,
-        in_specs=[
-            pl.BlockSpec((8, 128), lambda t, j: (0, 0)),
-            block,
-            pl.BlockSpec((2, rows, 3 * part), lambda t, j: (t, 0, 0)),
-            block,
-            block,
-        ],
-        out_specs=(block,) * 3,
-        cost_estimate=pl.CostEstimate(flops=0, bytes_accessed=7 * 4 * weight.size, transcendentals=0),
-    )(factor, weight, grad, first, second)
+    )(factor, weight, first, second, *grads)
 
 
 def on_device(
@@ -1389,32 +1666,15 @@
         v = jnp.roll(v.reshape(v.shape[0], length, 4, pair), z, axis=1)
         return v.swapaxes(1, 2).reshape(v.shape[0], model)
 
-    def gain_tile(v):
-        return jnp.where(
-            x == 0,
-            jnp.pad(v, ((0, 6), (0, 128 - share))),
-            jnp.pad(v, ((0, 6), (share, 128 - 2 * share))),
-        )
-
-    def gain_rows(v):
-        return jnp.where(x == 0, v[:2, :share], v[:2, share : 2 * share])
-
-    def gate_pack(rows, channels):
-        pack = jnp.concatenate([rows, channels.T], axis=1)
-        return jnp.pad(pack, ((0, gate_pad - gate_rows), (0, rc - 2 * head - 8)))
-
-    gain_state = [gain_tile(v) for v in (norm_gains, first_gains, second_gains)]
-    gate_state = [
-        gate_pack(*pair_of)
-        for pair_of in ((gate_weight, chan_params), (first_gate, first_chan), (second_gate, second_chan))
-    ]
     normed_one, mixer_full, mlp_gu, mlp_down, gains, gate_in, inputs, above = first(
         turned(block_input[0]),
         turned(out_grad[0]),
         mixer_weight,
         mlp_weight,
-        gain_state[0],
-        gate_state[0].astype(BF16),
+        norm_gains,
+        gate_weight,
+        chan_params,
+        rc,
         length,
         1,
     )
@@ -1449,50 +1709,28 @@
     )
     normed_two = normed_two.reshape(8 * tokens, model)
     mlp_gu = mlp_gu.reshape(model, 2 * f8)
-    mlp_gate, mlp_up = mlp_gu[:, :f8], mlp_gu[:, f8:]
     mlp_down = mlp_down.reshape(model, f8)
-    gg = jnp.dot(normed_two, mlp_gate, preferred_element_type=F32)
-    uu = jnp.dot(normed_two, mlp_up, preferred_element_type=F32)
-    dhid = jnp.dot(grad_out, mlp_down, preferred_element_type=F32)
-    gelu, inner = gelu_parts(gg)
-    hid = (gelu * uu).astype(BF16)
-    dgg = (dhid * uu * gelu_slope(gg, inner)).astype(BF16)
-    duu = (dhid * gelu).astype(BF16)
-    dnormed_two = contract_last(dgg, mlp_gate) + contract_last(duu, mlp_up)
-
-    def terms(v):
-        return v.astype(BF16).reshape(length, 8 * share, f8)
-
-    gate_terms = terms(contract_first(normed_two, dgg))
-    up_terms = terms(contract_first(normed_two, duu))
-    down_terms = terms(contract_first(grad_out, hid))
-    up_cut = f8 // 256 * 128
-    down_cut = f8 // 384 * 128
+    hid, dgg, duu, mlp_part, dnormed_two = feed_forward_back(normed_two, grad_out, mlp_gu, mlp_down)
+    gate_terms, up_terms, down_terms = (
+        v.reshape(length, 8 * share, f8) for v in feed_grads(normed_two, grad_out, hid, dgg, duu)
+    )
+    up_cut, down_cut = f8 // 384 * 256, f8 // 384 * 256
 
     grad_residual, gain_two, dmz, sums_one, squares_one = turn(
-        dnormed_two.astype(BF16), residual, above, gains,
-        (gate_terms, up_terms), ((0, f8), (0, up_cut)), length, 4,
+        dnormed_two, residual, above, gains,
+        (gate_terms, up_terms), ((0, 0, f8), (1, 0, up_cut)), length, 4,
     )
     dmz = dmz.reshape(8 * tokens, model)
-    block_output, sums_two, squares_two = output(
-        contract_last(hid, mlp_down).astype(BF16), residual,
-        (up_terms, down_terms), ((up_cut, f8 - up_cut), (0, down_cut)), length, 5,
-    )
     dmix = jnp.dot(dmz, mixer_last, preferred_element_type=F32).reshape(4, span, rc)
-    dproj, dgate, chan_grad, sums_three, squares_three = recur_backward(
-        dmix, gate, chan, kept, projected, (down_terms,), ((down_cut, f8 - down_cut),), length, 6
+    dproj, dgate, chan_grad, sums_two, squares_two, back_one = recur_backward(
+        dmix, gate, chan, kept, projected, sums_one.reshape(8, share, sums_one.shape[1]),
+        (up_terms, down_terms), ((0, up_cut, f8 - up_cut), (1, 0, down_cut)), length, 6,
     )
     dproj = dproj.reshape(4 * span, 2 * rc)
     dgate = dgate.reshape(4 * span, 2 * rc)
-    proj_grad = contract_first(normed_one, dproj)
-    last_grad = contract_first(dmz, mixed)
-    mixer_terms = jnp.concatenate(
-        [proj_grad[:, :r8], proj_grad[:, rc : rc + r8], last_grad[:, :r8]], axis=1
-    )
-    mixer_terms = mixer_terms.astype(BF16).reshape(length, 8 * share, 3 * r8)
-    dnormed_one, mlp_back, mixer_sums, squares_four = closing(
-        contract_last(dproj, mixer_first).astype(BF16), (sums_one, sums_two, sums_three), mixer_terms,
-        length, 7,
+    dnormed_one, block_output, back_two, rest_sums, squares_three = closing(
+        normed_one, dmz, dproj, mixed, mixer_first, mlp_part, residual,
+        down_terms, (down_cut, f8 - down_cut), sums_two, r8, length, 7,
     )
 
     gate_full_grad = contract_first(kept[4].reshape(4 * span, rc), dgate)
@@ -1510,19 +1748,29 @@
         gate_back, ((0, 0), (0, gate_pad - gate_rows), (0, rc - 2 * head - 8))
     )
     gate_back = jnp.roll(gate_back, -z, axis=0)
-    mixer_back, input_grad, *small, norm, factor = last(
-        mixer_sums.reshape(8, share, 3 * r8), dnormed_one, inputs, grad_residual, gains, gain_two,
-        gate_back, squares_one + squares_two + squares_three + squares_four, gain_state, gate_state,
-        share, 2 * head, length, 8,
-    )
-    gains_up = [gain_rows(v) for v in small[:3]]
-    gate_up = [v[:gate_rows, : 2 * head] for v in small[3:]]
-    chan_up = [v[:gate_rows, 2 * head : 2 * head + 8].T for v in small[3:]]
-    mixer_up = adam_pairs(
-        mixer_weight, mixer_back, first_mixer, second_mixer, factor, rate_matrix, decay_matrix
-    )
-    mlp_up = adam_blocks(
-        mlp_weight, mlp_back, first_mlp, second_mlp, factor, rate_matrix, decay_matrix
+    rest_back, input_grad, *small, norm, factor = last(
+        rest_sums.reshape(8, share, rest_sums.shape[1]), dnormed_one, inputs, grad_residual, gains, gain_two,
+        gate_back, squares_one + squares_two + squares_three,
+        (
+            norm_gains, first_gains, second_gains, gate_weight, first_gate, second_gate,
+            chan_params, first_chan, second_chan,
+        ),
+        length, 8,
+    )
+    gains_up, gate_up, chan_up = small[:3], small[3:6], small[6:]
+    rest = f8 - down_cut
+    mixer_up = adam_rows(
+        mixer_weight, (rest_back,), ([(rest + n * r8, r8, n * lru, r8) for n in range(3)],),
+        first_mixer, second_mixer, factor, rate_matrix, decay_matrix,
+    )
+    mlp_up = adam_rows(
+        mlp_weight, (back_one, back_two, rest_back),
+        (
+            [(0, f8, 0, f8), (f8, up_cut, hidden, f8)],
+            [(0, f8 - up_cut, hidden + up_cut, f8), (f8 - up_cut, down_cut, 2 * hidden, f8)],
+            [(0, rest, 2 * hidden + down_cut, f8)],
+        ),
+        first_mlp, second_mlp, factor, rate_matrix, decay_matrix,
     )
     return (
         turned_back(block_output)[None],

time: 863 us -> 736 us (0.85)
  matrix products: 162 us -> 29.4 us
  Pallas kernels: 643 us -> 666 us
  other arithmetic: 14.7 us -> 4.82 us
    dot_general x6 -> x1, matrix products: 50 us -> 3.93 us  [contract_first(): lax.dot_general(left, right, (((0,), (0,)), ((), ())), preferred_element_...]
    pallas_call x6 -> x7, Pallas kernels: 249 us -> 296 us  [the longest x1 106 us: closing(): pl.pallas_call(functools.partial(closing_kernel, length, cut, part), out_...]
    dot_general x5 -> x1, matrix products: 50.1 us -> 8.38 us  [contract_last(): lax.dot_general(left, right, (((1,), (1,)), ((), ())), preferred_element_...]
    dot_general x3 -> x0, matrix products: 40.7 us -> none  [the longest x1 17.4 us: on_device(): gg = jnp.dot(normed_two, mlp_gate, preferred_element_type=F32)]
    pallas_call x1, Pallas kernels: 113 us -> 98.4 us  [first(): pl.pallas_call(functools.partial(first_kernel, length), out_shape=(jax.Sh...]
    slice x5 -> x0, local copies, waits for them, and re-layouts: 8.98 us -> none  [the longest x2 4.3 us: on_device(): proj_grad[:, :r8]]
    unnamed x100 -> x102, local copies, waits for them, and re-layouts: 24.1 us -> 25.2 us
where the time goes in v4:
time: 736 us; the launch traced here: 731 us
  Pallas kernels  666 us (90%)
  matrix products  29.4 us (4%)
  local copies, waits for them, and re-layouts  29.2 us (4%)
    pallas_call x1, Pallas kernels, middle(): pl.pallas_call(functools.partial(middle_kernel, length), out_shape=(jax.S...  112 us
    pallas_call x1, Pallas kernels, closing(): pl.pallas_call(functools.partial(closing_kernel, length, cut, part), out_...  106 us
    pallas_call x1, Pallas kernels, first(): pl.pallas_call(functools.partial(first_kernel, length), out_shape=(jax.Sh...  98.4 us
    pallas_call x1, Pallas kernels, turn(): pl.pallas_call(functools.partial(turn_kernel, length, cuts), out_shape=(j...  92.7 us
    pallas_call x1, Pallas kernels, recur_backward(): pl.pallas_call(functools.partial(backward_kernel, length, cuts), out_shap...  67.6 us
    pallas_call x1, Pallas kernels, recur_forward(): pl.pallas_call(functools.partial(forward_kernel, length), out_shape=(low,...  67.1 us
    pallas_call x1, Pallas kernels, feed_forward_back(): pl.pallas_call(functools.partial(feed_kernel, 256), grid=(tokens // rows,...  47.4 us
    pallas_call x1, Pallas kernels, last(): pl.pallas_call(functools.partial(last_kernel, length), out_shape=(jax.Sha...  29.8 us

profile of v4, /device:TPU:0, one launch (start us, length us, event | category | flops | bytes accessed | tf_op | source)
XLA Modules:
  0.0 731.0 jit_solution(11937717472638929289)
XLA Ops:
  0.7 1.5 copy-done
  2.2 1.2 copy-done.14
  3.4 1.2 copy-done.15
  4.7 0.9 copy-done.19
  5.6 0.7 copy-done.24
  6.2 0.7 copy-done.28
  6.9 98.4 %shard_map.304 = (bf16[8,256,2048]{2,1,0:T(8,128)(2,1)}, bf16[4,8,64,960]{3,2,1,0:T(8,128)(2,1)S(1)}, bf16[4,8,64,1536]{3,2,1,0:T(8,128)(2,1)}, bf16[4,8,64,768]...) custom-call(bf16[256,2048]{1,0:T(8,128)(2,1)S(1)} %bitcast.55, ...), custom_call_target="tpu_custom_call" | custom-call | bytes 314572800 | tf_op jit(solution)/shard_map/pallas_call | solution.py:941
  105.3 0.0 copy-start.3
  105.3 0.0 copy-start.4
  105.4 0.0 copy-start.41
  105.4 2.1 fusion.28
  107.5 0.7 copy-done.6
  108.2 0.2 slice_select_fusion
  108.4 2.7 copy-done.42
  111.1 8.6 %fusion.2.proj = f32[4,512,768]{2,1,0:T(8,128)} fusion(bf16[4,512,2048]{2,1,0:T(8,128)(2,1)S(1)} %bitcast.71, bf16[2048,320]{1,0:T(8,128)(2,1)S(1)} %get-tuple-element.149, bf16[2048,384]{1,0:T(8,128)(2,1)S(1)} %slice_select_fusion), kind=kOutput, calls=%fused_computation.4 | convolution fusion | flops 6451888128 | bytes 17563648 | tf_op jit(solution)/shard_map/dot_general | solution.py:1702
  119.7 0.1 fusion.30
  119.8 0.1 fusion.21
  119.9 0.9 pad.38.gate
  120.8 0.1 slice.84
  120.9 0.1 copy.46
  121.0 0.7 pad_maximum_fusion.1.chan
  121.7 67.1 %shard_map.305 = (bf16[4,512,384]{2,1,0:T(8,128)(2,1)}, f32[4,512,384]{2,1,0:T(8,128)}, f32[4,512,384]{2,1,0:T(8,128)}, f32[4,512,384]{2,1,0:T(8,128)}, f32[4,51...) custom-call(f32[4,512,768]{2,1,0:T(8,128)} %fusion.2.proj, ...), custom_call_target="tpu_custom_call", output_to_operand_aliasing={{10}: (4, {})} | custom-call | flops 1207959552 | bytes 104857600 | tf_op jit(solution)/shard_map/pallas_call | solution.py:1295
  188.8 8.4 %convolution_convert_fusion = bf16[2048,2048]{1,0:T(8,128)(2,1)} fusion(bf16[2048,384]{1,0:T(8,128)(2,1)} %bitcast.79, bf16[2048,320]{1,0:T(8,128)(2,1)S(1)} %copy-done.34), kind=kOutput, calls=%fused_computation | convolution fusion | flops 3225419776 | bytes 11272192 | tf_op jit(solution)/shard_map/dot_general | solution.py:1497
  197.3 112.1 %shard_map.306 = (f32[256,2048]{1,0:T(8,128)S(1)}, bf16[8,256,2048]{2,1,0:T(8,128)(2,1)}, bf16[4,8,64,1536]{3,2,1,0:T(8,128)(2,1)S(1)}) custom-call(bf16[8,256,2048]{2,1,0:T(8,128)(2,1)} %bitcast.62, bf16[256,2048]{1,0:T(8,128)(2,1)S(1)} %get-tuple-element.89.inputs, f32[8,2048]{1,0:T(8,128)S(1)} %get-tuple-element.90.gains, ...), custom_call_target="tpu_custom_call", output_to_operand_aliasing={{2}: (3, {})} | custom-call | bytes 314572800 | tf_op jit(solution)/shard_map/pallas_call | solution.py:573
  309.3 2.7 copy-done.2
  312.0 47.4 %shard_map.307 = (bf16[2048,768]{1,0:T(8,128)(2,1)S(1)}, bf16[2048,768]{1,0:T(8,128)(2,1)}, bf16[2048,768]{1,0:T(8,128)(2,1)}, bf16[2048,2048]{1,0:T(8,128)(2,1)}, bf16[2048,2048]{1,0:T(8,128)(2,1)}) custom-call(bf16[2048,2048]{1,0:T(8,128)(2,1)} %bitcast.76, bf16[2048,2048]{1,0:T(8,128)(2,1)} %bitcast.74, bf16[2048,1536]{1,0:T(8,128)(2,1)} %bitcast.48, ...), custom_call_target="tpu_custom_call" | custom-call | flops 38654705664 | bytes 41943040 | tf_op jit(solution)/shard_map/pallas_call | solution.py:1538
  359.4 0.0 copy-start.32
  359.4 1.7 copy-done.32
  361.1 26.6 %shard_map.308 = (bf16[2048,768]{1,0:T(8,128)(2,1)S(1)}, bf16[2048,768]{1,0:T(8,128)(2,1)}, bf16[2048,768]{1,0:T(8,128)(2,1)}) custom-call(bf16[2048,2048]{1,0:T(8,128)(2,1)} %bitcast.77, bf16[2048,2048]{1,0:T(8,128)(2,1)} %bitcast.75, bf16[2048,768]{1,0:T(8,128)(2,1)} %copy-done.32, bf16[2048,768]{1,0:T(8,128)(2,1)} %get-tuple-element.99.dgate, ...), custom_call_target="tpu_custom_call" | custom-call | flops 19327352832 | bytes 41943040 | tf_op jit(solution)/shard_map/pallas_call | solution.py:1561
  387.7 1.7 copy-done.7
  389.3 92.7 %shard_map.309 = (f32[256,2048]{1,0:T(8,128)}, f32[8,2048]{1,0:T(8,128)}, bf16[8,256,2048]{2,1,0:T(8,128)(2,1)}, bf16[512,1280]{1,0:T(8,128)(2,1)}, f32[8,128]{1,0:T(8,128)}) custom-call(bf16[8,256,2048]{2,1,0:T(8,128)(2,1)} %bitcast.61, f32[256,2048]{1,0:T(8,128)} %copy-done.8, bf16[256,2048]{1,0:T(8,128)(2,1)} %copy-done.3, f32[8,2048]{1,0:T(8,128)} %copy-done.17, ...), custom_call_target="tpu_custom_call" | custom-call | bytes 314572800 | tf_op jit(solution)/shard_map/pallas_call | solution.py:630
  482.0 8.6 %fusion.4.dmix = f32[4,512,384]{2,1,0:T(8,128)} fusion(bf16[4,512,2048]{2,1,0:T(8,128)(2,1)} %bitcast.72, bf16[2048,320]{1,0:T(8,128)(2,1)S(1)} %copy-done.34), kind=kOutput, calls=%fused_computation.7 | convolution fusion | flops 3221225472 | bytes 12845056 | tf_op jit(solution)/shard_map/dot_general | solution.py:1724
  490.6 67.6 %shard_map.310 = (bf16[4,512,768]{2,1,0:T(8,128)(2,1)}, bf16[4,512,768]{2,1,0:T(8,128)(2,1)}, f32[8,8,384]{2,1,0:T(8,128)}, bf16[512,768]{1,0:T(8,128)(2,1)}, f3...) custom-call(f32[4,512,384]{2,1,0:T(8,128)} %fusion.4.dmix, bf16[384,768]{1,0:T(8,128)(2,1)} %pad.38.gate, ...), custom_call_target="tpu_custom_call" | custom-call | flops 1207959552 | bytes 125829120 | tf_op jit(solution)/shard_map/pallas_call | solution.py:1463
  558.2 3.4 fusion.1.first_w
  561.6 106.0 %shard_map.311 = (f32[256,2048]{1,0:T(8,128)}, bf16[256,2048]{1,0:T(8,128)(2,1)}, bf16[8,64,768]{2,1,0:T(8,128)(2,1)}, bf16[512,1216]{1,0:T(8,128)(2,1)}, f32[8,128]{1,0:T(8,128)}) custom-call(bf16[2048,2048]{1,0:T(8,128)(2,1)} %bitcast.70, bf16[2048,2048]{1,0:T(8,128)(2,1)} %bitcast.73, bf16[2048,768]{1,0:T(8,128)(2,1)} %bitcast.78, ...), custom_call_target="tpu_custom_call" | custom-call | flops 16106127360 | bytes 367001600 | tf_op jit(solution)/shard_map/pallas_call | solution.py:769
  667.7 0.1 copy.44
  667.9 0.0 copy-start.22
  667.9 3.9 convolution_bitcast_fusion
  671.8 0.0 copy-start.5
  671.9 0.0 copy-start.18
  671.9 0.0 copy-start.26
  671.9 0.0 copy-start.27
  672.0 0.0 copy-start.31
  672.0 0.2 fusion.29
  672.1 0.2 pad_maximum_fusion
  672.4 0.1 fusion.23.gp
  672.5 0.5 copy-done.5
  673.1 0.7 copy-done.9
  673.8 0.3 copy-done.13
  674.2 29.8 %shard_map.312 = (bf16[8,64,1216]{2,1,0:T(8,128)(2,1)S(1)}, f32[256,2048]{1,0:T(8,128)S(1)}, f32[2,64]{1,0:T(2,128)S(1)}, f32[2,64]{1,0:T(2,128)S(1)}, f32[2,64]...) custom-call(bf16[8,64,1216]{2,1,0:T(8,128)(2,1)S(1)} %bitcast.54, ...), custom_call_target="tpu_custom_call" | custom-call | tf_op jit(solution)/shard_map/pallas_call | solution.py:1112
  704.0 0.5 slice.77
  704.5 5.4 shard_map.313
  709.9 13.0 %shard_map.314 = (f32[64,18432]{1,0:T(8,128)}, f32[64,18432]{1,0:T(8,128)}, f32[64,18432]{1,0:T(8,128)}) custom-call(f32[8,128]{1,0:T(8,128)S(1)} %get-tuple-element.132.factor, f32[64,18432]{1,0:T(8,128)} %w.3, f32[64,18432]{1,0:T(8,128)} %m.3, f32[64,18432]{1,0:T(8,128)} %v.3, bf16[8,64,1280]{2,1,0:T(8,128)(2,1)S(1)} %copy-done.12, ...), custom_call_target="tpu_custom_call" | custom-call | bytes 33030144 | tf_op jit(solution)/shard_map/pallas_call | solution.py:1608
  722.8 1.0 copy.60
  723.8 1.3 copy.61
  725.1 0.6 copy.62
  725.7 0.6 copy.63
  726.2 0.6 copy.64
  726.8 0.6 copy.65
  727.5 0.6 copy.66
  728.1 0.6 copy.67
  728.8 0.6 copy.68
  729.3 0.6 copy.69
  729.9 0.6 copy.70
  (74 shorter events, 0.3 us)
Async XLA Ops:
  0.7 1.5 copy-start
  2.2 1.2 copy-start.14
  3.4 1.2 copy-start.15
  4.7 0.9 copy-start.19
  5.6 0.7 copy-start.24
  6.2 0.7 copy-start.28
  105.3 2.1 copy-start.3
  105.3 2.9 copy-start.6
  105.3 91.9 %copy-start.4 = (bf16[256,2048]{1,0:T(8,128)(2,1)}, bf16[256,2048]{1,0:T(8,128)(2,1)S(1)}, u32[]{:S(2)}) copy-start(bf16[256,2048]{1,0:T(8,128)(2,1)S(1)} %get-tuple-element.89.inputs) | copy-start | bytes 3145732
  105.3 91.9 %copy-start.17 = (f32[8,2048]{1,0:T(8,128)}, f32[8,2048]{1,0:T(8,128)S(1)}, u32[]{:S(2)}) copy-start(f32[8,2048]{1,0:T(8,128)S(1)} %get-tuple-element.90.gains) | copy-start | bytes 196612
  105.4 2.8 copy-start.41
  105.4 5.8 copy-start.42
  111.1 8.6 %copy-start.33 = (bf16[2048,384]{1,0:T(8,128)(2,1)}, bf16[2048,384]{1,0:T(8,128)(2,1)S(1)}, u32[]{:S(2)}) copy-start(bf16[2048,384]{1,0:T(8,128)(2,1)S(1)} %slice_select_fusion) | copy-start | bytes 4718596
  111.1 9.9 %copy-start.40 = (f32[8,64]{1,0:T(8,128)S(1)}, f32[8,64]{1,0:T(8,128)}, u32[]{:S(2)}) copy-start(f32[8,64]{1,0:T(8,128)} %constant.47.clone.1) | copy-start | bytes 6148
  121.7 67.1 %copy-start.34 = (bf16[2048,320]{1,0:T(8,128)(2,1)S(1)}, bf16[2048,320]{1,0:T(8,128)(2,1)}, u32[]{:S(2)}) copy-start(bf16[2048,320]{1,0:T(8,128)(2,1)} %get-tuple-element.148) | copy-start | bytes 3932164
  188.8 8.4 %slice-start = ((s8[6291456]{0:T(1024)(128)(4,1)}), s8[4194304]{0:T(1024)(128)(4,1)S(1)}, s32[]{:S(2)}) async-start(s8[6291456]{0:T(1024)(128)(4,1)} %bitcast.46), calls=%async_computation | async-start | bytes 8388608
  188.8 8.4 %slice-start.1 = ((s8[6291456]{0:T(1024)(128)(4,1)}), s8[2097152]{0:T(1024)(128)(4,1)S(1)}, s32[]{:S(2)}) async-start(s8[6291456]{0:T(1024)(128)(4,1)} %bitcast.46), calls=%async_computation.1 | async-start | bytes 4194304
  309.3 2.7 copy-start.2
  312.0 47.4 %copy-start.8 = (f32[256,2048]{1,0:T(8,128)}, f32[256,2048]{1,0:T(8,128)S(1)}, u32[]{:S(2)}) copy-start(f32[256,2048]{1,0:T(8,128)S(1)} %get-tuple-element.97.residual) | copy-start | bytes 6291460
  359.4 1.7 copy-start.32
  387.7 1.7 copy-start.7
  561.6 106.0 %copy-start.36 = (f32[8,8,384]{2,1,0:T(8,128)S(1)}, f32[8,8,384]{2,1,0:T(8,128)}, u32[]{:S(2)}) copy-start(f32[8,8,384]{2,1,0:T(8,128)} %get-tuple-element.123) | copy-start | bytes 294916
  667.8 4.6 copy-start.37
  667.8 4.6 copy-start.38
  667.8 4.6 copy-start.39
  667.9 4.7 copy-start.10
  667.9 4.7 copy-start.20
  667.9 4.7 copy-start.21
  667.9 4.6 copy-start.22
  671.8 1.2 copy-start.5
  671.8 1.9 copy-start.9
  671.9 2.3 copy-start.13
  671.9 2.2 copy-start.18
  671.9 2.2 copy-start.23
  671.9 2.2 copy-start.25
  671.9 2.2 copy-start.26
  671.9 2.2 copy-start.27
  671.9 2.2 copy-start.29
  671.9 2.2 copy-start.30
  672.0 2.2 copy-start.31
  674.2 30.3 %copy-start.1 = (f32[64,7680]{1,0:T(8,128)S(1)}, f32[64,7680]{1,0:T(8,128)}, u32[]{:S(2)}) copy-start(f32[64,7680]{1,0:T(8,128)} %w.2) | copy-start | bytes 5898244
  674.2 30.3 %copy-start.11 = (f32[64,7680]{1,0:T(8,128)S(1)}, f32[64,7680]{1,0:T(8,128)}, u32[]{:S(2)}) copy-start(f32[64,7680]{1,0:T(8,128)} %m.2) | copy-start | bytes 5898244
  704.5 5.4 copy-start.12
  704.5 5.4 copy-start.16
  709.9 13.0 %copy-start.35 = (bf16[256,2048]{1,0:T(8,128)(2,1)S(1)}, bf16[256,2048]{1,0:T(8,128)(2,1)}, u32[]{:S(2)}) copy-start(bf16[256,2048]{1,0:T(8,128)(2,1)} %get-tuple-element.117) | copy-start | bytes 3145732

commit v5 on v4

--- a/solution.py
+++ b/solution.py
@@ -62,9 +62,12 @@
     return copy
 
 
-def params(collective_id, vmem=None):
+VMEM_BYTES = 63 * 2**20
+
+
+def params(collective_id):
     return pltpu.CompilerParams(
-        collective_id=collective_id, has_side_effects=True, vmem_limit_bytes=vmem
+        collective_id=collective_id, has_side_effects=True, vmem_limit_bytes=VMEM_BYTES
     )
 
 
@@ -283,6 +286,16 @@
     def start(self, hop):
         self.sends(hop, lambda copy: copy.start())
 
+    def start_piece(self, n):
+        for way, last, dst in ((0, self.z + 1 < self.length, self.length - 1), (1, self.z >= 1, 1)):
+
+            @pl.when(last)
+            def _():
+                remote(
+                    self.buf.at[0, n], self.buf.at[dst, n], self.ss.at[way, 0], self.rs.at[way, 0],
+                    (self.up, self.down)[way],
+                )
+
     def arrive(self, hop):
         z, length = self.z, self.length
 
@@ -294,8 +307,8 @@
         def _():
             self.copy(hop, False).wait_recv()
 
-    def finish(self):
-        for hop in range(1, self.length):
+    def finish(self, first_hop=1, last_hop=None):
+        for hop in range(first_hop, (last_hop or self.length - 1) + 1):
             self.sends(hop, lambda copy: copy.wait_send())
 
 
@@ -396,17 +409,18 @@
 
 
 class HeldLine(LineScatter):
-    def __init__(self, g, up_got, down_got, ss, rs):
+    def __init__(self, g, first_column, up_got, down_got, ss, rs):
         y, c, z, x = place()
         self.length = length = g.shape[0]
-        self.sources, self.g, self.total = (), g, g.at[0]
+        self.columns = pl.ds(first_column, up_got.shape[2])
+        self.sources, self.g, self.total = (), g, g.at[0, :, self.columns]
         self.got, self.ss, self.rs = (up_got, down_got), ss, rs
         self.to = line_neighbours(length)
         self.far = (z, length - 1 - z)
         self.next = 1
 
     def term(self, way, hop):
-        return self.g.at[self.length - hop if way == 0 else hop]
+        return self.g.at[self.length - hop if way == 0 else hop, :, self.columns]
 
 
 def chains_of(cuts):
@@ -532,12 +546,24 @@
     return inverse * (moved - scaled * inner), fold(grad * scaled)
 
 
-def middle_kernel(length, p, inputs, gains, w_in, residual, normed_o, w, *scratch):
-    scatter_refs, (low, loc, gs, gr, hs, hr) = scratch[:SCATTER_REFS], scratch[SCATTER_REFS:]
+def middle_kernel(length, mixed, mixer, inputs, gains, w_in, late_in, residual, normed_o, w, late, *scratch):
+    scatter_refs, (p, low, loc, gs, gr, hs, hr, late_s, late_r) = scratch[:SCATTER_REFS], scratch[SCATTER_REFS:]
     greet(gather_peers() + line_neighbours(length))
     hops = LineGather(w, length, hs, hr)
     hops.start(1)
+    late_hops = LineGather(late, length, late_s, late_r)
+    late_hops.start(1)
     started = [1]
+    part = mixed.shape[1]
+    rows, width = low.shape
+
+    @pl.loop(0, 4)
+    def _(i):
+        mine = mixed[pl.ds(pl.multiple_of(i * 2 * rows, rows), 2 * rows)]
+        for first_column in range(0, width, 512):
+            at = slice(first_column, first_column + 512)
+            both = contract_last(mine, mixer[at, 2 * part :]).astype(BF16)
+            p[pl.ds(2 * i, 2), :, at] = both.reshape(2, rows, 512)
 
     def advance():
         if started[0] < length - 1:
@@ -553,22 +579,26 @@
     half = low.shape[0] // 2
     gather = Gather(low, normed_o, loc, gs, gr)
     for name in scatter_steps(p, residual, *scatter_refs):
+        if name == "late":
+            advance()
         if name == "low half":
             rows_loop(half, body)
             gather.begin_half(0)
         if name == "high half":
             rows_loop(half, body, half)
             gather.begin_half(1)
-            advance()
     gather.middle()
-    gather.end(advance)
+    advance()
+    gather.end()
     while started[0] < length - 1:
         advance()
     hops.arrive(length - 1)
     hops.finish()
-
-
-def middle(p, inputs, gains, w, length, collective_id):
+    late_hops.arrive(1)
+    late_hops.finish(1, 1)
+
+
+def middle(mixed, mixer, inputs, gains, w, late, length, collective_id):
     rows, width = inputs.shape
     return pl.pallas_call(
         functools.partial(middle_kernel, length),
@@ -576,23 +606,25 @@
             jax.ShapeDtypeStruct((rows, width), F32),
             jax.ShapeDtypeStruct((8, rows, width), BF16),
             jax.ShapeDtypeStruct(w.shape, w.dtype),
+            jax.ShapeDtypeStruct(late.shape, late.dtype),
         ),
-        in_specs=[ANY, VM, VM, ANY],
-        out_specs=(VM, ANY, ANY),
+        in_specs=[VM, VM, VM, VM, ANY, ANY],
+        out_specs=(VM, ANY, ANY, ANY),
         scratch_shapes=scatter_scratch(rows // 2, width)
-        + [pltpu.VMEM((rows, width), BF16), DMA, DMA((14,)), DMA((14,)), DMA((2, length)), DMA((2, length))],
-        input_output_aliases={3: 2},
-        compiler_params=params(collective_id, 40 * 2**20),
+        + [pltpu.VMEM((8, rows, width), BF16), pltpu.VMEM((rows, width), BF16), DMA, DMA((14,)), DMA((14,))]
+        + [DMA((2, length))] * 4,
+        input_output_aliases={4: 2, 5: 3},
+        compiler_params=params(collective_id),
         cost_estimate=pl.CostEstimate(flops=0, bytes_accessed=300 * 2**20, transcendentals=0),
-    )(p.reshape(8, rows, width), inputs, gains, w)
-
-
-def turn_kernel(length, cuts, p, residual, above, gains, *refs):
+    )(mixed, mixer, inputs, gains, w, late)
+
+
+def turn_kernel(length, cuts, p, residual, above, gains, mixer, *refs):
     parts = 1 + max(cut[0] for cut in cuts)
     terms, refs = refs[:parts], refs[parts:]
-    back, gain, low_o, sums, squares, *scratch = refs
-    scatter_refs, (total, low, loc, gs, gr), line_refs = (
-        scratch[:SCATTER_REFS], scratch[SCATTER_REFS : SCATTER_REFS + 5], scratch[SCATTER_REFS + 5 :]
+    back, gain, low_o, dmix, sums, squares, *scratch = refs
+    scatter_refs, (total, low, loc, gs, gr, parts_in, load_s), line_refs = (
+        scratch[:SCATTER_REFS], scratch[SCATTER_REFS : SCATTER_REFS + 7], scratch[SCATTER_REFS + 7 :]
     )
     greet(gather_peers() + line_neighbours(length))
     line = Lines(terms, cuts, length, line_refs)
@@ -621,10 +653,32 @@
     gather.middle()
     line.start()
     gather.end()
+    rows = low.shape[0]
+    part = mixer.shape[1] // 3
+
+    def load(n, slot):
+        return pltpu.make_async_copy(low_o.at[pl.ds(2 * n, 2)], parts_in.at[slot], load_s.at[slot])
+
+    load(0, 0).start()
+
+    @pl.loop(0, 4)
+    def _(n):
+        slot = n - n // 2 * 2
+
+        @pl.when(n + 1 < 4)
+        def _():
+            load(n + 1, 1 - slot).start()
+
+        load(n, slot).wait()
+        lines = parts_in[slot].reshape(2 * rows, parts_in.shape[3])
+        mix = jnp.dot(lines, mixer[:, 2 * part :], preferred_element_type=F32)
+        none = jnp.zeros((2 * rows, dmix.shape[1] - part), F32)
+        dmix[pl.ds(pl.multiple_of(n * 2 * rows, rows), 2 * rows)] = jnp.concatenate([mix, none], axis=1)
+
     line.end(sums, squares)
 
 
-def turn(p, residual, above, gains, terms, cuts, length, collective_id):
+def turn(p, residual, above, gains, mixer, rc, terms, cuts, length, collective_id):
     rows, width = residual.shape
     line_rows, columns = terms[0].shape[1], sum(cut[2] for cut in cuts)
     return pl.pallas_call(
@@ -633,27 +687,29 @@
             jax.ShapeDtypeStruct((rows, width), F32),
             jax.ShapeDtypeStruct((8, width), F32),
             jax.ShapeDtypeStruct((8, rows, width), BF16),
+            jax.ShapeDtypeStruct((8 * rows, rc), F32),
             jax.ShapeDtypeStruct((line_rows, columns), BF16),
             TILE,
         ),
-        in_specs=[ANY, VM, VM, VM] + [ANY] * len(terms),
-        out_specs=(VM, VM, ANY, VM, VM),
+        in_specs=[ANY, VM, VM, VM, VM] + [ANY] * len(terms),
+        out_specs=(VM, VM, ANY, VM, VM, VM),
         scratch_shapes=scatter_scratch(rows // 2, width)
         + [pltpu.VMEM((rows, width), F32), pltpu.VMEM((rows, width), BF16), DMA, DMA((14,)), DMA((14,))]
+        + [pltpu.VMEM((2, 2, rows, width), BF16), DMA((2,))]
         + lines_scratch(length, line_rows, cuts),
-        compiler_params=params(collective_id, 56 * 2**20),
+        compiler_params=params(collective_id),
         cost_estimate=pl.CostEstimate(flops=0, bytes_accessed=300 * 2**20, transcendentals=0),
-    )(p.reshape(8, rows, width), residual, above, gains, *terms)
+    )(p.reshape(8, rows, width), residual, above, gains, mixer, *terms)
 
 
 def closing_kernel(
-    length, cut, part, x_in, dmz_in, dproj, mixed, first_w, q, residual, terms, block,
+    length, cut, part, x_in, dmz_in, dproj, mixed, mixer, q, residual, terms, block,
     o, out, e_o, sums, squares,
-    x_part, dmz_part, g, back, total, up_got, down_got, ls, lr, load_s, free, loc, es, er, *scratch,
+    x_part, dmz_part, g, back, total, up_a, down_a, up_b, down_b, ls, lr, load_s, free, loc, es, er, *scratch,
 ):
     scatter_refs, line_refs = scratch[:SCATTER_REFS], scratch[SCATTER_REFS:]
     greet(plane_peers() + line_neighbours(length))
-    model, rc = first_w.shape[0], mixed.shape[1]
+    model = mixer.shape[0]
     tokens = dproj.shape[0]
     columns = x_part.shape[2]
     steps = model // columns
@@ -679,7 +735,16 @@
     rest.load((1,))
     rest.start()
     rest.load((*range(2, length), 0))
-    line = HeldLine(g, up_got, down_got, ls, lr)
+    split = up_a.shape[2]
+    line_a = HeldLine(g, 0, up_a, down_a, ls.at[0], lr.at[0])
+    line_b = HeldLine(g, split, up_b, down_b, ls.at[1], lr.at[1])
+    queue = [chain for _ in range(1, length) for chain in (line_a, line_b)]
+
+    def advance(times=1):
+        for _ in range(times):
+            if queue:
+                queue.pop(0).start()
+
     output = scatter_steps(q, total, *scatter_refs)
     next(output)
     copies, own = exchange_steps(block, e_o, loc, es, er)
@@ -707,35 +772,32 @@
             tail = contract_first(dmz_part[slot], mixed[...])
             k = i * columns // line_rows
             at = pl.ds(pl.multiple_of(i * columns - k * line_rows, columns), columns)
-            g[k, at] = jnp.concatenate(
-                [front[:, :part], front[:, rc : rc + part], tail[:, :part]], axis=1
-            ).astype(BF16)
+            g[k, at] = jnp.concatenate([front, tail], axis=1).astype(BF16)
             block_of = i * rows // 256
             at = pl.ds(pl.multiple_of(i * rows - block_of * 256, rows), rows)
             mine = dproj[pl.ds(pl.multiple_of(i * rows, rows), rows)]
             for first_column in range(0, model, 512):
                 cols = slice(first_column, first_column + 512)
-                back[block_of, at, cols] = contract_last(mine, first_w[cols]).astype(BF16)
+                back[block_of, at, cols] = contract_last(mine, mixer[cols, : 2 * part]).astype(BF16)
 
     compute(0)
     next(output)
+    rest.start()
     compute(1)
+    while rest.next < length:
+        rest.start()
     if length == 4:
-        line.start()
+        advance(2)
     next(output)
-    rest.start()
     compute(2)
     next(output)
     compute(3)
-    if length != 4:
-        line.start()
-    while rest.next < length:
-        rest.start()
+    advance(1 if length == 4 else 2)
     for _ in output:
         pass
     for peer in gather_peers():
         pl.semaphore_signal(free, inc=1, device_id=peer, device_id_type=MESH)
-    line.start()
+    advance()
     pl.semaphore_wait(free, 3)
     incoming = scatter_steps(back, o, *scatter_refs)
     next(incoming)
@@ -748,24 +810,26 @@
     squares[...] = jnp.zeros_like(squares)
     rest.end(sums, 0, squares)
     for name in incoming:
-        if name == "early" and line.next < length:
-            line.start()
-    while line.next < length:
-        line.start()
-    line.end(sums, cut[1], squares)
+        if name in ("sent", "late"):
+            advance()
+    while queue:
+        advance()
+    line_a.end(sums, cut[1], squares)
+    line_b.end(sums, cut[1] + split, squares)
     for copy in copies:
         copy.wait()
     own.wait()
 
 
-def closing(x, dmz, dproj, mixed, first_w, q, residual, terms, cut, block, part, length, collective_id):
+def closing(x, dmz, dproj, mixed, mixer, q, residual, terms, cut, block, part, length, collective_id):
     rows, width = residual.shape
     tokens, model = x.shape
     share = block.shape[0] // 8
     block = block.reshape(8, share, block.shape[1])
     line_rows = terms.shape[1]
     columns = min(256, line_rows)
-    held = pltpu.VMEM((length - 1, line_rows, 3 * part), BF16)
+    split = -(-3 * part // 256) * 128
+    held_a, held_b = (pltpu.VMEM((length - 1, line_rows, n), BF16) for n in (split, 3 * part - split))
     return pl.pallas_call(
         functools.partial(closing_kernel, length, cut, part),
         out_shape=(
@@ -783,25 +847,37 @@
             pltpu.VMEM((length, line_rows, 3 * part), BF16),
             pltpu.VMEM((8, rows, width), BF16),
             pltpu.VMEM((rows, width), F32),
-            held, held,
-            DMA((2, length)), DMA((2, length)), DMA((2, 2)), pltpu.SemaphoreType.REGULAR,
+            held_a, held_a, held_b, held_b,
+            DMA((2, 2, length)), DMA((2, 2, length)), DMA((2, 2)), pltpu.SemaphoreType.REGULAR,
             DMA, DMA((7,)), DMA((7,)),
         ]
         + scatter_scratch(rows // 2, width)
         + line_scratch(length, line_rows, cut[1], 1),
-        compiler_params=params(collective_id, 63 * 2**20),
+        compiler_params=params(collective_id),
         cost_estimate=pl.CostEstimate(
             flops=10 * tokens * model * dproj.shape[1] // 2, bytes_accessed=350 * 2**20, transcendentals=0
         ),
-    )(x, dmz, dproj, mixed, first_w, q.reshape(8, rows, width), residual, terms, block)
+    )(x, dmz, dproj, mixed, mixer, q.reshape(8, rows, width), residual, terms, block)
 
 
 def first_kernel(
-    length, inputs, above, mixer_w, mlp_w, gains_w, gate_w, chan_w,
-    normed_o, wm_o, wf_o, wd_o, gains_o, gp_o, inputs_o, above_o,
+    length, inputs_in, above_in, mixer_in, mlp_in, gains_in, gate_in, chan_in,
+    normed_o, wm_o, wf_o, wd_o, w2, gains_o, gp_o, inputs_o, above_o,
+    inputs, above, mixer_w, mlp_w, gains_w, gate_w, chan_w, load_s,
     gn, gp, normed, gn_all, wm, wf, wd, loc, ms, mr, fs, fr, line_s, line_r, gain_s, gain_r, move_s, move_r,
     gather_s, gather_r, hop_s, hop_r,
 ):
+    loads = [
+        pltpu.make_async_copy(src, dst, load_s.at[n])
+        for n, (src, dst) in enumerate(
+            (
+                (gains_in, gains_w), (gate_in, gate_w), (chan_in, chan_w), (mixer_in, mixer_w),
+                (mlp_in, mlp_w), (inputs_in, inputs), (above_in, above),
+            )
+        )
+    ]
+    for copy in loads:
+        copy.start()
     y, c, z, x = place()
     s = 2 * z + x
     me = rank(y, c, x)
@@ -825,6 +901,8 @@
 
     pl.semaphore_wait(barrier, len(line) + len(plane) + 2 * moves)
 
+    for copy in loads[:3]:
+        copy.wait()
     share = gains_w.shape[1]
     gn[...] = jnp.zeros_like(gn)
     for n in (0, 1):
@@ -855,13 +933,15 @@
     pl.when(moves == 1)(lambda: gate_move.start())
     pl.when(moves == 0)(lambda: gate_stay.start())
 
-    def fill(pack, source, js):
+    def fill(pack, source, js, offset=0):
         part = pack.shape[2] // len(js)
+        whole = source.shape[1] // 24
         for t in range(8):
             for n, j in enumerate(js):
-                start = (j * 8 + t) * part
+                start = (j * 8 + t) * whole + offset
                 pack[t, :, n * part : (n + 1) * part] = source[:, start : start + part].astype(BF16)
 
+    loads[3].wait()
     fill(wm, mixer_w, (0, 1, 2))
     mixer, mixer_own = exchange_steps(wm, wm_o.at[0], loc.at[0], ms, mr)
     for copy in gains:
@@ -875,10 +955,24 @@
         remote(gp_o.at[z], gp_o.at[z], line_s.at[1, k], line_r.at[1, k], line[k])
         for k in range(length - 1)
     ]
+    hops = LineGather(wm_o, length, hop_s, hop_r)
+    mixer_own.wait()
+    hops.start_piece(me)
+
+    def pass_piece(n):
+        fy, fc, fx = FLIPS[n]
+        mixer[n].wait_recv()
+        hops.start_piece(rank(flip(y, fy), flip(c, fc), flip(x, fx)))
+
+    pass_piece(1)
+    loads[4].wait()
     fill(wd, mlp_w, (2,))
     down, down_own = exchange_steps(wd, wd_o.at[0], loc.at[4], fs.at[1], fr.at[1])
     fill(wf, mlp_w, (0, 1))
     feed, feed_own = exchange_steps(wf, wf_o.at[0], loc.at[3], fs.at[0], fr.at[0])
+    for n in (0, 2, 3, 5, 4, 6):
+        pass_piece(n)
+    fill(w2, mlp_w, (0, 1, 2), wd.shape[2])
     for copy in spread:
         copy.wait()
     for k in range(length):
@@ -888,10 +982,7 @@
             tile = (gn_all[2 * b, other] + gn_all[2 * b + 1, other])[:, :pair]
             gains_o[:, at] = tile.astype(BF16).astype(F32)
     for copy in mixer:
-        copy.wait()
-    mixer_own.wait()
-    hops = LineGather(wm_o, length, hop_s, hop_r)
-    hops.start(1)
+        copy.wait_send()
 
     def body(at):
         v = load_turned(inputs, at, length, pair)
@@ -900,6 +991,8 @@
         normed[at] = (v * inverse_rms(v) * gains_o[0:1]).astype(BF16)
         above_o[at] = load_turned(above, at, length, pair)
 
+    for copy in loads[5:]:
+        copy.wait()
     half = rows // 2
     gather = Gather(normed, normed_o, loc.at[1], gather_s, gather_r)
     rows_loop(half, body)
@@ -926,6 +1019,10 @@
     hops.finish()
 
 
+def early(f8):
+    return f8 // 384 * 256
+
+
 def unit(n):
     return (
         lax.broadcasted_iota(jnp.int32, (n, n), 0) == lax.broadcasted_iota(jnp.int32, (n, n), 1)
@@ -936,7 +1033,10 @@
     rows, width = inputs.shape
     pack = (-(-gate.shape[0] // 16) * 16, rc)
     share = mixer.shape[0]
-    wm, wf, wd = ((8, share, n) for n in (mixer.shape[1] // 8, mlp.shape[1] // 12, mlp.shape[1] // 24))
+    f8 = mlp.shape[1] // 24
+    wm, wf, wd, w2 = (
+        (8, share, n) for n in (mixer.shape[1] // 8, 2 * early(f8), early(f8), 3 * (f8 - early(f8)))
+    )
     low = jax.ShapeDtypeStruct((rows, width), BF16)
     return pl.pallas_call(
         functools.partial(first_kernel, length),
@@ -945,14 +1045,17 @@
             jax.ShapeDtypeStruct((length,) + wm, BF16),
             jax.ShapeDtypeStruct((length,) + wf, BF16),
             jax.ShapeDtypeStruct((length,) + wd, BF16),
+            jax.ShapeDtypeStruct(w2, BF16),
             jax.ShapeDtypeStruct((8, width), F32),
             jax.ShapeDtypeStruct((length,) + pack, BF16),
             low,
             low,
         ),
-        in_specs=[VM] * 7,
-        out_specs=(ANY, ANY, ANY, ANY, VM, ANY, VM, VM),
+        in_specs=[ANY] * 7,
+        out_specs=(ANY, ANY, ANY, ANY, VM, VM, ANY, VM, VM),
         scratch_shapes=[
+            *[pltpu.VMEM(v.shape, v.dtype) for v in (inputs, above, mixer, mlp, gains, gate, chan)],
+            DMA((7,)),
             pltpu.VMEM((8, 128), F32),
             pltpu.VMEM(pack, BF16),
             pltpu.VMEM((rows, width), BF16),
@@ -964,15 +1067,14 @@
             DMA((2, length)), DMA((2, length)), DMA((7,)), DMA((7,)), DMA, DMA,
             DMA((14,)), DMA((14,)), DMA((2, length)), DMA((2, length)),
         ],
-        compiler_params=params(collective_id, 40 * 2**20),
+        compiler_params=params(collective_id),
         cost_estimate=pl.CostEstimate(flops=0, bytes_accessed=300 * 2**20, transcendentals=0),
     )(inputs, above, mixer, mlp, gains, gate, chan)
 
 
 def last_kernel(
-    length, wm, total, inputs, back, gains, gain_two, gp, sq,
-    gains_w, gains_m, gains_v, gate_w, gate_m, gate_v, chan_w, chan_m, chan_v,
-    wm_o, grad_o, gains_mo, gains_vo, gains_wo, gate_mo, gate_vo, gate_wo, chan_mo, chan_vo, chan_wo,
+    length, share, wm, total, inputs, back, gains, gain_two, gp, sq_one, sq_two, sq_three,
+    wm_o, grad_o, gains_o, gates_o,
     norm_o, factor_o,
     gain, row_sums, gn, gn_in, gn_mid, gn_got, gp_got, gp_sum, gp_fin, sq_plane, sq_line,
     loc, ss, rs, gs, gr, ls, lr, move_s, move_r,
@@ -999,7 +1101,8 @@
     pl.semaphore_wait(barrier, len(line) + len(plane) + 2 * moves)
 
     gate = [
-        remote(gp.at[k + 1], gp_got.at[k], ls.at[0, k], lr.at[0, k], line[k]) for k in range(length - 1)
+        remote(gp.at[lax.rem(z + k + 1, length)], gp_got.at[k], ls.at[0, k], lr.at[0, k], line[k])
+        for k in range(length - 1)
     ]
     rows, width = inputs.shape
     pair = width // (4 * length)
@@ -1027,7 +1130,7 @@
     copies, own = exchange_steps(wm, wm_o, loc, ss, rs)
     for copy in gate:
         copy.wait()
-    sums = gp[0]
+    sums = gp[z]
     for k in range(length - 1):
         sums = sums + gp_got[k]
     gp_sum[...] = sums
@@ -1056,12 +1159,11 @@
     sums = gn_mid[0]
     for k in range(length - 1):
         sums = sums + gn_got[k]
-    share = gains_w.shape[1]
     lane = lax.broadcasted_iota(jnp.int32, (8, 128), 1)
     mine = jnp.logical_and(lane >= x * share, lane < (x + 1) * share)
     gain_sum = jnp.where(mine, sums, 0.0)
     gate_sum = gp_fin[...]
-    sq_plane[me] = sq[...] + gain_sum * gain_sum + tile_of_squares(gate_sum)
+    sq_plane[me] = sq_one[...] + sq_two[...] + sq_three[...] + gain_sum * gain_sum + tile_of_squares(gate_sum)
     sends = [
         remote(sq_plane.at[me], sq_plane.at[me], gs.at[1, n], gr.at[1, n], plane[n]) for n in range(7)
     ]
@@ -1085,39 +1187,27 @@
     factor = clip_limit / jnp.maximum(norm, clip_limit)
     norm_o[...] = norm
     factor_o[...] = factor
-    gain_own = jnp.where(x == 0, gain_sum[:2, :share], gain_sum[:2, share : 2 * share])
-    one = factor[0:1, 0:1]
-    gains_mo[...], gains_vo[...], gains_wo[...] = adam_step(
-        gains_w[...], gain_own, gains_m[...], gains_v[...], one, rate_gains, 0.0
-    )
-    gate_rows, columns = gate_w.shape
-    gate_mo[...], gate_vo[...], gate_wo[...] = adam_step(
-        gate_w[...], gate_sum[:gate_rows, :columns], gate_m[...], gate_v[...], one, rate_matrix, decay_matrix
-    )
-    channels = lax.dot_general(
-        unit(8).astype(F32), gate_sum[:gate_rows, columns : columns + 8], (((1,), (1,)), ((), ())),
-        precision=lax.Precision.HIGHEST, preferred_element_type=F32,
-    )
-    chan_mo[...], chan_vo[...], chan_wo[...] = adam_step(
-        chan_w[...], channels, chan_m[...], chan_v[...], one, rate_channel, 0.0
-    )
+    gains_o[...] = jnp.where(x == 0, gain_sum[:2, :share], gain_sum[:2, share : 2 * share])
+    gates_o[...] = gate_sum
     for copy in copies:
         copy.wait()
     own.wait()
 
 
-def last(wm, total, inputs, back, gains, gain_two, gp, sq, small, length, collective_id):
+def last(wm, total, inputs, back, gains, gain_two, gp, squares, length, collective_id):
     rows, width = inputs.shape
-    states = [jax.ShapeDtypeStruct(v.shape, F32) for v in small]
+    share = wm.shape[1]
     return pl.pallas_call(
-        functools.partial(last_kernel, length),
+        functools.partial(last_kernel, length, share),
         out_shape=(
             jax.ShapeDtypeStruct(wm.shape, wm.dtype),
             jax.ShapeDtypeStruct((rows, width), F32),
-            *states, TILE, TILE,
+            jax.ShapeDtypeStruct((2, share), F32),
+            jax.ShapeDtypeStruct(gp.shape[1:], F32),
+            TILE, TILE,
         ),
-        in_specs=[ANY] + [VM] * 16,
-        out_specs=(ANY,) + (VM,) * 12,
+        in_specs=[ANY] + [VM] * 9,
+        out_specs=(ANY,) + (VM,) * 5,
         scratch_shapes=[
             pltpu.VMEM((8, width), F32),
             pltpu.VMEM((8, width), F32),
@@ -1133,8 +1223,8 @@
             DMA, DMA((7,)), DMA((7,)), DMA((2, 7)), DMA((2, 7)),
             DMA((3, length)), DMA((3, length)), DMA, DMA,
         ],
-        compiler_params=params(collective_id, 32 * 2**20),
-    )(wm, total, inputs, back, gains, gain_two, gp, sq, *small)
+        compiler_params=params(collective_id),
+    )(wm, total, inputs, back, gains, gain_two, gp, *squares)
 
 
 def minus_expm1(v):
@@ -1159,54 +1249,72 @@
 
 
 def forward_kernel(
-    length, proj, gate, chan, above, w_in, mixed, decay_o, width_o, recur_o, enter_o, conv_o, xe, se, ends_o, above_o, w,
-    pre, loc_h, ends, carry, hs, hr, es, er, gather_l, gather_s, gather_r, hop_s, hop_r,
-    keep_s, *kept,
+    length, x_in, mixer, gate, chan, above, w2, w_in,
+    mixed, branch_o, decay_o, width_o, recur_o, enter_o, conv_o, xe_o, se_o, ends_o, above_o, w2_o, w,
+    x_part, pre, loc_h, ends, carry, hs, hr, es, er, gather_l, gather_s, gather_r, hop_s, hop_r, load_s, keep_s, w2_l, w2_s, w2_r,
+    branch, decay_k, width_k, recur_k, enter_k, conv_k, xe, se,
 ):
     keeps = [
         pltpu.make_async_copy(src, dst, keep_s.at[n])
         for n, (src, dst) in enumerate(
-            zip(kept, (decay_o, width_o, recur_o, enter_o, conv_o, xe, se))
+            (
+                (branch, branch_o), (decay_k, decay_o), (width_k, width_o), (recur_k, recur_o),
+                (enter_k, enter_o), (conv_k, conv_o), (xe, xe_o), (se, se_o),
+            )
         )
     ]
-    decay_o, width_o, recur_o, enter_o, conv_o, xe, se = kept
     y, c, z, x = place()
     line = line_peers(length)
-    greet(line + gather_peers())
-    seqs, span, rc = mixed.shape
+    seqs, span, rc = branch.shape
+    part = mixed.shape[2]
+    rows = x_part.shape[1]
     chunks = span // CHUNK
-    gather = Gather(above, above_o, gather_l, gather_s, gather_r)
-    ahead = device(y, c, lax.rem(z + 1, length), x)
-    for b in range(seqs):
-        xe[b, span : span + 8] = proj[b, span - 8 : span, rc:].astype(BF16).astype(F32)
-    halo = remote(xe.at[:, pl.ds(span, 8)], xe.at[:, pl.ds(0, 8)], hs, hr, ahead)
-    halo.wait_send()
+
+    def load(n, slot):
+        half = 1 - n // seqs
+        b = n - n // seqs * seqs
+        at = pl.ds(pl.multiple_of((b * 2 + half) * rows, rows), rows)
+        return pltpu.make_async_copy(x_in.at[at], x_part.at[slot], load_s.at[slot])
+
+    load(0, 0).start()
+    greet(line + plane_peers())
     hops = LineGather(w, length, hop_s, hop_r)
     hops.start(1)
+    gather = Gather(above, above_o, gather_l, gather_s, gather_r)
     gather.begin()
-
-    @pl.loop(0, seqs * chunks)
-    def _(i):
-        b = i // chunks
-        r = pl.multiple_of((i - b * chunks) * CHUNK, CHUNK)
-        xe[b, pl.ds(r + 8, CHUNK)] = proj[b, pl.ds(r, CHUNK), rc:].astype(BF16).astype(F32)
-
-    halo.wait_recv()
-
-    @pl.when(z == 0)
-    def _():
-        xe[:, 0:8] = jnp.zeros((seqs, 8, rc), F32)
-
-    def coefficients(i):
-        b = i // chunks
-        r = pl.multiple_of((i - b * chunks) * CHUNK, CHUNK)
+    shares, share_own = exchange_steps(w2, w2_o.at[0], w2_l, w2_s, w2_r)
+
+    def project(n):
+        slot = n - n // 2 * 2
+
+        @pl.when(n + 1 < 2 * seqs)
+        def _():
+            load(n + 1, 1 - slot).start()
+
+        load(n, slot).wait()
+        both = jnp.dot(x_part[slot], mixer[:, : 2 * part], preferred_element_type=F32)
+        none = jnp.zeros((rows, rc - part), F32)
+        half = 1 - n // seqs
+        b = n - n // seqs * seqs
+        at = pl.multiple_of(half * rows, rows)
+        branch[b, pl.ds(at, rows)] = jnp.concatenate([both[:, :part], none], axis=1)
+        low = both[:, part:].astype(BF16).astype(F32)
+        xe[b, pl.ds(at + 8, rows)] = jnp.concatenate([low, none], axis=1)
+
+    pl.loop(0, seqs)(project)
+    ahead = device(y, c, lax.rem(z + 1, length), x)
+    halo = remote(xe.at[:, pl.ds(span, 8)], xe.at[:, pl.ds(0, 8)], hs, hr, ahead)
+    pl.loop(seqs, 2 * seqs)(project)
+
+    def coefficients(b, chunk):
+        r = pl.multiple_of(chunk * CHUNK, CHUNK)
         at = pl.ds(r, CHUNK)
         window = xe[b, pl.ds(r, CHUNK + 8)]
         total = chan[4:5] + chan[0:1] * window[8:]
         for k in (1, 2, 3):
             total = total + chan[k : k + 1] * pltpu.roll(window, k, 0)[8:]
         low = total.astype(BF16)
-        conv_o[b, at] = low
+        conv_k[b, at] = low
         value = low.astype(F32)
         gates = jnp.dot(low, gate[...], preferred_element_type=F32)
         recur = jax.nn.sigmoid(gates[:, :rc] + chan[5:6])
@@ -1214,18 +1322,32 @@
         log_decay = -chan[7:8] * recur
         decay = jnp.exp(log_decay)
         width = jnp.sqrt(minus_expm1(2.0 * log_decay))
-        recur_o[b, at] = recur
-        enter_o[b, at] = enter
-        decay_o[b, at] = decay
-        width_o[b, at] = width
+        recur_k[b, at] = recur
+        enter_k[b, at] = enter
+        decay_k[b, at] = decay
+        width_k[b, at] = width
         loc_h[b, at] = width * enter * value
 
-    half = seqs * chunks // 2
-    pl.loop(0, half)(coefficients)
+    def later_chunks(i):
+        b = i // (chunks - 1)
+        coefficients(b, 1 + i - b * (chunks - 1))
+
+    many = seqs * (chunks - 1)
+    pl.loop(0, many // 2)(later_chunks)
     hops.arrive(1)
     if length > 2:
         hops.start(2)
-    pl.loop(half, seqs * chunks)(coefficients)
+    pl.loop(many // 2, many)(later_chunks)
+    halo.wait()
+
+    @pl.when(z == 0)
+    def _():
+        xe[:, 0:8] = jnp.zeros((seqs, 8, rc), F32)
+
+    @pl.loop(0, seqs)
+    def _(b):
+        coefficients(b, 0)
+
     for copy in keeps[:-1]:
         copy.start()
     row = lax.broadcasted_iota(jnp.int32, (8, rc), 0)
@@ -1234,7 +1356,7 @@
         at = pl.ds(pl.multiple_of(i * 8, 8), 8)
         new = []
         for b in range(seqs):
-            a, h = decay_o[b, at], loc_h[b, at]
+            a, h = decay_k[b, at], loc_h[b, at]
             for n in (1, 2, 4):
                 keep = row >= n
                 h = h + jnp.where(keep, a * pltpu.roll(h, n, 0), 0.0)
@@ -1253,11 +1375,11 @@
         ends[z, 1, b] = jnp.broadcast_to(final[b][1], (8, rc))
         ends_o[b] = jnp.broadcast_to(final[b][0], (8, rc))
     moves = [remote(ends.at[z], ends.at[z], es.at[k], er.at[k], line[k]) for k in range(length - 1)]
-    for copy in moves:
-        copy.wait()
     if length > 3:
         hops.arrive(2)
         hops.start(3)
+    for copy in moves:
+        copy.wait()
     gather.middle()
     carry[...] = jnp.zeros_like(carry)
     for k in range(length):
@@ -1273,8 +1395,8 @@
         at = pl.ds(r, CHUNK)
         state = loc_h[b, at] + pre[b, at] * carry[b, 0:1]
         se[b, pl.ds(r + 8, CHUNK)] = state
-        gelu, _ = gelu_parts(proj[b, at, :rc])
-        mixed[b, at] = (state * gelu).astype(BF16)
+        gelu, _ = gelu_parts(branch[b, at])
+        mixed[b, at] = (state * gelu)[:, :part].astype(BF16)
 
     keeps[-1].start()
     gather.end()
@@ -1283,55 +1405,63 @@
         if hop + 1 < length:
             hops.start(hop + 1)
     hops.finish()
-    for copy in keeps:
+    for copy in keeps + shares:
         copy.wait()
-
-
-def recur_forward(proj, gate, chan, above, w, length, collective_id):
-    seqs, span, rc = proj.shape[0], proj.shape[1], proj.shape[2] // 2
+    share_own.wait()
+
+
+def recur_forward(x, mixer, gate, chan, above, w2, w, length, collective_id):
+    rc = gate.shape[0]
+    part = mixer.shape[1] // 3
+    rows = x.shape[0] // 8
+    seqs, span = 4, 2 * rows
     full = jax.ShapeDtypeStruct((seqs, span, rc), F32)
     longer = jax.ShapeDtypeStruct((seqs, span + 8, rc), F32)
-    low = jax.ShapeDtypeStruct((seqs, span, rc), BF16)
+    kept = (full, full, full, full, full, jax.ShapeDtypeStruct((seqs, span, rc), BF16), longer, longer)
     return pl.pallas_call(
         functools.partial(forward_kernel, length),
         out_shape=(
-            low, full, full, full, full, low, longer, longer,
+            jax.ShapeDtypeStruct((seqs, span, part), BF16),
+            *kept,
             jax.ShapeDtypeStruct((seqs, 8, rc), F32),
             jax.ShapeDtypeStruct((8,) + above.shape, above.dtype),
+            jax.ShapeDtypeStruct((length,) + w2.shape, w2.dtype),
             jax.ShapeDtypeStruct(w.shape, w.dtype),
         ),
-        in_specs=[VM, VM, VM, ANY, ANY],
-        out_specs=(VM,) + (ANY,) * 7 + (VM, ANY, ANY),
+        in_specs=[ANY, VM, VM, VM, ANY, ANY, ANY],
+        out_specs=(VM,) + (ANY,) * 8 + (VM, ANY, ANY, ANY),
         scratch_shapes=[
+            pltpu.VMEM((2, rows, x.shape[1]), BF16),
             pltpu.VMEM((seqs, span, rc), F32),
             pltpu.VMEM((seqs, span, rc), F32),
             pltpu.VMEM((length, 2, seqs, 8, rc), F32),
             pltpu.VMEM((seqs, 8, rc), F32),
             DMA, DMA, DMA((length,)), DMA((length,)),
             DMA, DMA((14,)), DMA((14,)), DMA((2, length)), DMA((2, length)),
-            DMA((7,)),
-            *[pltpu.VMEM(v.shape, v.dtype) for v in (full, full, full, full, low, longer, longer)],
+            DMA((2,)), DMA((8,)), DMA, DMA((7,)), DMA((7,)),
+            *[pltpu.VMEM(v.shape, v.dtype) for v in kept],
         ],
-        input_output_aliases={4: 10},
-        compiler_params=params(collective_id, 56 * 2**20),
+        input_output_aliases={6: 12},
+        compiler_params=params(collective_id),
         cost_estimate=pl.CostEstimate(
             flops=2 * seqs * span * rc * rc * 2, bytes_accessed=100 * 2**20, transcendentals=0
         ),
-    )(proj, gate, chan, above, w)
+    )(x, mixer, gate, chan, above, w2, w)
 
 
 def backward_kernel(
-    length, cuts, dmix, gate, chan, decay, width, recur, enter, conv, xe, se, ends_f, proj, block, *refs
+    length, cuts, head, dmix, gate, chan, decay, width, recur, enter, conv, xe, se, ends_f, proj, block, *refs
 ):
     parts = 1 + max(cut[0] for cut in cuts)
     terms, refs = refs[:parts], refs[parts:]
-    dproj, dgate, gchan, sums, squares, block_o, *refs = refs
+    dproj, gates_o, sums, squares, block_o, *refs = refs
+    dgate, gchan, *refs = refs
     suffix, grad, de, ends, carry, hs, hr, es, er, keep_s, move_l, move_s, move_r, *refs = refs
     kept, line_refs = refs[:8], refs[8:]
     loads = [
         pltpu.make_async_copy(src, dst, keep_s.at[n])
         for n, (src, dst) in enumerate(
-            zip((dmix, proj.at[:, :, pl.ds(0, decay.shape[2])], se, decay, width, recur, enter, conv, xe), (de.at[:, pl.ds(0, decay.shape[1])], *kept))
+            zip((dmix, proj, se, decay, width, recur, enter, conv, xe), (de.at[:, pl.ds(0, decay.shape[1])], *kept))
         )
     ]
     proj, se, decay, width, recur, enter, conv, xe = kept
@@ -1344,6 +1474,7 @@
         copy.start()
     moves, own = exchange_steps(block, block_o, move_l, move_s, move_r)
     seqs, span, rc = decay.shape
+    part = dproj.shape[2] // 2
     chunks = span // CHUNK
     for copy in loads[:3]:
         copy.wait()
@@ -1358,7 +1489,7 @@
         above = de[b, at]
         state = se[b, pl.ds(r + 8, CHUNK)]
         grad[b, at] = above * gelu
-        dproj[b, at, :rc] = (above * state * gelu_slope(branch, inner)).astype(BF16)
+        proj[b, at] = above * state * gelu_slope(branch, inner)
 
     loads[3].wait()
     row = lax.broadcasted_iota(jnp.int32, (8, rc), 0)
@@ -1429,6 +1560,10 @@
     halo.wait()
     scatter.start()
     scatter.start()
+    low = conv[...].reshape(seqs * span, rc)
+    recur_grad, enter_grad = (
+        contract_first(low, dgate[:, :, at].reshape(seqs * span, rc)) for at in (slice(0, rc), slice(rc, 2 * rc))
+    )
 
     @pl.when(z == length - 1)
     def _():
@@ -1447,29 +1582,51 @@
         for k in (1, 2, 3):
             total = total + chan[k : k + 1] * pltpu.roll(window, CHUNK + 8 - k, 0)[:CHUNK]
             gchan[k] += fold(dcv * pltpu.roll(inputs, k, 0)[8:])
-        dproj[b, at, rc:] = total.astype(BF16)
-
+        dproj[b, at] = jnp.concatenate([proj[b, at, :part], total[:, :part]], axis=1).astype(BF16)
+
+    rates = 8.0 * minus_expm1(chan[7:8] * (-1.0 / 8.0))
+    channels = [jnp.sum(gchan[n], axis=0, keepdims=True) for n in range(8)]
+    channels[7] = channels[7] * rates
+    channels = lax.dot_general(
+        jnp.concatenate(channels), unit(8).astype(F32), (((0,), (0,)), ((), ())),
+        precision=lax.Precision.HIGHEST, preferred_element_type=F32,
+    )
+    blocks = []
+    for first_row in range(0, part, head):
+        at = slice(first_row, first_row + head)
+        blocks.append(jnp.concatenate([recur_grad[at, at], enter_grad[at, at]], axis=1))
+    pack = jnp.concatenate(
+        [jnp.concatenate(blocks), channels[:part], jnp.zeros((part, rc - 2 * head - 8), F32)], axis=1
+    )
+    rows = part // length
+    if rows < gates_o.shape[1]:
+        gates_o[...] = jnp.zeros_like(gates_o)
+    for n in range(length):
+        gates_o[n, :rows] = pack[n * rows : (n + 1) * rows]
     scatter.end(sums, squares)
     for copy in moves:
         copy.wait()
     own.wait()
 
 
-def recur_backward(dmix, gate, chan, kept, proj, block, terms, cuts, length, collective_id):
-    decay, width, recur, enter, conv, xe, se, ends = kept
+def recur_backward(dmix, gate, chan, kept, part, head, block, terms, cuts, length, collective_id):
+    proj, decay, width, recur, enter, conv, xe, se, ends = kept
     seqs, span, rc = decay.shape
-    wide = jax.ShapeDtypeStruct((seqs, span, 2 * rc), BF16)
+    gate_pad = -(-(part // length) // 16) * 16
     line_rows, columns = terms[0].shape[1], sum(cut[2] for cut in cuts)
     return pl.pallas_call(
-        functools.partial(backward_kernel, length, cuts),
+        functools.partial(backward_kernel, length, cuts, head),
         out_shape=(
-            wide, wide, jax.ShapeDtypeStruct((8, 8, rc), F32),
+            jax.ShapeDtypeStruct((seqs, span, 2 * part), BF16),
+            jax.ShapeDtypeStruct((length, gate_pad, rc), F32),
             jax.ShapeDtypeStruct((line_rows, columns), BF16), TILE,
             jax.ShapeDtypeStruct(block.shape, BF16),
         ),
         in_specs=[ANY, VM, VM] + [ANY] * 7 + [VM] + [ANY] * (2 + len(terms)),
-        out_specs=(VM,) * 5 + (ANY,),
+        out_specs=(VM,) * 4 + (ANY,),
         scratch_shapes=[
+            pltpu.VMEM((seqs, span, 2 * rc), BF16),
+            pltpu.VMEM((8, 8, rc), F32),
             pltpu.VMEM((seqs, span, rc), F32),
             pltpu.VMEM((seqs, span, rc), F32),
             pltpu.VMEM((seqs, span + 8, rc), F32),
@@ -1486,7 +1643,7 @@
             ],
         ]
         + lines_scratch(length, line_rows, cuts),
-        compiler_params=params(collective_id, 62 * 2**20),
+        compiler_params=params(collective_id),
         cost_estimate=pl.CostEstimate(
             flops=2 * seqs * span * rc * rc * 2, bytes_accessed=120 * 2**20, transcendentals=0
         ),
@@ -1509,66 +1666,148 @@
     return pl.BlockSpec(shape, lambda i: (0, 0), pipeline_mode=pl.Buffered(1))
 
 
-def feed_kernel(cut, x, above, gate_up, down, hid, dgate, dup, out, back):
+def feed_forward(x, above, gate_up, down, hid, dgate, dup):
     f = hid.shape[1]
-    for first_column in range(0, f, cut):
-        at = slice(first_column, first_column + cut)
+    for first_column in range(0, f, 256):
+        at = slice(first_column, first_column + 256)
         gg = jnp.dot(x[...], gate_up[:, at], preferred_element_type=F32)
-        uu = jnp.dot(x[...], gate_up[:, f + first_column : f + first_column + cut], preferred_element_type=F32)
+        uu = jnp.dot(x[...], gate_up[:, f + first_column : f + first_column + 256], preferred_element_type=F32)
         dhid = jnp.dot(above[...], down[:, at], preferred_element_type=F32)
         gelu, inner = gelu_parts(gg)
         hid[:, at] = (gelu * uu).astype(BF16)
         dgate[:, at] = (dhid * uu * gelu_slope(gg, inner)).astype(BF16)
         dup[:, at] = (dhid * gelu).astype(BF16)
-    for first_column in range(0, x.shape[1], 512):
-        at = slice(first_column, first_column + 512)
-        out[:, at] = contract_last(hid[...], down[at]).astype(BF16)
-        both = contract_last(dgate[...], gate_up[at, :f]) + contract_last(dup[...], gate_up[at, f:])
-        back[:, at] = both.astype(BF16)
-
-
-def feed_forward_back(x, above, gate_up, down):
-    tokens, model = x.shape
-    f = down.shape[1]
-    rows = 256
-
-    def block(width):
-        return pl.BlockSpec((rows, width), lambda i: (i, 0))
-
-    return pl.pallas_call(
-        functools.partial(feed_kernel, 256),
-        grid=(tokens // rows,),
-        out_shape=tuple(jax.ShapeDtypeStruct((tokens, n), BF16) for n in (f, f, f, model, model)),
-        in_specs=[block(model), block(model), resident(gate_up.shape), resident(down.shape)],
-        out_specs=tuple(block(n) for n in (f, f, f, model, model)),
-        compiler_params=pltpu.CompilerParams(vmem_limit_bytes=48 * 2**20),
-        cost_estimate=pl.CostEstimate(
-            flops=12 * tokens * model * f, bytes_accessed=40 * 2**20, transcendentals=0
-        ),
-    )(x, above, gate_up, down)
-
-
-def feed_grads_kernel(x, above, hid, dgate, dup, gate_o, up_o, down_o):
+
+
+def grads_compute(x, above, hid, dgate, dup, gate_o, up_o, down_o):
     gate_o[...] = contract_first(x[...], dgate[...]).astype(BF16)
     up_o[...] = contract_first(x[...], dup[...]).astype(BF16)
     down_o[...] = contract_first(above[...], hid[...]).astype(BF16)
 
 
-def feed_grads(x, above, hid, dgate, dup):
+def with_hops(length, first_hop, last_hop, buf, ss, rs, steps, compute):
+    i = pl.program_id(0)
+    hops = LineGather(buf, length, ss, rs)
+
+    @pl.when(i == 0)
+    def _():
+        greet(line_neighbours(length))
+        hops.start(first_hop)
+
+    @pl.when(i == steps // 2)
+    def _():
+        for hop in range(first_hop, last_hop):
+            hops.arrive(hop)
+            hops.start(hop + 1)
+
+    compute()
+
+    @pl.when(i == steps - 1)
+    def _():
+        hops.arrive(last_hop)
+        hops.finish(first_hop, last_hop)
+
+
+def early_feed_kernel(length, x, above, gate_up, down, w_in, hid, dgate, dup, w, ss, rs):
+    with_hops(
+        length, 2, length - 2, w, ss, rs, 8,
+        lambda: feed_forward(x, above, gate_up, down, hid, dgate, dup),
+    )
+
+
+def early_feed(x, above, gate_up, down, w, length, collective_id):
+    tokens, model = x.shape
+    f = down.shape[1]
+
+    def block(width):
+        return pl.BlockSpec((tokens // 8, width), lambda i: (i, 0))
+
+    return pl.pallas_call(
+        functools.partial(early_feed_kernel, length),
+        grid=(8,),
+        out_shape=(jax.ShapeDtypeStruct((tokens, f), BF16),) * 3 + (jax.ShapeDtypeStruct(w.shape, w.dtype),),
+        in_specs=[block(model), block(model), resident(gate_up.shape), resident(down.shape), ANY],
+        out_specs=(block(f),) * 3 + (ANY,),
+        scratch_shapes=[DMA((2, length)), DMA((2, length))],
+        input_output_aliases={4: 3},
+        compiler_params=params(collective_id),
+        cost_estimate=pl.CostEstimate(flops=6 * tokens * model * f, bytes_accessed=30 * 2**20, transcendentals=0),
+    )(x, above, gate_up, down, w)
+
+
+def late_feed_kernel(
+    x, above, hid_one, dgate_one, dup_one, gate_up, down, late, hid, dgate, dup, out, back
+):
+    f, g = down.shape[1], hid.shape[1]
+    feed_forward(x, above, late.at[:, : 2 * g], late.at[:, 2 * g :], hid, dgate, dup)
+    for first_column in range(0, x.shape[1], 512):
+        at = slice(first_column, first_column + 512)
+        ahead = contract_last(hid_one[...], down[at]) + contract_last(hid[...], late[at, 2 * g :])
+        out[:, at] = ahead.astype(BF16)
+        both = contract_last(dgate_one[...], gate_up[at, :f]) + contract_last(dup_one[...], gate_up[at, f:])
+        both = both + contract_last(dgate[...], late[at, :g]) + contract_last(dup[...], late[at, g : 2 * g])
+        back[:, at] = both.astype(BF16)
+
+
+def late_feed(x, above, early_units, gate_up, down, late):
+    tokens, model = x.shape
+    f, g = down.shape[1], late.shape[1] // 3
+
+    def block(width):
+        return pl.BlockSpec((tokens // 8, width), lambda i: (i, 0))
+
+    widths = (g, g, g, model, model)
+    return pl.pallas_call(
+        late_feed_kernel,
+        grid=(8,),
+        out_shape=tuple(jax.ShapeDtypeStruct((tokens, n), BF16) for n in widths),
+        in_specs=[block(model), block(model)]
+        + [block(f)] * 3
+        + [resident(v.shape) for v in (gate_up, down, late)],
+        out_specs=tuple(block(n) for n in widths),
+        compiler_params=pltpu.CompilerParams(vmem_limit_bytes=VMEM_BYTES),
+        cost_estimate=pl.CostEstimate(
+            flops=6 * tokens * model * (f + 2 * g), bytes_accessed=60 * 2**20, transcendentals=0
+        ),
+    )(x, above, *early_units, gate_up, down, late)
+
+
+def early_grads_kernel(length, x, above, hid, dgate, dup, w_in, gate_o, up_o, down_o, w, ss, rs):
+    with_hops(
+        length, length - 1, length - 1, w, ss, rs, 8,
+        lambda: grads_compute(x, above, hid, dgate, dup, gate_o, up_o, down_o),
+    )
+
+
+def feed_grads(x, above, hid, dgate, dup, w=None, length=0, collective_id=None):
     tokens, model = x.shape
     f = hid.shape[1]
-    columns = pl.BlockSpec((tokens, 256), lambda i: (0, i))
+    columns = pl.BlockSpec((tokens, model // 8), lambda i: (0, i))
+    in_specs = [columns, columns] + [resident(hid.shape)] * 3
+    shapes = (jax.ShapeDtypeStruct((model, f), BF16),) * 3
+    out_specs = (pl.BlockSpec((model // 8, f), lambda i: (i, 0)),) * 3
+    cost = pl.CostEstimate(flops=6 * tokens * model * f, bytes_accessed=40 * 2**20, transcendentals=0)
+    if w is None:
+        return pl.pallas_call(
+            grads_compute,
+            grid=(8,),
+            out_shape=shapes,
+            in_specs=in_specs,
+            out_specs=out_specs,
+            compiler_params=pltpu.CompilerParams(vmem_limit_bytes=VMEM_BYTES),
+            cost_estimate=cost,
+        )(x, above, hid, dgate, dup)
     return pl.pallas_call(
-        feed_grads_kernel,
-        grid=(model // 256,),
-        out_shape=(jax.ShapeDtypeStruct((model, f), BF16),) * 3,
-        in_specs=[columns, columns] + [resident(hid.shape)] * 3,
-        out_specs=(pl.BlockSpec((256, f), lambda i: (i, 0)),) * 3,
-        compiler_params=pltpu.CompilerParams(vmem_limit_bytes=48 * 2**20),
-        cost_estimate=pl.CostEstimate(
-            flops=6 * tokens * model * f, bytes_accessed=40 * 2**20, transcendentals=0
-        ),
-    )(x, above, hid, dgate, dup)
+        functools.partial(early_grads_kernel, length),
+        grid=(8,),
+        out_shape=shapes + (jax.ShapeDtypeStruct(w.shape, w.dtype),),
+        in_specs=in_specs + [ANY],
+        out_specs=out_specs + (ANY,),
+        scratch_shapes=[DMA((2, length)), DMA((2, length))],
+        input_output_aliases={5: 3},
+        compiler_params=params(collective_id),
+        cost_estimate=cost,
+    )(x, above, hid, dgate, dup, w)
 
 
 def adam_step(weight, grad, first, second, factor, rate, decay_rate):
@@ -1583,8 +1822,28 @@
     return (first_new, second_new, weight_new)
 
 
+def small_steps(factor, refs, outs):
+    gains_sum, gates_sum, *states = refs
+    rows, columns = states[3].shape
+    channels = lax.dot_general(
+        unit(8).astype(F32), gates_sum[:rows, columns : columns + 8], (((1,), (1,)), ((), ())),
+        precision=lax.Precision.HIGHEST, preferred_element_type=F32,
+    )
+    grads = gains_sum[...], gates_sum[:rows, :columns], channels
+    rates = (rate_gains, 0.0), (rate_matrix, decay_matrix), (rate_channel, 0.0)
+    for n in range(3):
+        w, m, v = states[3 * n : 3 * n + 3]
+        results = adam_step(w[...], grads[n], m[...], v[...], factor, *rates[n])
+        for out, result in zip(outs[3 * n : 3 * n + 3], results):
+            out[...] = result
+
+
 def adam_kernel(rate, decay_rate, sources, factor, w, m, v, *refs):
-    grads, (m_o, v_o, w_o) = refs[: len(sources)], refs[len(sources) :]
+    grads, refs = refs[: len(sources)], refs[len(sources) :]
+    if len(refs) > 3:
+        small, refs = refs[:11], refs[11:]
+        pl.when(pl.program_id(0) == 0)(lambda: small_steps(factor[0:1, 0:1], small, refs[3:]))
+    m_o, v_o, w_o = refs[:3]
     parts = []
     for ref, pieces in zip(grads, sources):
         for first, columns, at, stride in pieces:
@@ -1600,21 +1859,27 @@
     w_o[...] = weight_new
 
 
-def adam_rows(weight, grads, sources, first, second, factor, rate, decay_rate):
+def adam_rows(weight, grads, sources, first, second, factor, rate, decay_rate, small=()):
     rows, width = weight.shape
     step = min(rows, 16)
     block = pl.BlockSpec((step, width), lambda i: (i, 0))
     shape = jax.ShapeDtypeStruct(weight.shape, F32)
-    return pl.pallas_call(
+
+    def whole(v):
+        return pl.BlockSpec(v.shape, lambda i: (0, 0))
+
+    results = pl.pallas_call(
         functools.partial(adam_kernel, rate, decay_rate, sources),
         grid=(rows // step,),
-        out_shape=(shape,) * 3,
+        out_shape=(shape,) * 3 + tuple(jax.ShapeDtypeStruct(v.shape, F32) for v in small[2:]),
         in_specs=[pl.BlockSpec((8, 128), lambda i: (0, 0)), block, block, block]
-        + [pl.BlockSpec((8, step, g.shape[2]), lambda i: (0, i, 0)) for g in grads],
-        out_specs=(block,) * 3,
-        compiler_params=pltpu.CompilerParams(vmem_limit_bytes=48 * 2**20),
+        + [pl.BlockSpec((8, step, g.shape[2]), lambda i: (0, i, 0)) for g in grads]
+        + [whole(v) for v in small],
+        out_specs=(block,) * 3 + tuple(whole(v) for v in small[2:]),
+        compiler_params=pltpu.CompilerParams(vmem_limit_bytes=VMEM_BYTES),
         cost_estimate=pl.CostEstimate(flops=0, bytes_accessed=7 * 4 * weight.size, transcendentals=0),
-    )(factor, weight, first, second, *grads)
+    )(factor, weight, first, second, *grads, *small)
+    return (*results[:3], results[3:]) if small else results
 
 
 def on_device(
@@ -1666,7 +1931,7 @@
         v = jnp.roll(v.reshape(v.shape[0], length, 4, pair), z, axis=1)
         return v.swapaxes(1, 2).reshape(v.shape[0], model)
 
-    normed_one, mixer_full, mlp_gu, mlp_down, gains, gate_in, inputs, above = first(
+    normed_one, mixer_full, mlp_gu, mlp_down, late_pack, gains, gate_in, inputs, above = first(
         turned(block_input[0]),
         turned(out_grad[0]),
         mixer_weight,
@@ -1695,80 +1960,70 @@
     gate = jnp.pad(jnp.concatenate(gate), ((0, rc - r8), (0, 0)))
 
     mixer_full = mixer_full.reshape(model, 3 * r8)
-    parts = [jnp.pad(mixer_full[:, n * r8 : (n + 1) * r8], ((0, 0), (0, rc - r8))) for n in range(3)]
-    mixer_first = jnp.concatenate(parts[:2], axis=1)
-    mixer_last = parts[2]
+    mixed, *kept, grad_out, late, mlp_down = recur_forward(
+        normed_one, mixer_full, gate, chan, above, late_pack, mlp_down, length, 2
+    )
+    grad_out = grad_out.reshape(8 * tokens, model)
+    mixed = mixed.reshape(8 * tokens, r8)
+    residual, normed_two, mlp_gu, late = middle(mixed, mixer_full, inputs, gains, mlp_gu, late, length, 3)
+    normed_two = normed_two.reshape(8 * tokens, model)
+    h1 = early(f8)
+    h2 = f8 - h1
+    mlp_gu = mlp_gu.reshape(model, 2 * h1)
+    mlp_down = mlp_down.reshape(model, h1)
+    *early_units, late = early_feed(normed_two, grad_out, mlp_gu, mlp_down, late, length, 9)
+    *early_terms, late = feed_grads(
+        normed_two, grad_out, *early_units, w=late, length=length, collective_id=10
+    )
+    late = late.reshape(model, 3 * h2)
+    *late_units, mlp_part, dnormed_two = late_feed(
+        normed_two, grad_out, early_units, mlp_gu, mlp_down, late
+    )
+    late_terms = feed_grads(normed_two, grad_out, *late_units)
+    gate_one, up_one, down_one = (v.reshape(length, 8 * share, h1) for v in early_terms)
+    gate_two, up_two, down_two = (v.reshape(length, 8 * share, h2) for v in late_terms)
+    down_cut = h1 // 2
+
+    grad_residual, gain_two, dmz, dmix, sums_one, squares_one = turn(
+        dnormed_two, residual, above, gains, mixer_full, rc,
+        (gate_one, up_one, down_one), ((0, 0, h1), (1, 0, h1), (2, 0, down_cut)), length, 4,
+    )
+    dmz = dmz.reshape(8 * tokens, model)
     span = 2 * tokens
-    projected = jnp.dot(normed_one, mixer_first, preferred_element_type=F32)
-    projected = projected.reshape(4, span, 2 * rc)
-    mixed, *kept, grad_out, mlp_down = recur_forward(projected, gate, chan, above, mlp_down, length, 2)
-    grad_out = grad_out.reshape(8 * tokens, model)
-    mixed = mixed.reshape(4 * span, rc)
-    residual, normed_two, mlp_gu = middle(
-        contract_last(mixed, mixer_last).astype(BF16), inputs, gains, mlp_gu, length, 3
-    )
-    normed_two = normed_two.reshape(8 * tokens, model)
-    mlp_gu = mlp_gu.reshape(model, 2 * f8)
-    mlp_down = mlp_down.reshape(model, f8)
-    hid, dgg, duu, mlp_part, dnormed_two = feed_forward_back(normed_two, grad_out, mlp_gu, mlp_down)
-    gate_terms, up_terms, down_terms = (
-        v.reshape(length, 8 * share, f8) for v in feed_grads(normed_two, grad_out, hid, dgg, duu)
-    )
-    up_cut, down_cut = f8 // 384 * 256, f8 // 384 * 256
-
-    grad_residual, gain_two, dmz, sums_one, squares_one = turn(
-        dnormed_two, residual, above, gains,
-        (gate_terms, up_terms), ((0, 0, f8), (1, 0, up_cut)), length, 4,
-    )
-    dmz = dmz.reshape(8 * tokens, model)
-    dmix = jnp.dot(dmz, mixer_last, preferred_element_type=F32).reshape(4, span, rc)
-    dproj, dgate, chan_grad, sums_two, squares_two, back_one = recur_backward(
-        dmix, gate, chan, kept, projected, sums_one.reshape(8, share, sums_one.shape[1]),
-        (up_terms, down_terms), ((0, up_cut, f8 - up_cut), (1, 0, down_cut)), length, 6,
-    )
-    dproj = dproj.reshape(4 * span, 2 * rc)
-    dgate = dgate.reshape(4 * span, 2 * rc)
+    dmix = dmix.reshape(4, span, rc)
+    dproj, gate_back, sums_two, squares_two, back_one = recur_backward(
+        dmix, gate, chan, kept, r8, head, sums_one.reshape(8, share, sums_one.shape[1]),
+        (down_one, gate_two, up_two), ((0, down_cut, h1 - down_cut), (1, 0, h2), (2, 0, h2)), length, 6,
+    )
+    dproj = dproj.reshape(4 * span, 2 * r8)
     dnormed_one, block_output, back_two, rest_sums, squares_three = closing(
-        normed_one, dmz, dproj, mixed, mixer_first, mlp_part, residual,
-        down_terms, (down_cut, f8 - down_cut), sums_two, r8, length, 7,
-    )
-
-    gate_full_grad = contract_first(kept[4].reshape(4 * span, rc), dgate)
-    blocks = []
-    for h in range(heads):
-        at = slice(h * head, (h + 1) * head)
-        blocks.append(
-            jnp.concatenate([gate_full_grad[at, at], gate_full_grad[at, rc + h * head : rc + (h + 1) * head]], axis=1)
-        )
-    gate_grad_own = jnp.concatenate(blocks)
-    chan_grad = jnp.sum(chan_grad, axis=1)[:, :r8]
-    chan_grad = jnp.concatenate([chan_grad[:7], (8.0 * jax.nn.sigmoid(-lam) * chan_grad[7])[None]])
-    gate_back = jnp.concatenate([gate_grad_own, chan_grad.T], axis=1).reshape(length, gate_rows, 2 * head + 8)
-    gate_back = jnp.pad(
-        gate_back, ((0, 0), (0, gate_pad - gate_rows), (0, rc - 2 * head - 8))
-    )
-    gate_back = jnp.roll(gate_back, -z, axis=0)
-    rest_back, input_grad, *small, norm, factor = last(
+        normed_one, dmz, dproj, mixed, mixer_full, mlp_part, residual,
+        down_two, (0, h2), sums_two, r8, length, 7,
+    )
+
+    rest_back, input_grad, gains_sum, gates_sum, norm, factor = last(
         rest_sums.reshape(8, share, rest_sums.shape[1]), dnormed_one, inputs, grad_residual, gains, gain_two,
-        gate_back, squares_one + squares_two + squares_three,
+        gate_back, (squares_one, squares_two, squares_three), length, 8,
+    )
+    *mixer_up, small = adam_rows(
+        mixer_weight, (rest_back,), ([(h2 + n * r8, r8, n * lru, r8) for n in range(3)],),
+        first_mixer, second_mixer, factor, rate_matrix, decay_matrix,
         (
-            norm_gains, first_gains, second_gains, gate_weight, first_gate, second_gate,
+            gains_sum, gates_sum, norm_gains, first_gains, second_gains, gate_weight, first_gate, second_gate,
             chan_params, first_chan, second_chan,
         ),
-        length, 8,
     )
     gains_up, gate_up, chan_up = small[:3], small[3:6], small[6:]
-    rest = f8 - down_cut
-    mixer_up = adam_rows(
-        mixer_weight, (rest_back,), ([(rest + n * r8, r8, n * lru, r8) for n in range(3)],),
-        first_mixer, second_mixer, factor, rate_matrix, decay_matrix,
-    )
     mlp_up = adam_rows(
         mlp_weight, (back_one, back_two, rest_back),
         (
-            [(0, f8, 0, f8), (f8, up_cut, hidden, f8)],
-            [(0, f8 - up_cut, hidden + up_cut, f8), (f8 - up_cut, down_cut, 2 * hidden, f8)],
-            [(0, rest, 2 * hidden + down_cut, f8)],
+            [(0, h1, 0, f8), (h1, h1, hidden, f8), (2 * h1, down_cut, 2 * hidden, f8)],
+            [
+                (0, h1 - down_cut, 2 * hidden + down_cut, f8),
+                (h1 - down_cut, h2, h1, f8),
+                (h1 - down_cut + h2, h2, hidden + h1, f8),
+            ],
+            [(0, h2, 2 * hidden + h1, f8)],
         ),
         first_mlp, second_mlp, factor, rate_matrix, decay_matrix,
     )

time: 736 us -> 665 us (0.904)
  matrix products: 29.4 us -> 0 us
  local copies, waits for them, and re-layouts: 29.2 us -> 7.99 us
  Pallas kernels: 666 us -> 654 us
    dot_general x4 -> x0, matrix products: 29.4 us -> none  [the longest x1 8.56 us: on_device(): jnp.dot(dmz, mixer_last, preferred_element_type=F32).reshape(4, span, rc)]
    unnamed x102 -> x7, local copies, waits for them, and re-layouts: 25.2 us -> 3.86 us
    pallas_call x5 -> x7, Pallas kernels: 238 us -> 253 us  [the longest x1 70.3 us: recur_backward(): pl.pallas_call(functools.partial(backward_kernel, length, cuts, head), ou...]
    pallas_call x1, Pallas kernels: 112 us -> 101 us  [middle(): pl.pallas_call(functools.partial(middle_kernel, length), out_shape=(jax.S...]
    pallas_call x1, Pallas kernels: 98.4 us -> 87.7 us  [first(): pl.pallas_call(functools.partial(first_kernel, length), out_shape=(jax.Sh...]
    pallas_call x1, Pallas kernels: 106 us -> 95.8 us  [closing(): pl.pallas_call(functools.partial(closing_kernel, length, cut, part), out_...]
where the time goes in v5:
time: 665 us; the launch traced here: 664 us
  Pallas kernels  654 us (98%)
  local copies, waits for them, and re-layouts  7.99 us (1%)
    pallas_call x1, Pallas kernels, middle(): pl.pallas_call(functools.partial(middle_kernel, length), out_shape=(jax.S...  101 us
    pallas_call x1, Pallas kernels, turn(): pl.pallas_call(functools.partial(turn_kernel, length, cuts), out_shape=(j...  96.3 us
    pallas_call x1, Pallas kernels, closing(): pl.pallas_call(functools.partial(closing_kernel, length, cut, part), out_...  95.8 us
    pallas_call x1, Pallas kernels, first(): pl.pallas_call(functools.partial(first_kernel, length), out_shape=(jax.Sh...  87.7 us
    pallas_call x1, Pallas kernels, recur_backward(): pl.pallas_call(functools.partial(backward_kernel, length, cuts, head), ou...  70.3 us
    pallas_call x1, Pallas kernels, recur_forward(): pl.pallas_call(functools.partial(forward_kernel, length), out_shape=(jax....  55.9 us
    pallas_call x1, Pallas kernels, late_feed(): pl.pallas_call(late_feed_kernel, grid=(8,), out_shape=tuple((jax.ShapeDty...  34.7 us
    pallas_call x1, Pallas kernels, last(): pl.pallas_call(functools.partial(last_kernel, length, share), out_shape=(...  34.4 us

profile of v5, /device:TPU:0, one launch (start us, length us, event | category | flops | bytes accessed | tf_op | source)
XLA Modules:
  0.0 664.0 jit_solution(8036729526507567722)
XLA Ops:
  0.7 0.0 copy-start.1
  0.7 87.7 %shard_map.304 = (bf16[8,256,2048]{2,1,0:T(8,128)(2,1)}, bf16[4,8,64,960]{3,2,1,0:T(8,128)(2,1)}, bf16[4,8,64,1024]{3,2,1,0:T(8,128)(2,1)}, bf16[4,8,64,512]{3,2...) custom-call(bf16[256,2048]{1,0:T(8,128)(2,1)} %bitcast.53, ...), custom_call_target="tpu_custom_call" | custom-call | bytes 314572800 | tf_op jit(solution)/shard_map/pallas_call | solution.py:1041
  88.4 1.0 slice.42
  89.4 0.1 copy.44
  89.5 0.0 copy-done.1
  89.5 0.7 pad_maximum_fusion.chan
  90.2 1.1 fusion.16
  91.3 0.1 fusion.13
  91.4 0.9 pad.22.gate
  92.3 55.9 %shard_map.305 = (bf16[4,512,320]{2,1,0:T(8,128)(2,1)}, f32[4,512,384]{2,1,0:T(8,128)}, f32[4,512,384]{2,1,0:T(8,128)}, f32[4,512,384]{2,1,0:T(8,128)}, f32[4,51...) custom-call(bf16[2048,2048]{1,0:T(8,128)(2,1)} %bitcast.35, ...), custom_call_target="tpu_custom_call", output_to_operand_aliasing={{12}: (6, {})} | custom-call | flops 1207959552 | bytes 104857600 | tf_op jit(solution)/shard_map/pallas_call | solution.py:1421
  148.2 101.2 %shard_map.306 = (f32[256,2048]{1,0:T(8,128)}, bf16[8,256,2048]{2,1,0:T(8,128)(2,1)}, bf16[4,8,64,1024]{3,2,1,0:T(8,128)(2,1)}, bf16[4,8,64,768]{3,2,1,0:T(8,128)(2,1)}) custom-call(bf16[2048,320]{1,0:T(8,128)(2,1)} %bitcast.49, bf16[2048,960]{1,0:T(8,128)(2,1)} %bitcast.32, ...), custom_call_target="tpu_custom_call", output_to_operand_aliasing={{2}: (4, {}), {3}: (5, {})} | custom-call | bytes 314572800 | tf_op jit(solution)/shard_map/pallas_call | solution.py:603
  249.5 22.4 %shard_map.307 = (bf16[2048,512]{1,0:T(8,128)(2,1)}, bf16[2048,512]{1,0:T(8,128)(2,1)}, bf16[2048,512]{1,0:T(8,128)(2,1)}, bf16[4,8,64,768]{3,2,1,0:T(8,128)(2,1)}) custom-call(bf16[2048,2048]{1,0:T(8,128)(2,1)} %bitcast.66, bf16[2048,2048]{1,0:T(8,128)(2,1)} %bitcast.61, bf16[2048,1024]{1,0:T(8,128)(2,1)} %bitcast.40, ...), custom_call_target="tpu_custom_call", output_to_operand_aliasing={{3}: (4, {})} | custom-call | flops 12884901888 | bytes 31457280 | tf_op jit(solution)/shard_map/pallas_call | solution.py:1725
  271.9 21.6 %shard_map.308 = (bf16[2048,512]{1,0:T(8,128)(2,1)}, bf16[2048,512]{1,0:T(8,128)(2,1)}, bf16[2048,512]{1,0:T(8,128)(2,1)}, bf16[4,8,64,768]{3,2,1,0:T(8,128)(2,1)}) custom-call(bf16[2048,2048]{1,0:T(8,128)(2,1)} %bitcast.67, bf16[2048,2048]{1,0:T(8,128)(2,1)} %bitcast.62, ...), custom_call_target="tpu_custom_call", output_to_operand_aliasing={{3}: (5, {})} | custom-call | flops 12884901888 | bytes 41943040 | tf_op jit(solution)/shard_map/pallas_call | solution.py:1800
  293.5 34.7 %shard_map.309 = (bf16[2048,256]{1,0:T(8,128)(2,1)}, bf16[2048,256]{1,0:T(8,128)(2,1)}, bf16[2048,256]{1,0:T(8,128)(2,1)}, bf16[2048,2048]{1,0:T(8,128)(2,1)}, bf16[2048,2048]{1,0:T(8,128)(2,1)}) custom-call(bf16[2048,2048]{1,0:T(8,128)(2,1)} %bitcast.68, bf16[2048,2048]{1,0:T(8,128)(2,1)} %bitcast.63, bf16[2048,512]{1,0:T(8,128)(2,1)} %get-tuple-element.113.hid.hid_one, ...), custom_call_target="tpu_custom_call" | custom-call | flops 25769803776 | bytes 62914560 | tf_op jit(solution)/shard_map/pallas_call | solution.py:1760
  328.2 13.7 %shard_map.311 = (bf16[2048,256]{1,0:T(8,128)(2,1)}, bf16[2048,256]{1,0:T(8,128)(2,1)}, bf16[2048,256]{1,0:T(8,128)(2,1)}) custom-call(bf16[2048,2048]{1,0:T(8,128)(2,1)} %bitcast.69, bf16[2048,2048]{1,0:T(8,128)(2,1)} %bitcast.64, bf16[2048,256]{1,0:T(8,128)(2,1)} %get-tuple-element.135.hid, bf16[2048,256]{1,0:T(8,128)(2,1)} %get-tuple-element.136.dgate, ...), custom_call_target="tpu_custom_call" | custom-call | flops 6442450944 | bytes 41943040 | tf_op jit(solution)/shard_map/pallas_call | solution.py:1791
  341.9 96.3 %shard_map.310 = (f32[256,2048]{1,0:T(8,128)}, f32[8,2048]{1,0:T(8,128)}, bf16[8,256,2048]{2,1,0:T(8,128)(2,1)}, f32[2048,384]{1,0:T(8,128)}, bf16[512,1280]{1,0:T(8,128)(2,1)}, /*index=5*/f32[8,128]{1,0:T(8,128)}) custom-call(bf16[8,256,2048]{2,1,0:T(8,128)(2,1)} %bitcast.37, f32[256,2048]{1,0:T(8,128)} %get-tuple-element.119.residual, ...), custom_call_target="tpu_custom_call" | custom-call | bytes 314572800 | tf_op jit(solution)/shard_map/pallas_call | solution.py:684
  438.2 70.3 %shard_map.312 = (bf16[4,512,640]{2,1,0:T(8,128)(2,1)}, f32[4,80,384]{2,1,0:T(8,128)}, bf16[512,768]{1,0:T(8,128)(2,1)}, f32[8,128]{1,0:T(8,128)}, bf16[8,64,1280]{2,1,0:T(8,128)(2,1)}) custom-call(f32[4,512,384]{2,1,0:T(8,128)} %bitcast.42, bf16[384,768]{1,0:T(8,128)(2,1)} %pad.22.gate, f32[8,384]{1,0:T(8,128)} %pad_maximum_fusion.chan, ...), custom_call_target="tpu_custom_call" | custom-call | flops 1207959552 | bytes 125829120 | tf_op jit(solution)/shard_map/pallas_call | solution.py:1617
  508.5 95.8 %shard_map.313 = (f32[256,2048]{1,0:T(8,128)}, bf16[256,2048]{1,0:T(8,128)(2,1)}, bf16[8,64,768]{2,1,0:T(8,128)(2,1)}, bf16[512,1216]{1,0:T(8,128)(2,1)}, f32[8,128]{1,0:T(8,128)}) custom-call(bf16[2048,2048]{1,0:T(8,128)(2,1)} %bitcast.36, bf16[2048,2048]{1,0:T(8,128)(2,1)} %bitcast.65, bf16[2048,640]{1,0:T(8,128)(2,1)} %bitcast.70, ...), custom_call_target="tpu_custom_call" | custom-call | flops 13421772800 | bytes 367001600 | tf_op jit(solution)/shard_map/pallas_call | solution.py:833
  604.3 34.4 %shard_map.314 = (bf16[8,64,1216]{2,1,0:T(8,128)(2,1)}, f32[256,2048]{1,0:T(8,128)}, f32[2,64]{1,0:T(2,128)}, f32[80,384]{1,0:T(8,128)}, f32[8,128]{1,0:T(8,128)}, /*index=5*/f32[8,128]{1,0:T(8,128)}) custom-call(bf16[8,64,1216]{2,1,0:T(8,128)(2,1)} %bitcast.52, f32[256,2048]{1,0:T(8,128)} %get-tuple-element.146.total, ...), custom_call_target="tpu_custom_call" | custom-call | tf_op jit(solution)/shard_map/pallas_call | solution.py:1200
  638.7 1.2 slice.37
  639.8 7.0 %shard_map.315 = (f32[64,7680]{1,0:T(8,128)}, f32[64,7680]{1,0:T(8,128)}, f32[64,7680]{1,0:T(8,128)}, f32[2,64]{1,0:T(2,128)}, f32[2,64]{1,0:T(2,128)}, /*index=...) custom-call(f32[8,128]{1,0:T(8,128)} %get-tuple-element.155.factor, ...), custom_call_target="tpu_custom_call" | custom-call | bytes 13762560 | tf_op jit(solution)/shard_map/pallas_call | solution.py:1871
  646.9 13.3 %shard_map.316 = (f32[64,18432]{1,0:T(8,128)}, f32[64,18432]{1,0:T(8,128)}, f32[64,18432]{1,0:T(8,128)}) custom-call(f32[8,128]{1,0:T(8,128)} %get-tuple-element.155.factor, f32[64,18432]{1,0:T(8,128)} %w.3, f32[64,18432]{1,0:T(8,128)} %m.3, f32[64,18432]{1,0:T(8,128)} %v.3, bf16[8,64,1280]{2,1,0:T(8,128)(2,1)} %get-tuple-element.171.refs_0_, ...), custom_call_target="tpu_custom_call" | custom-call | bytes 33030144 | tf_op jit(solution)/shard_map/pallas_call | solution.py:1871
  660.2 0.0 copy-start
  660.2 2.5 copy.52
  662.7 0.0 copy-done
  662.7 1.3 copy.53
  (2 shorter events, 0.0 us)
Async XLA Ops:
  0.7 88.8 %copy-start.1 = (f32[8,64]{1,0:T(8,128)S(1)}, f32[8,64]{1,0:T(8,128)}, u32[]{:S(2)}) copy-start(f32[8,64]{1,0:T(8,128)} %constant.9.clone.1) | copy-start | bytes 6148
  660.2 2.5 copy-start

commit v6 on v5

--- a/solution.py
+++ b/solution.py
@@ -135,19 +135,20 @@
         self.s6.wait_recv()
         self.last.append(self.relay(self.bd, self.hi, 12, self.to_c))
 
-    def finish(self):
-        for copy in self.last:
+    def finish(self, skip=0, own=True):
+        for copy in self.last[skip:]:
             copy.wait_recv()
         for copy in self.done:
             copy.wait_send()
-        self.own.wait()
+        if own:
+            self.own.wait()
 
     def end(self, mark=lambda: None):
         self.relays(mark)
         self.finish()
 
 
-def scatter_steps(p, o, mine, sib, part, got, loc, ss, rs):
+def scatter_steps(p, o, mine, sib, part, got, loc, ss, rs, prepare=None):
     y, c, z, x = place()
     to_x, to_y, to_c = gather_peers()
     half = o.shape[0] // 2
@@ -158,6 +159,9 @@
     from_c, own, sends = {}, {}, []
     for n, (t, h) in enumerate(order):
         ty, tx = where[t]
+        if prepare and all(key[0] != t for key in own):
+            prepare(rank(ty, c, tx))
+            prepare(rank(ty, 1 - c, tx))
         own[t, h] = pltpu.make_async_copy(
             p.at[rank(ty, c, tx), cut[h]], mine.at[t, h], loc.at[n]
         )
@@ -497,6 +501,25 @@
     ]
 
 
+def starts(copies):
+    for copy in copies:
+        copy.start()
+    return copies
+
+
+def waits(copies):
+    for copy in copies:
+        copy.wait()
+
+
+def local_copies(pairs, sems):
+    return [pltpu.make_async_copy(src, dst, sems.at[n]) for n, (src, dst) in enumerate(pairs)]
+
+
+def held(*arrays):
+    return [pltpu.VMEM(v.shape, v.dtype) for v in arrays]
+
+
 LINE_REFS = 8
 SCATTER_REFS = 7
 TILE = jax.ShapeDtypeStruct((8, 128), F32)
@@ -546,8 +569,14 @@
     return inverse * (moved - scaled * inner), fold(grad * scaled)
 
 
-def middle_kernel(length, mixed, mixer, inputs, gains, w_in, late_in, residual, normed_o, w, late, *scratch):
-    scatter_refs, (p, low, loc, gs, gr, hs, hr, late_s, late_r) = scratch[:SCATTER_REFS], scratch[SCATTER_REFS:]
+def middle_kernel(length, mixed_in, mixer_in, inputs_in, gains_in, w_in, late_in, residual_o, normed_o, w, late, *scratch):
+    scatter_refs, (p, low, loc, gs, gr, hs, hr, late_s, late_r, *scratch) = scratch[:SCATTER_REFS], scratch[SCATTER_REFS:]
+    mixed, mixer, inputs, gains, residual, load_s, keep_s = scratch
+    loads = starts(
+        local_copies(
+            ((mixed_in, mixed), (mixer_in, mixer), (inputs_in, inputs), (gains_in, gains)), load_s
+        )
+    )
     greet(gather_peers() + line_neighbours(length))
     hops = LineGather(w, length, hs, hr)
     hops.start(1)
@@ -557,13 +586,13 @@
     part = mixed.shape[1]
     rows, width = low.shape
 
-    @pl.loop(0, 4)
-    def _(i):
-        mine = mixed[pl.ds(pl.multiple_of(i * 2 * rows, rows), 2 * rows)]
+    waits(loads[:2])
+
+    def prepare(i):
+        mine = mixed[pl.ds(pl.multiple_of(i * rows, rows), rows)]
         for first_column in range(0, width, 512):
             at = slice(first_column, first_column + 512)
-            both = contract_last(mine, mixer[at, 2 * part :]).astype(BF16)
-            p[pl.ds(2 * i, 2), :, at] = both.reshape(2, rows, 512)
+            p[i, :, at] = contract_last(mine, mixer[at, 2 * part :]).astype(BF16)
 
     def advance():
         if started[0] < length - 1:
@@ -578,18 +607,21 @@
 
     half = low.shape[0] // 2
     gather = Gather(low, normed_o, loc, gs, gr)
-    for name in scatter_steps(p, residual, *scatter_refs):
+    for name in scatter_steps(p, residual, *scatter_refs, prepare=prepare):
         if name == "late":
             advance()
         if name == "low half":
+            waits(loads[2:])
             rows_loop(half, body)
             gather.begin_half(0)
         if name == "high half":
             rows_loop(half, body, half)
             gather.begin_half(1)
+    keeps = starts(local_copies(((residual, residual_o),), keep_s))
     gather.middle()
     advance()
     gather.end()
+    waits(keeps)
     while started[0] < length - 1:
         advance()
     hops.arrive(length - 1)
@@ -608,27 +640,33 @@
             jax.ShapeDtypeStruct(w.shape, w.dtype),
             jax.ShapeDtypeStruct(late.shape, late.dtype),
         ),
-        in_specs=[VM, VM, VM, VM, ANY, ANY],
-        out_specs=(VM, ANY, ANY, ANY),
+        in_specs=[ANY] * 6,
+        out_specs=(ANY,) * 4,
         scratch_shapes=scatter_scratch(rows // 2, width)
         + [pltpu.VMEM((8, rows, width), BF16), pltpu.VMEM((rows, width), BF16), DMA, DMA((14,)), DMA((14,))]
-        + [DMA((2, length))] * 4,
+        + [DMA((2, length))] * 4
+        + held(mixed, mixer, inputs, gains)
+        + [pltpu.VMEM((rows, width), F32), DMA((4,)), DMA((1,))],
         input_output_aliases={4: 2, 5: 3},
         compiler_params=params(collective_id),
         cost_estimate=pl.CostEstimate(flops=0, bytes_accessed=300 * 2**20, transcendentals=0),
     )(mixed, mixer, inputs, gains, w, late)
 
 
-def turn_kernel(length, cuts, p, residual, above, gains, mixer, *refs):
+def turn_kernel(length, cuts, p, residual_in, above_in, gains_in, mixer_in, *refs):
     parts = 1 + max(cut[0] for cut in cuts)
     terms, refs = refs[:parts], refs[parts:]
-    back, gain, low_o, dmix, sums, squares, *scratch = refs
-    scatter_refs, (total, low, loc, gs, gr, parts_in, load_s), line_refs = (
-        scratch[:SCATTER_REFS], scratch[SCATTER_REFS : SCATTER_REFS + 7], scratch[SCATTER_REFS + 7 :]
+    back_o, gain, low_o, dmix_o, sums, squares, *scratch = refs
+    scatter_refs, scratch = scratch[:SCATTER_REFS], scratch[SCATTER_REFS:]
+    total, low, loc, gs, gr, parts_in, load_s, residual, above, gains, mixer, back, dmix, in_s, keep_s = scratch[:15]
+    line_refs = scratch[15:]
+    loads = local_copies(
+        ((residual_in, residual), (above_in, above), (gains_in, gains), (mixer_in, mixer)), in_s
     )
     greet(gather_peers() + line_neighbours(length))
     line = Lines(terms, cuts, length, line_refs)
     line.begin()
+    starts(loads)
     gain[...] = jnp.zeros_like(gain)
 
     def body(at):
@@ -644,38 +682,63 @@
         if name in ("early", "late"):
             line.start()
         if name == "low half":
+            waits(loads)
             rows_loop(half, body)
             gather.begin_half(0)
         if name == "high half":
             rows_loop(half, body, half)
             gather.begin_half(1)
             line.start()
+    keeps = starts(local_copies(((back, back_o),), keep_s))
+    rows = low.shape[0]
+    part = mixer.shape[1] // 3
+    y, c, z, x = place()
+    near = (gather.me, gather.bx), (gather.by, rank(y, 1 - c, x))
+    rest = (gather.bd, rank(1 - y, 1 - c, x)), (rank(y, 1 - c, 1 - x), rank(1 - y, 1 - c, 1 - x))
+
+    def fetch(blocks, slot):
+        copies = []
+        for n in (0, 1):
+            copies.append(
+                pltpu.make_async_copy(low_o.at[blocks[n]], parts_in.at[slot, n], load_s.at[slot, n])
+            )
+        return copies
+
+    def mix(blocks, slot):
+        waits(fetch(blocks, slot))
+        lines = parts_in[slot].reshape(2 * rows, parts_in.shape[3])
+        both = jnp.dot(lines, mixer[:, 2 * part :], preferred_element_type=F32)
+        none = jnp.zeros((rows, dmix.shape[2] - part), F32)
+        for n in (0, 1):
+            dmix[blocks[n]] = jnp.concatenate([both[n * rows : (n + 1) * rows], none], axis=1)
+            pltpu.make_async_copy(dmix.at[blocks[n]], dmix_o.at[blocks[n]], keep_s.at[1 + n + 2 * slot]).start()
+
+    def mixed(blocks, slot):
+        for n in (0, 1):
+            pltpu.make_async_copy(dmix.at[blocks[n]], dmix_o.at[blocks[n]], keep_s.at[1 + n + 2 * slot]).wait()
+
+    def near_blocks():
+        gather.own.wait()
+        for copy in gather.last[:2]:
+            copy.wait_recv()
+        starts(fetch(near[0], 0))
+        starts(fetch(near[1], 1))
+        mix(near[0], 0)
+        mix(near[1], 1)
+
     gather.middle()
     line.start()
-    gather.end()
-    rows = low.shape[0]
-    part = mixer.shape[1] // 3
-
-    def load(n, slot):
-        return pltpu.make_async_copy(low_o.at[pl.ds(2 * n, 2)], parts_in.at[slot], load_s.at[slot])
-
-    load(0, 0).start()
-
-    @pl.loop(0, 4)
-    def _(n):
-        slot = n - n // 2 * 2
-
-        @pl.when(n + 1 < 4)
-        def _():
-            load(n + 1, 1 - slot).start()
-
-        load(n, slot).wait()
-        lines = parts_in[slot].reshape(2 * rows, parts_in.shape[3])
-        mix = jnp.dot(lines, mixer[:, 2 * part :], preferred_element_type=F32)
-        none = jnp.zeros((2 * rows, dmix.shape[1] - part), F32)
-        dmix[pl.ds(pl.multiple_of(n * 2 * rows, rows), 2 * rows)] = jnp.concatenate([mix, none], axis=1)
-
+    gather.relays(near_blocks)
+    gather.finish(2, own=False)
+    for n in (0, 1):
+        mixed(near[n], n)
+        starts(fetch(rest[n], n))
+    for n in (0, 1):
+        mix(rest[n], n)
+    waits(keeps)
     line.end(sums, squares)
+    for n in (0, 1):
+        mixed(rest[n], n)
 
 
 def turn(p, residual, above, gains, mixer, rc, terms, cuts, length, collective_id):
@@ -687,15 +750,17 @@
             jax.ShapeDtypeStruct((rows, width), F32),
             jax.ShapeDtypeStruct((8, width), F32),
             jax.ShapeDtypeStruct((8, rows, width), BF16),
-            jax.ShapeDtypeStruct((8 * rows, rc), F32),
+            jax.ShapeDtypeStruct((8, rows, rc), F32),
             jax.ShapeDtypeStruct((line_rows, columns), BF16),
             TILE,
         ),
-        in_specs=[ANY, VM, VM, VM, VM] + [ANY] * len(terms),
-        out_specs=(VM, VM, ANY, VM, VM, VM),
+        in_specs=[ANY] * (5 + len(terms)),
+        out_specs=(ANY, VM, ANY, ANY, VM, VM),
         scratch_shapes=scatter_scratch(rows // 2, width)
         + [pltpu.VMEM((rows, width), F32), pltpu.VMEM((rows, width), BF16), DMA, DMA((14,)), DMA((14,))]
-        + [pltpu.VMEM((2, 2, rows, width), BF16), DMA((2,))]
+        + [pltpu.VMEM((2, 2, rows, width), BF16), DMA((2, 2))]
+        + held(residual, above, gains, mixer)
+        + [pltpu.VMEM((rows, width), F32), pltpu.VMEM((8, rows, rc), F32), DMA((4,)), DMA((5,))]
         + lines_scratch(length, line_rows, cuts),
         compiler_params=params(collective_id),
         cost_estimate=pl.CostEstimate(flops=0, bytes_accessed=300 * 2**20, transcendentals=0),
@@ -703,14 +768,42 @@
 
 
 def closing_kernel(
-    length, cut, part, x_in, dmz_in, dproj, mixed, mixer, q, residual, terms, block,
-    o, out, e_o, sums, squares,
-    x_part, dmz_part, g, back, total, up_a, down_a, up_b, down_b, ls, lr, load_s, free, loc, es, er, *scratch,
+    length, x_in, dmz_in, dproj_in, mixed_in, mixer_in, q, residual_in, block, inputs_in, above_in, gains_in, gp_in,
+    grad_out, gain, gates_o, out_out, e_o, sums, squares,
+    x_part, dmz_part, g, back, total, o, up_a, down_a, up_b, down_b, gp_got, gp_sum,
+    ls, lr, load_s, free, loc, es, er, gate_s, gate_r, move_s, move_r,
+    dproj, mixed, mixer, residual, inputs, above, gains, gp, grad_o, out, in_s, keep_s, *scatter_refs,
 ):
-    scatter_refs, line_refs = scratch[:SCATTER_REFS], scratch[SCATTER_REFS:]
-    greet(plane_peers() + line_neighbours(length))
+    inflow = starts(
+        local_copies(
+            (
+                (gp_in, gp), (dproj_in, dproj), (mixed_in, mixed), (mixer_in, mixer), (residual_in, residual),
+                (inputs_in, inputs), (above_in, above), (gains_in, gains),
+            ),
+            in_s,
+        )
+    )
+    y, c, z, x = place()
+    others = line_peers(length)
+    s = 2 * z + x
+    owner = x * length + z
+    to_z = owner // 2
+    to_x = owner - 2 * to_z
+    from_z, from_x = lax.rem(s, length), s // length
+    moves = jnp.where(jnp.logical_and(to_z == z, to_x == x), 0, 1)
+    barrier = pltpu.get_barrier_semaphore()
+    for peer in others + plane_peers():
+        pl.semaphore_signal(barrier, inc=1, device_id=peer, device_id_type=MESH)
+
+    @pl.when(moves == 1)
+    def _():
+        pl.semaphore_signal(barrier, inc=1, device_id=device(y, c, to_z, to_x), device_id_type=MESH)
+        pl.semaphore_signal(barrier, inc=1, device_id=device(y, c, from_z, from_x), device_id_type=MESH)
+
+    pl.semaphore_wait(barrier, len(others) + 7 + 2 * moves)
     model = mixer.shape[0]
     tokens = dproj.shape[0]
+    part = mixed.shape[1]
     columns = x_part.shape[2]
     steps = model // columns
     rows = tokens // steps
@@ -731,10 +824,11 @@
             copy.start()
 
     fetch(order[0] * group, 0)
-    rest = LineScatter([(terms, *cut)], length, *line_refs)
-    rest.load((1,))
-    rest.start()
-    rest.load((*range(2, length), 0))
+    inflow[0].wait()
+    gate = [
+        remote(gp.at[lax.rem(z + k + 1, length)], gp_got.at[k], gate_s.at[k], gate_r.at[k], others[k])
+        for k in range(length - 1)
+    ]
     split = up_a.shape[2]
     line_a = HeldLine(g, 0, up_a, down_a, ls.at[0], lr.at[0])
     line_b = HeldLine(g, split, up_b, down_b, ls.at[1], lr.at[1])
@@ -780,19 +874,18 @@
                 cols = slice(first_column, first_column + 512)
                 back[block_of, at, cols] = contract_last(mine, mixer[cols, : 2 * part]).astype(BF16)
 
+    waits(inflow[1:4])
     compute(0)
     next(output)
-    rest.start()
     compute(1)
-    while rest.next < length:
-        rest.start()
     if length == 4:
         advance(2)
     next(output)
     compute(2)
     next(output)
     compute(3)
-    advance(1 if length == 4 else 2)
+    if length != 4:
+        advance(2)
     for _ in output:
         pass
     for peer in gather_peers():
@@ -803,68 +896,111 @@
     next(incoming)
     pair = out.shape[1] // (4 * length)
 
-    def body(at):
+    def finish_output(at):
         store_turned(out, at, (residual[at] + total[at]).astype(BF16), length, pair)
 
-    rows_loop(out.shape[0], body)
-    squares[...] = jnp.zeros_like(squares)
-    rest.end(sums, 0, squares)
+    waits(inflow[4:])
+    rows_loop(out.shape[0], finish_output)
+    keeps = local_copies(((out, out_out), (grad_o, grad_out)), keep_s)
+    keeps[0].start()
+    for copy in gate:
+        copy.wait()
+    rows_sum = gp[z]
+    for k in range(length - 1):
+        rows_sum = rows_sum + gp_got[k]
+    gp_sum[...] = rows_sum
+    move = pltpu.make_async_remote_copy(
+        src_ref=gp_sum, dst_ref=gates_o, send_sem=move_s, recv_sem=move_r,
+        device_id=device(y, c, to_z, to_x), device_id_type=MESH,
+    )
+    pl.when(moves == 1)(lambda: move.start())
+
+    @pl.when(moves == 0)
+    def _():
+        gates_o[...] = rows_sum
+
+    gain[...] = jnp.zeros_like(gain)
+
+    def finish_grad(at):
+        grad, gain_part = norm_rows_back(inputs[at].astype(F32), gains[0:1], o[at])
+        store_turned(grad_o, at, above[at] + grad, length, pair)
+        gain[...] += gain_part
+
+    half = grad_o.shape[0] // 2
     for name in incoming:
-        if name in ("sent", "late"):
+        if name in ("sent", "early", "late"):
             advance()
+        if name == "low half":
+            rows_loop(half, finish_grad)
+        if name == "high half":
+            rows_loop(half, finish_grad, half)
+            keeps[1].start()
     while queue:
         advance()
-    line_a.end(sums, cut[1], squares)
-    line_b.end(sums, cut[1] + split, squares)
+    squares[...] = jnp.zeros_like(squares)
+    line_a.end(sums, 0, squares)
+    line_b.end(sums, split, squares)
+    pl.when(moves == 1)(lambda: move.wait())
+    waits(keeps)
     for copy in copies:
         copy.wait()
     own.wait()
 
 
-def closing(x, dmz, dproj, mixed, mixer, q, residual, terms, cut, block, part, length, collective_id):
+def closing(x, dmz, dproj, mixed, mixer, q, residual, block, inputs, above, gains, gp, length, collective_id):
     rows, width = residual.shape
     tokens, model = x.shape
+    part = mixed.shape[1]
     share = block.shape[0] // 8
     block = block.reshape(8, share, block.shape[1])
-    line_rows = terms.shape[1]
+    line_rows = model // length
     columns = min(256, line_rows)
     split = -(-3 * part // 256) * 128
-    held_a, held_b = (pltpu.VMEM((length - 1, line_rows, n), BF16) for n in (split, 3 * part - split))
+    slots_a, slots_b = (pltpu.VMEM((length - 1, line_rows, n), BF16) for n in (split, 3 * part - split))
+    pack = gp.shape[1:]
     return pl.pallas_call(
-        functools.partial(closing_kernel, length, cut, part),
+        functools.partial(closing_kernel, length),
         out_shape=(
             jax.ShapeDtypeStruct((rows, width), F32),
+            jax.ShapeDtypeStruct((8, width), F32),
+            jax.ShapeDtypeStruct(pack, F32),
             jax.ShapeDtypeStruct((rows, width), BF16),
             jax.ShapeDtypeStruct(block.shape, BF16),
-            jax.ShapeDtypeStruct((line_rows, cut[1] + 3 * part), BF16),
+            jax.ShapeDtypeStruct((line_rows, 3 * part), BF16),
             TILE,
         ),
-        in_specs=[ANY, ANY, VM, VM, VM, ANY, VM, ANY, ANY],
-        out_specs=(VM, VM, ANY, VM, VM),
+        in_specs=[ANY] * 12,
+        out_specs=(ANY, VM, VM, ANY, ANY, VM, VM),
         scratch_shapes=[
             pltpu.VMEM((2, tokens, columns), BF16),
             pltpu.VMEM((2, tokens, columns), BF16),
             pltpu.VMEM((length, line_rows, 3 * part), BF16),
             pltpu.VMEM((8, rows, width), BF16),
             pltpu.VMEM((rows, width), F32),
-            held_a, held_a, held_b, held_b,
+            pltpu.VMEM((rows, width), F32),
+            slots_a, slots_a, slots_b, slots_b,
+            pltpu.VMEM((length - 1,) + pack, F32),
+            pltpu.VMEM(pack, F32),
             DMA((2, 2, length)), DMA((2, 2, length)), DMA((2, 2)), pltpu.SemaphoreType.REGULAR,
-            DMA, DMA((7,)), DMA((7,)),
+            DMA, DMA((7,)), DMA((7,)), DMA((length,)), DMA((length,)), DMA, DMA,
+            *held(dproj, mixed, mixer, residual, inputs, above, gains, gp),
+            pltpu.VMEM((rows, width), F32),
+            pltpu.VMEM((rows, width), BF16),
+            DMA((8,)), DMA((2,)),
         ]
-        + scatter_scratch(rows // 2, width)
-        + line_scratch(length, line_rows, cut[1], 1),
+        + scatter_scratch(rows // 2, width),
         compiler_params=params(collective_id),
         cost_estimate=pl.CostEstimate(
             flops=10 * tokens * model * dproj.shape[1] // 2, bytes_accessed=350 * 2**20, transcendentals=0
         ),
-    )(x, dmz, dproj, mixed, mixer, q.reshape(8, rows, width), residual, terms, block)
+    )(x, dmz, dproj, mixed, mixer, q.reshape(8, rows, width), residual, block, inputs, above, gains, gp)
 
 
 def first_kernel(
     length, inputs_in, above_in, mixer_in, mlp_in, gains_in, gate_in, chan_in,
-    normed_o, wm_o, wf_o, wd_o, w2, gains_o, gp_o, inputs_o, above_o,
+    normed_o, wm_o, wf_o, wd_o, w2, gains_o, gate_o, chan_o, inputs_o, above_o,
     inputs, above, mixer_w, mlp_w, gains_w, gate_w, chan_w, load_s,
-    gn, gp, normed, gn_all, wm, wf, wd, loc, ms, mr, fs, fr, line_s, line_r, gain_s, gain_r, move_s, move_r,
+    gp_o, gn, gp, normed, gn_all, wm, wf, wd, loc, ms, mr, fs, fr, line_s, line_r, gain_s, gain_r, move_s, move_r,
     gather_s, gather_r, hop_s, hop_r,
 ):
     loads = [
@@ -899,8 +1035,16 @@
         pl.semaphore_signal(barrier, inc=1, device_id=device(y, c, to_z, to_x), device_id_type=MESH)
         pl.semaphore_signal(barrier, inc=1, device_id=device(y, c, from_z, from_x), device_id_type=MESH)
 
-    pl.semaphore_wait(barrier, len(line) + len(plane) + 2 * moves)
-
+    def fill(pack, source, js, offset=0):
+        part = pack.shape[2] // len(js)
+        whole = source.shape[1] // 24
+        for t in range(8):
+            for n, j in enumerate(js):
+                start = (j * 8 + t) * whole + offset
+                pack[t, :, n * part : (n + 1) * part] = source[:, start : start + part].astype(BF16)
+
+    loads[3].wait()
+    fill(wm, mixer_w, (0, 1, 2))
     for copy in loads[:3]:
         copy.wait()
     share = gains_w.shape[1]
@@ -922,6 +1066,7 @@
         axis=1,
     ).astype(BF16)
     gn_all[me, z] = gn[...]
+    pl.semaphore_wait(barrier, len(line) + len(plane) + 2 * moves)
     gains = [
         remote(gn, gn_all.at[me, z], line_s.at[0, k], line_r.at[0, k], line[k]) for k in range(length - 1)
     ]
@@ -933,45 +1078,35 @@
     pl.when(moves == 1)(lambda: gate_move.start())
     pl.when(moves == 0)(lambda: gate_stay.start())
 
-    def fill(pack, source, js, offset=0):
-        part = pack.shape[2] // len(js)
-        whole = source.shape[1] // 24
-        for t in range(8):
-            for n, j in enumerate(js):
-                start = (j * 8 + t) * whole + offset
-                pack[t, :, n * part : (n + 1) * part] = source[:, start : start + part].astype(BF16)
-
-    loads[3].wait()
-    fill(wm, mixer_w, (0, 1, 2))
     mixer, mixer_own = exchange_steps(wm, wm_o.at[0], loc.at[0], ms, mr)
+    hops = LineGather(wm_o, length, hop_s, hop_r)
+    mixer_own.wait()
+    hops.start_piece(me)
+
+    def pass_piece(n):
+        fy, fc, fx = FLIPS[n]
+        mixer[n].wait_recv()
+        hops.start_piece(rank(flip(y, fy), flip(c, fc), flip(x, fx)))
+
+    pass_piece(1)
     for copy in gains:
         copy.wait()
     spread = [
         remote(gn_all.at[me], gn_all.at[me], gain_s.at[n], gain_r.at[n], plane[n]) for n in range(7)
     ]
+    loads[4].wait()
+    fill(wd, mlp_w, (2,))
+    down, down_own = exchange_steps(wd, wd_o.at[0], loc.at[4], fs.at[1], fr.at[1])
+    for n in (0, 2, 3, 5, 4, 6):
+        pass_piece(n)
+    fill(wf, mlp_w, (0, 1))
+    feed, feed_own = exchange_steps(wf, wf_o.at[0], loc.at[3], fs.at[0], fr.at[0])
     pl.when(moves == 1)(lambda: gate_move.wait())
     pl.when(moves == 0)(lambda: gate_stay.wait())
     gates = [
         remote(gp_o.at[z], gp_o.at[z], line_s.at[1, k], line_r.at[1, k], line[k])
         for k in range(length - 1)
     ]
-    hops = LineGather(wm_o, length, hop_s, hop_r)
-    mixer_own.wait()
-    hops.start_piece(me)
-
-    def pass_piece(n):
-        fy, fc, fx = FLIPS[n]
-        mixer[n].wait_recv()
-        hops.start_piece(rank(flip(y, fy), flip(c, fc), flip(x, fx)))
-
-    pass_piece(1)
-    loads[4].wait()
-    fill(wd, mlp_w, (2,))
-    down, down_own = exchange_steps(wd, wd_o.at[0], loc.at[4], fs.at[1], fr.at[1])
-    fill(wf, mlp_w, (0, 1))
-    feed, feed_own = exchange_steps(wf, wf_o.at[0], loc.at[3], fs.at[0], fr.at[0])
-    for n in (0, 2, 3, 5, 4, 6):
-        pass_piece(n)
     fill(w2, mlp_w, (0, 1, 2), wd.shape[2])
     for copy in spread:
         copy.wait()
@@ -1012,7 +1147,31 @@
         if hop + 1 < length:
             hops.start(hop + 1)
     gather.finish()
-    for copy in down + feed + gates:
+    for copy in gates:
+        copy.wait()
+    gate_rows, columns = gate_w.shape
+    head = columns // 2
+    own = jnp.concatenate([gp_o[n, :gate_rows].astype(F32) for n in range(length)]).astype(BF16)
+    part, rc = own.shape[0], gate_o.shape[0]
+    gate_o[...] = jnp.zeros_like(gate_o)
+    for first_row in range(0, part, head):
+        at = slice(first_row, first_row + head)
+        wide = [jnp.zeros((head, first_row), F32)] if first_row else []
+        for n in (0, 1):
+            block = own[at, n * head : (n + 1) * head].astype(F32)
+            rest = jnp.zeros((head, rc - first_row - head), F32)
+            gate_o[at, n * rc : (n + 1) * rc] = jnp.concatenate([*wide, block, rest], axis=1).astype(BF16)
+    rows_of = contract_last(unit(8), own[:, columns : columns + 8])
+    lam = rows_of[7:8]
+    u = jnp.exp(-jnp.abs(lam))
+    t = u / (2.0 + u)
+    series = jnp.full_like(t, 1.0 / 17.0)
+    for n in range(15, 0, -2):
+        series = series * t * t + 1.0 / n
+    rate = 8.0 * (jnp.maximum(-lam, 0.0) + 2.0 * t * series)
+    fill_rows = jnp.concatenate([jnp.zeros((7, rc - part), F32), jnp.ones((1, rc - part), F32)])
+    chan_o[...] = jnp.concatenate([jnp.concatenate([rows_of[:7], rate]), fill_rows], axis=1)
+    for copy in down + feed:
         copy.wait()
     down_own.wait()
     feed_own.wait()
@@ -1047,15 +1206,17 @@
             jax.ShapeDtypeStruct((length,) + wd, BF16),
             jax.ShapeDtypeStruct(w2, BF16),
             jax.ShapeDtypeStruct((8, width), F32),
-            jax.ShapeDtypeStruct((length,) + pack, BF16),
+            jax.ShapeDtypeStruct((rc, 2 * rc), BF16),
+            jax.ShapeDtypeStruct((8, rc), F32),
             low,
             low,
         ),
         in_specs=[ANY] * 7,
-        out_specs=(ANY, ANY, ANY, ANY, VM, VM, ANY, VM, VM),
+        out_specs=(ANY, ANY, ANY, ANY, VM, VM, VM, VM, VM, VM),
         scratch_shapes=[
             *[pltpu.VMEM(v.shape, v.dtype) for v in (inputs, above, mixer, mlp, gains, gate, chan)],
             DMA((7,)),
+            pltpu.VMEM((length,) + pack, BF16),
             pltpu.VMEM((8, 128), F32),
             pltpu.VMEM(pack, BF16),
             pltpu.VMEM((rows, width), BF16),
@@ -1073,158 +1234,77 @@
 
 
 def last_kernel(
-    length, share, wm, total, inputs, back, gains, gain_two, gp, sq_one, sq_two, sq_three,
-    wm_o, grad_o, gains_o, gates_o,
-    norm_o, factor_o,
-    gain, row_sums, gn, gn_in, gn_mid, gn_got, gp_got, gp_sum, gp_fin, sq_plane, sq_line,
-    loc, ss, rs, gs, gr, ls, lr, move_s, move_r,
+    length, share, wm, gain, gain_two, gates, sq_a, sq_b, sq_c, sq_d,
+    wm_o, gains_o, norm_o, factor_o, by_plane, by_line, loc, ss, rs, gs, gr, ls, lr,
 ):
     y, c, z, x = place()
-    s = 2 * z + x
     me = rank(y, c, x)
     line = line_peers(length)
     plane = plane_peers()
-    owner = x * length + z
-    to_z = owner // 2
-    to_x = owner - 2 * to_z
-    from_z, from_x = lax.rem(s, length), s // length
-    moves = jnp.where(jnp.logical_and(to_z == z, to_x == x), 0, 1)
-    barrier = pltpu.get_barrier_semaphore()
-    for peer in line + plane:
-        pl.semaphore_signal(barrier, inc=1, device_id=peer, device_id_type=MESH)
-
-    @pl.when(moves == 1)
-    def _():
-        pl.semaphore_signal(barrier, inc=1, device_id=device(y, c, to_z, to_x), device_id_type=MESH)
-        pl.semaphore_signal(barrier, inc=1, device_id=device(y, c, from_z, from_x), device_id_type=MESH)
-
-    pl.semaphore_wait(barrier, len(line) + len(plane) + 2 * moves)
-
-    gate = [
-        remote(gp.at[lax.rem(z + k + 1, length)], gp_got.at[k], ls.at[0, k], lr.at[0, k], line[k])
-        for k in range(length - 1)
+    width = gain.shape[1]
+    pair = width // (4 * length)
+    squares = sq_a[...] + sq_b[...] + sq_c[...] + sq_d[...] + tile_of_squares(gates[...])
+    squares = jnp.concatenate([squares, jnp.zeros((8, width - 128), F32)], axis=1)
+    rows = [jnp.sum(v, axis=0, keepdims=True) for v in (gain[...], gain_two[...], squares)]
+    by_plane[me] = jnp.concatenate(rows + [jnp.zeros((1, width), F32)])
+    greet(line + plane)
+    sends = [
+        remote(by_plane.at[me], by_plane.at[me], gs.at[n], gr.at[n], plane[n]) for n in range(7)
     ]
-    rows, width = inputs.shape
-    pair = width // (4 * length)
-    gain[...] = jnp.zeros_like(gain)
-
-    def body(at):
-        grad, gain_part = norm_rows_back(inputs[at].astype(F32), gains[0:1], total[at])
-        store_turned(grad_o, at, back[at] + grad, length, pair)
-        gain[...] += gain_part
-
-    rows_loop(rows, body)
-    row = lax.broadcasted_iota(jnp.int32, (8, width), 0)
-    ones = jnp.sum(gain[...], axis=0, keepdims=True)
-    twos = jnp.sum(gain_two[...], axis=0, keepdims=True)
-    row_sums[...] = jnp.where(row == 0, ones, jnp.where(row == 1, twos, 0.0))
-    if pair < 128:
-        gn[...] = jnp.zeros_like(gn)
-    for k in range(length):
-        for b in range(4):
-            gn[b, k, :, :pair] = row_sums[:, (4 * k + b) * pair : (4 * k + b + 1) * pair]
-    sends = []
-    for n, (fy, fc, fx) in enumerate(FLIPS):
-        to = flip(y, fy) * 2 + flip(c, fc)
-        sends.append(remote(gn.at[to], gn_in.at[n], gs.at[0, n], gr.at[0, n], plane[n]))
     copies, own = exchange_steps(wm, wm_o, loc, ss, rs)
-    for copy in gate:
-        copy.wait()
-    sums = gp[z]
-    for k in range(length - 1):
-        sums = sums + gp_got[k]
-    gp_sum[...] = sums
     for copy in sends:
         copy.wait()
-    sums = gn[2 * y + c]
-    for n in range(7):
-        sums = sums + gn_in[n]
-    gn_mid[...] = sums
+    total = by_plane[0]
+    for n in range(1, 8):
+        total = total + by_plane[n]
+    group = 4 * pair
+    for k in range(length):
+        at = pl.ds(pl.multiple_of(lax.rem(z + k, length) * group, group), group)
+        by_line[z, :, at] = total[:, k * group : (k + 1) * group]
     sends = [
-        remote(gn_mid.at[k + 1], gn_got.at[k], ls.at[1, k], lr.at[1, k], line[k])
-        for k in range(length - 1)
-    ]
-
-    @pl.when(moves == 1)
-    def _():
-        copy = remote(gp_sum, gp_fin, move_s, move_r, device(y, c, to_z, to_x))
-        copy.wait()
-
-    @pl.when(moves == 0)
-    def _():
-        gp_fin[...] = gp_sum[...]
-
-    for copy in sends:
-        copy.wait()
-    sums = gn_mid[0]
-    for k in range(length - 1):
-        sums = sums + gn_got[k]
-    lane = lax.broadcasted_iota(jnp.int32, (8, 128), 1)
-    mine = jnp.logical_and(lane >= x * share, lane < (x + 1) * share)
-    gain_sum = jnp.where(mine, sums, 0.0)
-    gate_sum = gp_fin[...]
-    sq_plane[me] = sq_one[...] + sq_two[...] + sq_three[...] + gain_sum * gain_sum + tile_of_squares(gate_sum)
-    sends = [
-        remote(sq_plane.at[me], sq_plane.at[me], gs.at[1, n], gr.at[1, n], plane[n]) for n in range(7)
+        remote(by_line.at[z], by_line.at[z], ls.at[k], lr.at[k], line[k]) for k in range(length - 1)
     ]
     for copy in sends:
         copy.wait()
-    sums = sq_plane[0]
-    for n in range(1, 8):
-        sums = sums + sq_plane[n]
-    sq_line[z] = sums
-    sends = [
-        remote(sq_line.at[z], sq_line.at[z], ls.at[2, k], lr.at[2, k], line[k])
-        for k in range(length - 1)
-    ]
-    for copy in sends:
-        copy.wait()
-    sums = sq_line[0]
+    total = by_line[0]
     for n in range(1, length):
-        sums = sums + sq_line[n]
-    sums = jnp.sum(jnp.sum(sums, axis=0, keepdims=True), axis=1, keepdims=True)
-    norm = jnp.broadcast_to(jnp.sqrt(sums), (8, 128))
-    factor = clip_limit / jnp.maximum(norm, clip_limit)
+        total = total + by_line[n]
+    squares = jnp.sum(total[:2] * total[:2], axis=0, keepdims=True) + total[2:3]
+    norm = jnp.broadcast_to(jnp.sqrt(jnp.sum(squares, axis=1, keepdims=True)), (8, 128))
     norm_o[...] = norm
-    factor_o[...] = factor
-    gains_o[...] = jnp.where(x == 0, gain_sum[:2, :share], gain_sum[:2, share : 2 * share])
-    gates_o[...] = gate_sum
+    factor_o[...] = clip_limit / jnp.maximum(norm, clip_limit)
+    gains = jnp.zeros((2, pair), F32)
+    for there in range(length):
+        for b in range(4):
+            first_lane = (there * 4 + b) * pair
+            mine = jnp.logical_and(there == z, b == 2 * y + c)
+            gains = jnp.where(mine, total[:2, first_lane : first_lane + pair], gains)
+    gains_o[...] = jnp.where(x == 0, gains[:, :share], gains[:, share:])
     for copy in copies:
         copy.wait()
     own.wait()
 
 
-def last(wm, total, inputs, back, gains, gain_two, gp, squares, length, collective_id):
-    rows, width = inputs.shape
+def last(wm, gain, gain_two, gates, squares, length, collective_id):
+    width = gain.shape[1]
     share = wm.shape[1]
     return pl.pallas_call(
         functools.partial(last_kernel, length, share),
         out_shape=(
             jax.ShapeDtypeStruct(wm.shape, wm.dtype),
-            jax.ShapeDtypeStruct((rows, width), F32),
             jax.ShapeDtypeStruct((2, share), F32),
-            jax.ShapeDtypeStruct(gp.shape[1:], F32),
             TILE, TILE,
         ),
-        in_specs=[ANY] + [VM] * 9,
-        out_specs=(ANY,) + (VM,) * 5,
+        in_specs=[ANY] + [VM] * 7,
+        out_specs=(ANY,) + (VM,) * 3,
         scratch_shapes=[
-            pltpu.VMEM((8, width), F32),
-            pltpu.VMEM((8, width), F32),
-            pltpu.VMEM((4, length, 8, 128), F32),
-            pltpu.VMEM((7, length, 8, 128), F32),
-            pltpu.VMEM((length, 8, 128), F32),
-            pltpu.VMEM((length, 8, 128), F32),
-            pltpu.VMEM(gp.shape, F32),
-            pltpu.VMEM(gp.shape[1:], F32),
-            pltpu.VMEM(gp.shape[1:], F32),
-            pltpu.VMEM((8, 8, 128), F32),
-            pltpu.VMEM((length, 8, 128), F32),
-            DMA, DMA((7,)), DMA((7,)), DMA((2, 7)), DMA((2, 7)),
-            DMA((3, length)), DMA((3, length)), DMA, DMA,
+            pltpu.VMEM((8, 4, width), F32),
+            pltpu.VMEM((length, 4, width), F32),
+            DMA, DMA((7,)), DMA((7,)), DMA((7,)), DMA((7,)),
+            DMA((length,)), DMA((length,)),
         ],
         compiler_params=params(collective_id),
-    )(wm, total, inputs, back, gains, gain_two, gp, *squares)
+    )(wm, gain, gain_two, gates, *squares)
 
 
 def minus_expm1(v):
@@ -1450,11 +1530,11 @@
 
 
 def backward_kernel(
-    length, cuts, head, dmix, gate, chan, decay, width, recur, enter, conv, xe, se, ends_f, proj, block, *refs
+    length, cuts, head, dmix, gate, chan, decay, width, recur, enter, conv, xe, se, ends_f, proj, block_a, block_b, *refs
 ):
     parts = 1 + max(cut[0] for cut in cuts)
     terms, refs = refs[:parts], refs[parts:]
-    dproj, gates_o, sums, squares, block_o, *refs = refs
+    dproj, gates_o, sums, squares, block_ao, block_bo, *refs = refs
     dgate, gchan, *refs = refs
     suffix, grad, de, ends, carry, hs, hr, es, er, keep_s, move_l, move_s, move_r, *refs = refs
     kept, line_refs = refs[:8], refs[8:]
@@ -1472,7 +1552,10 @@
     scatter.begin()
     for copy in loads:
         copy.start()
-    moves, own = exchange_steps(block, block_o, move_l, move_s, move_r)
+    moves = [
+        exchange_steps(block_a, block_ao, move_l.at[0], move_s.at[0], move_r.at[0]),
+        exchange_steps(block_b, block_bo, move_l.at[1], move_s.at[1], move_r.at[1]),
+    ]
     seqs, span, rc = decay.shape
     part = dproj.shape[2] // 2
     chunks = span // CHUNK
@@ -1604,12 +1687,13 @@
     for n in range(length):
         gates_o[n, :rows] = pack[n * rows : (n + 1) * rows]
     scatter.end(sums, squares)
-    for copy in moves:
-        copy.wait()
-    own.wait()
-
-
-def recur_backward(dmix, gate, chan, kept, part, head, block, terms, cuts, length, collective_id):
+    for copies, own in moves:
+        for copy in copies:
+            copy.wait()
+        own.wait()
+
+
+def recur_backward(dmix, gate, chan, kept, part, head, blocks, terms, cuts, length, collective_id):
     proj, decay, width, recur, enter, conv, xe, se, ends = kept
     seqs, span, rc = decay.shape
     gate_pad = -(-(part // length) // 16) * 16
@@ -1620,10 +1704,10 @@
             jax.ShapeDtypeStruct((seqs, span, 2 * part), BF16),
             jax.ShapeDtypeStruct((length, gate_pad, rc), F32),
             jax.ShapeDtypeStruct((line_rows, columns), BF16), TILE,
-            jax.ShapeDtypeStruct(block.shape, BF16),
+            *[jax.ShapeDtypeStruct(block.shape, BF16) for block in blocks],
         ),
-        in_specs=[ANY, VM, VM] + [ANY] * 7 + [VM] + [ANY] * (2 + len(terms)),
-        out_specs=(VM,) * 4 + (ANY,),
+        in_specs=[ANY, VM, VM] + [ANY] * 7 + [VM] + [ANY] * (3 + len(terms)),
+        out_specs=(VM,) * 4 + (ANY, ANY),
         scratch_shapes=[
             pltpu.VMEM((seqs, span, 2 * rc), BF16),
             pltpu.VMEM((8, 8, rc), F32),
@@ -1633,7 +1717,7 @@
             pltpu.VMEM((length, 2, seqs, 8, rc), F32),
             pltpu.VMEM((seqs, 8, rc), F32),
             DMA, DMA, DMA((length,)), DMA((length,)),
-            DMA((9,)), DMA, DMA((7,)), DMA((7,)),
+            DMA((9,)), DMA((2,)), DMA((2, 7)), DMA((2, 7)),
             *[
                 pltpu.VMEM(shape, dtype)
                 for shape, dtype in (
@@ -1647,7 +1731,7 @@
         cost_estimate=pl.CostEstimate(
             flops=2 * seqs * span * rc * rc * 2, bytes_accessed=120 * 2**20, transcendentals=0
         ),
-    )(dmix, gate, chan, decay, width, recur, enter, conv, xe, se, ends, proj, block, *terms)
+    )(dmix, gate, chan, decay, width, recur, enter, conv, xe, se, ends, proj, *blocks, *terms)
 
 
 def contract_last(left, right):
@@ -1685,129 +1769,150 @@
     down_o[...] = contract_first(above[...], hid[...]).astype(BF16)
 
 
-def with_hops(length, first_hop, last_hop, buf, ss, rs, steps, compute):
-    i = pl.program_id(0)
-    hops = LineGather(buf, length, ss, rs)
-
-    @pl.when(i == 0)
+def mlp_specs(tokens, model, f):
+    def rows(width):
+        return pl.BlockSpec((tokens // 8, width), lambda i: (jnp.minimum(i, 7), 0))
+
+    columns = pl.BlockSpec((tokens, model // 8), lambda i: (0, jnp.maximum(i - 8, 0)))
+    grads = pl.BlockSpec((model // 8, f), lambda i: (jnp.maximum(i - 8, 0), 0))
+    return rows, columns, grads
+
+
+def keep_units(step, held, outs):
+    at = pl.ds(pl.multiple_of(step * outs[0].shape[0], outs[0].shape[0]), outs[0].shape[0])
+    for kept, out in zip(held, outs):
+        kept[at] = out[...]
+
+
+def early_mlp_kernel(
+    length, x, above, x_columns, above_columns, gate_up, down, w_in,
+    hid, dgate, dup, gate_o, up_o, down_o, w, hid_all, dgate_all, dup_all, ss, rs
+):
+    step = pl.program_id(0)
+    hops = LineGather(w, length, ss, rs)
+
+    @pl.when(step == 0)
     def _():
         greet(line_neighbours(length))
-        hops.start(first_hop)
-
-    @pl.when(i == steps // 2)
+        if length > 2:
+            hops.start(2)
+
+    @pl.when(step == 7)
     def _():
-        for hop in range(first_hop, last_hop):
+        for hop in range(2, length - 1):
             hops.arrive(hop)
             hops.start(hop + 1)
 
-    compute()
-
-    @pl.when(i == steps - 1)
+    @pl.when(step < 8)
     def _():
-        hops.arrive(last_hop)
-        hops.finish(first_hop, last_hop)
-
-
-def early_feed_kernel(length, x, above, gate_up, down, w_in, hid, dgate, dup, w, ss, rs):
-    with_hops(
-        length, 2, length - 2, w, ss, rs, 8,
-        lambda: feed_forward(x, above, gate_up, down, hid, dgate, dup),
-    )
-
-
-def early_feed(x, above, gate_up, down, w, length, collective_id):
+        feed_forward(x, above, gate_up, down, hid, dgate, dup)
+        keep_units(step, (hid_all, dgate_all, dup_all), (hid, dgate, dup))
+
+    @pl.when(step >= 8)
+    def _():
+        grads_compute(x_columns, above_columns, hid_all, dgate_all, dup_all, gate_o, up_o, down_o)
+
+    @pl.when(step == 15)
+    def _():
+        hops.arrive(length - 1)
+        hops.finish(2, length - 1)
+
+
+def early_mlp(x, above, gate_up, down, w, length, collective_id):
     tokens, model = x.shape
     f = down.shape[1]
-
-    def block(width):
-        return pl.BlockSpec((tokens // 8, width), lambda i: (i, 0))
-
+    rows, columns, grads = mlp_specs(tokens, model, f)
+    unit_shape = jax.ShapeDtypeStruct((tokens, f), BF16)
+    grad_shape = jax.ShapeDtypeStruct((model, f), BF16)
     return pl.pallas_call(
-        functools.partial(early_feed_kernel, length),
-        grid=(8,),
-        out_shape=(jax.ShapeDtypeStruct((tokens, f), BF16),) * 3 + (jax.ShapeDtypeStruct(w.shape, w.dtype),),
-        in_specs=[block(model), block(model), resident(gate_up.shape), resident(down.shape), ANY],
-        out_specs=(block(f),) * 3 + (ANY,),
-        scratch_shapes=[DMA((2, length)), DMA((2, length))],
-        input_output_aliases={4: 3},
+        functools.partial(early_mlp_kernel, length),
+        grid=(16,),
+        out_shape=(unit_shape,) * 3 + (grad_shape,) * 3 + (jax.ShapeDtypeStruct(w.shape, w.dtype),),
+        in_specs=[rows(model), rows(model), columns, columns, resident(gate_up.shape), resident(down.shape), ANY],
+        out_specs=(rows(f),) * 3 + (grads,) * 3 + (ANY,),
+        scratch_shapes=[pltpu.VMEM((tokens, f), BF16)] * 3 + [DMA((2, length)), DMA((2, length))],
+        input_output_aliases={6: 6},
         compiler_params=params(collective_id),
-        cost_estimate=pl.CostEstimate(flops=6 * tokens * model * f, bytes_accessed=30 * 2**20, transcendentals=0),
-    )(x, above, gate_up, down, w)
-
-
-def late_feed_kernel(
-    x, above, hid_one, dgate_one, dup_one, gate_up, down, late, hid, dgate, dup, out, back
+        cost_estimate=pl.CostEstimate(flops=12 * tokens * model * f, bytes_accessed=50 * 2**20, transcendentals=0),
+    )(x, above, x, above, gate_up, down, w)
+
+
+def late_mlp_kernel(
+    length, cuts, x, above, x_columns, above_columns, hid_one, dgate_one, dup_one, gate_up, down, late, *refs
 ):
+    terms, refs = refs[: len(cuts)], refs[len(cuts) :]
+    out, back, gate_o, up_o, down_o, sums, squares, hid, dgate, dup, *refs = refs
+    (hid_all, dgate_all, dup_all), line_refs = refs[:3], refs[3:]
+    step = pl.program_id(0)
+    line = LineScatter([(ref, *cut) for ref, cut in zip(terms, cuts)], length, *line_refs)
+
+    @pl.when(step == 0)
+    def _():
+        greet(line_neighbours(length))
+        line.load((1,))
+        line.start()
+        line.load((*range(2, length), 0))
+
+    for hop in range(2, length):
+
+        @pl.when(step == min(10, 4 * (hop - 1)))
+        def _():
+            line.next = hop
+            line.start()
+
     f, g = down.shape[1], hid.shape[1]
-    feed_forward(x, above, late.at[:, : 2 * g], late.at[:, 2 * g :], hid, dgate, dup)
-    for first_column in range(0, x.shape[1], 512):
-        at = slice(first_column, first_column + 512)
-        ahead = contract_last(hid_one[...], down[at]) + contract_last(hid[...], late[at, 2 * g :])
-        out[:, at] = ahead.astype(BF16)
-        both = contract_last(dgate_one[...], gate_up[at, :f]) + contract_last(dup_one[...], gate_up[at, f:])
-        both = both + contract_last(dgate[...], late[at, :g]) + contract_last(dup[...], late[at, g : 2 * g])
-        back[:, at] = both.astype(BF16)
-
-
-def late_feed(x, above, early_units, gate_up, down, late):
+
+    @pl.when(step < 8)
+    def _():
+        feed_forward(x, above, late.at[:, : 2 * g], late.at[:, 2 * g :], hid, dgate, dup)
+        keep_units(step, (hid_all, dgate_all, dup_all), (hid, dgate, dup))
+        for first_column in range(0, x.shape[1], 512):
+            at = slice(first_column, first_column + 512)
+            ahead = contract_last(hid_one[...], down[at]) + contract_last(hid[...], late[at, 2 * g :])
+            out[:, at] = ahead.astype(BF16)
+            both = contract_last(dgate_one[...], gate_up[at, :f]) + contract_last(dup_one[...], gate_up[at, f:])
+            both = both + contract_last(dgate[...], late[at, :g]) + contract_last(dup[...], late[at, g : 2 * g])
+            back[:, at] = both.astype(BF16)
+
+    @pl.when(step >= 8)
+    def _():
+        grads_compute(x_columns, above_columns, hid_all, dgate_all, dup_all, gate_o, up_o, down_o)
+
+    @pl.when(step == 15)
+    def _():
+        squares[...] = jnp.zeros_like(squares)
+        line.end(sums, 0, squares)
+
+
+def late_mlp(x, above, early_units, gate_up, down, late, terms, cuts, length, collective_id):
     tokens, model = x.shape
     f, g = down.shape[1], late.shape[1] // 3
-
-    def block(width):
-        return pl.BlockSpec((tokens // 8, width), lambda i: (i, 0))
-
-    widths = (g, g, g, model, model)
+    line_rows = terms[0].shape[1]
+    cut = sum(columns for _, columns in cuts)
+    rows, columns, grads = mlp_specs(tokens, model, g)
+
+    def whole(shape):
+        return pl.BlockSpec(shape, lambda i: (0, 0))
+
     return pl.pallas_call(
-        late_feed_kernel,
-        grid=(8,),
-        out_shape=tuple(jax.ShapeDtypeStruct((tokens, n), BF16) for n in widths),
-        in_specs=[block(model), block(model)]
-        + [block(f)] * 3
-        + [resident(v.shape) for v in (gate_up, down, late)],
-        out_specs=tuple(block(n) for n in widths),
-        compiler_params=pltpu.CompilerParams(vmem_limit_bytes=VMEM_BYTES),
+        functools.partial(late_mlp_kernel, length, cuts),
+        grid=(16,),
+        out_shape=(jax.ShapeDtypeStruct((tokens, model), BF16),) * 2
+        + (jax.ShapeDtypeStruct((model, g), BF16),) * 3
+        + (jax.ShapeDtypeStruct((line_rows, cut), BF16), TILE),
+        in_specs=[rows(model), rows(model), columns, columns]
+        + [rows(f)] * 3
+        + [resident(v.shape) for v in (gate_up, down, late)]
+        + [ANY] * len(terms),
+        out_specs=(rows(model),) * 2 + (grads,) * 3 + (whole((line_rows, cut)), whole((8, 128))),
+        scratch_shapes=[pltpu.VMEM((tokens // 8, g), BF16)] * 3
+        + [pltpu.VMEM((tokens, g), BF16)] * 3
+        + line_scratch(length, line_rows, cut, len(cuts)),
+        compiler_params=params(collective_id),
         cost_estimate=pl.CostEstimate(
-            flops=6 * tokens * model * (f + 2 * g), bytes_accessed=60 * 2**20, transcendentals=0
+            flops=6 * tokens * model * (f + 3 * g), bytes_accessed=70 * 2**20, transcendentals=0
         ),
-    )(x, above, *early_units, gate_up, down, late)
-
-
-def early_grads_kernel(length, x, above, hid, dgate, dup, w_in, gate_o, up_o, down_o, w, ss, rs):
-    with_hops(
-        length, length - 1, length - 1, w, ss, rs, 8,
-        lambda: grads_compute(x, above, hid, dgate, dup, gate_o, up_o, down_o),
-    )
-
-
-def feed_grads(x, above, hid, dgate, dup, w=None, length=0, collective_id=None):
-    tokens, model = x.shape
-    f = hid.shape[1]
-    columns = pl.BlockSpec((tokens, model // 8), lambda i: (0, i))
-    in_specs = [columns, columns] + [resident(hid.shape)] * 3
-    shapes = (jax.ShapeDtypeStruct((model, f), BF16),) * 3
-    out_specs = (pl.BlockSpec((model // 8, f), lambda i: (i, 0)),) * 3
-    cost = pl.CostEstimate(flops=6 * tokens * model * f, bytes_accessed=40 * 2**20, transcendentals=0)
-    if w is None:
-        return pl.pallas_call(
-            grads_compute,
-            grid=(8,),
-            out_shape=shapes,
-            in_specs=in_specs,
-            out_specs=out_specs,
-            compiler_params=pltpu.CompilerParams(vmem_limit_bytes=VMEM_BYTES),
-            cost_estimate=cost,
-        )(x, above, hid, dgate, dup)
-    return pl.pallas_call(
-        functools.partial(early_grads_kernel, length),
-        grid=(8,),
-        out_shape=shapes + (jax.ShapeDtypeStruct(w.shape, w.dtype),),
-        in_specs=in_specs + [ANY],
-        out_specs=out_specs + (ANY,),
-        scratch_shapes=[DMA((2, length)), DMA((2, length))],
-        input_output_aliases={5: 3},
-        compiler_params=params(collective_id),
-        cost_estimate=cost,
-    )(x, above, hid, dgate, dup, w)
+    )(x, above, x, above, *early_units, gate_up, down, late, *terms)
 
 
 def adam_step(weight, grad, first, second, factor, rate, decay_rate):
@@ -1838,48 +1943,77 @@
             out[...] = result
 
 
-def adam_kernel(rate, decay_rate, sources, factor, w, m, v, *refs):
-    grads, refs = refs[: len(sources)], refs[len(sources) :]
-    if len(refs) > 3:
-        small, refs = refs[:11], refs[11:]
-        pl.when(pl.program_id(0) == 0)(lambda: small_steps(factor[0:1, 0:1], small, refs[3:]))
-    m_o, v_o, w_o = refs[:3]
-    parts = []
-    for ref, pieces in zip(grads, sources):
-        for first, columns, at, stride in pieces:
-            for t in range(8):
-                parts.append((at + t * stride, ref[t, :, first : first + columns].astype(F32)))
-    parts.sort(key=lambda part: part[0])
-    grad = jnp.concatenate([part for _, part in parts], axis=1)
-    first_new, second_new, weight_new = adam_step(
-        w[...], grad, m[...], v[...], factor[0:1, 0:1], rate, decay_rate
-    )
-    m_o[...] = first_new
-    v_o[...] = second_new
-    w_o[...] = weight_new
-
-
-def adam_rows(weight, grads, sources, first, second, factor, rate, decay_rate, small=()):
-    rows, width = weight.shape
+def adam_kernel(sources, factor, *refs):
+    states, refs = refs[: 3 * len(sources)], refs[3 * len(sources) :]
+    count = sum(len(source) for source in sources)
+    grads, small, refs = refs[:count], refs[count : count + 11], refs[count + 11 :]
+    results, outs = refs[:2], refs[2:]
+    for result, out in zip(results, outs[-2:]):
+        out[...] = result[...]
+    one = factor[0:1, 0:1]
+    pl.when(pl.program_id(0) == 0)(lambda: small_steps(one, small, outs[3 * len(sources) : -2]))
+    for n, source in enumerate(sources):
+        parts = []
+        for pieces in source:
+            ref, *grads = grads
+            for first, columns, at, stride in pieces:
+                for t in range(8):
+                    parts.append((at + t * stride, columns, ref, t, first))
+        parts.sort(key=lambda part: part[0])
+        w, m, v = states[3 * n : 3 * n + 3]
+        m_o, v_o, w_o = outs[3 * n : 3 * n + 3]
+        run = []
+        for at, columns, ref, t, first in parts:
+            run.append((at, columns, ref[t, :, first : first + columns].astype(F32)))
+            end = at + columns
+            if end % 128:
+                continue
+            grad = jnp.concatenate([piece for _, _, piece in run], axis=1) if len(run) > 1 else run[0][2]
+            cols = slice(run[0][0], end)
+            run = []
+            first_new, second_new, weight_new = adam_step(
+                w[:, cols], grad, m[:, cols], v[:, cols], one, rate_matrix, decay_matrix
+            )
+            m_o[:, cols] = first_new
+            v_o[:, cols] = second_new
+            w_o[:, cols] = weight_new
+
+
+def adam(matrices, small, factor, passed):
+    rows = matrices[0][0].shape[0]
     step = min(rows, 16)
-    block = pl.BlockSpec((step, width), lambda i: (i, 0))
-    shape = jax.ShapeDtypeStruct(weight.shape, F32)
+
+    def block(v):
+        return pl.BlockSpec((step, v.shape[1]), lambda i: (i, 0))
 
     def whole(v):
         return pl.BlockSpec(v.shape, lambda i: (0, 0))
 
-    results = pl.pallas_call(
-        functools.partial(adam_kernel, rate, decay_rate, sources),
-        grid=(rows // step,),
-        out_shape=(shape,) * 3 + tuple(jax.ShapeDtypeStruct(v.shape, F32) for v in small[2:]),
-        in_specs=[pl.BlockSpec((8, 128), lambda i: (0, 0)), block, block, block]
+    states = [v for matrix in matrices for v in matrix[:3]]
+    grads = [g for matrix in matrices for g in matrix[3]]
+    results = [*states, *small[2:], *passed]
+    steps = rows // step
+
+    def slab(v):
+        return pl.BlockSpec((v.shape[0] // steps, v.shape[1]), lambda i: (i, 0))
+
+    return pl.pallas_call(
+        functools.partial(adam_kernel, [matrix[4] for matrix in matrices]),
+        grid=(steps,),
+        out_shape=tuple(jax.ShapeDtypeStruct(v.shape, v.dtype) for v in results),
+        in_specs=[pl.BlockSpec((8, 128), lambda i: (0, 0))]
+        + [block(v) for v in states]
         + [pl.BlockSpec((8, step, g.shape[2]), lambda i: (0, i, 0)) for g in grads]
-        + [whole(v) for v in small],
-        out_specs=(block,) * 3 + tuple(whole(v) for v in small[2:]),
+        + [whole(v) for v in small]
+        + [slab(v) for v in passed],
+        out_specs=tuple(block(v) for v in states)
+        + tuple(whole(v) for v in small[2:])
+        + tuple(slab(v) for v in passed),
         compiler_params=pltpu.CompilerParams(vmem_limit_bytes=VMEM_BYTES),
-        cost_estimate=pl.CostEstimate(flops=0, bytes_accessed=7 * 4 * weight.size, transcendentals=0),
-    )(factor, weight, first, second, *grads, *small)
-    return (*results[:3], results[3:]) if small else results
+        cost_estimate=pl.CostEstimate(
+            flops=0, bytes_accessed=sum(8 * v.size for v in states), transcendentals=0
+        ),
+    )(factor, *states, *grads, *small, *passed)
 
 
 def on_device(
@@ -1931,7 +2065,7 @@
         v = jnp.roll(v.reshape(v.shape[0], length, 4, pair), z, axis=1)
         return v.swapaxes(1, 2).reshape(v.shape[0], model)
 
-    normed_one, mixer_full, mlp_gu, mlp_down, late_pack, gains, gate_in, inputs, above = first(
+    normed_one, mixer_full, mlp_gu, mlp_down, late_pack, gains, gate, chan, inputs, above = first(
         turned(block_input[0]),
         turned(out_grad[0]),
         mixer_weight,
@@ -1944,21 +2078,6 @@
         1,
     )
     normed_one = normed_one.reshape(8 * tokens, model)
-    gate_own = gate_in[:, :gate_rows].reshape(r8, rc)
-    chan = gate_own[:, 2 * head : 2 * head + 8].astype(F32).T
-    lam = chan[7]
-    fill = jnp.concatenate([jnp.zeros((7, rc - r8), F32), jnp.ones((1, rc - r8), F32)])
-    chan = jnp.concatenate([chan[:7], 8.0 * jax.nn.softplus(-lam)[None]])
-    chan = jnp.concatenate([chan, fill], axis=1)
-    gate = []
-    for h in range(heads):
-        block = gate_own[h * head : (h + 1) * head, : 2 * head]
-        at = ((0, 0), (h * head, rc - (h + 1) * head))
-        gate.append(
-            jnp.concatenate([jnp.pad(block[:, :head], at), jnp.pad(block[:, head:], at)], axis=1)
-        )
-    gate = jnp.pad(jnp.concatenate(gate), ((0, rc - r8), (0, 0)))
-
     mixer_full = mixer_full.reshape(model, 3 * r8)
     mixed, *kept, grad_out, late, mlp_down = recur_forward(
         normed_one, mixer_full, gate, chan, above, late_pack, mlp_down, length, 2
@@ -1971,62 +2090,63 @@
     h2 = f8 - h1
     mlp_gu = mlp_gu.reshape(model, 2 * h1)
     mlp_down = mlp_down.reshape(model, h1)
-    *early_units, late = early_feed(normed_two, grad_out, mlp_gu, mlp_down, late, length, 9)
-    *early_terms, late = feed_grads(
-        normed_two, grad_out, *early_units, w=late, length=length, collective_id=10
-    )
-    late = late.reshape(model, 3 * h2)
-    *late_units, mlp_part, dnormed_two = late_feed(
-        normed_two, grad_out, early_units, mlp_gu, mlp_down, late
-    )
-    late_terms = feed_grads(normed_two, grad_out, *late_units)
+    hid, dgg, duu, *early_terms, late = early_mlp(normed_two, grad_out, mlp_gu, mlp_down, late, length, 9)
     gate_one, up_one, down_one = (v.reshape(length, 8 * share, h1) for v in early_terms)
+    cut = h1 // 4
+    mlp_part, dnormed_two, *late_terms, sums_zero, squares_zero = late_mlp(
+        normed_two, grad_out, (hid, dgg, duu), mlp_gu, mlp_down, late.reshape(model, 3 * h2),
+        (gate_one, up_one), ((0, h1), (0, cut)), length, 11,
+    )
     gate_two, up_two, down_two = (v.reshape(length, 8 * share, h2) for v in late_terms)
-    down_cut = h1 // 2
 
     grad_residual, gain_two, dmz, dmix, sums_one, squares_one = turn(
         dnormed_two, residual, above, gains, mixer_full, rc,
-        (gate_one, up_one, down_one), ((0, 0, h1), (1, 0, h1), (2, 0, down_cut)), length, 4,
+        (up_one, down_one, gate_two), ((0, cut, h1 - cut), (1, 0, h1), (2, 0, h2)),
+        length, 4,
     )
     dmz = dmz.reshape(8 * tokens, model)
     span = 2 * tokens
     dmix = dmix.reshape(4, span, rc)
-    dproj, gate_back, sums_two, squares_two, back_one = recur_backward(
-        dmix, gate, chan, kept, r8, head, sums_one.reshape(8, share, sums_one.shape[1]),
-        (down_one, gate_two, up_two), ((0, down_cut, h1 - down_cut), (1, 0, h2), (2, 0, h2)), length, 6,
+    sums_zero, sums_one = (v.reshape(8, share, v.shape[1]) for v in (sums_zero, sums_one))
+    dproj, gate_back, sums_two, squares_two, back_zero, back_one = recur_backward(
+        dmix, gate, chan, kept, r8, head, (sums_zero, sums_one),
+        (up_two, down_two), ((0, 0, h2), (1, 0, h2)), length, 6,
     )
     dproj = dproj.reshape(4 * span, 2 * r8)
-    dnormed_one, block_output, back_two, rest_sums, squares_three = closing(
-        normed_one, dmz, dproj, mixed, mixer_full, mlp_part, residual,
-        down_two, (0, h2), sums_two, r8, length, 7,
-    )
-
-    rest_back, input_grad, gains_sum, gates_sum, norm, factor = last(
-        rest_sums.reshape(8, share, rest_sums.shape[1]), dnormed_one, inputs, grad_residual, gains, gain_two,
-        gate_back, (squares_one, squares_two, squares_three), length, 8,
-    )
-    *mixer_up, small = adam_rows(
-        mixer_weight, (rest_back,), ([(h2 + n * r8, r8, n * lru, r8) for n in range(3)],),
-        first_mixer, second_mixer, factor, rate_matrix, decay_matrix,
+    input_grad, gain_one, gates_sum, block_output, back_two, mixer_sums, squares_three = closing(
+        normed_one, dmz, dproj, mixed, mixer_full, mlp_part, residual, sums_two,
+        inputs, grad_residual, gains, gate_back, length, 7,
+    )
+    mixer_back, gains_sum, norm, factor = last(
+        mixer_sums.reshape(8, share, 3 * r8), gain_one, gain_two, gates_sum,
+        (squares_zero, squares_one, squares_two, squares_three), length, 8,
+    )
+    mlp_sources = (
+        [(0, h1, 0, f8), (h1, cut, hidden, f8)],
+        [
+            (0, h1 - cut, hidden + cut, f8),
+            (h1 - cut, h1, 2 * hidden, f8),
+            (2 * h1 - cut, h2, h1, f8),
+        ],
+        [(0, h2, hidden + h1, f8), (h2, h2, 2 * hidden + h1, f8)],
+    )
+    states = adam(
+        (
+            (
+                mixer_weight, first_mixer, second_mixer, (mixer_back,),
+                ([(n * r8, r8, n * lru, r8) for n in range(3)],),
+            ),
+            (mlp_weight, first_mlp, second_mlp, (back_zero, back_one, back_two), mlp_sources),
+        ),
         (
             gains_sum, gates_sum, norm_gains, first_gains, second_gains, gate_weight, first_gate, second_gate,
             chan_params, first_chan, second_chan,
         ),
-    )
-    gains_up, gate_up, chan_up = small[:3], small[3:6], small[6:]
-    mlp_up = adam_rows(
-        mlp_weight, (back_one, back_two, rest_back),
-        (
-            [(0, h1, 0, f8), (h1, h1, hidden, f8), (2 * h1, down_cut, 2 * hidden, f8)],
-            [
-                (0, h1 - down_cut, 2 * hidden + down_cut, f8),
-                (h1 - down_cut, h2, h1, f8),
-                (h1 - down_cut + h2, h2, hidden + h1, f8),
-            ],
-            [(0, h2, 2 * hidden + h1, f8)],
-        ),
-        first_mlp, second_mlp, factor, rate_matrix, decay_matrix,
-    )
+        factor,
+        (block_output, input_grad),
+    )
+    *states, block_output, input_grad = states
+    mixer_up, mlp_up, gains_up, gate_up, chan_up = (states[3 * n : 3 * n + 3] for n in range(5))
     return (
         turned_back(block_output)[None],
         turned_back(input_grad)[None],

time: 665 us -> 617 us (0.928)
  Pallas kernels: 654 us -> 607 us
  local copies, waits for them, and re-layouts: 7.99 us -> 1.19 us
    pallas_call x1, Pallas kernels: 70.3 us -> 54.9 us  [recur_backward(): pl.pallas_call(functools.partial(backward_kernel, length, cuts, head), ou...]
    pallas_call x1, Pallas kernels: 34.4 us -> 22.2 us  [last(): pl.pallas_call(functools.partial(last_kernel, length, share), out_shape=(...]
    pallas_call x1, Pallas kernels: 96.3 us -> 88.1 us  [turn(): pl.pallas_call(functools.partial(turn_kernel, length, cuts), out_shape=(j...]
    pallas_call x7 -> x4, Pallas kernels: 209 us -> 204 us  [the longest x1 91.9 us: closing(): pl.pallas_call(functools.partial(closing_kernel, length), out_shape=(jax....]
where the time goes in v6:
time: 617 us; the launch traced here: 609 us
  Pallas kernels  607 us (98%)
    pallas_call x1, Pallas kernels, middle(): pl.pallas_call(functools.partial(middle_kernel, length), out_shape=(jax.S...  95.1 us
    pallas_call x1, Pallas kernels, closing(): pl.pallas_call(functools.partial(closing_kernel, length), out_shape=(jax....  91.9 us
    pallas_call x1, Pallas kernels, turn(): pl.pallas_call(functools.partial(turn_kernel, length, cuts), out_shape=(j...  88.1 us
    pallas_call x1, Pallas kernels, first(): pl.pallas_call(functools.partial(first_kernel, length), out_shape=(jax.Sh...  87.6 us
    pallas_call x1, Pallas kernels, recur_forward(): pl.pallas_call(functools.partial(forward_kernel, length), out_shape=(jax....  55.2 us
    pallas_call x1, Pallas kernels, recur_backward(): pl.pallas_call(functools.partial(backward_kernel, length, cuts, head), ou...  54.9 us
    pallas_call x1, Pallas kernels, late_mlp(): pl.pallas_call(functools.partial(late_mlp_kernel, length, cuts), grid=(16...  51.4 us
    pallas_call x1, Pallas kernels, early_mlp(): pl.pallas_call(functools.partial(early_mlp_kernel, length), grid=(16,), o...  43.1 us

profile of v6, /device:TPU:0, one launch (start us, length us, event | category | flops | bytes accessed | tf_op | source)
XLA Modules:
  0.0 609.4 jit_solution(11029925784770061275)
XLA Ops:
  0.7 87.6 %shard_map.304 = (bf16[8,256,2048]{2,1,0:T(8,128)(2,1)}, bf16[4,8,64,960]{3,2,1,0:T(8,128)(2,1)}, bf16[4,8,64,1024]{3,2,1,0:T(8,128)(2,1)}, bf16[4,8,64,512]{3,2...) custom-call(bf16[256,2048]{1,0:T(8,128)(2,1)} %bitcast.47, ...), custom_call_target="tpu_custom_call" | custom-call | bytes 314572800 | tf_op jit(solution)/shard_map/pallas_call | solution.py:1200
  88.2 55.2 %shard_map.305 = (bf16[4,512,320]{2,1,0:T(8,128)(2,1)}, f32[4,512,384]{2,1,0:T(8,128)}, f32[4,512,384]{2,1,0:T(8,128)}, f32[4,512,384]{2,1,0:T(8,128)}, f32[4,51...) custom-call(bf16[2048,2048]{1,0:T(8,128)(2,1)} %bitcast.32, ...), custom_call_target="tpu_custom_call", output_to_operand_aliasing={{12}: (6, {})} | custom-call | flops 1207959552 | bytes 104857600 | tf_op jit(solution)/shard_map/pallas_call | solution.py:1501
  143.5 95.1 %shard_map.306 = (f32[256,2048]{1,0:T(8,128)}, bf16[8,256,2048]{2,1,0:T(8,128)(2,1)}, bf16[4,8,64,1024]{3,2,1,0:T(8,128)(2,1)}, bf16[4,8,64,768]{3,2,1,0:T(8,128)(2,1)}) custom-call(bf16[2048,320]{1,0:T(8,128)(2,1)} %bitcast.44, bf16[2048,960]{1,0:T(8,128)(2,1)} %bitcast.29, ...), custom_call_target="tpu_custom_call", output_to_operand_aliasing={{2}: (4, {}), {3}: (5, {})} | custom-call | bytes 314572800 | tf_op jit(solution)/shard_map/pallas_call | solution.py:635
  238.6 43.1 %shard_map.307 = (bf16[2048,512]{1,0:T(8,128)(2,1)}, bf16[2048,512]{1,0:T(8,128)(2,1)}, bf16[2048,512]{1,0:T(8,128)(2,1)}, bf16[2048,512]{1,0:T(8,128)(2,1)}, bf...) custom-call(bf16[2048,2048]{1,0:T(8,128)(2,1)} %bitcast.59, ...), custom_call_target="tpu_custom_call", output_to_operand_aliasing={{6}: (6, {})} | custom-call | flops 25769803776 | bytes 52428800 | tf_op jit(solution)/shard_map/pallas_call | solution.py:1827
  281.8 51.4 %shard_map.308 = (bf16[2048,2048]{1,0:T(8,128)(2,1)}, bf16[2048,2048]{1,0:T(8,128)(2,1)}, bf16[2048,256]{1,0:T(8,128)(2,1)}, bf16[2048,256]{1,0:T(8,128)(2,1)}, ...) custom-call(bf16[2048,2048]{1,0:T(8,128)(2,1)} %bitcast.61, bf16[2048,2048]{1,0:T(8,128)(2,1)} %bitcast.57, ...), custom_call_target="tpu_custom_call" | custom-call | flops 32212254720 | bytes 73400320 | tf_op jit(solution)/shard_map/pallas_call | solution.py:1897
  333.2 88.1 %shard_map.309 = (f32[256,2048]{1,0:T(8,128)}, f32[8,2048]{1,0:T(8,128)}, bf16[8,256,2048]{2,1,0:T(8,128)(2,1)}, f32[8,256,384]{2,1,0:T(8,128)}, bf16[512,1152]{1,0:T(8,128)(2,1)}, /*index=5*/f32[8,128]{1,0:T(8,128)}) custom-call(bf16[8,256,2048]{2,1,0:T(8,128)(2,1)} %bitcast.34, f32[256,2048]{1,0:T(8,128)} %get-tuple-element.123.residual_in, ...), custom_call_target="tpu_custom_call" | custom-call | bytes 314572800 | tf_op jit(solution)/shard_map/pallas_call | solution.py:747
  421.3 54.9 %shard_map.310 = (bf16[4,512,640]{2,1,0:T(8,128)(2,1)}, f32[4,80,384]{2,1,0:T(8,128)}, bf16[512,512]{1,0:T(8,128)(2,1)}, f32[8,128]{1,0:T(8,128)}, bf16[8,64,640...) custom-call(f32[4,512,384]{2,1,0:T(8,128)} %bitcast.37, bf16[384,768]{1,0:T(8,128)(2,1)} %get-tuple-element.101.gate, ...), custom_call_target="tpu_custom_call" | custom-call | flops 1207959552 | bytes 125829120 | tf_op jit(solution)/shard_map/pallas_call | solution.py:1701
  476.2 91.9 %shard_map.311 = (f32[256,2048]{1,0:T(8,128)}, f32[8,2048]{1,0:T(8,128)}, f32[80,384]{1,0:T(8,128)}, bf16[256,2048]{1,0:T(8,128)(2,1)}, bf16[8,64,512]{2,1,0:T(8...) custom-call(bf16[2048,2048]{1,0:T(8,128)(2,1)} %bitcast.33, bf16[2048,2048]{1,0:T(8,128)(2,1)} %bitcast.54, ...), custom_call_target="tpu_custom_call" | custom-call | flops 13421772800 | bytes 367001600 | tf_op jit(solution)/shard_map/pallas_call | solution.py:961
  568.2 22.2 %shard_map.312 = (bf16[8,64,960]{2,1,0:T(8,128)(2,1)}, f32[2,64]{1,0:T(2,128)}, f32[8,128]{1,0:T(8,128)}, f32[8,128]{1,0:T(8,128)}) custom-call(bf16[8,64,960]{2,1,0:T(8,128)(2,1)} %bitcast.52, f32[8,2048]{1,0:T(8,128)} %get-tuple-element.147.gain, f32[8,2048]{1,0:T(8,128)} %get-tuple-element.148.gain_two, f32[80,384]{1,0:T(8,128)} %get-tuple-element.149.gates.refs_11_, ...), custom_call_target="tpu_custom_call" | custom-call | tf_op jit(solution)/shard_map/pallas_call | solution.py:1291
  590.4 1.2 slice.3
  591.6 17.4 %shard_map.313 = (f32[64,7680]{1,0:T(8,128)}, f32[64,7680]{1,0:T(8,128)}, f32[64,7680]{1,0:T(8,128)}, f32[64,18432]{1,0:T(8,128)}, f32[64,18432]{1,0:T(8,128)}, ...) custom-call(f32[8,128]{1,0:T(8,128)} %get-tuple-element.154.factor, ...), custom_call_target="tpu_custom_call" | custom-call | bytes 40108032 | tf_op jit(solution)/shard_map/pallas_call | solution.py:2000

commit v7 on v6

--- a/solution.py
+++ b/solution.py
@@ -26,6 +26,7 @@
 VM = pl.BlockSpec(memory_space=pltpu.VMEM)
 FLIPS = [(fy, fc, fx) for fy in (0, 1) for fc in (0, 1) for fx in (0, 1) if fy + fc + fx]
 GELU_SCALE = math.sqrt(2.0 / math.pi)
+GELU_CUBE = 0.044715 * GELU_SCALE
 
 
 def place():
@@ -113,8 +114,14 @@
             self.own.start()
 
     def begin(self):
-        self.begin_half(0)
-        self.begin_half(1)
+        a, o, me, lo, hi = self.a, self.o, self.me, self.lo, self.hi
+        self.s0 = self.send(a.at[lo], o.at[me, lo], 0, self.to_x)
+        self.s1 = self.send(a.at[hi], o.at[me, hi], 1, self.to_y)
+        self.s2 = self.send(a.at[hi], o.at[me, hi], 2, self.to_x)
+        self.s3 = self.send(a.at[lo], o.at[me, lo], 3, self.to_y)
+        self.last += [self.send(a.at[part], o.at[me, part], k, self.to_c) for part, k in ((lo, 4), (hi, 13))]
+        self.own = pltpu.make_async_copy(a, o.at[me], self.loc)
+        self.own.start()
 
     def middle(self):
         self.s0.wait_recv()
@@ -590,9 +597,7 @@
 
     def prepare(i):
         mine = mixed[pl.ds(pl.multiple_of(i * rows, rows), rows)]
-        for first_column in range(0, width, 512):
-            at = slice(first_column, first_column + 512)
-            p[i, :, at] = contract_last(mine, mixer[at, 2 * part :]).astype(BF16)
+        p[i] = contract_last(mine, mixer[:, 2 * part :]).astype(BF16)
 
     def advance():
         if started[0] < length - 1:
@@ -870,9 +875,7 @@
             block_of = i * rows // 256
             at = pl.ds(pl.multiple_of(i * rows - block_of * 256, rows), rows)
             mine = dproj[pl.ds(pl.multiple_of(i * rows, rows), rows)]
-            for first_column in range(0, model, 512):
-                cols = slice(first_column, first_column + 512)
-                back[block_of, at, cols] = contract_last(mine, mixer[cols, : 2 * part]).astype(BF16)
+            back[block_of, at] = contract_last(mine, mixer[:, : 2 * part]).astype(BF16)
 
     waits(inflow[1:4])
     compute(0)
@@ -998,9 +1001,9 @@
 
 def first_kernel(
     length, inputs_in, above_in, mixer_in, mlp_in, gains_in, gate_in, chan_in,
-    normed_o, wm_o, wf_o, wd_o, w2, gains_o, gate_o, chan_o, inputs_o, above_o,
+    normed_o, wm_o, wf_o, wd_o, w2_o, gains_o, gate_o, chan_o, inputs_o, above_o,
     inputs, above, mixer_w, mlp_w, gains_w, gate_w, chan_w, load_s,
-    gp_o, gn, gp, normed, gn_all, wm, wf, wd, loc, ms, mr, fs, fr, line_s, line_r, gain_s, gain_r, move_s, move_r,
+    inputs_k, above_k, w2, keep_s, gp_o, gn, gp, normed, gn_all, wm, wf, wd, loc, ms, mr, fs, fr, line_s, line_r, gain_s, gain_r, move_s, move_r,
     gather_s, gather_r, hop_s, hop_r,
 ):
     loads = [
@@ -1121,10 +1124,10 @@
 
     def body(at):
         v = load_turned(inputs, at, length, pair)
-        inputs_o[at] = v
+        inputs_k[at] = v
         v = v.astype(F32)
         normed[at] = (v * inverse_rms(v) * gains_o[0:1]).astype(BF16)
-        above_o[at] = load_turned(above, at, length, pair)
+        above_k[at] = load_turned(above, at, length, pair)
 
     for copy in loads[5:]:
         copy.wait()
@@ -1132,21 +1135,17 @@
     gather = Gather(normed, normed_o, loc.at[1], gather_s, gather_r)
     rows_loop(half, body)
     gather.begin_half(0)
-    rows_loop(half, body, half)
-    gather.begin_half(1)
     hops.arrive(1)
     if length > 2:
         hops.start(2)
+    rows_loop(half, body, half)
+    gather.begin_half(1)
+    keeps = starts(local_copies(((inputs_k, inputs_o), (above_k, above_o)), keep_s))
     gather.middle()
+    late, late_own = exchange_steps(w2, w2_o.at[0], loc.at[0], fs.at[2], fr.at[2])
     if length > 3:
         hops.arrive(2)
         hops.start(3)
-    gather.relays()
-    for hop in range(min(3, length - 1), length):
-        hops.arrive(hop)
-        if hop + 1 < length:
-            hops.start(hop + 1)
-    gather.finish()
     for copy in gates:
         copy.wait()
     gate_rows, columns = gate_w.shape
@@ -1171,8 +1170,16 @@
     rate = 8.0 * (jnp.maximum(-lam, 0.0) + 2.0 * t * series)
     fill_rows = jnp.concatenate([jnp.zeros((7, rc - part), F32), jnp.ones((1, rc - part), F32)])
     chan_o[...] = jnp.concatenate([jnp.concatenate([rows_of[:7], rate]), fill_rows], axis=1)
-    for copy in down + feed:
+    gather.relays()
+    for hop in range(min(3, length - 1), length):
+        hops.arrive(hop)
+        if hop + 1 < length:
+            hops.start(hop + 1)
+    gather.finish()
+    waits(keeps)
+    for copy in down + feed + late:
         copy.wait()
+    late_own.wait()
     down_own.wait()
     feed_own.wait()
     hops.finish()
@@ -1204,7 +1211,7 @@
             jax.ShapeDtypeStruct((length,) + wm, BF16),
             jax.ShapeDtypeStruct((length,) + wf, BF16),
             jax.ShapeDtypeStruct((length,) + wd, BF16),
-            jax.ShapeDtypeStruct(w2, BF16),
+            jax.ShapeDtypeStruct((length,) + w2, BF16),
             jax.ShapeDtypeStruct((8, width), F32),
             jax.ShapeDtypeStruct((rc, 2 * rc), BF16),
             jax.ShapeDtypeStruct((8, rc), F32),
@@ -1212,10 +1219,14 @@
             low,
         ),
         in_specs=[ANY] * 7,
-        out_specs=(ANY, ANY, ANY, ANY, VM, VM, VM, VM, VM, VM),
+        out_specs=(ANY, ANY, ANY, ANY, ANY, VM, VM, VM, ANY, ANY),
         scratch_shapes=[
             *[pltpu.VMEM(v.shape, v.dtype) for v in (inputs, above, mixer, mlp, gains, gate, chan)],
             DMA((7,)),
+            pltpu.VMEM((rows, width), BF16),
+            pltpu.VMEM((rows, width), BF16),
+            pltpu.VMEM(w2, BF16),
+            DMA((2,)),
             pltpu.VMEM((length,) + pack, BF16),
             pltpu.VMEM((8, 128), F32),
             pltpu.VMEM(pack, BF16),
@@ -1224,7 +1235,7 @@
             pltpu.VMEM(wm, BF16),
             pltpu.VMEM(wf, BF16),
             pltpu.VMEM(wd, BF16),
-            DMA((5,)), DMA((7,)), DMA((7,)), DMA((2, 7)), DMA((2, 7)),
+            DMA((5,)), DMA((7,)), DMA((7,)), DMA((3, 7)), DMA((3, 7)),
             DMA((2, length)), DMA((2, length)), DMA((7,)), DMA((7,)), DMA, DMA,
             DMA((14,)), DMA((14,)), DMA((2, length)), DMA((2, length)),
         ],
@@ -1315,23 +1326,22 @@
 
 
 def gelu_parts(v):
-    inner = jnp.tanh(GELU_SCALE * (v + 0.044715 * v * v * v))
-    return 0.5 * v * (1.0 + inner), inner
-
-
-def gelu_slope(v, inner):
-    return 0.5 * (1.0 + inner) + 0.5 * v * (1.0 - inner * inner) * GELU_SCALE * (
-        1.0 + 3.0 * 0.044715 * v * v
-    )
-
-
-CHUNK = 64
+    square = v * v
+    h = 0.5 * jnp.tanh(v * (GELU_CUBE * square + GELU_SCALE)) + 0.5
+    return v * h, h, square
+
+
+def gelu_slope(gelu, h, square):
+    return h + gelu * (1.0 - h) * (6.0 * GELU_CUBE * square + 2.0 * GELU_SCALE)
+
+
+CHUNK = 128
 
 
 def forward_kernel(
-    length, x_in, mixer, gate, chan, above, w2, w_in,
-    mixed, branch_o, decay_o, width_o, recur_o, enter_o, conv_o, xe_o, se_o, ends_o, above_o, w2_o, w,
-    x_part, pre, loc_h, ends, carry, hs, hr, es, er, gather_l, gather_s, gather_r, hop_s, hop_r, load_s, keep_s, w2_l, w2_s, w2_r,
+    length, x_in, mixer, gate, chan, above, w_in,
+    mixed, branch_o, decay_o, width_o, recur_o, enter_o, conv_o, xe_o, se_o, ends_o, above_o, w,
+    x_part, pre, loc_h, ends, carry, hs, hr, es, er, gather_l, gather_s, gather_r, hop_s, hop_r, load_s, keep_s,
     branch, decay_k, width_k, recur_k, enter_k, conv_k, xe, se,
 ):
     keeps = [
@@ -1347,44 +1357,36 @@
     line = line_peers(length)
     seqs, span, rc = branch.shape
     part = mixed.shape[2]
-    rows = x_part.shape[1]
     chunks = span // CHUNK
 
-    def load(n, slot):
-        half = 1 - n // seqs
-        b = n - n // seqs * seqs
-        at = pl.ds(pl.multiple_of((b * 2 + half) * rows, rows), rows)
+    def load(b, slot):
+        at = pl.ds(pl.multiple_of(b * span, span), span)
         return pltpu.make_async_copy(x_in.at[at], x_part.at[slot], load_s.at[slot])
 
     load(0, 0).start()
-    greet(line + plane_peers())
+    greet(line + gather_peers())
     hops = LineGather(w, length, hop_s, hop_r)
     hops.start(1)
     gather = Gather(above, above_o, gather_l, gather_s, gather_r)
     gather.begin()
-    shares, share_own = exchange_steps(w2, w2_o.at[0], w2_l, w2_s, w2_r)
-
-    def project(n):
-        slot = n - n // 2 * 2
-
-        @pl.when(n + 1 < 2 * seqs)
+
+    @pl.loop(0, seqs)
+    def _(b):
+        slot = b - b // 2 * 2
+
+        @pl.when(b + 1 < seqs)
         def _():
-            load(n + 1, 1 - slot).start()
-
-        load(n, slot).wait()
+            load(b + 1, 1 - slot).start()
+
+        load(b, slot).wait()
         both = jnp.dot(x_part[slot], mixer[:, : 2 * part], preferred_element_type=F32)
-        none = jnp.zeros((rows, rc - part), F32)
-        half = 1 - n // seqs
-        b = n - n // seqs * seqs
-        at = pl.multiple_of(half * rows, rows)
-        branch[b, pl.ds(at, rows)] = jnp.concatenate([both[:, :part], none], axis=1)
+        none = jnp.zeros((span, rc - part), F32)
+        branch[b] = jnp.concatenate([both[:, :part], none], axis=1)
         low = both[:, part:].astype(BF16).astype(F32)
-        xe[b, pl.ds(at + 8, rows)] = jnp.concatenate([low, none], axis=1)
-
-    pl.loop(0, seqs)(project)
+        xe[b, 8:] = jnp.concatenate([low, none], axis=1)
+
     ahead = device(y, c, lax.rem(z + 1, length), x)
     halo = remote(xe.at[:, pl.ds(span, 8)], xe.at[:, pl.ds(0, 8)], hs, hr, ahead)
-    pl.loop(seqs, 2 * seqs)(project)
 
     def coefficients(b, chunk):
         r = pl.multiple_of(chunk * CHUNK, CHUNK)
@@ -1417,6 +1419,7 @@
     hops.arrive(1)
     if length > 2:
         hops.start(2)
+    gather.middle()
     pl.loop(many // 2, many)(later_chunks)
     halo.wait()
 
@@ -1460,7 +1463,6 @@
         hops.start(3)
     for copy in moves:
         copy.wait()
-    gather.middle()
     carry[...] = jnp.zeros_like(carry)
     for k in range(length):
         carry[...] = jnp.where(k < z, ends[k, 0] * carry[...] + ends[k, 1], carry[...])
@@ -1475,7 +1477,7 @@
         at = pl.ds(r, CHUNK)
         state = loc_h[b, at] + pre[b, at] * carry[b, 0:1]
         se[b, pl.ds(r + 8, CHUNK)] = state
-        gelu, _ = gelu_parts(branch[b, at])
+        gelu, _, _ = gelu_parts(branch[b, at])
         mixed[b, at] = (state * gelu)[:, :part].astype(BF16)
 
     keeps[-1].start()
@@ -1485,12 +1487,10 @@
         if hop + 1 < length:
             hops.start(hop + 1)
     hops.finish()
-    for copy in keeps + shares:
-        copy.wait()
-    share_own.wait()
-
-
-def recur_forward(x, mixer, gate, chan, above, w2, w, length, collective_id):
+    waits(keeps)
+
+
+def recur_forward(x, mixer, gate, chan, above, w, length, collective_id):
     rc = gate.shape[0]
     part = mixer.shape[1] // 3
     rows = x.shape[0] // 8
@@ -1505,28 +1505,27 @@
             *kept,
             jax.ShapeDtypeStruct((seqs, 8, rc), F32),
             jax.ShapeDtypeStruct((8,) + above.shape, above.dtype),
-            jax.ShapeDtypeStruct((length,) + w2.shape, w2.dtype),
             jax.ShapeDtypeStruct(w.shape, w.dtype),
         ),
-        in_specs=[ANY, VM, VM, VM, ANY, ANY, ANY],
-        out_specs=(VM,) + (ANY,) * 8 + (VM, ANY, ANY, ANY),
+        in_specs=[ANY, VM, VM, VM, ANY, ANY],
+        out_specs=(VM,) + (ANY,) * 8 + (VM, ANY, ANY),
         scratch_shapes=[
-            pltpu.VMEM((2, rows, x.shape[1]), BF16),
+            pltpu.VMEM((2, span, x.shape[1]), BF16),
             pltpu.VMEM((seqs, span, rc), F32),
             pltpu.VMEM((seqs, span, rc), F32),
             pltpu.VMEM((length, 2, seqs, 8, rc), F32),
             pltpu.VMEM((seqs, 8, rc), F32),
             DMA, DMA, DMA((length,)), DMA((length,)),
             DMA, DMA((14,)), DMA((14,)), DMA((2, length)), DMA((2, length)),
-            DMA((2,)), DMA((8,)), DMA, DMA((7,)), DMA((7,)),
+            DMA((2,)), DMA((8,)),
             *[pltpu.VMEM(v.shape, v.dtype) for v in kept],
         ],
-        input_output_aliases={6: 12},
+        input_output_aliases={5: 11},
         compiler_params=params(collective_id),
         cost_estimate=pl.CostEstimate(
             flops=2 * seqs * span * rc * rc * 2, bytes_accessed=100 * 2**20, transcendentals=0
         ),
-    )(x, mixer, gate, chan, above, w2, w)
+    )(x, mixer, gate, chan, above, w)
 
 
 def backward_kernel(
@@ -1568,11 +1567,11 @@
         r = pl.multiple_of((i - b * chunks) * CHUNK, CHUNK)
         at = pl.ds(r, CHUNK)
         branch = proj[b, at]
-        gelu, inner = gelu_parts(branch)
+        gelu, h, square = gelu_parts(branch)
         above = de[b, at]
         state = se[b, pl.ds(r + 8, CHUNK)]
         grad[b, at] = above * gelu
-        proj[b, at] = above * state * gelu_slope(branch, inner)
+        proj[b, at] = above * state * gelu_slope(gelu, h, square)
 
     loads[3].wait()
     row = lax.broadcasted_iota(jnp.int32, (8, rc), 0)
@@ -1750,43 +1749,47 @@
     return pl.BlockSpec(shape, lambda i: (0, 0), pipeline_mode=pl.Buffered(1))
 
 
-def feed_forward(x, above, gate_up, down, hid, dgate, dup):
+STEPS = 4
+
+
+def feed_forward(x, above, gate_up, down, hid, dboth):
     f = hid.shape[1]
-    for first_column in range(0, f, 256):
-        at = slice(first_column, first_column + 256)
-        gg = jnp.dot(x[...], gate_up[:, at], preferred_element_type=F32)
-        uu = jnp.dot(x[...], gate_up[:, f + first_column : f + first_column + 256], preferred_element_type=F32)
-        dhid = jnp.dot(above[...], down[:, at], preferred_element_type=F32)
-        gelu, inner = gelu_parts(gg)
-        hid[:, at] = (gelu * uu).astype(BF16)
-        dgate[:, at] = (dhid * uu * gelu_slope(gg, inner)).astype(BF16)
-        dup[:, at] = (dhid * gelu).astype(BF16)
-
-
-def grads_compute(x, above, hid, dgate, dup, gate_o, up_o, down_o):
-    gate_o[...] = contract_first(x[...], dgate[...]).astype(BF16)
-    up_o[...] = contract_first(x[...], dup[...]).astype(BF16)
+    both = jnp.dot(x[...], gate_up, preferred_element_type=F32)
+    gg, uu = both[:, :f], both[:, f:]
+    dhid = jnp.dot(above[...], down, preferred_element_type=F32)
+    gelu, h, square = gelu_parts(gg)
+    hid[...] = (gelu * uu).astype(BF16)
+    dboth[:, :f] = (dhid * uu * gelu_slope(gelu, h, square)).astype(BF16)
+    dboth[:, f:] = (dhid * gelu).astype(BF16)
+
+
+def grads_compute(x, above, hid, dboth, gate_o, up_o, down_o):
+    f = hid.shape[1]
+    both = contract_first(x[...], dboth[...]).astype(BF16)
+    gate_o[...] = both[:, :f]
+    up_o[...] = both[:, f:]
     down_o[...] = contract_first(above[...], hid[...]).astype(BF16)
 
 
 def mlp_specs(tokens, model, f):
     def rows(width):
-        return pl.BlockSpec((tokens // 8, width), lambda i: (jnp.minimum(i, 7), 0))
-
-    columns = pl.BlockSpec((tokens, model // 8), lambda i: (0, jnp.maximum(i - 8, 0)))
-    grads = pl.BlockSpec((model // 8, f), lambda i: (jnp.maximum(i - 8, 0), 0))
+        return pl.BlockSpec((tokens // STEPS, width), lambda i: (jnp.minimum(i, STEPS - 1), 0))
+
+    columns = pl.BlockSpec((tokens, model // STEPS), lambda i: (0, jnp.maximum(i - STEPS, 0)))
+    grads = pl.BlockSpec((model // STEPS, f), lambda i: (jnp.maximum(i - STEPS, 0), 0))
     return rows, columns, grads
 
 
-def keep_units(step, held, outs):
-    at = pl.ds(pl.multiple_of(step * outs[0].shape[0], outs[0].shape[0]), outs[0].shape[0])
-    for kept, out in zip(held, outs):
-        kept[at] = out[...]
+def keep_units(step, hid_all, dboth_all, hid, dboth):
+    rows = hid.shape[0]
+    at = pl.ds(pl.multiple_of(step * rows, rows), rows)
+    hid_all[at] = hid[...]
+    dboth_all[at] = dboth[...]
 
 
 def early_mlp_kernel(
     length, x, above, x_columns, above_columns, gate_up, down, w_in,
-    hid, dgate, dup, gate_o, up_o, down_o, w, hid_all, dgate_all, dup_all, ss, rs
+    hid, dboth, gate_o, up_o, down_o, w, hid_all, dboth_all, ss, rs
 ):
     step = pl.program_id(0)
     hops = LineGather(w, length, ss, rs)
@@ -1797,22 +1800,22 @@
         if length > 2:
             hops.start(2)
 
-    @pl.when(step == 7)
+    @pl.when(step == STEPS)
     def _():
         for hop in range(2, length - 1):
             hops.arrive(hop)
             hops.start(hop + 1)
 
-    @pl.when(step < 8)
+    @pl.when(step < STEPS)
     def _():
-        feed_forward(x, above, gate_up, down, hid, dgate, dup)
-        keep_units(step, (hid_all, dgate_all, dup_all), (hid, dgate, dup))
-
-    @pl.when(step >= 8)
+        feed_forward(x, above, gate_up[...], down[...], hid, dboth)
+        keep_units(step, hid_all, dboth_all, hid, dboth)
+
+    @pl.when(step >= STEPS)
     def _():
-        grads_compute(x_columns, above_columns, hid_all, dgate_all, dup_all, gate_o, up_o, down_o)
-
-    @pl.when(step == 15)
+        grads_compute(x_columns, above_columns, hid_all, dboth_all, gate_o, up_o, down_o)
+
+    @pl.when(step == 2 * STEPS - 1)
     def _():
         hops.arrive(length - 1)
         hops.finish(2, length - 1)
@@ -1822,63 +1825,75 @@
     tokens, model = x.shape
     f = down.shape[1]
     rows, columns, grads = mlp_specs(tokens, model, f)
-    unit_shape = jax.ShapeDtypeStruct((tokens, f), BF16)
     grad_shape = jax.ShapeDtypeStruct((model, f), BF16)
     return pl.pallas_call(
         functools.partial(early_mlp_kernel, length),
-        grid=(16,),
-        out_shape=(unit_shape,) * 3 + (grad_shape,) * 3 + (jax.ShapeDtypeStruct(w.shape, w.dtype),),
+        grid=(2 * STEPS,),
+        out_shape=(
+            jax.ShapeDtypeStruct((tokens, f), BF16),
+            jax.ShapeDtypeStruct((tokens, 2 * f), BF16),
+            grad_shape, grad_shape, grad_shape,
+            jax.ShapeDtypeStruct(w.shape, w.dtype),
+        ),
         in_specs=[rows(model), rows(model), columns, columns, resident(gate_up.shape), resident(down.shape), ANY],
-        out_specs=(rows(f),) * 3 + (grads,) * 3 + (ANY,),
-        scratch_shapes=[pltpu.VMEM((tokens, f), BF16)] * 3 + [DMA((2, length)), DMA((2, length))],
-        input_output_aliases={6: 6},
+        out_specs=(rows(f), rows(2 * f)) + (grads,) * 3 + (ANY,),
+        scratch_shapes=[pltpu.VMEM((tokens, f), BF16), pltpu.VMEM((tokens, 2 * f), BF16)]
+        + [DMA((2, length)), DMA((2, length))],
+        input_output_aliases={6: 5},
         compiler_params=params(collective_id),
         cost_estimate=pl.CostEstimate(flops=12 * tokens * model * f, bytes_accessed=50 * 2**20, transcendentals=0),
     )(x, above, x, above, gate_up, down, w)
 
 
 def late_mlp_kernel(
-    length, cuts, x, above, x_columns, above_columns, hid_one, dgate_one, dup_one, gate_up, down, late, *refs
+    length, cuts, x, above, x_columns, above_columns, hid_one, dboth_one, gate_up_in, down_in, late_in, *refs
 ):
     terms, refs = refs[: len(cuts)], refs[len(cuts) :]
-    out, back, gate_o, up_o, down_o, sums, squares, hid, dgate, dup, *refs = refs
-    (hid_all, dgate_all, dup_all), line_refs = refs[:3], refs[3:]
+    out, back, gate_o, up_o, down_o, sums, squares, *refs = refs
+    gate_up, down, hid, dboth, hid_all, dboth_all, load_s, *line_refs = refs
     step = pl.program_id(0)
     line = LineScatter([(ref, *cut) for ref, cut in zip(terms, cuts)], length, *line_refs)
+    f, g = hid_one.shape[1], hid.shape[1]
+    loads = local_copies(
+        (
+            (late_in.at[:, pl.ds(0, 2 * g)], gate_up.at[:, pl.ds(2 * f, 2 * g)]),
+            (late_in.at[:, pl.ds(2 * g, g)], down.at[:, pl.ds(f, g)]),
+            (down_in, down.at[:, pl.ds(0, f)]),
+            (gate_up_in, gate_up.at[:, pl.ds(0, 2 * f)]),
+        ),
+        load_s,
+    )
 
     @pl.when(step == 0)
     def _():
+        starts(loads)
         greet(line_neighbours(length))
         line.load((1,))
         line.start()
         line.load((*range(2, length), 0))
+        waits(loads)
 
     for hop in range(2, length):
 
-        @pl.when(step == min(10, 4 * (hop - 1)))
+        @pl.when(step == min(2 * STEPS - 2, 2 * (hop - 1)))
         def _():
             line.next = hop
             line.start()
 
-    f, g = down.shape[1], hid.shape[1]
-
-    @pl.when(step < 8)
+    @pl.when(step < STEPS)
     def _():
-        feed_forward(x, above, late.at[:, : 2 * g], late.at[:, 2 * g :], hid, dgate, dup)
-        keep_units(step, (hid_all, dgate_all, dup_all), (hid, dgate, dup))
-        for first_column in range(0, x.shape[1], 512):
-            at = slice(first_column, first_column + 512)
-            ahead = contract_last(hid_one[...], down[at]) + contract_last(hid[...], late[at, 2 * g :])
-            out[:, at] = ahead.astype(BF16)
-            both = contract_last(dgate_one[...], gate_up[at, :f]) + contract_last(dup_one[...], gate_up[at, f:])
-            both = both + contract_last(dgate[...], late[at, :g]) + contract_last(dup[...], late[at, g : 2 * g])
-            back[:, at] = both.astype(BF16)
-
-    @pl.when(step >= 8)
+        feed_forward(x, above, gate_up[:, 2 * f :], down[:, f:], hid, dboth)
+        keep_units(step, hid_all, dboth_all, hid, dboth)
+        units = jnp.concatenate([hid_one[...], hid[...]], axis=1)
+        out[...] = contract_last(units, down[...]).astype(BF16)
+        units = jnp.concatenate([dboth_one[...], dboth[...]], axis=1)
+        back[...] = contract_last(units, gate_up[...]).astype(BF16)
+
+    @pl.when(step >= STEPS)
     def _():
-        grads_compute(x_columns, above_columns, hid_all, dgate_all, dup_all, gate_o, up_o, down_o)
-
-    @pl.when(step == 15)
+        grads_compute(x_columns, above_columns, hid_all, dboth_all, gate_o, up_o, down_o)
+
+    @pl.when(step == 2 * STEPS - 1)
     def _():
         squares[...] = jnp.zeros_like(squares)
         line.end(sums, 0, squares)
@@ -1896,17 +1911,22 @@
 
     return pl.pallas_call(
         functools.partial(late_mlp_kernel, length, cuts),
-        grid=(16,),
+        grid=(2 * STEPS,),
         out_shape=(jax.ShapeDtypeStruct((tokens, model), BF16),) * 2
         + (jax.ShapeDtypeStruct((model, g), BF16),) * 3
         + (jax.ShapeDtypeStruct((line_rows, cut), BF16), TILE),
-        in_specs=[rows(model), rows(model), columns, columns]
-        + [rows(f)] * 3
-        + [resident(v.shape) for v in (gate_up, down, late)]
-        + [ANY] * len(terms),
+        in_specs=[rows(model), rows(model), columns, columns, rows(f), rows(2 * f)]
+        + [ANY] * (3 + len(terms)),
         out_specs=(rows(model),) * 2 + (grads,) * 3 + (whole((line_rows, cut)), whole((8, 128))),
-        scratch_shapes=[pltpu.VMEM((tokens // 8, g), BF16)] * 3
-        + [pltpu.VMEM((tokens, g), BF16)] * 3
+        scratch_shapes=[
+            pltpu.VMEM((model, 2 * f + 2 * g), BF16),
+            pltpu.VMEM((model, f + g), BF16),
+            pltpu.VMEM((tokens // STEPS, g), BF16),
+            pltpu.VMEM((tokens // STEPS, 2 * g), BF16),
+            pltpu.VMEM((tokens, g), BF16),
+            pltpu.VMEM((tokens, 2 * g), BF16),
+            DMA((4,)),
+        ]
         + line_scratch(length, line_rows, cut, len(cuts)),
         compiler_params=params(collective_id),
         cost_estimate=pl.CostEstimate(
@@ -2065,7 +2085,7 @@
         v = jnp.roll(v.reshape(v.shape[0], length, 4, pair), z, axis=1)
         return v.swapaxes(1, 2).reshape(v.shape[0], model)
 
-    normed_one, mixer_full, mlp_gu, mlp_down, late_pack, gains, gate, chan, inputs, above = first(
+    normed_one, mixer_full, mlp_gu, mlp_down, late, gains, gate, chan, inputs, above = first(
         turned(block_input[0]),
         turned(out_grad[0]),
         mixer_weight,
@@ -2079,8 +2099,8 @@
     )
     normed_one = normed_one.reshape(8 * tokens, model)
     mixer_full = mixer_full.reshape(model, 3 * r8)
-    mixed, *kept, grad_out, late, mlp_down = recur_forward(
-        normed_one, mixer_full, gate, chan, above, late_pack, mlp_down, length, 2
+    mixed, *kept, grad_out, mlp_down = recur_forward(
+        normed_one, mixer_full, gate, chan, above, mlp_down, length, 2
     )
     grad_out = grad_out.reshape(8 * tokens, model)
     mixed = mixed.reshape(8 * tokens, r8)
@@ -2090,11 +2110,11 @@
     h2 = f8 - h1
     mlp_gu = mlp_gu.reshape(model, 2 * h1)
     mlp_down = mlp_down.reshape(model, h1)
-    hid, dgg, duu, *early_terms, late = early_mlp(normed_two, grad_out, mlp_gu, mlp_down, late, length, 9)
+    hid, dboth, *early_terms, late = early_mlp(normed_two, grad_out, mlp_gu, mlp_down, late, length, 9)
     gate_one, up_one, down_one = (v.reshape(length, 8 * share, h1) for v in early_terms)
     cut = h1 // 4
     mlp_part, dnormed_two, *late_terms, sums_zero, squares_zero = late_mlp(
-        normed_two, grad_out, (hid, dgg, duu), mlp_gu, mlp_down, late.reshape(model, 3 * h2),
+        normed_two, grad_out, (hid, dboth), mlp_gu, mlp_down, late.reshape(model, 3 * h2),
         (gate_one, up_one), ((0, h1), (0, cut)), length, 11,
     )
     gate_two, up_two, down_two = (v.reshape(length, 8 * share, h2) for v in late_terms)

time: 617 us -> 598 us (0.969)
  Pallas kernels: 607 us -> 588 us
    pallas_call x1, Pallas kernels: 95.1 us -> 86.6 us  [middle(): pl.pallas_call(functools.partial(middle_kernel, length), out_shape=(jax.S...]
where the time goes in v7:
time: 598 us; the launch traced here: 590 us
  Pallas kernels  588 us (98%)
    pallas_call x1, Pallas kernels, closing(): pl.pallas_call(functools.partial(closing_kernel, length), out_shape=(jax....  91.3 us
    pallas_call x1, Pallas kernels, turn(): pl.pallas_call(functools.partial(turn_kernel, length, cuts), out_shape=(j...  90.1 us
    pallas_call x1, Pallas kernels, middle(): pl.pallas_call(functools.partial(middle_kernel, length), out_shape=(jax.S...  86.6 us
    pallas_call x1, Pallas kernels, first(): pl.pallas_call(functools.partial(first_kernel, length), out_shape=(jax.Sh...  86.4 us
    pallas_call x1, Pallas kernels, recur_backward(): pl.pallas_call(functools.partial(backward_kernel, length, cuts, head), ou...  54.2 us
    pallas_call x1, Pallas kernels, late_mlp(): pl.pallas_call(functools.partial(late_mlp_kernel, length, cuts), grid=(2...  50.6 us
    pallas_call x1, Pallas kernels, recur_forward(): pl.pallas_call(functools.partial(forward_kernel, length), out_shape=(jax....  49.5 us
    pallas_call x1, Pallas kernels, early_mlp(): pl.pallas_call(functools.partial(early_mlp_kernel, length), grid=(2 * STE...  38.7 us

profile of v7, /device:TPU:0, one launch (start us, length us, event | category | flops | bytes accessed | tf_op | source)
XLA Modules:
  0.0 590.2 jit_solution(6146630907799850463)
XLA Ops:
  0.7 86.4 %shard_map.304 = (bf16[8,256,2048]{2,1,0:T(8,128)(2,1)}, bf16[4,8,64,960]{3,2,1,0:T(8,128)(2,1)}, bf16[4,8,64,1024]{3,2,1,0:T(8,128)(2,1)}, bf16[4,8,64,512]{3,2...) custom-call(bf16[256,2048]{1,0:T(8,128)(2,1)} %bitcast.47, ...), custom_call_target="tpu_custom_call" | custom-call | bytes 314572800 | tf_op jit(solution)/shard_map/pallas_call | solution.py:1207
  87.0 49.5 %shard_map.305 = (bf16[4,512,320]{2,1,0:T(8,128)(2,1)}, f32[4,512,384]{2,1,0:T(8,128)}, f32[4,512,384]{2,1,0:T(8,128)}, f32[4,512,384]{2,1,0:T(8,128)}, f32[4,51...) custom-call(bf16[2048,2048]{1,0:T(8,128)(2,1)} %bitcast.32, ...), custom_call_target="tpu_custom_call", output_to_operand_aliasing={{11}: (5, {})} | custom-call | flops 1207959552 | bytes 104857600 | tf_op jit(solution)/shard_map/pallas_call | solution.py:1501
  136.5 86.6 %shard_map.306 = (f32[256,2048]{1,0:T(8,128)}, bf16[8,256,2048]{2,1,0:T(8,128)(2,1)}, bf16[4,8,64,1024]{3,2,1,0:T(8,128)(2,1)}, bf16[4,8,64,768]{3,2,1,0:T(8,128)(2,1)}) custom-call(bf16[2048,320]{1,0:T(8,128)(2,1)} %bitcast.44, bf16[2048,960]{1,0:T(8,128)(2,1)} %bitcast.29, ...), custom_call_target="tpu_custom_call", output_to_operand_aliasing={{2}: (4, {}), {3}: (5, {})} | custom-call | bytes 314572800 | tf_op jit(solution)/shard_map/pallas_call | solution.py:640
  223.2 38.7 %shard_map.307 = (bf16[2048,512]{1,0:T(8,128)(2,1)}, bf16[2048,1024]{1,0:T(8,128)(2,1)}, bf16[2048,512]{1,0:T(8,128)(2,1)}, bf16[2048,512]{1,0:T(8,128)(2,1)}, b...) custom-call(bf16[2048,2048]{1,0:T(8,128)(2,1)} %bitcast.59, ...), custom_call_target="tpu_custom_call", output_to_operand_aliasing={{5}: (6, {})} | custom-call | flops 25769803776 | bytes 52428800 | tf_op jit(solution)/shard_map/pallas_call | solution.py:1829
  261.9 50.6 %shard_map.308 = (bf16[2048,2048]{1,0:T(8,128)(2,1)}, bf16[2048,2048]{1,0:T(8,128)(2,1)}, bf16[2048,256]{1,0:T(8,128)(2,1)}, bf16[2048,256]{1,0:T(8,128)(2,1)}, ...) custom-call(bf16[2048,2048]{1,0:T(8,128)(2,1)} %bitcast.61, bf16[2048,2048]{1,0:T(8,128)(2,1)} %bitcast.57, ...), custom_call_target="tpu_custom_call" | custom-call | flops 32212254720 | bytes 73400320 | tf_op jit(solution)/shard_map/pallas_call | solution.py:1912
  312.5 90.1 %shard_map.309 = (f32[256,2048]{1,0:T(8,128)}, f32[8,2048]{1,0:T(8,128)}, bf16[8,256,2048]{2,1,0:T(8,128)(2,1)}, f32[8,256,384]{2,1,0:T(8,128)}, bf16[512,1152]{1,0:T(8,128)(2,1)}, /*index=5*/f32[8,128]{1,0:T(8,128)}) custom-call(bf16[8,256,2048]{2,1,0:T(8,128)(2,1)} %bitcast.34, f32[256,2048]{1,0:T(8,128)} %get-tuple-element.119.residual_in, ...), custom_call_target="tpu_custom_call" | custom-call | bytes 314572800 | tf_op jit(solution)/shard_map/pallas_call | solution.py:752
  402.6 54.2 %shard_map.310 = (bf16[4,512,640]{2,1,0:T(8,128)(2,1)}, f32[4,80,384]{2,1,0:T(8,128)}, bf16[512,512]{1,0:T(8,128)(2,1)}, f32[8,128]{1,0:T(8,128)}, bf16[8,64,640...) custom-call(f32[4,512,384]{2,1,0:T(8,128)} %bitcast.37, bf16[384,768]{1,0:T(8,128)(2,1)} %get-tuple-element.99.gate, ...), custom_call_target="tpu_custom_call" | custom-call | flops 1207959552 | bytes 125829120 | tf_op jit(solution)/shard_map/pallas_call | solution.py:1700
  456.8 91.3 %shard_map.311 = (f32[256,2048]{1,0:T(8,128)}, f32[8,2048]{1,0:T(8,128)}, f32[80,384]{1,0:T(8,128)}, bf16[256,2048]{1,0:T(8,128)(2,1)}, bf16[8,64,512]{2,1,0:T(8...) custom-call(bf16[2048,2048]{1,0:T(8,128)(2,1)} %bitcast.33, bf16[2048,2048]{1,0:T(8,128)(2,1)} %bitcast.54, ...), custom_call_target="tpu_custom_call" | custom-call | flops 13421772800 | bytes 367001600 | tf_op jit(solution)/shard_map/pallas_call | solution.py:964
  548.1 23.2 %shard_map.312 = (bf16[8,64,960]{2,1,0:T(8,128)(2,1)}, f32[2,64]{1,0:T(2,128)}, f32[8,128]{1,0:T(8,128)}, f32[8,128]{1,0:T(8,128)}) custom-call(bf16[8,64,960]{2,1,0:T(8,128)(2,1)} %bitcast.52, f32[8,2048]{1,0:T(8,128)} %get-tuple-element.143.gain, f32[8,2048]{1,0:T(8,128)} %get-tuple-element.144.gain_two, f32[80,384]{1,0:T(8,128)} %get-tuple-element.145.gates.refs_11_, ...), custom_call_target="tpu_custom_call" | custom-call | tf_op jit(solution)/shard_map/pallas_call | solution.py:1302
  571.3 1.2 slice.3
  572.5 17.4 %shard_map.313 = (f32[64,7680]{1,0:T(8,128)}, f32[64,7680]{1,0:T(8,128)}, f32[64,7680]{1,0:T(8,128)}, f32[64,18432]{1,0:T(8,128)}, f32[64,18432]{1,0:T(8,128)}, ...) custom-call(f32[8,128]{1,0:T(8,128)} %get-tuple-element.150.factor, ...), custom_call_target="tpu_custom_call" | custom-call | bytes 40108032 | tf_op jit(solution)/shard_map/pallas_call | solution.py:2020

commit v8 on v7

--- a/solution.py
+++ b/solution.py
@@ -243,15 +243,22 @@
     ]
 
 
-def exchange_steps(a, o, loc, ss, rs, columns=None):
+def exchange_steps(a, o, loc, ss, rs):
     y, c, z, x = place()
     me = rank(y, c, x)
-    dst = o.at[me] if columns is None else o.at[me, :, columns]
+    dst = o.at[me]
+    rows = o.shape[1]
+
+    def block(t):
+        if len(a.shape) == 3:
+            return a.at[t]
+        return a.at[pl.ds(pl.multiple_of(t * rows, rows), rows)]
+
     copies = []
     for n, (fy, fc, fx) in enumerate(FLIPS):
         ty, tc, tx = flip(y, fy), flip(c, fc), flip(x, fx)
-        copies.append(remote(a.at[rank(ty, tc, tx)], dst, ss.at[n], rs.at[n], device(ty, tc, z, tx)))
-    own = pltpu.make_async_copy(a.at[me], dst, loc)
+        copies.append(remote(block(rank(ty, tc, tx)), dst, ss.at[n], rs.at[n], device(ty, tc, z, tx)))
+    own = pltpu.make_async_copy(block(me), dst, loc)
     own.start()
     return copies, own
 
@@ -774,8 +781,8 @@
 
 def closing_kernel(
     length, x_in, dmz_in, dproj_in, mixed_in, mixer_in, q, residual_in, block, inputs_in, above_in, gains_in, gp_in,
-    grad_out, gain, gates_o, out_out, e_o, sums, squares,
-    x_part, dmz_part, g, back, total, o, up_a, down_a, up_b, down_b, gp_got, gp_sum,
+    grad_out, gain, gates_o, out_out, e_o, early_o, sums, squares,
+    early_sums, early_l, early_s, early_r, x_part, dmz_part, g, back, total, o, up_a, down_a, up_b, down_b, gp_got, gp_sum,
     ls, lr, load_s, free, loc, es, er, gate_s, gate_r, move_s, move_r,
     dproj, mixed, mixer, residual, inputs, above, gains, gp, grad_o, out, in_s, keep_s, *scatter_refs,
 ):
@@ -941,13 +948,15 @@
     while queue:
         advance()
     squares[...] = jnp.zeros_like(squares)
-    line_a.end(sums, 0, squares)
-    line_b.end(sums, split, squares)
+    line_a.end(early_sums, 0, squares)
+    early_copies, early_own = exchange_steps(early_sums, early_o, early_l, early_s, early_r)
+    line_b.end(sums, 0, squares)
     pl.when(moves == 1)(lambda: move.wait())
     waits(keeps)
-    for copy in copies:
+    for copy in copies + early_copies:
         copy.wait()
     own.wait()
+    early_own.wait()
 
 
 def closing(x, dmz, dproj, mixed, mixer, q, residual, block, inputs, above, gains, gp, length, collective_id):
@@ -969,12 +978,14 @@
             jax.ShapeDtypeStruct(pack, F32),
             jax.ShapeDtypeStruct((rows, width), BF16),
             jax.ShapeDtypeStruct(block.shape, BF16),
-            jax.ShapeDtypeStruct((line_rows, 3 * part), BF16),
+            jax.ShapeDtypeStruct((8, share, split), BF16),
+            jax.ShapeDtypeStruct((line_rows, 3 * part - split), BF16),
             TILE,
         ),
         in_specs=[ANY] * 12,
-        out_specs=(ANY, VM, VM, ANY, ANY, VM, VM),
+        out_specs=(ANY, VM, VM, ANY, ANY, ANY, VM, VM),
         scratch_shapes=[
+            pltpu.VMEM((line_rows, split), BF16), DMA, DMA((7,)), DMA((7,)),
             pltpu.VMEM((2, tokens, columns), BF16),
             pltpu.VMEM((2, tokens, columns), BF16),
             pltpu.VMEM((length, line_rows, 3 * part), BF16),
@@ -1141,11 +1152,6 @@
     rows_loop(half, body, half)
     gather.begin_half(1)
     keeps = starts(local_copies(((inputs_k, inputs_o), (above_k, above_o)), keep_s))
-    gather.middle()
-    late, late_own = exchange_steps(w2, w2_o.at[0], loc.at[0], fs.at[2], fr.at[2])
-    if length > 3:
-        hops.arrive(2)
-        hops.start(3)
     for copy in gates:
         copy.wait()
     gate_rows, columns = gate_w.shape
@@ -1170,6 +1176,11 @@
     rate = 8.0 * (jnp.maximum(-lam, 0.0) + 2.0 * t * series)
     fill_rows = jnp.concatenate([jnp.zeros((7, rc - part), F32), jnp.ones((1, rc - part), F32)])
     chan_o[...] = jnp.concatenate([jnp.concatenate([rows_of[:7], rate]), fill_rows], axis=1)
+    if length > 3:
+        hops.arrive(2)
+        hops.start(3)
+    gather.middle()
+    late, late_own = exchange_steps(w2, w2_o.at[0], loc.at[0], fs.at[2], fr.at[2])
     gather.relays()
     for hop in range(min(3, length - 1), length):
         hops.arrive(hop)
@@ -1339,9 +1350,9 @@
 
 
 def forward_kernel(
-    length, x_in, mixer, gate, chan, above, w_in,
+    length, x_in, mixer_in, gate, chan, above, w_in,
     mixed, branch_o, decay_o, width_o, recur_o, enter_o, conv_o, xe_o, se_o, ends_o, above_o, w,
-    x_part, pre, loc_h, ends, carry, hs, hr, es, er, gather_l, gather_s, gather_r, hop_s, hop_r, load_s, keep_s,
+    x_part, pre, loc_h, ends, carry, hs, hr, es, er, gather_l, gather_s, gather_r, hop_s, hop_r, load_s, keep_s, mixer,
     branch, decay_k, width_k, recur_k, enter_k, conv_k, xe, se,
 ):
     keeps = [
@@ -1364,11 +1375,15 @@
         return pltpu.make_async_copy(x_in.at[at], x_part.at[slot], load_s.at[slot])
 
     load(0, 0).start()
+    mixer_load = pltpu.make_async_copy(mixer_in, mixer, load_s.at[2])
+    mixer_load.start()
     greet(line + gather_peers())
     hops = LineGather(w, length, hop_s, hop_r)
     hops.start(1)
     gather = Gather(above, above_o, gather_l, gather_s, gather_r)
     gather.begin()
+
+    mixer_load.wait()
 
     @pl.loop(0, seqs)
     def _(b):
@@ -1507,7 +1522,7 @@
             jax.ShapeDtypeStruct((8,) + above.shape, above.dtype),
             jax.ShapeDtypeStruct(w.shape, w.dtype),
         ),
-        in_specs=[ANY, VM, VM, VM, ANY, ANY],
+        in_specs=[ANY, ANY, VM, VM, ANY, ANY],
         out_specs=(VM,) + (ANY,) * 8 + (VM, ANY, ANY),
         scratch_shapes=[
             pltpu.VMEM((2, span, x.shape[1]), BF16),
@@ -1517,7 +1532,8 @@
             pltpu.VMEM((seqs, 8, rc), F32),
             DMA, DMA, DMA((length,)), DMA((length,)),
             DMA, DMA((14,)), DMA((14,)), DMA((2, length)), DMA((2, length)),
-            DMA((2,)), DMA((8,)),
+            DMA((3,)), DMA((8,)),
+            *held(mixer),
             *[pltpu.VMEM(v.shape, v.dtype) for v in kept],
         ],
         input_output_aliases={5: 11},
@@ -1602,8 +1618,6 @@
     tails = [remote(ends.at[z], ends.at[z], es.at[k], er.at[k], line[k]) for k in range(length - 1)]
     for copy in tails:
         copy.wait()
-    scatter.start()
-    scatter.start()
     for copy in loads[4:]:
         copy.wait()
     carry[...] = jnp.zeros_like(carry)
@@ -1612,10 +1626,8 @@
 
     gchan[...] = jnp.zeros_like(gchan)
 
-    @pl.loop(0, seqs * chunks)
-    def _(i):
-        b = i // chunks
-        r = pl.multiple_of((i - b * chunks) * CHUNK, CHUNK)
+    def gradients(b, chunk):
+        r = pl.multiple_of(chunk * CHUNK, CHUNK)
         at = pl.ds(r, CHUNK)
         g = grad[b, at] + suffix[b, at] * carry[b, 0:1]
         a, w, ra, ri = decay[b, at], width[b, at], recur[b, at], enter[b, at]
@@ -1637,11 +1649,20 @@
         de[b, at] = dcv
         gchan[4] += fold(dcv)
 
+    pl.loop(0, seqs)(lambda b: gradients(b, 0))
     behind = device(y, c, lax.rem(z + length - 1, length), x)
     halo = remote(de.at[:, pl.ds(0, 8)], de.at[:, pl.ds(span, 8)], hs, hr, behind)
-    halo.wait()
     scatter.start()
     scatter.start()
+
+    @pl.loop(0, seqs * (chunks - 1))
+    def _(i):
+        b = i // (chunks - 1)
+        gradients(b, 1 + i - b * (chunks - 1))
+
+    scatter.start()
+    scatter.start()
+    halo.wait()
     low = conv[...].reshape(seqs * span, rc)
     recur_grad, enter_grad = (
         contract_first(low, dgate[:, :, at].reshape(seqs * span, rc)) for at in (slice(0, rc), slice(rc, 2 * rc))
@@ -1967,11 +1988,12 @@
     states, refs = refs[: 3 * len(sources)], refs[3 * len(sources) :]
     count = sum(len(source) for source in sources)
     grads, small, refs = refs[:count], refs[count : count + 11], refs[count + 11 :]
-    results, outs = refs[:2], refs[2:]
-    for result, out in zip(results, outs[-2:]):
+    results, norm, outs = refs[:2], refs[2], refs[3:]
+    for result, out in zip(results, outs[-3:]):
         out[...] = result[...]
+    outs[-1][...] = norm[0:1, 0:1]
     one = factor[0:1, 0:1]
-    pl.when(pl.program_id(0) == 0)(lambda: small_steps(one, small, outs[3 * len(sources) : -2]))
+    pl.when(pl.program_id(0) == 0)(lambda: small_steps(one, small, outs[3 * len(sources) : -3]))
     for n, source in enumerate(sources):
         parts = []
         for pieces in source:
@@ -1999,7 +2021,7 @@
             w_o[:, cols] = weight_new
 
 
-def adam(matrices, small, factor, passed):
+def adam(matrices, small, factor, norm, passed):
     rows = matrices[0][0].shape[0]
     step = min(rows, 16)
 
@@ -2020,20 +2042,23 @@
     return pl.pallas_call(
         functools.partial(adam_kernel, [matrix[4] for matrix in matrices]),
         grid=(steps,),
-        out_shape=tuple(jax.ShapeDtypeStruct(v.shape, v.dtype) for v in results),
+        out_shape=tuple(jax.ShapeDtypeStruct(v.shape, v.dtype) for v in results)
+        + (jax.ShapeDtypeStruct((1, 1), F32),),
         in_specs=[pl.BlockSpec((8, 128), lambda i: (0, 0))]
         + [block(v) for v in states]
         + [pl.BlockSpec((8, step, g.shape[2]), lambda i: (0, i, 0)) for g in grads]
         + [whole(v) for v in small]
-        + [slab(v) for v in passed],
+        + [slab(v) for v in passed]
+        + [whole(norm)],
         out_specs=tuple(block(v) for v in states)
         + tuple(whole(v) for v in small[2:])
-        + tuple(slab(v) for v in passed),
+        + tuple(slab(v) for v in passed)
+        + (pl.BlockSpec((1, 1), lambda i: (0, 0)),),
         compiler_params=pltpu.CompilerParams(vmem_limit_bytes=VMEM_BYTES),
         cost_estimate=pl.CostEstimate(
             flops=0, bytes_accessed=sum(8 * v.size for v in states), transcendentals=0
         ),
-    )(factor, *states, *grads, *small, *passed)
+    )(factor, *states, *grads, *small, *passed, norm)
 
 
 def on_device(
@@ -2133,14 +2158,15 @@
         (up_two, down_two), ((0, 0, h2), (1, 0, h2)), length, 6,
     )
     dproj = dproj.reshape(4 * span, 2 * r8)
-    input_grad, gain_one, gates_sum, block_output, back_two, mixer_sums, squares_three = closing(
+    input_grad, gain_one, gates_sum, block_output, back_two, mixer_early, mixer_sums, squares_three = closing(
         normed_one, dmz, dproj, mixed, mixer_full, mlp_part, residual, sums_two,
         inputs, grad_residual, gains, gate_back, length, 7,
     )
     mixer_back, gains_sum, norm, factor = last(
-        mixer_sums.reshape(8, share, 3 * r8), gain_one, gain_two, gates_sum,
+        mixer_sums.reshape(8, share, mixer_sums.shape[1]), gain_one, gain_two, gates_sum,
         (squares_zero, squares_one, squares_two, squares_three), length, 8,
     )
+    split = mixer_early.shape[2]
     mlp_sources = (
         [(0, h1, 0, f8), (h1, cut, hidden, f8)],
         [
@@ -2153,8 +2179,11 @@
     states = adam(
         (
             (
-                mixer_weight, first_mixer, second_mixer, (mixer_back,),
-                ([(n * r8, r8, n * lru, r8) for n in range(3)],),
+                mixer_weight, first_mixer, second_mixer, (mixer_early, mixer_back),
+                (
+                    [(0, r8, 0, r8), (r8, split - r8, lru, r8)],
+                    [(0, 2 * r8 - split, lru + split - r8, r8), (2 * r8 - split, r8, 2 * lru, r8)],
+                ),
             ),
             (mlp_weight, first_mlp, second_mlp, (back_zero, back_one, back_two), mlp_sources),
         ),
@@ -2163,14 +2192,15 @@
             chan_params, first_chan, second_chan,
         ),
         factor,
+        norm,
         (block_output, input_grad),
     )
-    *states, block_output, input_grad = states
+    *states, block_output, input_grad, norm = states
     mixer_up, mlp_up, gains_up, gate_up, chan_up = (states[3 * n : 3 * n + 3] for n in range(5))
     return (
         turned_back(block_output)[None],
         turned_back(input_grad)[None],
-        norm[0, 0],
+        norm.reshape(()),
         *gains_up,
         *mixer_up,
         *gate_up,

time: 598 us -> 591 us (0.988)
    pallas_call x1, Pallas kernels: 91.3 us -> 102 us  [closing(): pl.pallas_call(functools.partial(closing_kernel, length), out_shape=(jax....]
    pallas_call x1, Pallas kernels: 23.2 us -> 16.5 us  [last(): pl.pallas_call(functools.partial(last_kernel, length, share), out_shape=(...]
where the time goes in v8:
time: 591 us; the launch traced here: 586 us
  Pallas kernels  585 us (99%)
    pallas_call x1, Pallas kernels, closing(): pl.pallas_call(functools.partial(closing_kernel, length), out_shape=(jax....  102 us
    pallas_call x1, Pallas kernels, turn(): pl.pallas_call(functools.partial(turn_kernel, length, cuts), out_shape=(j...  87.5 us
    pallas_call x1, Pallas kernels, middle(): pl.pallas_call(functools.partial(middle_kernel, length), out_shape=(jax.S...  86.5 us
    pallas_call x1, Pallas kernels, first(): pl.pallas_call(functools.partial(first_kernel, length), out_shape=(jax.Sh...  85.7 us
    pallas_call x1, Pallas kernels, recur_backward(): pl.pallas_call(functools.partial(backward_kernel, length, cuts, head), ou...  52.4 us
    pallas_call x1, Pallas kernels, late_mlp(): pl.pallas_call(functools.partial(late_mlp_kernel, length, cuts), grid=(2...  50.6 us
    pallas_call x1, Pallas kernels, recur_forward(): pl.pallas_call(functools.partial(forward_kernel, length), out_shape=(jax....  47.7 us
    pallas_call x1, Pallas kernels, early_mlp(): pl.pallas_call(functools.partial(early_mlp_kernel, length), grid=(2 * STE...  38.7 us

profile of v8, /device:TPU:0, one launch (start us, length us, event | category | flops | bytes accessed | tf_op | source)
XLA Modules:
  0.0 586.4 jit_solution(708166050063009638)
XLA Ops:
  0.7 85.7 %shard_map.304 = (bf16[8,256,2048]{2,1,0:T(8,128)(2,1)}, bf16[4,8,64,960]{3,2,1,0:T(8,128)(2,1)}, bf16[4,8,64,1024]{3,2,1,0:T(8,128)(2,1)}, bf16[4,8,64,512]{3,2...) custom-call(bf16[256,2048]{1,0:T(8,128)(2,1)} %bitcast.47, ...), custom_call_target="tpu_custom_call" | custom-call | bytes 314572800 | tf_op jit(solution)/shard_map/pallas_call | solution.py:1218
  86.3 47.7 %shard_map.305 = (bf16[4,512,320]{2,1,0:T(8,128)(2,1)}, f32[4,512,384]{2,1,0:T(8,128)}, f32[4,512,384]{2,1,0:T(8,128)}, f32[4,512,384]{2,1,0:T(8,128)}, f32[4,51...) custom-call(bf16[2048,2048]{1,0:T(8,128)(2,1)} %bitcast.32, ...), custom_call_target="tpu_custom_call", output_to_operand_aliasing={{11}: (5, {})} | custom-call | flops 1207959552 | bytes 104857600 | tf_op jit(solution)/shard_map/pallas_call | solution.py:1516
  134.1 86.5 %shard_map.306 = (f32[256,2048]{1,0:T(8,128)}, bf16[8,256,2048]{2,1,0:T(8,128)(2,1)}, bf16[4,8,64,1024]{3,2,1,0:T(8,128)(2,1)}, bf16[4,8,64,768]{3,2,1,0:T(8,128)(2,1)}) custom-call(bf16[2048,320]{1,0:T(8,128)(2,1)} %bitcast.44, bf16[2048,960]{1,0:T(8,128)(2,1)} %bitcast.29, ...), custom_call_target="tpu_custom_call", output_to_operand_aliasing={{2}: (4, {}), {3}: (5, {})} | custom-call | bytes 314572800 | tf_op jit(solution)/shard_map/pallas_call | solution.py:647
  220.6 38.7 %shard_map.307 = (bf16[2048,512]{1,0:T(8,128)(2,1)}, bf16[2048,1024]{1,0:T(8,128)(2,1)}, bf16[2048,512]{1,0:T(8,128)(2,1)}, bf16[2048,512]{1,0:T(8,128)(2,1)}, b...) custom-call(bf16[2048,2048]{1,0:T(8,128)(2,1)} %bitcast.59, ...), custom_call_target="tpu_custom_call", output_to_operand_aliasing={{5}: (6, {})} | custom-call | flops 25769803776 | bytes 52428800 | tf_op jit(solution)/shard_map/pallas_call | solution.py:1850
  259.3 50.6 %shard_map.308 = (bf16[2048,2048]{1,0:T(8,128)(2,1)}, bf16[2048,2048]{1,0:T(8,128)(2,1)}, bf16[2048,256]{1,0:T(8,128)(2,1)}, bf16[2048,256]{1,0:T(8,128)(2,1)}, ...) custom-call(bf16[2048,2048]{1,0:T(8,128)(2,1)} %bitcast.61, bf16[2048,2048]{1,0:T(8,128)(2,1)} %bitcast.57, ...), custom_call_target="tpu_custom_call" | custom-call | flops 32212254720 | bytes 73400320 | tf_op jit(solution)/shard_map/pallas_call | solution.py:1933
  309.9 87.5 %shard_map.309 = (f32[256,2048]{1,0:T(8,128)}, f32[8,2048]{1,0:T(8,128)}, bf16[8,256,2048]{2,1,0:T(8,128)(2,1)}, f32[8,256,384]{2,1,0:T(8,128)}, bf16[512,1152]{1,0:T(8,128)(2,1)}, /*index=5*/f32[8,128]{1,0:T(8,128)}) custom-call(bf16[8,256,2048]{2,1,0:T(8,128)(2,1)} %bitcast.34, f32[256,2048]{1,0:T(8,128)} %get-tuple-element.121.residual_in, ...), custom_call_target="tpu_custom_call" | custom-call | bytes 314572800 | tf_op jit(solution)/shard_map/pallas_call | solution.py:759
  397.4 52.4 %shard_map.310 = (bf16[4,512,640]{2,1,0:T(8,128)(2,1)}, f32[4,80,384]{2,1,0:T(8,128)}, bf16[512,512]{1,0:T(8,128)(2,1)}, f32[8,128]{1,0:T(8,128)}, bf16[8,64,640...) custom-call(f32[4,512,384]{2,1,0:T(8,128)} %bitcast.37, bf16[384,768]{1,0:T(8,128)(2,1)} %get-tuple-element.101.gate, ...), custom_call_target="tpu_custom_call" | custom-call | flops 1207959552 | bytes 125829120 | tf_op jit(solution)/shard_map/pallas_call | solution.py:1721
  449.7 102.4 %shard_map.311 = (f32[256,2048]{1,0:T(8,128)}, f32[8,2048]{1,0:T(8,128)}, f32[80,384]{1,0:T(8,128)}, bf16[256,2048]{1,0:T(8,128)(2,1)}, bf16[8,64,512]{2,1,0:T(8...) custom-call(bf16[2048,2048]{1,0:T(8,128)(2,1)} %bitcast.33, ...), custom_call_target="tpu_custom_call" | custom-call | flops 13421772800 | bytes 367001600 | tf_op jit(solution)/shard_map/pallas_call | solution.py:973
  552.1 16.5 %shard_map.312 = (bf16[8,64,448]{2,1,0:T(8,128)(2,1)}, f32[2,64]{1,0:T(2,128)}, f32[8,128]{1,0:T(8,128)}, f32[8,128]{1,0:T(8,128)}) custom-call(bf16[8,64,448]{2,1,0:T(8,128)(2,1)} %bitcast.53, f32[8,2048]{1,0:T(8,128)} %get-tuple-element.145.gain, f32[8,2048]{1,0:T(8,128)} %get-tuple-element.146.gain_two, f32[80,384]{1,0:T(8,128)} %get-tuple-element.147.gates.refs_12_, ...), custom_call_target="tpu_custom_call" | custom-call | tf_op jit(solution)/shard_map/pallas_call | solution.py:1313
  568.6 17.6 %shard_map.313 = (f32[64,7680]{1,0:T(8,128)}, f32[64,7680]{1,0:T(8,128)}, f32[64,7680]{1,0:T(8,128)}, f32[64,18432]{1,0:T(8,128)}, f32[64,18432]{1,0:T(8,128)}, ...) custom-call(f32[8,128]{1,0:T(8,128)} %get-tuple-element.152.factor, ...), custom_call_target="tpu_custom_call" | custom-call | bytes 40108032 | tf_op jit(solution)/shard_map/pallas_call | solution.py:2042

commit v9 on v8

--- a/solution.py
+++ b/solution.py
@@ -166,57 +166,70 @@
     from_c, own, sends = {}, {}, []
     for n, (t, h) in enumerate(order):
         ty, tx = where[t]
-        if prepare and all(key[0] != t for key in own):
+        if mine is not None and prepare and all(key[0] != t for key in own):
             prepare(rank(ty, c, tx))
             prepare(rank(ty, 1 - c, tx))
-        own[t, h] = pltpu.make_async_copy(
-            p.at[rank(ty, c, tx), cut[h]], mine.at[t, h], loc.at[n]
-        )
-        own[t, h].start()
+        if mine is None:
+            own[t, h] = None
+        else:
+            own[t, h] = pltpu.make_async_copy(
+                p.at[rank(ty, c, tx), cut[h]], mine.at[t, h], loc.at[n]
+            )
+            own[t, h].start()
         from_c[t, h] = remote(
             p.at[rank(ty, 1 - c, tx), cut[h]], sib.at[t, h], ss.at[n], rs.at[n], to_c
         )
         sends.append(from_c[t, h])
     yield "begun"
 
+    def own_ref(t, h):
+        return p.at[rank(where[t][0], c, where[t][1]), cut[h]] if mine is None else mine.at[t, h]
+
+    pieces = ((0, 0), (0, 1), (1, 0), (2, 1), (2, 0), (1, 1))
+
+    def part_ref(k):
+        return own_ref(*pieces[k]) if part is None else part.at[k]
+
     def add(dst, t, h, extra):
-        own[t, h].wait()
+        if own[t, h] is not None:
+            own[t, h].wait()
+        term = own_ref(t, h)
         from_c[t, h].wait_recv()
 
         @pl.loop(0, half // step)
         def _(i):
             at = pl.ds(pl.multiple_of(i * step, step), step)
-            total = mine[t, h, at].astype(F32) + sib[t, h, at].astype(F32)
+            total = term[at].astype(F32) + sib[t, h, at].astype(F32)
             for ref in extra:
                 total = total + ref[at].astype(F32)
             dst[at] = total.astype(dst.dtype)
 
     def send(k, slot, to):
-        copy = remote(part.at[k], got.at[slot], ss.at[8 + k], rs.at[8 + slot], to)
+        copy = remote(part_ref(k), got.at[slot], ss.at[8 + k], rs.at[8 + slot], to)
         sends.append(copy)
         return copy
 
     def arrival(slot):
         return pltpu.make_async_remote_copy(
-            src_ref=part.at[0], dst_ref=got.at[slot], send_sem=ss.at[8], recv_sem=rs.at[8 + slot],
+            src_ref=got.at[slot], dst_ref=got.at[slot], send_sem=ss.at[8], recv_sem=rs.at[8 + slot],
             device_id=to_x, device_id_type=MESH,
         )
 
-    add(part.at[0], 0, 0, ())
+    add(part_ref(0), 0, 0, ())
     send(0, 1, to_y)
-    add(part.at[1], 0, 1, ())
+    add(part_ref(1), 0, 1, ())
     send(1, 3, to_x)
-    add(part.at[2], 1, 0, ())
+    add(part_ref(2), 1, 0, ())
     send(2, 0, to_y)
-    add(part.at[3], 2, 1, ())
+    add(part_ref(3), 2, 1, ())
     send(3, 2, to_x)
     yield "sent"
     arrival(1).wait_recv()
-    add(part.at[4], 2, 0, (got.at[1],))
+    add(part_ref(4), 2, 0, (got.at[1],))
     send(4, 4, to_x)
     yield "early"
     arrival(3).wait_recv()
-    add(part.at[5], 1, 1, (got.at[3],))
+    add(part_ref(5), 1, 1, (got.at[3],))
     send(5, 5, to_y)
     yield "late"
     arrival(0).wait_recv()
@@ -783,8 +796,9 @@
     length, x_in, dmz_in, dproj_in, mixed_in, mixer_in, q, residual_in, block, inputs_in, above_in, gains_in, gp_in,
     grad_out, gain, gates_o, out_out, e_o, early_o, sums, squares,
     early_sums, early_l, early_s, early_r, x_part, dmz_part, g, back, total, o, up_a, down_a, up_b, down_b, gp_got, gp_sum,
-    ls, lr, load_s, free, loc, es, er, gate_s, gate_r, move_s, move_r,
-    dproj, mixed, mixer, residual, inputs, above, gains, gp, grad_o, out, in_s, keep_s, *scatter_refs,
+    ls, lr, load_s, loc, es, er, gate_s, gate_r, move_s, move_r,
+    dproj, mixed, mixer, residual, inputs, above, gains, gp, in_s, keep_s,
+    mine, sib_q, got_q, loc_q, ss_q, rs_q, sib_p, got_p, ss_p, rs_p,
 ):
     inflow = starts(
         local_copies(
@@ -818,7 +832,8 @@
     part = mixed.shape[1]
     columns = x_part.shape[2]
     steps = model // columns
-    rows = tokens // steps
+    rows, width = residual.shape
+    half = rows // 2
     line_rows = g.shape[1]
 
     def loads(i, slot):
@@ -851,12 +866,12 @@
             if queue:
                 queue.pop(0).start()
 
-    output = scatter_steps(q, total, *scatter_refs)
+    output = scatter_steps(q, total, mine, sib_q, None, got_q, loc_q, ss_q, rs_q)
     next(output)
     copies, own = exchange_steps(block, e_o, loc, es, er)
 
-    def compute(n):
-        @pl.loop(0, group)
+    def compute(n, start=0, stop=None):
+        @pl.loop(start, group if stop is None else stop)
         def _(j):
             count = n * group + j
             slot = count - count // 2 * 2
@@ -879,40 +894,48 @@
             k = i * columns // line_rows
             at = pl.ds(pl.multiple_of(i * columns - k * line_rows, columns), columns)
             g[k, at] = jnp.concatenate([front, tail], axis=1).astype(BF16)
-            block_of = i * rows // 256
-            at = pl.ds(pl.multiple_of(i * rows - block_of * 256, rows), rows)
-            mine = dproj[pl.ds(pl.multiple_of(i * rows, rows), rows)]
-            back[block_of, at] = contract_last(mine, mixer[:, : 2 * part]).astype(BF16)
 
     waits(inflow[1:4])
-    compute(0)
+    compute(0, 0, group // 2)
     next(output)
+    compute(0, group // 2)
     compute(1)
     if length == 4:
         advance(2)
     next(output)
+
+    @pl.loop(0, 8)
+    def _(i):
+        lines = dproj[pl.ds(pl.multiple_of(i * rows, rows), rows)]
+        back[i] = contract_last(lines, mixer[:, : 2 * part]).astype(BF16)
+
+    incoming = scatter_steps(back, o, None, sib_p, None, got_p, None, ss_p, rs_p)
+    next(incoming)
+    next(output)
+    next(incoming)
     compute(2)
-    next(output)
-    compute(3)
-    if length != 4:
-        advance(2)
+    advance(1 if length == 4 else 0)
     for _ in output:
         pass
-    for peer in gather_peers():
-        pl.semaphore_signal(free, inc=1, device_id=peer, device_id_type=MESH)
+    next(incoming)
+    compute(3)
+    advance(1 if length == 4 else 2)
+    pair = width // (4 * length)
+    waits(inflow[4:])
+    keeps = []
+    for n in (0, 1):
+
+        def finish_output(at):
+            whole = pl.ds(pl.multiple_of(at.start + n * half, 16), 16)
+            store_turned(mine.at[0, n], at, (residual[whole] + total[whole]).astype(BF16), length, pair)
+
+        rows_loop(half, finish_output)
+        keeps.append(
+            pltpu.make_async_copy(mine.at[0, n], out_out.at[pl.ds(n * half, half)], keep_s.at[n])
+        )
+        keeps[n].start()
+    keeps.append(pltpu.make_async_copy(above, grad_out, keep_s.at[2]))
     advance()
-    pl.semaphore_wait(free, 3)
-    incoming = scatter_steps(back, o, *scatter_refs)
-    next(incoming)
-    pair = out.shape[1] // (4 * length)
-
-    def finish_output(at):
-        store_turned(out, at, (residual[at] + total[at]).astype(BF16), length, pair)
-
-    waits(inflow[4:])
-    rows_loop(out.shape[0], finish_output)
-    keeps = local_copies(((out, out_out), (grad_o, grad_out)), keep_s)
-    keeps[0].start()
     for copy in gate:
         copy.wait()
     rows_sum = gp[z]
@@ -933,18 +956,17 @@
 
     def finish_grad(at):
         grad, gain_part = norm_rows_back(inputs[at].astype(F32), gains[0:1], o[at])
-        store_turned(grad_o, at, above[at] + grad, length, pair)
+        store_turned(above, at, above[at] + grad, length, pair)
         gain[...] += gain_part
 
-    half = grad_o.shape[0] // 2
     for name in incoming:
-        if name in ("sent", "early", "late"):
+        if name == "late":
             advance()
         if name == "low half":
             rows_loop(half, finish_grad)
         if name == "high half":
             rows_loop(half, finish_grad, half)
-            keeps[1].start()
+            keeps[2].start()
     while queue:
         advance()
     squares[...] = jnp.zeros_like(squares)
@@ -995,14 +1017,18 @@
             slots_a, slots_a, slots_b, slots_b,
             pltpu.VMEM((length - 1,) + pack, F32),
             pltpu.VMEM(pack, F32),
-            DMA((2, 2, length)), DMA((2, 2, length)), DMA((2, 2)), pltpu.SemaphoreType.REGULAR,
+            DMA((2, 2, length)), DMA((2, 2, length)), DMA((2, 2)),
             DMA, DMA((7,)), DMA((7,)), DMA((length,)), DMA((length,)), DMA, DMA,
             *held(dproj, mixed, mixer, residual, inputs, above, gains, gp),
-            pltpu.VMEM((rows, width), F32),
-            pltpu.VMEM((rows, width), BF16),
-            DMA((8,)), DMA((2,)),
-        ]
-        + scatter_scratch(rows // 2, width),
+            DMA((8,)), DMA((3,)),
+            pltpu.VMEM((4, 2, rows // 2, width), BF16),
+            pltpu.VMEM((4, 2, rows // 2, width), BF16),
+            pltpu.VMEM((6, rows // 2, width), BF16),
+            DMA((8,)), DMA((14,)), DMA((14,)),
+            pltpu.VMEM((4, 2, rows // 2, width), BF16),
+            pltpu.VMEM((6, rows // 2, width), BF16),
+            DMA((14,)), DMA((14,)),
+        ],
         compiler_params=params(collective_id),
         cost_estimate=pl.CostEstimate(
             flops=10 * tokens * model * dproj.shape[1] // 2, bytes_accessed=350 * 2**20, transcendentals=0

time: 591 us -> 591 us (level)
  no operation moved by 1% of the time
where the time goes in v9:
time: 591 us; the launch traced here: 587 us
  Pallas kernels  586 us (99%)
    pallas_call x1, Pallas kernels, closing(): pl.pallas_call(functools.partial(closing_kernel, length), out_shape=(jax....  96.8 us
    pallas_call x1, Pallas kernels, turn(): pl.pallas_call(functools.partial(turn_kernel, length, cuts), out_shape=(j...  87.7 us
    pallas_call x1, Pallas kernels, middle(): pl.pallas_call(functools.partial(middle_kernel, length), out_shape=(jax.S...  86.5 us
    pallas_call x1, Pallas kernels, first(): pl.pallas_call(functools.partial(first_kernel, length), out_shape=(jax.Sh...  85.7 us
    pallas_call x1, Pallas kernels, recur_backward(): pl.pallas_call(functools.partial(backward_kernel, length, cuts, head), ou...  52.3 us
    pallas_call x1, Pallas kernels, late_mlp(): pl.pallas_call(functools.partial(late_mlp_kernel, length, cuts), grid=(2...  50.4 us
    pallas_call x1, Pallas kernels, recur_forward(): pl.pallas_call(functools.partial(forward_kernel, length), out_shape=(jax....  47.7 us
    pallas_call x1, Pallas kernels, early_mlp(): pl.pallas_call(functools.partial(early_mlp_kernel, length), grid=(2 * STE...  38.7 us

profile of v9, /device:TPU:0, one launch (start us, length us, event | category | flops | bytes accessed | tf_op | source)
XLA Modules:
  0.0 586.6 jit_solution(6442895207253948961)
XLA Ops:
  0.7 85.7 %shard_map.304 = (bf16[8,256,2048]{2,1,0:T(8,128)(2,1)}, bf16[4,8,64,960]{3,2,1,0:T(8,128)(2,1)}, bf16[4,8,64,1024]{3,2,1,0:T(8,128)(2,1)}, bf16[4,8,64,512]{3,2...) custom-call(bf16[256,2048]{1,0:T(8,128)(2,1)} %bitcast.47, ...), custom_call_target="tpu_custom_call" | custom-call | bytes 314572800 | tf_op jit(solution)/shard_map/pallas_call | solution.py:1244
  86.3 47.7 %shard_map.305 = (bf16[4,512,320]{2,1,0:T(8,128)(2,1)}, f32[4,512,384]{2,1,0:T(8,128)}, f32[4,512,384]{2,1,0:T(8,128)}, f32[4,512,384]{2,1,0:T(8,128)}, f32[4,51...) custom-call(bf16[2048,2048]{1,0:T(8,128)(2,1)} %bitcast.32, ...), custom_call_target="tpu_custom_call", output_to_operand_aliasing={{11}: (5, {})} | custom-call | flops 1207959552 | bytes 104857600 | tf_op jit(solution)/shard_map/pallas_call | solution.py:1542
  134.1 86.5 %shard_map.306 = (f32[256,2048]{1,0:T(8,128)}, bf16[8,256,2048]{2,1,0:T(8,128)(2,1)}, bf16[4,8,64,1024]{3,2,1,0:T(8,128)(2,1)}, bf16[4,8,64,768]{3,2,1,0:T(8,128)(2,1)}) custom-call(bf16[2048,320]{1,0:T(8,128)(2,1)} %bitcast.44, bf16[2048,960]{1,0:T(8,128)(2,1)} %bitcast.29, ...), custom_call_target="tpu_custom_call", output_to_operand_aliasing={{2}: (4, {}), {3}: (5, {})} | custom-call | bytes 314572800 | tf_op jit(solution)/shard_map/pallas_call | solution.py:660
  220.6 38.7 %shard_map.307 = (bf16[2048,512]{1,0:T(8,128)(2,1)}, bf16[2048,1024]{1,0:T(8,128)(2,1)}, bf16[2048,512]{1,0:T(8,128)(2,1)}, bf16[2048,512]{1,0:T(8,128)(2,1)}, b...) custom-call(bf16[2048,2048]{1,0:T(8,128)(2,1)} %bitcast.59, ...), custom_call_target="tpu_custom_call", output_to_operand_aliasing={{5}: (6, {})} | custom-call | flops 25769803776 | bytes 52428800 | tf_op jit(solution)/shard_map/pallas_call | solution.py:1876
  259.3 50.4 %shard_map.308 = (bf16[2048,2048]{1,0:T(8,128)(2,1)}, bf16[2048,2048]{1,0:T(8,128)(2,1)}, bf16[2048,256]{1,0:T(8,128)(2,1)}, bf16[2048,256]{1,0:T(8,128)(2,1)}, ...) custom-call(bf16[2048,2048]{1,0:T(8,128)(2,1)} %bitcast.61, bf16[2048,2048]{1,0:T(8,128)(2,1)} %bitcast.57, ...), custom_call_target="tpu_custom_call" | custom-call | flops 32212254720 | bytes 73400320 | tf_op jit(solution)/shard_map/pallas_call | solution.py:1959
  309.7 87.7 %shard_map.309 = (f32[256,2048]{1,0:T(8,128)}, f32[8,2048]{1,0:T(8,128)}, bf16[8,256,2048]{2,1,0:T(8,128)(2,1)}, f32[8,256,384]{2,1,0:T(8,128)}, bf16[512,1152]{1,0:T(8,128)(2,1)}, /*index=5*/f32[8,128]{1,0:T(8,128)}) custom-call(bf16[8,256,2048]{2,1,0:T(8,128)(2,1)} %bitcast.34, f32[256,2048]{1,0:T(8,128)} %get-tuple-element.121.residual_in, ...), custom_call_target="tpu_custom_call" | custom-call | bytes 314572800 | tf_op jit(solution)/shard_map/pallas_call | solution.py:772
  397.4 52.3 %shard_map.310 = (bf16[4,512,640]{2,1,0:T(8,128)(2,1)}, f32[4,80,384]{2,1,0:T(8,128)}, bf16[512,512]{1,0:T(8,128)(2,1)}, f32[8,128]{1,0:T(8,128)}, bf16[8,64,640...) custom-call(f32[4,512,384]{2,1,0:T(8,128)} %bitcast.37, bf16[384,768]{1,0:T(8,128)(2,1)} %get-tuple-element.101.gate, ...), custom_call_target="tpu_custom_call" | custom-call | flops 1207959552 | bytes 125829120 | tf_op jit(solution)/shard_map/pallas_call | solution.py:1747
  449.7 96.8 %shard_map.311 = (f32[256,2048]{1,0:T(8,128)}, f32[8,2048]{1,0:T(8,128)}, f32[80,384]{1,0:T(8,128)}, bf16[256,2048]{1,0:T(8,128)(2,1)}, bf16[8,64,512]{2,1,0:T(8...) custom-call(bf16[2048,2048]{1,0:T(8,128)(2,1)} %bitcast.33, ...), custom_call_target="tpu_custom_call" | custom-call | flops 13421772800 | bytes 367001600 | tf_op jit(solution)/shard_map/pallas_call | solution.py:995
  546.5 22.4 %shard_map.312 = (bf16[8,64,448]{2,1,0:T(8,128)(2,1)}, f32[2,64]{1,0:T(2,128)}, f32[8,128]{1,0:T(8,128)}, f32[8,128]{1,0:T(8,128)}) custom-call(bf16[8,64,448]{2,1,0:T(8,128)(2,1)} %bitcast.53, f32[8,2048]{1,0:T(8,128)} %get-tuple-element.145.gain, f32[8,2048]{1,0:T(8,128)} %get-tuple-element.146.gain_two, f32[80,384]{1,0:T(8,128)} %get-tuple-element.147.gates.refs_12_, ...), custom_call_target="tpu_custom_call" | custom-call | tf_op jit(solution)/shard_map/pallas_call | solution.py:1339
  568.8 17.6 %shard_map.313 = (f32[64,7680]{1,0:T(8,128)}, f32[64,7680]{1,0:T(8,128)}, f32[64,7680]{1,0:T(8,128)}, f32[64,18432]{1,0:T(8,128)}, f32[64,18432]{1,0:T(8,128)}, ...) custom-call(f32[8,128]{1,0:T(8,128)} %get-tuple-element.152.factor, ...), custom_call_target="tpu_custom_call" | custom-call | bytes 40108032 | tf_op jit(solution)/shard_map/pallas_call | solution.py:2068

commit v10 on v9

--- a/solution.py
+++ b/solution.py
@@ -794,8 +794,8 @@
 
 def closing_kernel(
     length, x_in, dmz_in, dproj_in, mixed_in, mixer_in, q, residual_in, block, inputs_in, above_in, gains_in, gp_in,
-    grad_out, gain, gates_o, out_out, e_o, early_o, sums, squares,
-    early_sums, early_l, early_s, early_r, x_part, dmz_part, g, back, total, o, up_a, down_a, up_b, down_b, gp_got, gp_sum,
+    grad_out, gain, gates_o, out_out, e_o, sums, squares,
+    x_part, dmz_part, g, back, total, o, up_a, down_a, up_b, down_b, gp_got, gp_sum,
     ls, lr, load_s, loc, es, er, gate_s, gate_r, move_s, move_r,
     dproj, mixed, mixer, residual, inputs, above, gains, gp, in_s, keep_s,
     mine, sib_q, got_q, loc_q, ss_q, rs_q, sib_p, got_p, ss_p, rs_p,
@@ -970,15 +970,12 @@
     while queue:
         advance()
     squares[...] = jnp.zeros_like(squares)
-    line_a.end(early_sums, 0, squares)
-    early_copies, early_own = exchange_steps(early_sums, early_o, early_l, early_s, early_r)
-    line_b.end(sums, 0, squares)
+    line_a.end(sums, 0, squares)
+    line_b.end(sums, split, squares)
     pl.when(moves == 1)(lambda: move.wait())
     waits(keeps)
-    for copy in copies + early_copies:
-        copy.wait()
+    waits(copies)
     own.wait()
-    early_own.wait()
 
 
 def closing(x, dmz, dproj, mixed, mixer, q, residual, block, inputs, above, gains, gp, length, collective_id):
@@ -1000,14 +997,12 @@
             jax.ShapeDtypeStruct(pack, F32),
             jax.ShapeDtypeStruct((rows, width), BF16),
             jax.ShapeDtypeStruct(block.shape, BF16),
-            jax.ShapeDtypeStruct((8, share, split), BF16),
-            jax.ShapeDtypeStruct((line_rows, 3 * part - split), BF16),
+            jax.ShapeDtypeStruct((line_rows, 3 * part), BF16),
             TILE,
         ),
         in_specs=[ANY] * 12,
-        out_specs=(ANY, VM, VM, ANY, ANY, ANY, VM, VM),
+        out_specs=(ANY, VM, VM, ANY, ANY, VM, VM),
         scratch_shapes=[
-            pltpu.VMEM((line_rows, split), BF16), DMA, DMA((7,)), DMA((7,)),
             pltpu.VMEM((2, tokens, columns), BF16),
             pltpu.VMEM((2, tokens, columns), BF16),
             pltpu.VMEM((length, line_rows, 3 * part), BF16),
@@ -2184,7 +2179,7 @@
         (up_two, down_two), ((0, 0, h2), (1, 0, h2)), length, 6,
     )
     dproj = dproj.reshape(4 * span, 2 * r8)
-    input_grad, gain_one, gates_sum, block_output, back_two, mixer_early, mixer_sums, squares_three = closing(
+    input_grad, gain_one, gates_sum, block_output, back_two, mixer_sums, squares_three = closing(
         normed_one, dmz, dproj, mixed, mixer_full, mlp_part, residual, sums_two,
         inputs, grad_residual, gains, gate_back, length, 7,
     )
@@ -2192,7 +2187,6 @@
         mixer_sums.reshape(8, share, mixer_sums.shape[1]), gain_one, gain_two, gates_sum,
         (squares_zero, squares_one, squares_two, squares_three), length, 8,
     )
-    split = mixer_early.shape[2]
     mlp_sources = (
         [(0, h1, 0, f8), (h1, cut, hidden, f8)],
         [
@@ -2205,11 +2199,8 @@
     states = adam(
         (
             (
-                mixer_weight, first_mixer, second_mixer, (mixer_early, mixer_back),
-                (
-                    [(0, r8, 0, r8), (r8, split - r8, lru, r8)],
-                    [(0, 2 * r8 - split, lru + split - r8, r8), (2 * r8 - split, r8, 2 * lru, r8)],
-                ),
+                mixer_weight, first_mixer, second_mixer, (mixer_back,),
+                ([(n * r8, r8, n * lru, r8) for n in range(3)],),
             ),
             (mlp_weight, first_mlp, second_mlp, (back_zero, back_one, back_two), mlp_sources),
         ),

time: 591 us -> 596 us (level)
  no operation moved by 1% of the time
where the time goes in v10:
time: 596 us; the launch traced here: 590 us
  Pallas kernels  589 us (99%)
    pallas_call x1, Pallas kernels, closing(): pl.pallas_call(functools.partial(closing_kernel, length), out_shape=(jax....  96.9 us
    pallas_call x1, Pallas kernels, turn(): pl.pallas_call(functools.partial(turn_kernel, length, cuts), out_shape=(j...  87.7 us
    pallas_call x1, Pallas kernels, middle(): pl.pallas_call(functools.partial(middle_kernel, length), out_shape=(jax.S...  86.5 us
    pallas_call x1, Pallas kernels, first(): pl.pallas_call(functools.partial(first_kernel, length), out_shape=(jax.Sh...  85.7 us
    pallas_call x1, Pallas kernels, recur_backward(): pl.pallas_call(functools.partial(backward_kernel, length, cuts, head), ou...  52.3 us
    pallas_call x1, Pallas kernels, late_mlp(): pl.pallas_call(functools.partial(late_mlp_kernel, length, cuts), grid=(2...  50.4 us
    pallas_call x1, Pallas kernels, recur_forward(): pl.pallas_call(functools.partial(forward_kernel, length), out_shape=(jax....  47.7 us
    pallas_call x1, Pallas kernels, early_mlp(): pl.pallas_call(functools.partial(early_mlp_kernel, length), grid=(2 * STE...  38.7 us

profile of v10, /device:TPU:0, one launch (start us, length us, event | category | flops | bytes accessed | tf_op | source)
XLA Modules:
  0.0 589.5 jit_solution(12944907752931424971)
XLA Ops:
  0.7 85.7 %shard_map.304 = (bf16[8,256,2048]{2,1,0:T(8,128)(2,1)}, bf16[4,8,64,960]{3,2,1,0:T(8,128)(2,1)}, bf16[4,8,64,1024]{3,2,1,0:T(8,128)(2,1)}, bf16[4,8,64,512]{3,2...) custom-call(bf16[256,2048]{1,0:T(8,128)(2,1)} %bitcast.47, ...), custom_call_target="tpu_custom_call" | custom-call | bytes 314572800 | tf_op jit(solution)/shard_map/pallas_call | solution.py:1239
  86.3 47.7 %shard_map.305 = (bf16[4,512,320]{2,1,0:T(8,128)(2,1)}, f32[4,512,384]{2,1,0:T(8,128)}, f32[4,512,384]{2,1,0:T(8,128)}, f32[4,512,384]{2,1,0:T(8,128)}, f32[4,51...) custom-call(bf16[2048,2048]{1,0:T(8,128)(2,1)} %bitcast.32, ...), custom_call_target="tpu_custom_call", output_to_operand_aliasing={{11}: (5, {})} | custom-call | flops 1207959552 | bytes 104857600 | tf_op jit(solution)/shard_map/pallas_call | solution.py:1537
  134.1 86.5 %shard_map.306 = (f32[256,2048]{1,0:T(8,128)}, bf16[8,256,2048]{2,1,0:T(8,128)(2,1)}, bf16[4,8,64,1024]{3,2,1,0:T(8,128)(2,1)}, bf16[4,8,64,768]{3,2,1,0:T(8,128)(2,1)}) custom-call(bf16[2048,320]{1,0:T(8,128)(2,1)} %bitcast.44, bf16[2048,960]{1,0:T(8,128)(2,1)} %bitcast.29, ...), custom_call_target="tpu_custom_call", output_to_operand_aliasing={{2}: (4, {}), {3}: (5, {})} | custom-call | bytes 314572800 | tf_op jit(solution)/shard_map/pallas_call | solution.py:660
  220.6 38.7 %shard_map.307 = (bf16[2048,512]{1,0:T(8,128)(2,1)}, bf16[2048,1024]{1,0:T(8,128)(2,1)}, bf16[2048,512]{1,0:T(8,128)(2,1)}, bf16[2048,512]{1,0:T(8,128)(2,1)}, b...) custom-call(bf16[2048,2048]{1,0:T(8,128)(2,1)} %bitcast.59, ...), custom_call_target="tpu_custom_call", output_to_operand_aliasing={{5}: (6, {})} | custom-call | flops 25769803776 | bytes 52428800 | tf_op jit(solution)/shard_map/pallas_call | solution.py:1871
  259.3 50.4 %shard_map.308 = (bf16[2048,2048]{1,0:T(8,128)(2,1)}, bf16[2048,2048]{1,0:T(8,128)(2,1)}, bf16[2048,256]{1,0:T(8,128)(2,1)}, bf16[2048,256]{1,0:T(8,128)(2,1)}, ...) custom-call(bf16[2048,2048]{1,0:T(8,128)(2,1)} %bitcast.61, bf16[2048,2048]{1,0:T(8,128)(2,1)} %bitcast.57, ...), custom_call_target="tpu_custom_call" | custom-call | flops 32212254720 | bytes 73400320 | tf_op jit(solution)/shard_map/pallas_call | solution.py:1954
  309.7 87.7 %shard_map.309 = (f32[256,2048]{1,0:T(8,128)}, f32[8,2048]{1,0:T(8,128)}, bf16[8,256,2048]{2,1,0:T(8,128)(2,1)}, f32[8,256,384]{2,1,0:T(8,128)}, bf16[512,1152]{1,0:T(8,128)(2,1)}, /*index=5*/f32[8,128]{1,0:T(8,128)}) custom-call(bf16[8,256,2048]{2,1,0:T(8,128)(2,1)} %bitcast.34, f32[256,2048]{1,0:T(8,128)} %get-tuple-element.120.residual_in, ...), custom_call_target="tpu_custom_call" | custom-call | bytes 314572800 | tf_op jit(solution)/shard_map/pallas_call | solution.py:772
  397.4 52.3 %shard_map.310 = (bf16[4,512,640]{2,1,0:T(8,128)(2,1)}, f32[4,80,384]{2,1,0:T(8,128)}, bf16[512,512]{1,0:T(8,128)(2,1)}, f32[8,128]{1,0:T(8,128)}, bf16[8,64,640...) custom-call(f32[4,512,384]{2,1,0:T(8,128)} %bitcast.37, bf16[384,768]{1,0:T(8,128)(2,1)} %get-tuple-element.100.gate, ...), custom_call_target="tpu_custom_call" | custom-call | flops 1207959552 | bytes 125829120 | tf_op jit(solution)/shard_map/pallas_call | solution.py:1742
  449.7 96.9 %shard_map.311 = (f32[256,2048]{1,0:T(8,128)}, f32[8,2048]{1,0:T(8,128)}, f32[80,384]{1,0:T(8,128)}, bf16[256,2048]{1,0:T(8,128)(2,1)}, bf16[8,64,512]{2,1,0:T(8...) custom-call(bf16[2048,2048]{1,0:T(8,128)(2,1)} %bitcast.33, bf16[2048,2048]{1,0:T(8,128)(2,1)} %bitcast.54, ...), custom_call_target="tpu_custom_call" | custom-call | flops 13421772800 | bytes 367001600 | tf_op jit(solution)/shard_map/pallas_call | solution.py:992
  546.5 25.2 %shard_map.312 = (bf16[8,64,960]{2,1,0:T(8,128)(2,1)}, f32[2,64]{1,0:T(2,128)}, f32[8,128]{1,0:T(8,128)}, f32[8,128]{1,0:T(8,128)}) custom-call(bf16[8,64,960]{2,1,0:T(8,128)(2,1)} %bitcast.52, f32[8,2048]{1,0:T(8,128)} %get-tuple-element.144.gain, f32[8,2048]{1,0:T(8,128)} %get-tuple-element.145.gain_two, f32[80,384]{1,0:T(8,128)} %get-tuple-element.146.gates.refs_11_, ...), custom_call_target="tpu_custom_call" | custom-call | tf_op jit(solution)/shard_map/pallas_call | solution.py:1334
  571.8 17.5 %shard_map.313 = (f32[64,7680]{1,0:T(8,128)}, f32[64,7680]{1,0:T(8,128)}, f32[64,7680]{1,0:T(8,128)}, f32[64,18432]{1,0:T(8,128)}, f32[64,18432]{1,0:T(8,128)}, ...) custom-call(f32[8,128]{1,0:T(8,128)} %get-tuple-element.151.factor, ...), custom_call_target="tpu_custom_call" | custom-call | bytes 40108032 | tf_op jit(solution)/shard_map/pallas_call | solution.py:2063

commit v11 on v9

--- a/solution.py
+++ b/solution.py
@@ -557,7 +557,7 @@
     return [device(y, c, lax.rem(z + 1, length), x), device(y, c, lax.rem(z + length - 1, length), x)]
 
 
-def rows_loop(rows, body, start=0, unroll=2):
+def rows_loop(rows, body, start=0, unroll=4):
     @pl.loop(start // 16, (start + rows) // 16, unroll=unroll)
     def _(i):
         body(pl.ds(pl.multiple_of(i * 16, 16), 16))

time: 591 us -> 591 us (level)
  no operation moved by 1% of the time
where the time goes in v11:
time: 591 us; the launch traced here: 586 us
  Pallas kernels  585 us (99%)
    pallas_call x1, Pallas kernels, closing(): pl.pallas_call(functools.partial(closing_kernel, length), out_shape=(jax....  97.4 us
    pallas_call x1, Pallas kernels, turn(): pl.pallas_call(functools.partial(turn_kernel, length, cuts), out_shape=(j...  88.4 us
    pallas_call x1, Pallas kernels, middle(): pl.pallas_call(functools.partial(middle_kernel, length), out_shape=(jax.S...  86.5 us
    pallas_call x1, Pallas kernels, first(): pl.pallas_call(functools.partial(first_kernel, length), out_shape=(jax.Sh...  85.7 us
    pallas_call x1, Pallas kernels, recur_backward(): pl.pallas_call(functools.partial(backward_kernel, length, cuts, head), ou...  51.6 us
    pallas_call x1, Pallas kernels, late_mlp(): pl.pallas_call(functools.partial(late_mlp_kernel, length, cuts), grid=(2...  50.3 us
    pallas_call x1, Pallas kernels, recur_forward(): pl.pallas_call(functools.partial(forward_kernel, length), out_shape=(jax....  47.7 us
    pallas_call x1, Pallas kernels, early_mlp(): pl.pallas_call(functools.partial(early_mlp_kernel, length), grid=(2 * STE...  38.7 us

profile of v11, /device:TPU:0, one launch (start us, length us, event | category | flops | bytes accessed | tf_op | source)
XLA Modules:
  0.0 586.3 jit_solution(3872431327005963970)
XLA Ops:
  0.7 85.7 %shard_map.304 = (bf16[8,256,2048]{2,1,0:T(8,128)(2,1)}, bf16[4,8,64,960]{3,2,1,0:T(8,128)(2,1)}, bf16[4,8,64,1024]{3,2,1,0:T(8,128)(2,1)}, bf16[4,8,64,512]{3,2...) custom-call(bf16[256,2048]{1,0:T(8,128)(2,1)} %bitcast.47, ...), custom_call_target="tpu_custom_call" | custom-call | bytes 314572800 | tf_op jit(solution)/shard_map/pallas_call | solution.py:1244
  86.3 47.7 %shard_map.305 = (bf16[4,512,320]{2,1,0:T(8,128)(2,1)}, f32[4,512,384]{2,1,0:T(8,128)}, f32[4,512,384]{2,1,0:T(8,128)}, f32[4,512,384]{2,1,0:T(8,128)}, f32[4,51...) custom-call(bf16[2048,2048]{1,0:T(8,128)(2,1)} %bitcast.32, ...), custom_call_target="tpu_custom_call", output_to_operand_aliasing={{11}: (5, {})} | custom-call | flops 1207959552 | bytes 104857600 | tf_op jit(solution)/shard_map/pallas_call | solution.py:1542
  134.1 86.5 %shard_map.306 = (f32[256,2048]{1,0:T(8,128)}, bf16[8,256,2048]{2,1,0:T(8,128)(2,1)}, bf16[4,8,64,1024]{3,2,1,0:T(8,128)(2,1)}, bf16[4,8,64,768]{3,2,1,0:T(8,128)(2,1)}) custom-call(bf16[2048,320]{1,0:T(8,128)(2,1)} %bitcast.44, bf16[2048,960]{1,0:T(8,128)(2,1)} %bitcast.29, ...), custom_call_target="tpu_custom_call", output_to_operand_aliasing={{2}: (4, {}), {3}: (5, {})} | custom-call | bytes 314572800 | tf_op jit(solution)/shard_map/pallas_call | solution.py:660
  220.6 38.7 %shard_map.307 = (bf16[2048,512]{1,0:T(8,128)(2,1)}, bf16[2048,1024]{1,0:T(8,128)(2,1)}, bf16[2048,512]{1,0:T(8,128)(2,1)}, bf16[2048,512]{1,0:T(8,128)(2,1)}, b...) custom-call(bf16[2048,2048]{1,0:T(8,128)(2,1)} %bitcast.59, ...), custom_call_target="tpu_custom_call", output_to_operand_aliasing={{5}: (6, {})} | custom-call | flops 25769803776 | bytes 52428800 | tf_op jit(solution)/shard_map/pallas_call | solution.py:1876
  259.3 50.3 %shard_map.308 = (bf16[2048,2048]{1,0:T(8,128)(2,1)}, bf16[2048,2048]{1,0:T(8,128)(2,1)}, bf16[2048,256]{1,0:T(8,128)(2,1)}, bf16[2048,256]{1,0:T(8,128)(2,1)}, ...) custom-call(bf16[2048,2048]{1,0:T(8,128)(2,1)} %bitcast.61, bf16[2048,2048]{1,0:T(8,128)(2,1)} %bitcast.57, ...), custom_call_target="tpu_custom_call" | custom-call | flops 32212254720 | bytes 73400320 | tf_op jit(solution)/shard_map/pallas_call | solution.py:1959
  309.6 88.4 %shard_map.309 = (f32[256,2048]{1,0:T(8,128)}, f32[8,2048]{1,0:T(8,128)}, bf16[8,256,2048]{2,1,0:T(8,128)(2,1)}, f32[8,256,384]{2,1,0:T(8,128)}, bf16[512,1152]{1,0:T(8,128)(2,1)}, /*index=5*/f32[8,128]{1,0:T(8,128)}) custom-call(bf16[8,256,2048]{2,1,0:T(8,128)(2,1)} %bitcast.34, f32[256,2048]{1,0:T(8,128)} %get-tuple-element.121.residual_in, ...), custom_call_target="tpu_custom_call" | custom-call | bytes 314572800 | tf_op jit(solution)/shard_map/pallas_call | solution.py:772
  398.0 51.6 %shard_map.310 = (bf16[4,512,640]{2,1,0:T(8,128)(2,1)}, f32[4,80,384]{2,1,0:T(8,128)}, bf16[512,512]{1,0:T(8,128)(2,1)}, f32[8,128]{1,0:T(8,128)}, bf16[8,64,640...) custom-call(f32[4,512,384]{2,1,0:T(8,128)} %bitcast.37, bf16[384,768]{1,0:T(8,128)(2,1)} %get-tuple-element.101.gate, ...), custom_call_target="tpu_custom_call" | custom-call | flops 1207959552 | bytes 125829120 | tf_op jit(solution)/shard_map/pallas_call | solution.py:1747
  449.7 97.4 %shard_map.311 = (f32[256,2048]{1,0:T(8,128)}, f32[8,2048]{1,0:T(8,128)}, f32[80,384]{1,0:T(8,128)}, bf16[256,2048]{1,0:T(8,128)(2,1)}, bf16[8,64,512]{2,1,0:T(8...) custom-call(bf16[2048,2048]{1,0:T(8,128)(2,1)} %bitcast.33, ...), custom_call_target="tpu_custom_call" | custom-call | flops 13421772800 | bytes 367001600 | tf_op jit(solution)/shard_map/pallas_call | solution.py:995
  547.1 21.4 %shard_map.312 = (bf16[8,64,448]{2,1,0:T(8,128)(2,1)}, f32[2,64]{1,0:T(2,128)}, f32[8,128]{1,0:T(8,128)}, f32[8,128]{1,0:T(8,128)}) custom-call(bf16[8,64,448]{2,1,0:T(8,128)(2,1)} %bitcast.53, f32[8,2048]{1,0:T(8,128)} %get-tuple-element.145.gain, f32[8,2048]{1,0:T(8,128)} %get-tuple-element.146.gain_two, f32[80,384]{1,0:T(8,128)} %get-tuple-element.147.gates.refs_12_, ...), custom_call_target="tpu_custom_call" | custom-call | tf_op jit(solution)/shard_map/pallas_call | solution.py:1339
  568.5 17.6 %shard_map.313 = (f32[64,7680]{1,0:T(8,128)}, f32[64,7680]{1,0:T(8,128)}, f32[64,7680]{1,0:T(8,128)}, f32[64,18432]{1,0:T(8,128)}, f32[64,18432]{1,0:T(8,128)}, ...) custom-call(f32[8,128]{1,0:T(8,128)} %get-tuple-element.152.factor, ...), custom_call_target="tpu_custom_call" | custom-call | bytes 40108032 | tf_op jit(solution)/shard_map/pallas_call | solution.py:2068
